TPU v7x, 32 devices: a whole 2x2x4 slice. The times are simulated.
32 devices in a mesh: section: 2 (over x), expert: 4 (over z), hidden: 4 (over y, core).
Axes of the slice: x: 2, y: 2, z: 4, core: 2. Of those that a mesh axis runs over, the one named last changes fastest.
Arguments:
- tokens: bfloat16 [4, 64, 7168], P(None, 'expert', 'hidden'), may hold values from -12 to 12
- gate_up: bfloat16 [2, 7168, 2, 16384], P('section', 'hidden', None, 'expert'), may hold values from -0.0625 to 0.0625
- down_proj: bfloat16 [2, 16384, 7168], P('section', 'expert', 'hidden'), may hold values from -0.1875 to 0.1875
- routes: int32 [2, 4, 64, 2], P('section', None, 'expert'), may hold values from 0 to 15, all different within a row; in each aligned block of 16 rows (0 to 15, 16 to 31, ..., all dimensions but the last counted through in order) at most 3 rows name the same one
- gate_weights: bfloat16 [2, 4, 64, 2], P('section', None, 'expert'), may hold values from 0.099609375 to 0.59765625
Outputs:
- layer_outputs: bfloat16 [2, 4, 64, 7168], P('section', None, 'expert', 'hidden')
Inputs may be any that keep to these rules, and one draw needn't show every extreme that they name: `routes`: in every layer and micro-batch a token names 2 different experts, and the 16 tokens of one device (aligned blocks of 16 rows) name any one expert at most 3 times; some expert is named exactly 3 times in some block.
All inputs are finite; a program needn't handle non-finite values.
Results may differ from a plain program's by a relative error of at most 0.008.
Values may be sent and summed in bfloat16 or wider, within the bound.
No kernel may reach another device: no remote copies, remote signals or barrier semaphores. Data moves between devices by JAX's collectives and lax.ppermute only.
A program may use at most 192 MiB of HBM per device.

v0:
```python
import functools

import jax
import jax.numpy as jnp
from jax import lax
from jax.experimental import pallas as pl
from jax.experimental.pallas import tpu as pltpu
from jax.sharding import PartitionSpec as P

D = 7168
FFE = 1024
CAP = 3
EPS = 1e-06
EXTRA = 16
VMEM = pl.BlockSpec(memory_space=pltpu.VMEM)
HBM = pl.BlockSpec(memory_space=pltpu.HBM)
BF16 = jnp.bfloat16
F32 = jnp.float32
I32 = jnp.int32
ACROSS = (((1,), (1,)), ((), ()))
DOWN = (((0,), (0,)), ((), ()))


def padded(count, unit):
    return -(-count // unit) * unit


def dot(a, b, dims=(((1,), (0,)), ((), ()))):
    return lax.dot_general(a, b, dims, preferred_element_type=F32)


def one_hot(mask):
    return jnp.where(mask, F32(1.0), F32(0.0))


def divided(value, divisor):
    if divisor == 1:
        return value, jnp.zeros_like(value)
    quotient = lax.shift_right_logical(value * (2**20 // divisor + 1), 20)
    return quotient, value - quotient * divisor


class Sizes:
    def __init__(self, tokens, gate_up, peers, splits):
        self.peers, self.splits = peers, splits
        self.micro, self.tok, self.width = tokens.shape
        self.rows = self.micro * self.tok
        self.units_dev = gate_up.shape[3]
        self.units = min(FFE, self.units_dev)
        self.half = self.units // 2
        self.local = self.units_dev // self.units
        self.groups = 2 if self.local % 2 == 0 else 1
        self.members = self.local // self.groups
        self.slots = self.micro * CAP
        self.pay = padded(self.members * self.slots, 8)
        self.pieces = peers if peers <= 8 else 1
        self.near = self.pieces // 2
        self.group_pay = peers * self.pay
        self.piece = self.group_pay // self.pieces
        self.all_pay = self.groups * self.group_pay
        self.all_piece = self.groups * self.piece
        self.each = padded(peers * self.slots, 8)
        self.group_each = self.members * self.each
        self.partial = (self.group_each + EXTRA, 2 * self.half)

    def order(self):
        shape = (self.group_each, self.group_pay)
        row = lax.broadcasted_iota(I32, (self.group_each, 1), 0)
        expert, rest = divided(row, self.each)
        step, slot = divided(rest, self.slots)
        target = jnp.where(step < self.peers, step * self.pay + expert * self.slots + slot, -1)
        return one_hot(lax.broadcasted_iota(I32, shape, 1) == target).astype(BF16)


def line_up(z, ref):
    total = None
    for batch in range(z.micro):
        shape = (z.tok, z.rows)
        place = lax.broadcasted_iota(I32, shape, 1) == lax.broadcasted_iota(I32, shape, 0) + batch * z.tok
        value = dot(ref[batch].astype(F32).astype(BF16), one_hot(place).astype(BF16))
        total = value if total is None else total + value
    return total


def slot_hits(z, routes_ref):
    row = lax.broadcasted_iota(I32, (z.all_pay, 1), 0)
    step, rest = divided(row, z.groups * z.pay)
    group, place = divided(rest, z.pay)
    member, inside = divided(place, z.slots)
    batch, rank = divided(inside, CAP)
    rank = jnp.where(member < z.members, rank, -1)
    owner = step ^ lax.axis_index("expert") if z.pieces > 1 else step
    if z.units_dev >= FFE:
        expert = owner * z.local + group * z.members + member
    else:
        expert = lax.shift_right_logical(owner, (FFE // z.units_dev).bit_length() - 1)
    routes = line_up(z, routes_ref)
    token = lax.broadcasted_iota(I32, (z.all_pay, z.rows), 1)
    start = batch * z.tok
    same = (token >= start) & (token < start + z.tok)
    expert = expert.astype(F32)
    first = (routes[0:1, :] == expert) & same
    second = (routes[1:2, :] == expert) & same
    chosen = one_hot(first | second)
    shape = (z.rows, z.rows)
    before = lax.broadcasted_iota(I32, shape, 0) < lax.broadcasted_iota(I32, shape, 1)
    count = dot(chosen.astype(BF16), one_hot(before).astype(BF16))
    hits = jnp.where(count == rank.astype(F32), chosen, F32(0.0))
    return hits, first, second


def send_rows(z, hits, rows, outs, first):
    low = first * z.all_piece
    value = dot(hits[low:low + len(outs) * z.all_piece].astype(BF16), rows)
    for index, out in enumerate(outs):
        out[...] = value[index * z.all_piece:(index + 1) * z.all_piece].astype(BF16)


def near_kernel(z, routes_ref, rows_ref, *outs):
    hits, _, _ = slot_hits(z, routes_ref)
    send_rows(z, hits, rows_ref[...], outs, 0)


def group_rows(z, group, pieces):
    result = []
    for piece in pieces:
        value = piece[...].astype(F32)
        for step in range(z.peers // z.pieces):
            low = (step * z.groups + group) * z.pay
            result.append(value[low:low + z.pay])
    return jnp.concatenate(result, axis=0)


def pack_kernel(z, *refs):
    sources, outs = refs[:3], refs[3:-4]
    routes_ref, gates_ref, rows_ref, sems = refs[-4:]
    copies = [
        pltpu.make_async_copy(source, target, sems.at[index])
        for index, (source, target) in enumerate(zip(sources, refs[-4:-1]))
    ]
    for copy in copies:
        copy.start()
    for copy in copies:
        copy.wait()
    hits, first, second = slot_hits(z, routes_ref)
    gates = line_up(z, gates_ref)
    weight = jnp.where(first, gates[0:1, :], F32(0.0)) + jnp.where(second, gates[1:2, :], F32(0.0))
    outs[-1][...] = (hits * weight).astype(BF16)
    send_rows(z, hits, rows_ref[...], outs[:-1], 0)


def load_kernel(z, parts, gate_up, *refs):
    outs, sems = refs[:-1], refs[-1]
    flat = gate_up.reshape(2 * z.width, z.units_dev)
    depth = 2 * z.width // parts
    copies = []
    for expert in range(z.local):
        for part in range(parts):
            copies.append(
                pltpu.make_async_copy(
                    flat.at[pl.ds(part * depth, depth), pl.ds(expert * z.units, z.units)],
                    outs[expert].at[pl.ds(part * depth, depth)],
                    sems.at[expert * parts + part],
                )
            )
    for copy in copies:
        copy.start()
    for copy in copies:
        copy.wait()


def load_down_kernel(z, group, down_proj, *refs):
    outs, sems = refs[:z.members], refs[-1]
    copies = []
    for index in range(z.members):
        low = (group * z.members + index) * z.units
        copies.append(
            pltpu.make_async_copy(down_proj.at[0, pl.ds(low, z.units), :], outs[index], sems.at[index])
        )
    for copy in copies:
        copy.start()
    for copy in copies:
        copy.wait()


def split_sums(sums, lanes):
    high = sums.astype(BF16).astype(F32)
    row = lax.broadcasted_iota(I32, sums.shape, 0)
    both = jnp.where(row == 0, high, jnp.where(row == 1, sums - high, F32(0.0)))
    if both.shape[1] < lanes:
        both = jnp.concatenate([both, jnp.zeros((EXTRA, lanes - both.shape[1]), F32)], axis=1)
    return both


def up_kernel(z, group, *refs):
    weights, refs = refs[:z.members], refs[z.members:]
    received, refs = refs[:z.pieces], refs[z.pieces:]
    own, sent, spread, staged = refs
    rows = dot(z.order(), group_rows(z, group, received).astype(BF16))
    squares = rows * rows
    high = squares.astype(BF16)
    low = (squares - high.astype(F32)).astype(BF16)
    ones = jnp.ones((EXTRA, z.width), BF16)
    sums = dot(ones, high, ACROSS) + dot(ones, low, ACROSS)
    rows = rows.astype(BF16)
    block = 128
    shape = (block, 2 * block)
    target = lax.broadcasted_iota(I32, shape, 1) - 2 * lax.broadcasted_iota(I32, shape, 0)
    placing = [one_hot(target == side).astype(BF16) for side in range(2)]
    for piece in range(z.width // block):
        columns = slice(piece * block, (piece + 1) * block)
        gate, up = dot(rows[:, columns], placing[0]), dot(rows[:, columns], placing[1])
        for expert in range(z.members):
            here = slice(expert * z.each, (expert + 1) * z.each)
            both = jnp.concatenate([gate[here], up[here]], axis=0).astype(BF16)
            spread[expert, :, 2 * piece * block:2 * (piece + 1) * block] = both
    totals = [dot(spread[expert], weights[expert][...]) for expert in range(z.members)]
    extra = split_sums(sums, 2 * z.half)
    for side in range(2):
        columns = slice(side * z.half, (side + 1) * z.half)
        gate = jnp.concatenate([total[:z.each, columns] for total in totals], axis=0)
        up = jnp.concatenate([total[z.each:, columns] for total in totals], axis=0)
        staged[side, :z.group_each, :] = jnp.concatenate([gate, up], axis=1)
        staged[side, z.group_each:, :] = extra
    core = lax.axis_index("hidden") & 1
    own[...] = staged[core]
    sent[...] = staged[1 - core].astype(BF16)


def joined(z, refs):
    total = refs[0][...].astype(F32)
    for ref in refs[1:]:
        total = total + ref[...].astype(F32)
    products, extra = total[:z.group_each], total[z.group_each:]
    row = lax.broadcasted_iota(I32, extra.shape, 0)
    sums = jnp.sum(jnp.where(row < 2, extra, F32(0.0)), axis=0, keepdims=True)
    return products, sums


def pair_kernel(z, own, other, out):
    products, sums = joined(z, (own, other))
    out[:z.group_each, :] = products.astype(BF16)
    sums = jnp.broadcast_to(sums, (EXTRA, 2 * z.half))
    out[z.group_each:, :] = split_sums(sums, 2 * z.half).astype(BF16)


def act_kernel(z, *refs):
    out = refs[-1]
    products, sums = joined(z, refs[:-1])
    shape = (z.group_each, z.group_each)
    diagonal = lax.broadcasted_iota(I32, shape, 0) == lax.broadcasted_iota(I32, shape, 1)
    sums = jnp.sum(jnp.where(diagonal, sums[:, :z.group_each], F32(0.0)), axis=1, keepdims=True)
    scale = lax.rsqrt(sums / D + EPS)
    gate = scale * products[:, :z.half]
    up = scale * products[:, z.half:]
    out[...] = (gate / (F32(1.0) + jnp.exp(-gate)) * up).astype(BF16)


def down_kernel(z, *refs):
    weights, refs = refs[:z.members], refs[z.members:]
    halves, outs = refs[:2], refs[2:]
    if len(outs) > z.pieces:
        outs[-1][...] = outs[0][...]
        outs = outs[1:-1]
    core = lax.axis_index("hidden") & 1
    results = []
    for expert in range(z.members):
        total = None
        for step in range(2):
            units = halves[step][...].astype(F32)[expert * z.each:(expert + 1) * z.each].astype(BF16)
            low = pl.multiple_of((core ^ step) * z.half, z.half)
            value = dot(units, weights[expert][pl.ds(low, z.half), :])
            total = value if total is None else total + value
        results.append(total)
    value = dot(z.order(), jnp.concatenate(results, axis=0).astype(BF16), DOWN)
    for index, out in enumerate(outs):
        out[...] = value[index * z.piece:(index + 1) * z.piece].astype(BF16)


def combine_kernel(z, tick, last, weight_ref, rows_ref, kept_ref, *refs):
    count = z.groups * z.pieces
    returned, refs = refs[:count], refs[count:]
    stacked = []
    for piece in range(z.pieces):
        values = [returned[group * z.pieces + piece][...].astype(F32) for group in range(z.groups)]
        for step in range(z.peers // z.pieces):
            stacked += [value[step * z.pay:(step + 1) * z.pay] for value in values]
    stacked = jnp.concatenate(stacked, axis=0).astype(BF16)
    mixed = dot(weight_ref[...], stacked, DOWN)
    value = (rows_ref[...].astype(F32) + mixed).astype(BF16)
    if last:
        refs[0][...] = jnp.where(lax.axis_index("section") == tick, value, kept_ref[...])
        return
    routes_ref, out, outs = refs[0], refs[1], refs[2:]
    out[...] = jnp.where(lax.axis_index("section") == tick, value, kept_ref[...])
    hits, _, _ = slot_hits(z, routes_ref)
    send_rows(z, hits, value, outs, z.near)


def after_waits(waits, kernel, *refs):
    return kernel(*refs[waits:])


def call(kernel, sizes, megabytes, outs, in_specs, scratch, *args, waits=()):
    results = pl.pallas_call(
        functools.partial(after_waits, len(waits), functools.partial(kernel, *sizes)),
        out_shape=outs,
        in_specs=[VMEM] * len(waits) + in_specs,
        out_specs=[VMEM] * len(outs),
        scratch_shapes=scratch,
        compiler_params=pltpu.CompilerParams(vmem_limit_bytes=megabytes * 2**20),
    )(*waits, *args)
    return list(results)


def on_device(tokens, gate_up, down_proj, routes, gate_weights):
    sections = lax.axis_size("section")
    z = Sizes(tokens, gate_up, lax.axis_size("expert"), lax.axis_size("hidden"))
    parts = 2 if z.width % 256 == 0 else 1
    shape = jax.ShapeDtypeStruct
    pay = shape((z.piece, z.width), BF16)
    all_pay = shape((z.all_piece, z.width), BF16)
    whole = shape((z.rows, z.width), BF16)
    steps = sorted(range(z.peers), key=lambda step: -step.bit_length())

    def swap(value, step):
        pairs = [(i, i ^ step) for i in range(z.splits)]
        return lax.ppermute(value, "hidden", pairs)

    def exchanged(pieces):
        if z.pieces == 1:
            return [lax.all_to_all(pieces[0], "expert", split_axis=0, concat_axis=0, tiled=True)]
        result = list(pieces)
        for step in steps[:-1]:
            pairs = [(i, i ^ step) for i in range(z.peers)]
            result[step] = lax.ppermute(pieces[step], "expert", pairs)
        return result

    def relayed(pieces, kept, tick):
        hop = [(tick, tick + 1)]
        rows = lax.ppermute(kept, "section", hop)
        if z.pieces == 1:
            return rows, [lax.ppermute(exchanged(pieces)[0], "section", hop)]
        far = {}
        for step in steps:
            if step >= z.near:
                pairs = [(tick * z.peers + i, (tick + 1) * z.peers + (i ^ step)) for i in range(z.peers)]
                far[step] = lax.ppermute(pieces[step - z.near], ("section", "expert"), pairs)
        result = call(near_kernel, (z,), 4, [all_pay] * z.near, [VMEM] * 2, [], routes, rows)
        for step in range(1, z.near):
            pairs = [(i, i ^ step) for i in range(z.peers)]
            result[step] = lax.ppermute(result[step], "expert", pairs)
        return rows, result + [far[step] for step in range(z.near, z.peers)]

    def load_down(group, after):
        return call(
            load_down_kernel, (z, group), 1,
            [pltpu.VMEM((z.units, z.width), BF16)] * z.members,
            [HBM], [pltpu.SemaphoreType.DMA((z.members,))], down_proj, waits=[after],
        )

    def products(received, group, waits):
        own, sent = call(
            up_kernel, (z, group), 6,
            [shape(z.partial, F32), shape(z.partial, BF16)],
            [VMEM] * (z.members + z.pieces),
            [
                pltpu.VMEM((z.members, 2 * z.each, 2 * z.width), BF16),
                pltpu.VMEM((2,) + z.partial, F32),
            ],
            *wide[group * z.members:(group + 1) * z.members], *received,
            waits=waits if group else tall[0][:1],
        )
        return own, swap(sent, 1)

    def pair_sums(own, other, waits):
        pair = call(
            pair_kernel, (z,), 2, [shape(z.partial, BF16)], [VMEM] * 2, [], own, other, waits=waits
        )[0]
        return [pair] + [swap(pair, step) for step in range(2, z.splits, 2)]

    def activated(pairs, waits):
        units = call(
            act_kernel, (z,), 2,
            [shape((z.group_each, z.half), BF16)], [VMEM] * len(pairs), [], *pairs, waits=waits,
        )[0]
        return units, swap(units, 1)

    def down(halves, group, hand_on):
        return call(
            down_kernel, (z,), 4,
            [pay] * z.pieces + [shape(value.shape, value.dtype) for value in hand_on],
            [VMEM] * (z.members + 2 + len(hand_on)), [],
            *tall[group], *halves, *hand_on,
        )

    routes = routes[0].transpose(0, 2, 1)
    gates = gate_weights[0].transpose(0, 2, 1)
    rows = tokens.reshape(z.rows, z.width)
    kept = rows
    *sent, weight = call(
        pack_kernel, (z,), 3,
        [all_pay] * z.pieces + [shape((z.all_pay, z.rows), BF16)],
        [HBM] * 3,
        [
            pltpu.VMEM(routes.shape, routes.dtype),
            pltpu.VMEM(gates.shape, gates.dtype),
            pltpu.VMEM(rows.shape, rows.dtype),
            pltpu.SemaphoreType.DMA((3,)),
        ],
        *(pltpu.with_memory_space_constraint(value, pltpu.HBM) for value in (routes, gates, rows)),
    )
    received = exchanged(sent)
    gate_up = pltpu.with_memory_space_constraint(gate_up, pltpu.HBM)
    down_proj = pltpu.with_memory_space_constraint(down_proj, pltpu.HBM)
    wide = call(
        load_kernel, (z, parts), 1,
        [pltpu.VMEM((2 * z.width, z.units), BF16)] * z.local,
        [HBM], [pltpu.SemaphoreType.DMA((z.local * parts,))], gate_up, waits=[weight],
    )
    tall = [load_down(0, wide[-1])]
    groups = range(z.groups)
    for tick in range(sections):
        last = tick == sections - 1
        sums, returned = [], []
        early, waits = [], []
        for group in groups:
            own, other = products(received, group, [sums[-1][0]] if group else [])
            sums.append(pair_sums(own, other, waits))
            if tick == 0 and group + 1 < z.groups:
                tall.append(load_down(group + 1, sums[-1][0]))
                early = tall[-1][:1]
            if group == 0:
                halves = activated(sums[0], early)
                waits = list(halves[:1])
        for group in groups:
            if group:
                halves = activated(sums[group], outgoing[:1])
            hand_on = [routes] if tick == 0 and group == z.groups - 1 else []
            outgoing = down(halves, group, hand_on)
            if hand_on:
                pairs = [(i + 1, i) for i in range(sections - 1)]
                following = lax.ppermute(outgoing.pop(), "section", pairs)
            returned += exchanged(outgoing)
        kept, *sent = call(
            combine_kernel, (z, tick, last), 4,
            [whole] if last else [whole] + [all_pay] * (z.pieces - z.near),
            [VMEM] * (3 + len(returned) + (not last)), [],
            weight, rows, kept, *returned, *([] if last else [following]),
        )
        if not last:
            rows, received = relayed(sent, kept, tick)
    return kept.reshape(1, z.micro, z.tok, z.width)


def solution(mesh):
    placed = (
        P(None, "expert", "hidden"),
        P("section", "hidden", None, "expert"),
        P("section", "expert", "hidden"),
        P("section", None, "expert", None),
        P("section", None, "expert", None),
    )
    return jax.shard_map(
        on_device,
        mesh=mesh,
        in_specs=placed,
        out_specs=P("section", None, "expert", "hidden"),
        check_vma=False,
    )
```

profile of v0, /device:TPU:2, one launch (start us, length us, event | category | flops | bytes accessed | tf_op | source)
XLA Modules:
  0.0 122.2 jit_solution(6283305182131010270)
XLA Ops:
  0.0 1.6 %shard_map.55 = (bf16[48,1792]{1,0:T(8,128)(2,1)S(1)}, bf16[48,1792]{1,0:T(8,128)(2,1)S(1)}, bf16[48,1792]{1,0:T(8,128)(2,1)S(1)}, bf16[48,1792]{1,0:T(8,128)(2,1)S(1)}, bf16[192,64]{1,0:T(8,128)(2,1)S(1)}) custom-call(s32[4,2,16]{2,1,0:T(2,128)} %bitcast.11, bf16[4,2,16]{2,1,0:T(2,128)(2,1)} %bitcast.14, bf16[64,1792]{1,0:T(8,128)(2,1)} %bitcast.8), custom_call_target="tpu_custom_call" | custom-call | tf_op jit(solution)/shard_map/pallas_call | solution.py:305
  1.6 1.6 %collective-permute-start = (bf16[48,1792]{1,0:T(8,128)(2,1)S(1)}, bf16[48,1792]{1,0:T(8,128)(2,1)S(1)}, u32[]{:S(2)}, u32[]{:S(2)}) collective-permute-start(bf16[48,1792]{1,0:T(8,128)(2,1)S(1)} %get-tuple-element.55), channel_id=1, source_target_pairs={{0,4},{4,0},{8,12},{12,8},{1,5},{5,1},{9,13},{13,9},{2,6},{6,2},{1... | collective-permute-start | bytes 516104 | tf_op jit(solution)/shard_map/ppermute | solution.py:336
  3.3 2.6 %collective-permute-start.1 = (bf16[48,1792]{1,0:T(8,128)(2,1)S(1)}, bf16[48,1792]{1,0:T(8,128)(2,1)S(1)}, u32[]{:S(2)}, u32[]{:S(2)}) collective-permute-start(bf16[48,1792]{1,0:T(8,128)(2,1)S(1)} %get-tuple-element.56), channel_id=1, source_target_pairs={{0,8},{4,12},{8,0},{12,4},{1,9},{5,13},{9,1},{13,5},{2,10},{6,14},... | collective-permute-start | bytes 516104 | tf_op jit(solution)/shard_map/ppermute | solution.py:336
  6.1 9.6 %shard_map.56 = (bf16[3584,1024]{1,0:T(8,128)(2,1)S(1)}, bf16[3584,1024]{1,0:T(8,128)(2,1)S(1)}, bf16[3584,1024]{1,0:T(8,128)(2,1)S(1)}, bf16[3584,1024]{1,0:T(8,128)(2,1)S(1)}) custom-call(bf16[192,64]{1,0:T(8,128)(2,1)S(1)} %get-tuple-element.48.refs_0_, bf16[1,1792,2,4096]{3,2,1,0:T(2,128)(2,1)} %refs_1_.3), custom_call_target="tpu_custom_call" | custom-call | tf_op jit(solution)/shard_map/pallas_call | solution.py:305
  15.7 3.2 %shard_map.57 = (bf16[1024,1792]{1,0:T(8,128)(2,1)S(1)}, bf16[1024,1792]{1,0:T(8,128)(2,1)S(1)}) custom-call(bf16[3584,1024]{1,0:T(8,128)(2,1)S(1)} %get-tuple-element.49.refs_0_.refs_2_, bf16[1,4096,1792]{2,1,0:T(8,128)(2,1)} %refs_1_.5), custom_call_target="tpu_custom_call" | custom-call | tf_op jit(solution)/shard_map/pallas_call | solution.py:305
  19.0 3.2 %shard_map.58 = (f32[112,1024]{1,0:T(8,128)S(1)}, bf16[112,1024]{1,0:T(8,128)(2,1)S(1)}) custom-call(bf16[1024,1792]{1,0:T(8,128)(2,1)S(1)} %get-tuple-element.50.refs_0_, bf16[3584,1024]{1,0:T(8,128)(2,1)S(1)} %get-tuple-element.52.refs_1_, bf16[3584,1024]{1,0:T(8,128)(2,1)S(1)} %get-tuple-element.53.refs_2_, ...), custom_call_target="tpu_custom_call" | custom-call | tf_op jit(solution)/shard_map/pallas_call | solution.py:305
  25.4 3.2 %shard_map.63 = (f32[112,1024]{1,0:T(8,128)S(1)}, bf16[112,1024]{1,0:T(8,128)(2,1)S(1)}) custom-call(bf16[112,1024]{1,0:T(8,128)(2,1)S(1)} %shard_map.59.refs_0_.refs_1_, bf16[3584,1024]{1,0:T(8,128)(2,1)S(1)} %get-tuple-element.66.refs_1_, bf16[3584,1024]{1,0:T(8,128)(2,1)S(1)} %get-tuple-element.49.refs_0_.refs_2_, ...), custom_call_target="tpu_custom_call" | custom-call | tf_op jit(solution)/shard_map/pallas_call | solution.py:305
  28.6 3.2 %shard_map.60 = (bf16[1024,1792]{1,0:T(8,128)(2,1)S(1)}, bf16[1024,1792]{1,0:T(8,128)(2,1)S(1)}) custom-call(bf16[112,1024]{1,0:T(8,128)(2,1)S(1)} %shard_map.59.refs_0_.refs_1_, bf16[1,4096,1792]{2,1,0:T(8,128)(2,1)} %refs_1_.5), custom_call_target="tpu_custom_call" | custom-call | tf_op jit(solution)/shard_map/pallas_call | solution.py:305
  36.2 4.0 %collective-permute-done.10.refs_2_ = bf16[112,1024]{1,0:T(8,128)(2,1)S(1)} collective-permute-done((bf16[112,1024]{1,0:T(8,128)(2,1)S(1)}, bf16[112,1024]{1,0:T(8,128)(2,1)S(1)}, u32[]{:S(2)}, u32[]{:S(2)}) %collective-permute-start.10) | collective-permute-done | bytes 229408 | tf_op jit(solution)/shard_map/ppermute | solution.py:328
  40.4 2.8 %collective-permute-start.6 = (bf16[24,1792]{1,0:T(8,128)(2,1)S(1)}, bf16[24,1792]{1,0:T(8,128)(2,1)S(1)}, u32[]{:S(2)}, u32[]{:S(2)}) collective-permute-start(bf16[24,1792]{1,0:T(8,128)(2,1)S(1)} %get-tuple-element.62), channel_id=1, source_target_pairs={{0,4},{4,0},{8,12},{12,8},{1,5},{5,1},{9,13},{13,9},{2,6},{6,2},{1... | collective-permute-start | bytes 258056 | tf_op jit(solution)/shard_map/ppermute | solution.py:336
  48.3 2.3 %collective-permute-start.13 = (bf16[24,1792]{1,0:T(8,128)(2,1)S(1)}, bf16[24,1792]{1,0:T(8,128)(2,1)S(1)}, u32[]{:S(2)}, u32[]{:S(2)}) collective-permute-start(bf16[24,1792]{1,0:T(8,128)(2,1)S(1)} %get-tuple-element.71), channel_id=1, source_target_pairs={{0,8},{4,12},{8,0},{12,4},{1,9},{5,13},{9,1},{13,5},{2,10},{6,14},... | collective-permute-start | bytes 258056 | tf_op jit(solution)/shard_map/ppermute | solution.py:336
  53.0 2.4 %collective-permute-start.15 = (s32[4,2,16]{2,1,0:T(2,128)S(1)}, s32[4,2,16]{2,1,0:T(2,128)S(1)}, u32[]{:S(2)}, u32[]{:S(2)}) collective-permute-start(s32[4,2,16]{2,1,0:T(2,128)S(1)} %get-tuple-element.73), channel_id=1, source_target_pairs={{16,0},{17,1},{18,2},{19,3},{20,4},{21,5},{22,6},{23,7},{24,8},{25... | collective-permute-start | bytes 1544 | tf_op jit(solution)/shard_map/ppermute | solution.py:443
  56.8 3.6 %collective-permute-done.13.refs_9_ = bf16[24,1792]{1,0:T(8,128)(2,1)S(1)} collective-permute-done((bf16[24,1792]{1,0:T(8,128)(2,1)S(1)}, bf16[24,1792]{1,0:T(8,128)(2,1)S(1)}, u32[]{:S(2)}, u32[]{:S(2)}) %collective-permute-start.13) | collective-permute-done | bytes 86048 | tf_op jit(solution)/shard_map/ppermute | solution.py:336
  65.2 5.0 %collective-permute-done.16.refs_1_ = bf16[64,1792]{1,0:T(8,128)(2,1)S(1)} collective-permute-done((bf16[64,1792]{1,0:T(8,128)(2,1)S(1)}, bf16[64,1792]{1,0:T(8,128)(2,1)S(1)}, u32[]{:S(2)}, u32[]{:S(2)}) %collective-permute-start.16) | collective-permute-done | bytes 229408 | tf_op jit(solution)/shard_map/ppermute | solution.py:341
  70.7 5.4 %collective-permute-start.17 = (bf16[48,1792]{1,0:T(8,128)(2,1)S(1)}, bf16[48,1792]{1,0:T(8,128)(2,1)S(1)}, u32[]{:S(2)}, u32[]{:S(2)}) collective-permute-start(bf16[48,1792]{1,0:T(8,128)(2,1)S(1)} %get-tuple-element.76), channel_id=1, source_target_pairs={{0,4},{4,0},{8,12},{12,8},{1,5},{5,1},{9,13},{13,9},{2,6},{6,2},{1... | collective-permute-start | bytes 516104 | tf_op jit(solution)/shard_map/ppermute | solution.py:352
  76.1 4.6 %collective-permute-done.18.refs_5_ = bf16[48,1792]{1,0:T(8,128)(2,1)S(1)} collective-permute-done((bf16[48,1792]{1,0:T(8,128)(2,1)S(1)}, bf16[48,1792]{1,0:T(8,128)(2,1)S(1)}, u32[]{:S(2)}, u32[]{:S(2)}) %collective-permute-start.18) | collective-permute-done | bytes 172064 | tf_op jit(solution)/shard_map/ppermute | solution.py:348
  80.7 3.2 %shard_map.69 = (f32[112,1024]{1,0:T(8,128)S(1)}, bf16[112,1024]{1,0:T(8,128)(2,1)S(1)}) custom-call(bf16[1024,1792]{1,0:T(8,128)(2,1)S(1)} %get-tuple-element.50.refs_0_, bf16[3584,1024]{1,0:T(8,128)(2,1)S(1)} %get-tuple-element.52.refs_1_, bf16[3584,1024]{1,0:T(8,128)(2,1)S(1)} %get-tuple-element.53.refs_2_, ...), custom_call_target="tpu_custom_call" | custom-call | tf_op jit(solution)/shard_map/pallas_call | solution.py:305
  86.1 3.2 %shard_map.73 = (f32[112,1024]{1,0:T(8,128)S(1)}, bf16[112,1024]{1,0:T(8,128)(2,1)S(1)}) custom-call(bf16[112,1024]{1,0:T(8,128)(2,1)S(1)} %shard_map.70.refs_0_, bf16[3584,1024]{1,0:T(8,128)(2,1)S(1)} %get-tuple-element.66.refs_1_, bf16[3584,1024]{1,0:T(8,128)(2,1)S(1)} %get-tuple-element.49.refs_0_.refs_2_, ...), custom_call_target="tpu_custom_call" | custom-call | tf_op jit(solution)/shard_map/pallas_call | solution.py:305
  89.3 3.9 %collective-permute-done.21.refs_1_ = bf16[112,1024]{1,0:T(8,128)(2,1)S(1)} collective-permute-done((bf16[112,1024]{1,0:T(8,128)(2,1)S(1)}, bf16[112,1024]{1,0:T(8,128)(2,1)S(1)}, u32[]{:S(2)}, u32[]{:S(2)}) %collective-permute-start.21) | collective-permute-done | bytes 229408 | tf_op jit(solution)/shard_map/ppermute | solution.py:328
  96.9 3.5 %collective-permute-done.27.refs_2_ = bf16[112,1024]{1,0:T(8,128)(2,1)S(1)} collective-permute-done((bf16[112,1024]{1,0:T(8,128)(2,1)S(1)}, bf16[112,1024]{1,0:T(8,128)(2,1)S(1)}, u32[]{:S(2)}, u32[]{:S(2)}) %collective-permute-start.27) | collective-permute-done | bytes 229408 | tf_op jit(solution)/shard_map/ppermute | solution.py:328
  100.6 3.6 %collective-permute-start.23 = (bf16[24,1792]{1,0:T(8,128)(2,1)S(1)}, bf16[24,1792]{1,0:T(8,128)(2,1)S(1)}, u32[]{:S(2)}, u32[]{:S(2)}) collective-permute-start(bf16[24,1792]{1,0:T(8,128)(2,1)S(1)} %get-tuple-element.82), channel_id=1, source_target_pairs={{0,4},{4,0},{8,12},{12,8},{1,5},{5,1},{9,13},{13,9},{2,6},{6,2},{1... | collective-permute-start | bytes 258056 | tf_op jit(solution)/shard_map/ppermute | solution.py:336
  104.2 2.4 %collective-permute-start.25 = (bf16[24,1792]{1,0:T(8,128)(2,1)S(1)}, bf16[24,1792]{1,0:T(8,128)(2,1)S(1)}, u32[]{:S(2)}, u32[]{:S(2)}) collective-permute-start(bf16[24,1792]{1,0:T(8,128)(2,1)S(1)} %get-tuple-element.84), channel_id=1, source_target_pairs={{0,12},{4,8},{8,4},{12,0},{1,13},{5,9},{9,5},{13,1},{2,14},{6,10},... | collective-permute-start | bytes 258056 | tf_op jit(solution)/shard_map/ppermute | solution.py:336
  110.2 2.4 %collective-permute-start.31 = (bf16[24,1792]{1,0:T(8,128)(2,1)S(1)}, bf16[24,1792]{1,0:T(8,128)(2,1)S(1)}, u32[]{:S(2)}, u32[]{:S(2)}) collective-permute-start(bf16[24,1792]{1,0:T(8,128)(2,1)S(1)} %get-tuple-element.90), channel_id=1, source_target_pairs={{0,12},{4,8},{8,4},{12,0},{1,13},{5,9},{9,5},{13,1},{2,14},{6,10},... | collective-permute-start | bytes 258056 | tf_op jit(solution)/shard_map/ppermute | solution.py:336
  115.1 6.1 %collective-permute-done.30.refs_9_ = bf16[24,1792]{1,0:T(8,128)(2,1)S(1)} collective-permute-done((bf16[24,1792]{1,0:T(8,128)(2,1)S(1)}, bf16[24,1792]{1,0:T(8,128)(2,1)S(1)}, u32[]{:S(2)}, u32[]{:S(2)}) %collective-permute-start.30) | collective-permute-done | bytes 86048 | tf_op jit(solution)/shard_map/ppermute | solution.py:336
  (67 shorter events, 35.3 us)
Async XLA Ops:
  1.6 17.3 %collective-permute-start = (bf16[48,1792]{1,0:T(8,128)(2,1)S(1)}, bf16[48,1792]{1,0:T(8,128)(2,1)S(1)}, u32[]{:S(2)}, u32[]{:S(2)}) collective-permute-start(bf16[48,1792]{1,0:T(8,128)(2,1)S(1)} %get-tuple-element.55), channel_id=1, source_target_pairs={{0,4},{4,0},{8,12},{12,8},{1,5},{5,1},{9,13},{13,9},{2,6},{6,2},{1... | collective-permute-start | bytes 516104 | tf_op jit(solution)/shard_map/ppermute | solution.py:336
  3.3 15.7 %collective-permute-start.1 = (bf16[48,1792]{1,0:T(8,128)(2,1)S(1)}, bf16[48,1792]{1,0:T(8,128)(2,1)S(1)}, u32[]{:S(2)}, u32[]{:S(2)}) collective-permute-start(bf16[48,1792]{1,0:T(8,128)(2,1)S(1)} %get-tuple-element.56), channel_id=1, source_target_pairs={{0,8},{4,12},{8,0},{12,4},{1,9},{5,13},{9,1},{13,5},{2,10},{6,14},... | collective-permute-start | bytes 516104 | tf_op jit(solution)/shard_map/ppermute | solution.py:336
  5.9 13.1 %collective-permute-start.2 = (bf16[48,1792]{1,0:T(8,128)(2,1)S(1)}, bf16[48,1792]{1,0:T(8,128)(2,1)S(1)}, u32[]{:S(2)}, u32[]{:S(2)}) collective-permute-start(bf16[48,1792]{1,0:T(8,128)(2,1)S(1)} %get-tuple-element.57), channel_id=1, source_target_pairs={{0,12},{4,8},{8,4},{12,0},{1,13},{5,9},{9,5},{13,1},{2,14},{6,10},... | collective-permute-start | bytes 516104 | tf_op jit(solution)/shard_map/ppermute | solution.py:336
  23.8 8.0 %collective-permute-start.4 = (bf16[112,1024]{1,0:T(8,128)(2,1)S(1)}, bf16[112,1024]{1,0:T(8,128)(2,1)S(1)}, u32[]{:S(2)}, u32[]{:S(2)}) collective-permute-start(bf16[112,1024]{1,0:T(8,128)(2,1)S(1)} %shard_map.59.refs_0_.refs_1_), channel_id=1, source_target_pairs={{0,2},{1,3},{2,0},{3,1},{4,6},{5,7},{6,4},{7,5},{8,10},{9,11},{10,... | collective-permute-start | bytes 688136 | tf_op jit(solution)/shard_map/ppermute | solution.py:328
  32.1 8.1 %collective-permute-start.10 = (bf16[112,1024]{1,0:T(8,128)(2,1)S(1)}, bf16[112,1024]{1,0:T(8,128)(2,1)S(1)}, u32[]{:S(2)}, u32[]{:S(2)}) collective-permute-start(bf16[112,1024]{1,0:T(8,128)(2,1)S(1)} %shard_map.64.refs_1_), channel_id=1, source_target_pairs={{0,2},{1,3},{2,0},{3,1},{4,6},{5,7},{6,4},{7,5},{8,10},{9,11},{10,... | collective-permute-start | bytes 688136 | tf_op jit(solution)/shard_map/ppermute | solution.py:328
  40.4 10.2 %collective-permute-start.6 = (bf16[24,1792]{1,0:T(8,128)(2,1)S(1)}, bf16[24,1792]{1,0:T(8,128)(2,1)S(1)}, u32[]{:S(2)}, u32[]{:S(2)}) collective-permute-start(bf16[24,1792]{1,0:T(8,128)(2,1)S(1)} %get-tuple-element.62), channel_id=1, source_target_pairs={{0,4},{4,0},{8,12},{12,8},{1,5},{5,1},{9,13},{13,9},{2,6},{6,2},{1... | collective-permute-start | bytes 258056 | tf_op jit(solution)/shard_map/ppermute | solution.py:336
  43.2 9.8 %collective-permute-start.7 = (bf16[24,1792]{1,0:T(8,128)(2,1)S(1)}, bf16[24,1792]{1,0:T(8,128)(2,1)S(1)}, u32[]{:S(2)}, u32[]{:S(2)}) collective-permute-start(bf16[24,1792]{1,0:T(8,128)(2,1)S(1)} %get-tuple-element.63), channel_id=1, source_target_pairs={{0,8},{4,12},{8,0},{12,4},{1,9},{5,13},{9,1},{13,5},{2,10},{6,14},... | collective-permute-start | bytes 258056 | tf_op jit(solution)/shard_map/ppermute | solution.py:336
  44.6 10.8 %collective-permute-start.8 = (bf16[24,1792]{1,0:T(8,128)(2,1)S(1)}, bf16[24,1792]{1,0:T(8,128)(2,1)S(1)}, u32[]{:S(2)}, u32[]{:S(2)}) collective-permute-start(bf16[24,1792]{1,0:T(8,128)(2,1)S(1)} %get-tuple-element.64), channel_id=1, source_target_pairs={{0,12},{4,8},{8,4},{12,0},{1,13},{5,9},{9,5},{13,1},{2,14},{6,10},... | collective-permute-start | bytes 258056 | tf_op jit(solution)/shard_map/ppermute | solution.py:336
  47.2 9.5 %collective-permute-start.12 = (bf16[24,1792]{1,0:T(8,128)(2,1)S(1)}, bf16[24,1792]{1,0:T(8,128)(2,1)S(1)}, u32[]{:S(2)}, u32[]{:S(2)}) collective-permute-start(bf16[24,1792]{1,0:T(8,128)(2,1)S(1)} %get-tuple-element.70), channel_id=1, source_target_pairs={{0,4},{4,0},{8,12},{12,8},{1,5},{5,1},{9,13},{13,9},{2,6},{6,2},{1... | collective-permute-start | bytes 258056 | tf_op jit(solution)/shard_map/ppermute | solution.py:336
  48.3 12.1 %collective-permute-start.13 = (bf16[24,1792]{1,0:T(8,128)(2,1)S(1)}, bf16[24,1792]{1,0:T(8,128)(2,1)S(1)}, u32[]{:S(2)}, u32[]{:S(2)}) collective-permute-start(bf16[24,1792]{1,0:T(8,128)(2,1)S(1)} %get-tuple-element.71), channel_id=1, source_target_pairs={{0,8},{4,12},{8,0},{12,4},{1,9},{5,13},{9,1},{13,5},{2,10},{6,14},... | collective-permute-start | bytes 258056 | tf_op jit(solution)/shard_map/ppermute | solution.py:336
  50.7 9.7 %collective-permute-start.14 = (bf16[24,1792]{1,0:T(8,128)(2,1)S(1)}, bf16[24,1792]{1,0:T(8,128)(2,1)S(1)}, u32[]{:S(2)}, u32[]{:S(2)}) collective-permute-start(bf16[24,1792]{1,0:T(8,128)(2,1)S(1)} %get-tuple-element.72), channel_id=1, source_target_pairs={{0,12},{4,8},{8,4},{12,0},{1,13},{5,9},{9,5},{13,1},{2,14},{6,10},... | collective-permute-start | bytes 258056 | tf_op jit(solution)/shard_map/ppermute | solution.py:336
  61.1 9.0 %collective-permute-start.16 = (bf16[64,1792]{1,0:T(8,128)(2,1)S(1)}, bf16[64,1792]{1,0:T(8,128)(2,1)S(1)}, u32[]{:S(2)}, u32[]{:S(2)}) collective-permute-start(bf16[64,1792]{1,0:T(8,128)(2,1)S(1)} %get-tuple-element.74.refs_2_), channel_id=1, source_target_pairs={{0,16},{1,17},{2,18},{3,19},{4,20},{5,21},{6,22},{7,23},{8,24},{9,... | collective-permute-start | bytes 688136 | tf_op jit(solution)/shard_map/ppermute | solution.py:341
  62.4 18.3 %collective-permute-start.18 = (bf16[48,1792]{1,0:T(8,128)(2,1)S(1)}, bf16[48,1792]{1,0:T(8,128)(2,1)S(1)}, u32[]{:S(2)}, u32[]{:S(2)}) collective-permute-start(bf16[48,1792]{1,0:T(8,128)(2,1)S(1)} %get-tuple-element.77), channel_id=1, source_target_pairs={{0,24},{4,28},{8,16},{12,20},{1,25},{5,29},{9,17},{13,21},{2,26},{... | collective-permute-start | bytes 516104 | tf_op jit(solution)/shard_map/ppermute | solution.py:348
  63.7 17.0 %collective-permute-start.19 = (bf16[48,1792]{1,0:T(8,128)(2,1)S(1)}, bf16[48,1792]{1,0:T(8,128)(2,1)S(1)}, u32[]{:S(2)}, u32[]{:S(2)}) collective-permute-start(bf16[48,1792]{1,0:T(8,128)(2,1)S(1)} %get-tuple-element.78), channel_id=1, source_target_pairs={{0,28},{4,24},{8,20},{12,16},{1,29},{5,25},{9,21},{13,17},{2,30},{... | collective-permute-start | bytes 516104 | tf_op jit(solution)/shard_map/ppermute | solution.py:348
  70.7 10.1 %collective-permute-start.17 = (bf16[48,1792]{1,0:T(8,128)(2,1)S(1)}, bf16[48,1792]{1,0:T(8,128)(2,1)S(1)}, u32[]{:S(2)}, u32[]{:S(2)}) collective-permute-start(bf16[48,1792]{1,0:T(8,128)(2,1)S(1)} %get-tuple-element.76), channel_id=1, source_target_pairs={{0,4},{4,0},{8,12},{12,8},{1,5},{5,1},{9,13},{13,9},{2,6},{6,2},{1... | collective-permute-start | bytes 516104 | tf_op jit(solution)/shard_map/ppermute | solution.py:352
  85.5 7.7 %collective-permute-start.21 = (bf16[112,1024]{1,0:T(8,128)(2,1)S(1)}, bf16[112,1024]{1,0:T(8,128)(2,1)S(1)}, u32[]{:S(2)}, u32[]{:S(2)}) collective-permute-start(bf16[112,1024]{1,0:T(8,128)(2,1)S(1)} %shard_map.70.refs_0_), channel_id=1, source_target_pairs={{0,2},{1,3},{2,0},{3,1},{4,6},{5,7},{6,4},{7,5},{8,10},{9,11},{10,... | collective-permute-start | bytes 688136 | tf_op jit(solution)/shard_map/ppermute | solution.py:328
  93.5 6.9 %collective-permute-start.27 = (bf16[112,1024]{1,0:T(8,128)(2,1)S(1)}, bf16[112,1024]{1,0:T(8,128)(2,1)S(1)}, u32[]{:S(2)}, u32[]{:S(2)}) collective-permute-start(bf16[112,1024]{1,0:T(8,128)(2,1)S(1)} %shard_map.74.refs_1_), channel_id=1, source_target_pairs={{0,2},{1,3},{2,0},{3,1},{4,6},{5,7},{6,4},{7,5},{8,10},{9,11},{10,... | collective-permute-start | bytes 688136 | tf_op jit(solution)/shard_map/ppermute | solution.py:328
  100.5 6.1 %collective-permute-start.28 = (bf16[96,512]{1,0:T(8,128)(2,1)S(1)}, bf16[96,512]{1,0:T(8,128)(2,1)S(1)}, u32[]{:S(2)}, u32[]{:S(2)}) collective-permute-start(bf16[96,512]{1,0:T(8,128)(2,1)S(1)} %shard_map.75.refs_2_), channel_id=1, source_target_pairs={{0,1},{1,0},{2,3},{3,2},{4,5},{5,4},{6,7},{7,6},{8,9},{9,8},{10,11... | collective-permute-start | bytes 294920 | tf_op jit(solution)/shard_map/ppermute | solution.py:328
  100.6 9.6 %collective-permute-start.23 = (bf16[24,1792]{1,0:T(8,128)(2,1)S(1)}, bf16[24,1792]{1,0:T(8,128)(2,1)S(1)}, u32[]{:S(2)}, u32[]{:S(2)}) collective-permute-start(bf16[24,1792]{1,0:T(8,128)(2,1)S(1)} %get-tuple-element.82), channel_id=1, source_target_pairs={{0,4},{4,0},{8,12},{12,8},{1,5},{5,1},{9,13},{13,9},{2,6},{6,2},{1... | collective-permute-start | bytes 258056 | tf_op jit(solution)/shard_map/ppermute | solution.py:336
  104.2 10.0 %collective-permute-start.24 = (bf16[24,1792]{1,0:T(8,128)(2,1)S(1)}, bf16[24,1792]{1,0:T(8,128)(2,1)S(1)}, u32[]{:S(2)}, u32[]{:S(2)}) collective-permute-start(bf16[24,1792]{1,0:T(8,128)(2,1)S(1)} %get-tuple-element.83), channel_id=1, source_target_pairs={{0,8},{4,12},{8,0},{12,4},{1,9},{5,13},{9,1},{13,5},{2,10},{6,14},... | collective-permute-start | bytes 258056 | tf_op jit(solution)/shard_map/ppermute | solution.py:336
  104.2 10.0 %collective-permute-start.25 = (bf16[24,1792]{1,0:T(8,128)(2,1)S(1)}, bf16[24,1792]{1,0:T(8,128)(2,1)S(1)}, u32[]{:S(2)}, u32[]{:S(2)}) collective-permute-start(bf16[24,1792]{1,0:T(8,128)(2,1)S(1)} %get-tuple-element.84), channel_id=1, source_target_pairs={{0,12},{4,8},{8,4},{12,0},{1,13},{5,9},{9,5},{13,1},{2,14},{6,10},... | collective-permute-start | bytes 258056 | tf_op jit(solution)/shard_map/ppermute | solution.py:336
  108.2 7.0 %collective-permute-start.29 = (bf16[24,1792]{1,0:T(8,128)(2,1)S(1)}, bf16[24,1792]{1,0:T(8,128)(2,1)S(1)}, u32[]{:S(2)}, u32[]{:S(2)}) collective-permute-start(bf16[24,1792]{1,0:T(8,128)(2,1)S(1)} %get-tuple-element.88), channel_id=1, source_target_pairs={{0,4},{4,0},{8,12},{12,8},{1,5},{5,1},{9,13},{13,9},{2,6},{6,2},{1... | collective-permute-start | bytes 258056 | tf_op jit(solution)/shard_map/ppermute | solution.py:336
  109.3 11.9 %collective-permute-start.30 = (bf16[24,1792]{1,0:T(8,128)(2,1)S(1)}, bf16[24,1792]{1,0:T(8,128)(2,1)S(1)}, u32[]{:S(2)}, u32[]{:S(2)}) collective-permute-start(bf16[24,1792]{1,0:T(8,128)(2,1)S(1)} %get-tuple-element.89), channel_id=1, source_target_pairs={{0,8},{4,12},{8,0},{12,4},{1,9},{5,13},{9,1},{13,5},{2,10},{6,14},... | collective-permute-start | bytes 258056 | tf_op jit(solution)/shard_map/ppermute | solution.py:336
  110.2 11.0 %collective-permute-start.31 = (bf16[24,1792]{1,0:T(8,128)(2,1)S(1)}, bf16[24,1792]{1,0:T(8,128)(2,1)S(1)}, u32[]{:S(2)}, u32[]{:S(2)}) collective-permute-start(bf16[24,1792]{1,0:T(8,128)(2,1)S(1)} %get-tuple-element.90), channel_id=1, source_target_pairs={{0,12},{4,8},{8,4},{12,0},{1,13},{5,9},{9,5},{13,1},{2,14},{6,10},... | collective-permute-start | bytes 258056 | tf_op jit(solution)/shard_map/ppermute | solution.py:336
  (10 other events, 62.1 us)
where the time goes:
time: 123 us; the launch traced here: 122 us
  waiting for transfers between devices  41.3 us (34%)
  starting transfers between devices  41 us (33%)
  Pallas kernels  39.6 us (32%)
    pallas_call x23, Pallas kernels, call(): pl.pallas_call(functools.partial(after_waits, len(waits), functools.parti...  39.6 us
    ppermute x15, starting transfers between devices, exchanged(): result[step] = lax.ppermute(pieces[step], 'expert', pairs)  24.6 us
    ppermute x12, waiting for transfers between devices, swap(): return lax.ppermute(value, 'hidden', pairs)  16.9 us
    ppermute x15, waiting for transfers between devices, exchanged(): result[step] = lax.ppermute(pieces[step], 'expert', pairs)  13.6 us
    ppermute x1, starting transfers between devices, relayed(): result[step] = lax.ppermute(result[step], 'expert', pairs)  5.45 us
    ppermute x1, waiting for transfers between devices, relayed(): rows = lax.ppermute(kept, 'section', hop)  4.96 us
    ppermute x2, waiting for transfers between devices, relayed(): lax.ppermute(pieces[step - z.near], ('section', 'expert'), pairs)  4.61 us
    ppermute x12, starting transfers between devices, swap(): return lax.ppermute(value, 'hidden', pairs)  4.41 us
  transfers between devices with their start and end apart: 32, of which 15 were waited for; matrix products, arithmetic and copies ran while one was open for 0% of the time, Pallas kernels for 24%

commit v1 on v0

--- a/solution.py
+++ b/solution.py
@@ -54,6 +54,7 @@
         self.slots = self.micro * CAP
         self.pay = padded(self.members * self.slots, 8)
         self.pieces = peers if peers <= 8 else 1
+        self.pairs = self.groups - 1 if self.pieces == 4 else 0
         self.near = self.pieces // 2
         self.group_pay = peers * self.pay
         self.piece = self.group_pay // self.pieces
@@ -244,45 +245,74 @@
     out[z.group_each:, :] = split_sums(sums, 2 * z.half).astype(BF16)
 
 
-def act_kernel(z, *refs):
-    out = refs[-1]
-    products, sums = joined(z, refs[:-1])
+def act_kernel(z, count, *refs):
+    outs = refs[-count:]
+    products, sums = joined(z, refs[:-count])
     shape = (z.group_each, z.group_each)
     diagonal = lax.broadcasted_iota(I32, shape, 0) == lax.broadcasted_iota(I32, shape, 1)
     sums = jnp.sum(jnp.where(diagonal, sums[:, :z.group_each], F32(0.0)), axis=1, keepdims=True)
     scale = lax.rsqrt(sums / D + EPS)
     gate = scale * products[:, :z.half]
     up = scale * products[:, z.half:]
-    out[...] = (gate / (F32(1.0) + jnp.exp(-gate)) * up).astype(BF16)
-
-
-def down_kernel(z, *refs):
+    value = (gate / (F32(1.0) + jnp.exp(-gate)) * up).astype(BF16)
+    rows = z.group_each // count
+    for index, out in enumerate(outs):
+        out[...] = value[index * rows:(index + 1) * rows]
+
+
+def half_products(z, weights, units_refs, side):
+    low = pl.multiple_of(side * z.half, z.half)
+    units = jnp.concatenate([ref[...].astype(F32) for ref in units_refs], axis=0)
+    results = []
+    for expert in range(z.members):
+        rows = units[expert * z.each:(expert + 1) * z.each].astype(BF16)
+        results.append(dot(rows, weights[expert][pl.ds(low, z.half), :]))
+    return jnp.concatenate(results, axis=0)
+
+
+def own_down_kernel(z, *refs):
+    weights, units_ref, out = refs[:z.members], refs[z.members:-1], refs[-1]
+    out[...] = half_products(z, weights, units_ref, lax.axis_index("hidden") & 1)
+
+
+def down_kernel(z, hands_on, *refs):
     weights, refs = refs[:z.members], refs[z.members:]
-    halves, outs = refs[:2], refs[2:]
-    if len(outs) > z.pieces:
+    units_ref, own_ref, outs = refs[:1], refs[1], refs[2:]
+    if hands_on:
         outs[-1][...] = outs[0][...]
         outs = outs[1:-1]
-    core = lax.axis_index("hidden") & 1
-    results = []
-    for expert in range(z.members):
-        total = None
-        for step in range(2):
-            units = halves[step][...].astype(F32)[expert * z.each:(expert + 1) * z.each].astype(BF16)
-            low = pl.multiple_of((core ^ step) * z.half, z.half)
-            value = dot(units, weights[expert][pl.ds(low, z.half), :])
-            total = value if total is None else total + value
-        results.append(total)
-    value = dot(z.order(), jnp.concatenate(results, axis=0).astype(BF16), DOWN)
-    for index, out in enumerate(outs):
-        out[...] = value[index * z.piece:(index + 1) * z.piece].astype(BF16)
+    total = own_ref[...] + half_products(z, weights, units_ref, 1 - (lax.axis_index("hidden") & 1))
+    value = dot(z.order(), total.astype(BF16), DOWN)
+    low = 0
+    for out in outs:
+        out[...] = value[low:low + out.shape[0]].astype(BF16)
+        low += out.shape[0]
+
+
+def near_back_kernel(z, *refs):
+    *blocks, out = refs
+    values = [ref[...].astype(F32)[-z.piece:] for ref in blocks]
+    out[...] = jnp.concatenate(values, axis=0).astype(BF16)
 
 
 def combine_kernel(z, tick, last, weight_ref, rows_ref, kept_ref, *refs):
-    count = z.groups * z.pieces
-    returned, refs = refs[:count], refs[count:]
+    if z.pairs:
+        near = refs[0][...].astype(F32)
+        near = [near[low:low + z.piece] for low in range(0, near.shape[0], z.piece)]
+        returned, refs = [], refs[1:]
+        for group in range(z.groups):
+            if group < z.pairs:
+                values, refs = [ref[...].astype(F32)[:z.piece] for ref in refs[:2]], refs[2:]
+                returned += [values[0], near[group], values[1], near[z.groups + group]]
+            else:
+                values, refs = [ref[...].astype(F32) for ref in refs[:3]], refs[3:]
+                returned += [values[0], near[group], values[1], values[2]]
+    else:
+        count = z.groups * z.pieces
+        returned, refs = [ref[...].astype(F32) for ref in refs[:count]], refs[count:]
     stacked = []
     for piece in range(z.pieces):
-        values = [returned[group * z.pieces + piece][...].astype(F32) for group in range(z.groups)]
+        values = [returned[group * z.pieces + piece] for group in range(z.groups)]
         for step in range(z.peers // z.pieces):
             stacked += [value[step * z.pay:(step + 1) * z.pay] for value in values]
     stacked = jnp.concatenate(stacked, axis=0).astype(BF16)
@@ -320,6 +350,7 @@
     shape = jax.ShapeDtypeStruct
     pay = shape((z.piece, z.width), BF16)
     all_pay = shape((z.all_piece, z.width), BF16)
+    merged = [pay, pay, shape((2 * z.piece, z.width), BF16)]
     whole = shape((z.rows, z.width), BF16)
     steps = sorted(range(z.peers), key=lambda step: -step.bit_length())
 
@@ -335,6 +366,23 @@
             pairs = [(i, i ^ step) for i in range(z.peers)]
             result[step] = lax.ppermute(pieces[step], "expert", pairs)
         return result
+
+    def across(value, step):
+        return lax.ppermute(value, "expert", [(i, i ^ step) for i in range(z.peers)])
+
+    def sent_back(pieces, group):
+        if not z.pairs:
+            return exchanged(pieces)
+        own, near, *far = pieces
+        return [own, near] + [across(value, 2 + step) for step, value in enumerate(far)]
+
+    def near_back(returned):
+        if not z.pairs:
+            return sum(returned, [])
+        blocks = [pieces[1] for pieces in returned] + [pieces[2] for pieces in returned[:z.pairs]]
+        rows = shape((len(blocks) * z.piece, z.width), BF16)
+        joint = call(near_back_kernel, (z,), 4, [rows], [VMEM] * len(blocks), [], *blocks)[0]
+        return [across(joint, 1)] + sum([pieces[:1] + pieces[2:] for pieces in returned], [])
 
     def relayed(pieces, kept, tick):
         hop = [(tick, tick + 1)]
@@ -380,18 +428,24 @@
         return [pair] + [swap(pair, step) for step in range(2, z.splits, 2)]
 
     def activated(pairs, waits):
+        count = 1
         units = call(
-            act_kernel, (z,), 2,
-            [shape((z.group_each, z.half), BF16)], [VMEM] * len(pairs), [], *pairs, waits=waits,
+            act_kernel, (z, count), 2,
+            [shape((z.group_each // count, z.half), BF16)] * count, [VMEM] * len(pairs), [], *pairs, waits=waits,
+        )
+        return units, [swap(part, 1) for part in units]
+
+    def down(halves, group, hand_on):
+        own = call(
+            own_down_kernel, (z,), 4, [shape((z.group_each, z.width), F32)],
+            [VMEM] * (z.members + len(halves[0])), [], *tall[group], *halves[0],
         )[0]
-        return units, swap(units, 1)
-
-    def down(halves, group, hand_on):
         return call(
-            down_kernel, (z,), 4,
-            [pay] * z.pieces + [shape(value.shape, value.dtype) for value in hand_on],
-            [VMEM] * (z.members + 2 + len(hand_on)), [],
-            *tall[group], *halves, *hand_on,
+            down_kernel, (z, len(hand_on)), 4,
+            (merged if group < z.pairs else [pay] * z.pieces)
+            + [shape(value.shape, value.dtype) for value in hand_on],
+            [VMEM] * (z.members + 1 + len(halves[1]) + len(hand_on)), [],
+            *tall[group], *halves[1], own, *hand_on,
         )
 
     routes = routes[0].transpose(0, 2, 1)
@@ -432,7 +486,7 @@
                 early = tall[-1][:1]
             if group == 0:
                 halves = activated(sums[0], early)
-                waits = list(halves[:1])
+                waits = list(halves[0][:1])
         for group in groups:
             if group:
                 halves = activated(sums[group], outgoing[:1])
@@ -441,7 +495,8 @@
             if hand_on:
                 pairs = [(i + 1, i) for i in range(sections - 1)]
                 following = lax.ppermute(outgoing.pop(), "section", pairs)
-            returned += exchanged(outgoing)
+            returned.append(sent_back(outgoing, group))
+        returned = near_back(returned)
         kept, *sent = call(
             combine_kernel, (z, tick, last), 4,
             [whole] if last else [whole] + [all_pay] * (z.pieces - z.near),

time: 123 us -> 121 us (0.984)
  starting transfers between devices: 41 us -> 35.2 us
  waiting for transfers between devices: 41.3 us -> 43.4 us
    ppermute x0 -> x8, waiting for transfers between devices: none -> 22.1 us  [across(): lax.ppermute(value, 'expert', [(i, i ^ step) for i in range(z.peers)])]
    ppermute x15 -> x3, starting transfers between devices: 24.6 us -> 4.45 us  [exchanged(): result[step] = lax.ppermute(pieces[step], 'expert', pairs)]
    ppermute x0 -> x8, starting transfers between devices: none -> 16.9 us  [across(): lax.ppermute(value, 'expert', [(i, i ^ step) for i in range(z.peers)])]
    ppermute x15 -> x3, waiting for transfers between devices: 13.6 us -> 0.01 us  [exchanged(): result[step] = lax.ppermute(pieces[step], 'expert', pairs)]
    ppermute x12, waiting for transfers between devices: 16.9 us -> 9.34 us  [swap(): return lax.ppermute(value, 'hidden', pairs)]
    ppermute x1, starting transfers between devices: 5.45 us -> 2.03 us  [relayed(): result[step] = lax.ppermute(result[step], 'expert', pairs)]
    ppermute x2, waiting for transfers between devices: 4.61 us -> 6.16 us  [relayed(): lax.ppermute(pieces[step - z.near], ('section', 'expert'), pairs)]
    pallas_call x23 -> x29, Pallas kernels: 39.6 us -> 40.1 us  [call(): pl.pallas_call(functools.partial(after_waits, len(waits), functools.parti...]
  transfers between devices with their start and end apart: 32 -> 28, of which waited for: 15 -> 17; matrix products, arithmetic and copies ran while one was open for 0% -> 0% of each run, Pallas kernels for 24% -> 25%
where the time goes in v1:
time: 121 us; the launch traced here: 119 us
  waiting for transfers between devices  43.4 us (36%)
  Pallas kernels  40.1 us (33%)
  starting transfers between devices  35.2 us (29%)
    pallas_call x29, Pallas kernels, call(): pl.pallas_call(functools.partial(after_waits, len(waits), functools.parti...  40.1 us
    ppermute x8, waiting for transfers between devices, across(): lax.ppermute(value, 'expert', [(i, i ^ step) for i in range(z.peers)])  22.1 us
    ppermute x8, starting transfers between devices, across(): lax.ppermute(value, 'expert', [(i, i ^ step) for i in range(z.peers)])  16.9 us
    ppermute x12, waiting for transfers between devices, swap(): return lax.ppermute(value, 'hidden', pairs)  9.34 us
    ppermute x2, waiting for transfers between devices, relayed(): lax.ppermute(pieces[step - z.near], ('section', 'expert'), pairs)  6.16 us
    ppermute x12, starting transfers between devices, swap(): return lax.ppermute(value, 'hidden', pairs)  5.33 us
    ppermute x1, waiting for transfers between devices, relayed(): rows = lax.ppermute(kept, 'section', hop)  4.5 us
    ppermute x3, starting transfers between devices, exchanged(): result[step] = lax.ppermute(pieces[step], 'expert', pairs)  4.45 us
  transfers between devices with their start and end apart: 28, of which 17 were waited for; matrix products, arithmetic and copies ran while one was open for 0% of the time, Pallas kernels for 25%

profile of v1, /device:TPU:2, one launch (start us, length us, event | category | flops | bytes accessed | tf_op | source)
XLA Modules:
  0.0 119.1 jit_solution(16810891026424591770)
XLA Ops:
  1.6 1.6 %collective-permute-start = (bf16[48,1792]{1,0:T(8,128)(2,1)S(1)}, bf16[48,1792]{1,0:T(8,128)(2,1)S(1)}, u32[]{:S(2)}, u32[]{:S(2)}) collective-permute-start(bf16[48,1792]{1,0:T(8,128)(2,1)S(1)} %get-tuple-element.53), channel_id=1, source_target_pairs={{0,4},{4,0},{8,12},{12,8},{1,5},{5,1},{9,13},{13,9},{2,6},{6,2},{1... | collective-permute-start | bytes 516104 | tf_op jit(solution)/shard_map/ppermute | solution.py:367
  3.3 2.6 %collective-permute-start.1 = (bf16[48,1792]{1,0:T(8,128)(2,1)S(1)}, bf16[48,1792]{1,0:T(8,128)(2,1)S(1)}, u32[]{:S(2)}, u32[]{:S(2)}) collective-permute-start(bf16[48,1792]{1,0:T(8,128)(2,1)S(1)} %get-tuple-element.54), channel_id=1, source_target_pairs={{0,8},{4,12},{8,0},{12,4},{1,9},{5,13},{9,1},{13,5},{2,10},{6,14},... | collective-permute-start | bytes 516104 | tf_op jit(solution)/shard_map/ppermute | solution.py:367
  6.1 9.6 %shard_map.56 = (bf16[3584,1024]{1,0:T(8,128)(2,1)S(1)}, bf16[3584,1024]{1,0:T(8,128)(2,1)S(1)}, bf16[3584,1024]{1,0:T(8,128)(2,1)S(1)}, bf16[3584,1024]{1,0:T(8,128)(2,1)S(1)}) custom-call(bf16[192,64]{1,0:T(8,128)(2,1)S(1)} %get-tuple-element.46.refs_0_, bf16[1,1792,2,4096]{3,2,1,0:T(2,128)(2,1)} %refs_1_.3), custom_call_target="tpu_custom_call" | custom-call | tf_op jit(solution)/shard_map/pallas_call | solution.py:335
  15.7 3.2 %shard_map.57 = (bf16[1024,1792]{1,0:T(8,128)(2,1)S(1)}, bf16[1024,1792]{1,0:T(8,128)(2,1)S(1)}) custom-call(bf16[3584,1024]{1,0:T(8,128)(2,1)S(1)} %get-tuple-element.47.refs_0_.refs_2_, bf16[1,4096,1792]{2,1,0:T(8,128)(2,1)} %refs_1_.5), custom_call_target="tpu_custom_call" | custom-call | tf_op jit(solution)/shard_map/pallas_call | solution.py:335
  19.0 3.2 %shard_map.58 = (f32[112,1024]{1,0:T(8,128)S(1)}, bf16[112,1024]{1,0:T(8,128)(2,1)S(1)}) custom-call(bf16[1024,1792]{1,0:T(8,128)(2,1)S(1)} %get-tuple-element.48.refs_0_, bf16[3584,1024]{1,0:T(8,128)(2,1)S(1)} %get-tuple-element.50.refs_1_, bf16[3584,1024]{1,0:T(8,128)(2,1)S(1)} %get-tuple-element.51.refs_2_, ...), custom_call_target="tpu_custom_call" | custom-call | tf_op jit(solution)/shard_map/pallas_call | solution.py:335
  25.3 3.2 %shard_map.64 = (f32[112,1024]{1,0:T(8,128)S(1)}, bf16[112,1024]{1,0:T(8,128)(2,1)S(1)}) custom-call(bf16[112,1024]{1,0:T(8,128)(2,1)S(1)} %shard_map.59.refs_0_.refs_1_, bf16[3584,1024]{1,0:T(8,128)(2,1)S(1)} %get-tuple-element.62.refs_1_, bf16[3584,1024]{1,0:T(8,128)(2,1)S(1)} %get-tuple-element.47.refs_0_.refs_2_, ...), custom_call_target="tpu_custom_call" | custom-call | tf_op jit(solution)/shard_map/pallas_call | solution.py:335
  28.6 3.2 %shard_map.60 = (bf16[1024,1792]{1,0:T(8,128)(2,1)S(1)}, bf16[1024,1792]{1,0:T(8,128)(2,1)S(1)}) custom-call(bf16[112,1024]{1,0:T(8,128)(2,1)S(1)} %shard_map.59.refs_0_.refs_1_, bf16[1,4096,1792]{2,1,0:T(8,128)(2,1)} %refs_1_.5), custom_call_target="tpu_custom_call" | custom-call | tf_op jit(solution)/shard_map/pallas_call | solution.py:335
  35.5 3.8 %collective-permute-start.9 = (bf16[48,1792]{1,0:T(8,128)(2,1)S(1)}, bf16[48,1792]{1,0:T(8,128)(2,1)S(1)}, u32[]{:S(2)}, u32[]{:S(2)}) collective-permute-start(bf16[48,1792]{1,0:T(8,128)(2,1)S(1)} %get-tuple-element.66), channel_id=1, source_target_pairs={{0,8},{4,12},{8,0},{12,4},{1,9},{5,13},{9,1},{13,5},{2,10},{6,14},... | collective-permute-start | bytes 516104 | tf_op jit(solution)/shard_map/ppermute | solution.py:371
  42.6 5.1 %collective-permute-done.9.refs_2_.refs_5_ = bf16[48,1792]{1,0:T(8,128)(2,1)S(1)} collective-permute-done((bf16[48,1792]{1,0:T(8,128)(2,1)S(1)}, bf16[48,1792]{1,0:T(8,128)(2,1)S(1)}, u32[]{:S(2)}, u32[]{:S(2)}) %collective-permute-start.9) | collective-permute-done | bytes 172064 | tf_op jit(solution)/shard_map/ppermute | solution.py:371
  47.8 3.1 %collective-permute-start.11 = (bf16[24,1792]{1,0:T(8,128)(2,1)S(1)}, bf16[24,1792]{1,0:T(8,128)(2,1)S(1)}, u32[]{:S(2)}, u32[]{:S(2)}) collective-permute-start(bf16[24,1792]{1,0:T(8,128)(2,1)S(1)} %get-tuple-element.68), channel_id=1, source_target_pairs={{0,8},{4,12},{8,0},{12,4},{1,9},{5,13},{9,1},{13,5},{2,10},{6,14},... | collective-permute-start | bytes 258056 | tf_op jit(solution)/shard_map/ppermute | solution.py:371
  52.2 2.4 %collective-permute-start.13 = (s32[4,2,16]{2,1,0:T(2,128)S(1)}, s32[4,2,16]{2,1,0:T(2,128)S(1)}, u32[]{:S(2)}, u32[]{:S(2)}) collective-permute-start(s32[4,2,16]{2,1,0:T(2,128)S(1)} %get-tuple-element.70), channel_id=1, source_target_pairs={{16,0},{17,1},{18,2},{19,3},{20,4},{21,5},{22,6},{23,7},{24,8},{25... | collective-permute-start | bytes 1544 | tf_op jit(solution)/shard_map/ppermute | solution.py:497
  56.1 3.6 %collective-permute-done.12.refs_8_ = bf16[24,1792]{1,0:T(8,128)(2,1)S(1)} collective-permute-done((bf16[24,1792]{1,0:T(8,128)(2,1)S(1)}, bf16[24,1792]{1,0:T(8,128)(2,1)S(1)}, u32[]{:S(2)}, u32[]{:S(2)}) %collective-permute-start.12) | collective-permute-done | bytes 86048 | tf_op jit(solution)/shard_map/ppermute | solution.py:371
  64.5 4.5 %collective-permute-done.14.refs_1_ = bf16[64,1792]{1,0:T(8,128)(2,1)S(1)} collective-permute-done((bf16[64,1792]{1,0:T(8,128)(2,1)S(1)}, bf16[64,1792]{1,0:T(8,128)(2,1)S(1)}, u32[]{:S(2)}, u32[]{:S(2)}) %collective-permute-start.14) | collective-permute-done | bytes 229408 | tf_op jit(solution)/shard_map/ppermute | solution.py:389
  69.5 2.0 %collective-permute-start.15 = (bf16[48,1792]{1,0:T(8,128)(2,1)S(1)}, bf16[48,1792]{1,0:T(8,128)(2,1)S(1)}, u32[]{:S(2)}, u32[]{:S(2)}) collective-permute-start(bf16[48,1792]{1,0:T(8,128)(2,1)S(1)} %get-tuple-element.73), channel_id=1, source_target_pairs={{0,4},{4,0},{8,12},{12,8},{1,5},{5,1},{9,13},{13,9},{2,6},{6,2},{1... | collective-permute-start | bytes 516104 | tf_op jit(solution)/shard_map/ppermute | solution.py:400
  71.5 6.2 %collective-permute-done.16.refs_5_ = bf16[48,1792]{1,0:T(8,128)(2,1)S(1)} collective-permute-done((bf16[48,1792]{1,0:T(8,128)(2,1)S(1)}, bf16[48,1792]{1,0:T(8,128)(2,1)S(1)}, u32[]{:S(2)}, u32[]{:S(2)}) %collective-permute-start.16) | collective-permute-done | bytes 172064 | tf_op jit(solution)/shard_map/ppermute | solution.py:396
  77.7 3.2 %shard_map.72 = (f32[112,1024]{1,0:T(8,128)S(1)}, bf16[112,1024]{1,0:T(8,128)(2,1)S(1)}) custom-call(bf16[1024,1792]{1,0:T(8,128)(2,1)S(1)} %get-tuple-element.48.refs_0_, bf16[3584,1024]{1,0:T(8,128)(2,1)S(1)} %get-tuple-element.50.refs_1_, bf16[3584,1024]{1,0:T(8,128)(2,1)S(1)} %get-tuple-element.51.refs_2_, ...), custom_call_target="tpu_custom_call" | custom-call | tf_op jit(solution)/shard_map/pallas_call | solution.py:335
  83.5 3.2 %shard_map.77 = (f32[112,1024]{1,0:T(8,128)S(1)}, bf16[112,1024]{1,0:T(8,128)(2,1)S(1)}) custom-call(bf16[112,1024]{1,0:T(8,128)(2,1)S(1)} %shard_map.73.refs_0_, bf16[3584,1024]{1,0:T(8,128)(2,1)S(1)} %get-tuple-element.62.refs_1_, bf16[3584,1024]{1,0:T(8,128)(2,1)S(1)} %get-tuple-element.47.refs_0_.refs_2_, ...), custom_call_target="tpu_custom_call" | custom-call | tf_op jit(solution)/shard_map/pallas_call | solution.py:335
  86.7 3.4 %collective-permute-done.19.refs_1_ = bf16[112,1024]{1,0:T(8,128)(2,1)S(1)} collective-permute-done((bf16[112,1024]{1,0:T(8,128)(2,1)S(1)}, bf16[112,1024]{1,0:T(8,128)(2,1)S(1)}, u32[]{:S(2)}, u32[]{:S(2)}) %collective-permute-start.19) | collective-permute-done | bytes 229408 | tf_op jit(solution)/shard_map/ppermute | solution.py:359
  93.7 4.2 %collective-permute-start.24 = (bf16[48,1792]{1,0:T(8,128)(2,1)S(1)}, bf16[48,1792]{1,0:T(8,128)(2,1)S(1)}, u32[]{:S(2)}, u32[]{:S(2)}) collective-permute-start(bf16[48,1792]{1,0:T(8,128)(2,1)S(1)} %get-tuple-element.83), channel_id=1, source_target_pairs={{0,8},{4,12},{8,0},{12,4},{1,9},{5,13},{9,1},{13,5},{2,10},{6,14},... | collective-permute-start | bytes 516104 | tf_op jit(solution)/shard_map/ppermute | solution.py:371
  100.4 5.9 %collective-permute-done.24.refs_2_.refs_5_ = bf16[48,1792]{1,0:T(8,128)(2,1)S(1)} collective-permute-done((bf16[48,1792]{1,0:T(8,128)(2,1)S(1)}, bf16[48,1792]{1,0:T(8,128)(2,1)S(1)}, u32[]{:S(2)}, u32[]{:S(2)}) %collective-permute-start.24) | collective-permute-done | bytes 172064 | tf_op jit(solution)/shard_map/ppermute | solution.py:371
  106.4 2.5 %collective-permute-start.26 = (bf16[24,1792]{1,0:T(8,128)(2,1)S(1)}, bf16[24,1792]{1,0:T(8,128)(2,1)S(1)}, u32[]{:S(2)}, u32[]{:S(2)}) collective-permute-start(bf16[24,1792]{1,0:T(8,128)(2,1)S(1)} %get-tuple-element.85), channel_id=1, source_target_pairs={{0,8},{4,12},{8,0},{12,4},{1,9},{5,13},{9,1},{13,5},{2,10},{6,14},... | collective-permute-start | bytes 258056 | tf_op jit(solution)/shard_map/ppermute | solution.py:371
  108.9 1.8 %collective-permute-start.27 = (bf16[24,1792]{1,0:T(8,128)(2,1)S(1)}, bf16[24,1792]{1,0:T(8,128)(2,1)S(1)}, u32[]{:S(2)}, u32[]{:S(2)}) collective-permute-start(bf16[24,1792]{1,0:T(8,128)(2,1)S(1)} %get-tuple-element.86), channel_id=1, source_target_pairs={{0,12},{4,8},{8,4},{12,0},{1,13},{5,9},{9,5},{13,1},{2,14},{6,10},... | collective-permute-start | bytes 258056 | tf_op jit(solution)/shard_map/ppermute | solution.py:371
  110.8 3.9 %collective-permute-done.26.refs_7_ = bf16[24,1792]{1,0:T(8,128)(2,1)S(1)} collective-permute-done((bf16[24,1792]{1,0:T(8,128)(2,1)S(1)}, bf16[24,1792]{1,0:T(8,128)(2,1)S(1)}, u32[]{:S(2)}, u32[]{:S(2)}) %collective-permute-start.26) | collective-permute-done | bytes 86048 | tf_op jit(solution)/shard_map/ppermute | solution.py:371
  114.7 3.4 %collective-permute-done.27.refs_8_ = bf16[24,1792]{1,0:T(8,128)(2,1)S(1)} collective-permute-done((bf16[24,1792]{1,0:T(8,128)(2,1)S(1)}, bf16[24,1792]{1,0:T(8,128)(2,1)S(1)}, u32[]{:S(2)}, u32[]{:S(2)}) %collective-permute-start.27) | collective-permute-done | bytes 86048 | tf_op jit(solution)/shard_map/ppermute | solution.py:371
  (65 shorter events, 29.9 us)
Async XLA Ops:
  1.6 17.3 %collective-permute-start = (bf16[48,1792]{1,0:T(8,128)(2,1)S(1)}, bf16[48,1792]{1,0:T(8,128)(2,1)S(1)}, u32[]{:S(2)}, u32[]{:S(2)}) collective-permute-start(bf16[48,1792]{1,0:T(8,128)(2,1)S(1)} %get-tuple-element.53), channel_id=1, source_target_pairs={{0,4},{4,0},{8,12},{12,8},{1,5},{5,1},{9,13},{13,9},{2,6},{6,2},{1... | collective-permute-start | bytes 516104 | tf_op jit(solution)/shard_map/ppermute | solution.py:367
  3.3 15.7 %collective-permute-start.1 = (bf16[48,1792]{1,0:T(8,128)(2,1)S(1)}, bf16[48,1792]{1,0:T(8,128)(2,1)S(1)}, u32[]{:S(2)}, u32[]{:S(2)}) collective-permute-start(bf16[48,1792]{1,0:T(8,128)(2,1)S(1)} %get-tuple-element.54), channel_id=1, source_target_pairs={{0,8},{4,12},{8,0},{12,4},{1,9},{5,13},{9,1},{13,5},{2,10},{6,14},... | collective-permute-start | bytes 516104 | tf_op jit(solution)/shard_map/ppermute | solution.py:367
  5.9 13.1 %collective-permute-start.2 = (bf16[48,1792]{1,0:T(8,128)(2,1)S(1)}, bf16[48,1792]{1,0:T(8,128)(2,1)S(1)}, u32[]{:S(2)}, u32[]{:S(2)}) collective-permute-start(bf16[48,1792]{1,0:T(8,128)(2,1)S(1)} %get-tuple-element.55), channel_id=1, source_target_pairs={{0,12},{4,8},{8,4},{12,0},{1,13},{5,9},{9,5},{13,1},{2,14},{6,10},... | collective-permute-start | bytes 516104 | tf_op jit(solution)/shard_map/ppermute | solution.py:367
  22.1 1.6 %collective-permute-start.3 = (bf16[112,1024]{1,0:T(8,128)(2,1)S(1)}, bf16[112,1024]{1,0:T(8,128)(2,1)S(1)}, u32[]{:S(2)}, u32[]{:S(2)}) collective-permute-start(bf16[112,1024]{1,0:T(8,128)(2,1)S(1)} %get-tuple-element.57), channel_id=1, source_target_pairs={{0,1},{1,0},{2,3},{3,2},{4,5},{5,4},{6,7},{7,6},{8,9},{9,8},{10,11... | collective-permute-start | bytes 688136 | tf_op jit(solution)/shard_map/ppermute | solution.py:359
  23.7 8.0 %collective-permute-start.4 = (bf16[112,1024]{1,0:T(8,128)(2,1)S(1)}, bf16[112,1024]{1,0:T(8,128)(2,1)S(1)}, u32[]{:S(2)}, u32[]{:S(2)}) collective-permute-start(bf16[112,1024]{1,0:T(8,128)(2,1)S(1)} %shard_map.59.refs_0_.refs_1_), channel_id=1, source_target_pairs={{0,2},{1,3},{2,0},{3,1},{4,6},{5,7},{6,4},{7,5},{8,10},{9,11},{10,... | collective-permute-start | bytes 688136 | tf_op jit(solution)/shard_map/ppermute | solution.py:359
  28.5 3.5 %collective-permute-start.6 = (bf16[112,1024]{1,0:T(8,128)(2,1)S(1)}, bf16[112,1024]{1,0:T(8,128)(2,1)S(1)}, u32[]{:S(2)}, u32[]{:S(2)}) collective-permute-start(bf16[112,1024]{1,0:T(8,128)(2,1)S(1)} %get-tuple-element.64), channel_id=1, source_target_pairs={{0,1},{1,0},{2,3},{3,2},{4,5},{5,4},{6,7},{7,6},{8,9},{9,8},{10,11... | collective-permute-start | bytes 688136 | tf_op jit(solution)/shard_map/ppermute | solution.py:359
  32.0 8.1 %collective-permute-start.7 = (bf16[112,1024]{1,0:T(8,128)(2,1)S(1)}, bf16[112,1024]{1,0:T(8,128)(2,1)S(1)}, u32[]{:S(2)}, u32[]{:S(2)}) collective-permute-start(bf16[112,1024]{1,0:T(8,128)(2,1)S(1)} %shard_map.65.refs_1_), channel_id=1, source_target_pairs={{0,2},{1,3},{2,0},{3,1},{4,6},{5,7},{6,4},{7,5},{8,10},{9,11},{10,... | collective-permute-start | bytes 688136 | tf_op jit(solution)/shard_map/ppermute | solution.py:359
  35.5 12.2 %collective-permute-start.9 = (bf16[48,1792]{1,0:T(8,128)(2,1)S(1)}, bf16[48,1792]{1,0:T(8,128)(2,1)S(1)}, u32[]{:S(2)}, u32[]{:S(2)}) collective-permute-start(bf16[48,1792]{1,0:T(8,128)(2,1)S(1)} %get-tuple-element.66), channel_id=1, source_target_pairs={{0,8},{4,12},{8,0},{12,4},{1,9},{5,13},{9,1},{13,5},{2,10},{6,14},... | collective-permute-start | bytes 516104 | tf_op jit(solution)/shard_map/ppermute | solution.py:371
  47.7 12.0 %collective-permute-start.10 = (bf16[72,1792]{1,0:T(8,128)(2,1)S(1)}, bf16[72,1792]{1,0:T(8,128)(2,1)S(1)}, u32[]{:S(2)}, u32[]{:S(2)}) collective-permute-start(bf16[72,1792]{1,0:T(8,128)(2,1)S(1)} %shard_map.69), channel_id=1, source_target_pairs={{0,4},{4,0},{8,12},{12,8},{1,5},{5,1},{9,13},{13,9},{2,6},{6,2},{1... | collective-permute-start | bytes 774152 | tf_op jit(solution)/shard_map/ppermute | solution.py:371
  47.8 8.3 %collective-permute-start.11 = (bf16[24,1792]{1,0:T(8,128)(2,1)S(1)}, bf16[24,1792]{1,0:T(8,128)(2,1)S(1)}, u32[]{:S(2)}, u32[]{:S(2)}) collective-permute-start(bf16[24,1792]{1,0:T(8,128)(2,1)S(1)} %get-tuple-element.68), channel_id=1, source_target_pairs={{0,8},{4,12},{8,0},{12,4},{1,9},{5,13},{9,1},{13,5},{2,10},{6,14},... | collective-permute-start | bytes 258056 | tf_op jit(solution)/shard_map/ppermute | solution.py:371
  50.9 8.8 %collective-permute-start.12 = (bf16[24,1792]{1,0:T(8,128)(2,1)S(1)}, bf16[24,1792]{1,0:T(8,128)(2,1)S(1)}, u32[]{:S(2)}, u32[]{:S(2)}) collective-permute-start(bf16[24,1792]{1,0:T(8,128)(2,1)S(1)} %get-tuple-element.69), channel_id=1, source_target_pairs={{0,12},{4,8},{8,4},{12,0},{1,13},{5,9},{9,5},{13,1},{2,14},{6,10},... | collective-permute-start | bytes 258056 | tf_op jit(solution)/shard_map/ppermute | solution.py:371
  52.2 3.8 %collective-permute-start.13 = (s32[4,2,16]{2,1,0:T(2,128)S(1)}, s32[4,2,16]{2,1,0:T(2,128)S(1)}, u32[]{:S(2)}, u32[]{:S(2)}) collective-permute-start(s32[4,2,16]{2,1,0:T(2,128)S(1)} %get-tuple-element.70), channel_id=1, source_target_pairs={{16,0},{17,1},{18,2},{19,3},{20,4},{21,5},{22,6},{23,7},{24,8},{25... | collective-permute-start | bytes 1544 | tf_op jit(solution)/shard_map/ppermute | solution.py:497
  60.4 8.6 %collective-permute-start.14 = (bf16[64,1792]{1,0:T(8,128)(2,1)S(1)}, bf16[64,1792]{1,0:T(8,128)(2,1)S(1)}, u32[]{:S(2)}, u32[]{:S(2)}) collective-permute-start(bf16[64,1792]{1,0:T(8,128)(2,1)S(1)} %get-tuple-element.71.refs_2_), channel_id=1, source_target_pairs={{0,16},{1,17},{2,18},{3,19},{4,20},{5,21},{6,22},{7,23},{8,24},{9,... | collective-permute-start | bytes 688136 | tf_op jit(solution)/shard_map/ppermute | solution.py:389
  61.7 16.0 %collective-permute-start.16 = (bf16[48,1792]{1,0:T(8,128)(2,1)S(1)}, bf16[48,1792]{1,0:T(8,128)(2,1)S(1)}, u32[]{:S(2)}, u32[]{:S(2)}) collective-permute-start(bf16[48,1792]{1,0:T(8,128)(2,1)S(1)} %get-tuple-element.74), channel_id=1, source_target_pairs={{0,24},{4,28},{8,16},{12,20},{1,25},{5,29},{9,17},{13,21},{2,26},{... | collective-permute-start | bytes 516104 | tf_op jit(solution)/shard_map/ppermute | solution.py:396
  63.0 14.7 %collective-permute-start.17 = (bf16[48,1792]{1,0:T(8,128)(2,1)S(1)}, bf16[48,1792]{1,0:T(8,128)(2,1)S(1)}, u32[]{:S(2)}, u32[]{:S(2)}) collective-permute-start(bf16[48,1792]{1,0:T(8,128)(2,1)S(1)} %get-tuple-element.75), channel_id=1, source_target_pairs={{0,28},{4,24},{8,20},{12,16},{1,29},{5,25},{9,21},{13,17},{2,30},{... | collective-permute-start | bytes 516104 | tf_op jit(solution)/shard_map/ppermute | solution.py:396
  69.5 8.2 %collective-permute-start.15 = (bf16[48,1792]{1,0:T(8,128)(2,1)S(1)}, bf16[48,1792]{1,0:T(8,128)(2,1)S(1)}, u32[]{:S(2)}, u32[]{:S(2)}) collective-permute-start(bf16[48,1792]{1,0:T(8,128)(2,1)S(1)} %get-tuple-element.73), channel_id=1, source_target_pairs={{0,4},{4,0},{8,12},{12,8},{1,5},{5,1},{9,13},{13,9},{2,6},{6,2},{1... | collective-permute-start | bytes 516104 | tf_op jit(solution)/shard_map/ppermute | solution.py:400
  80.8 1.6 %collective-permute-start.18 = (bf16[112,1024]{1,0:T(8,128)(2,1)S(1)}, bf16[112,1024]{1,0:T(8,128)(2,1)S(1)}, u32[]{:S(2)}, u32[]{:S(2)}) collective-permute-start(bf16[112,1024]{1,0:T(8,128)(2,1)S(1)} %get-tuple-element.77), channel_id=1, source_target_pairs={{0,1},{1,0},{2,3},{3,2},{4,5},{5,4},{6,7},{7,6},{8,9},{9,8},{10,11... | collective-permute-start | bytes 688136 | tf_op jit(solution)/shard_map/ppermute | solution.py:359
  82.5 7.7 %collective-permute-start.19 = (bf16[112,1024]{1,0:T(8,128)(2,1)S(1)}, bf16[112,1024]{1,0:T(8,128)(2,1)S(1)}, u32[]{:S(2)}, u32[]{:S(2)}) collective-permute-start(bf16[112,1024]{1,0:T(8,128)(2,1)S(1)} %shard_map.73.refs_0_), channel_id=1, source_target_pairs={{0,2},{1,3},{2,0},{3,1},{4,6},{5,7},{6,4},{7,5},{8,10},{9,11},{10,... | collective-permute-start | bytes 688136 | tf_op jit(solution)/shard_map/ppermute | solution.py:359
  86.7 3.7 %collective-permute-start.21 = (bf16[112,1024]{1,0:T(8,128)(2,1)S(1)}, bf16[112,1024]{1,0:T(8,128)(2,1)S(1)}, u32[]{:S(2)}, u32[]{:S(2)}) collective-permute-start(bf16[112,1024]{1,0:T(8,128)(2,1)S(1)} %get-tuple-element.81), channel_id=1, source_target_pairs={{0,1},{1,0},{2,3},{3,2},{4,5},{5,4},{6,7},{7,6},{8,9},{9,8},{10,11... | collective-permute-start | bytes 688136 | tf_op jit(solution)/shard_map/ppermute | solution.py:359
  90.4 7.5 %collective-permute-start.22 = (bf16[112,1024]{1,0:T(8,128)(2,1)S(1)}, bf16[112,1024]{1,0:T(8,128)(2,1)S(1)}, u32[]{:S(2)}, u32[]{:S(2)}) collective-permute-start(bf16[112,1024]{1,0:T(8,128)(2,1)S(1)} %shard_map.78.refs_1_), channel_id=1, source_target_pairs={{0,2},{1,3},{2,0},{3,1},{4,6},{5,7},{6,4},{7,5},{8,10},{9,11},{10,... | collective-permute-start | bytes 688136 | tf_op jit(solution)/shard_map/ppermute | solution.py:359
  93.7 12.6 %collective-permute-start.24 = (bf16[48,1792]{1,0:T(8,128)(2,1)S(1)}, bf16[48,1792]{1,0:T(8,128)(2,1)S(1)}, u32[]{:S(2)}, u32[]{:S(2)}) collective-permute-start(bf16[48,1792]{1,0:T(8,128)(2,1)S(1)} %get-tuple-element.83), channel_id=1, source_target_pairs={{0,8},{4,12},{8,0},{12,4},{1,9},{5,13},{9,1},{13,5},{2,10},{6,14},... | collective-permute-start | bytes 516104 | tf_op jit(solution)/shard_map/ppermute | solution.py:371
  106.3 11.8 %collective-permute-start.25 = (bf16[72,1792]{1,0:T(8,128)(2,1)S(1)}, bf16[72,1792]{1,0:T(8,128)(2,1)S(1)}, u32[]{:S(2)}, u32[]{:S(2)}) collective-permute-start(bf16[72,1792]{1,0:T(8,128)(2,1)S(1)} %shard_map.82), channel_id=1, source_target_pairs={{0,4},{4,0},{8,12},{12,8},{1,5},{5,1},{9,13},{13,9},{2,6},{6,2},{1... | collective-permute-start | bytes 774152 | tf_op jit(solution)/shard_map/ppermute | solution.py:371
  106.4 8.3 %collective-permute-start.26 = (bf16[24,1792]{1,0:T(8,128)(2,1)S(1)}, bf16[24,1792]{1,0:T(8,128)(2,1)S(1)}, u32[]{:S(2)}, u32[]{:S(2)}) collective-permute-start(bf16[24,1792]{1,0:T(8,128)(2,1)S(1)} %get-tuple-element.85), channel_id=1, source_target_pairs={{0,8},{4,12},{8,0},{12,4},{1,9},{5,13},{9,1},{13,5},{2,10},{6,14},... | collective-permute-start | bytes 258056 | tf_op jit(solution)/shard_map/ppermute | solution.py:371
  108.9 9.1 %collective-permute-start.27 = (bf16[24,1792]{1,0:T(8,128)(2,1)S(1)}, bf16[24,1792]{1,0:T(8,128)(2,1)S(1)}, u32[]{:S(2)}, u32[]{:S(2)}) collective-permute-start(bf16[24,1792]{1,0:T(8,128)(2,1)S(1)} %get-tuple-element.86), channel_id=1, source_target_pairs={{0,12},{4,8},{8,4},{12,0},{1,13},{5,9},{9,5},{13,1},{2,14},{6,10},... | collective-permute-start | bytes 258056 | tf_op jit(solution)/shard_map/ppermute | solution.py:371
  (6 other events, 32.3 us)

commit v2 on v1

--- a/solution.py
+++ b/solution.py
@@ -12,6 +12,7 @@
 CAP = 3
 EPS = 1e-06
 EXTRA = 16
+CUTS = 2
 VMEM = pl.BlockSpec(memory_space=pltpu.VMEM)
 HBM = pl.BlockSpec(memory_space=pltpu.HBM)
 BF16 = jnp.bfloat16
@@ -56,6 +57,7 @@
         self.pieces = peers if peers <= 8 else 1
         self.pairs = self.groups - 1 if self.pieces == 4 else 0
         self.near = self.pieces // 2
+        self.repacked = [step for step in range(self.pieces) if step != self.near]
         self.group_pay = peers * self.pay
         self.piece = self.group_pay // self.pieces
         self.all_pay = self.groups * self.group_pay
@@ -110,16 +112,16 @@
     return hits, first, second
 
 
-def send_rows(z, hits, rows, outs, first):
-    low = first * z.all_piece
-    value = dot(hits[low:low + len(outs) * z.all_piece].astype(BF16), rows)
+def send_rows(z, hits, rows, outs, steps):
+    hits = [hits[step * z.all_piece:(step + 1) * z.all_piece] for step in steps]
+    value = dot(jnp.concatenate(hits, axis=0).astype(BF16), rows)
     for index, out in enumerate(outs):
         out[...] = value[index * z.all_piece:(index + 1) * z.all_piece].astype(BF16)
 
 
-def near_kernel(z, routes_ref, rows_ref, *outs):
+def repack_kernel(z, routes_ref, rows_ref, *outs):
     hits, _, _ = slot_hits(z, routes_ref)
-    send_rows(z, hits, rows_ref[...], outs, 0)
+    send_rows(z, hits, rows_ref[...], outs, z.repacked)
 
 
 def group_rows(z, group, pieces):
@@ -147,7 +149,7 @@
     gates = line_up(z, gates_ref)
     weight = jnp.where(first, gates[0:1, :], F32(0.0)) + jnp.where(second, gates[1:2, :], F32(0.0))
     outs[-1][...] = (hits * weight).astype(BF16)
-    send_rows(z, hits, rows_ref[...], outs[:-1], 0)
+    send_rows(z, hits, rows_ref[...], outs[:-1], range(z.pieces))
 
 
 def load_kernel(z, parts, gate_up, *refs):
@@ -196,7 +198,7 @@
 def up_kernel(z, group, *refs):
     weights, refs = refs[:z.members], refs[z.members:]
     received, refs = refs[:z.pieces], refs[z.pieces:]
-    own, sent, spread, staged = refs
+    own, *sent, spread, staged = refs
     rows = dot(z.order(), group_rows(z, group, received).astype(BF16))
     squares = rows * rows
     high = squares.astype(BF16)
@@ -225,7 +227,10 @@
         staged[side, z.group_each:, :] = extra
     core = lax.axis_index("hidden") & 1
     own[...] = staged[core]
-    sent[...] = staged[1 - core].astype(BF16)
+    rows = z.partial[0] // CUTS
+    value = staged[1 - core]
+    for index, out in enumerate(sent):
+        out[...] = value[index * rows:(index + 1) * rows].astype(BF16)
 
 
 def joined(z, refs):
@@ -238,8 +243,9 @@
     return products, sums
 
 
-def pair_kernel(z, own, other, out):
-    products, sums = joined(z, (own, other))
+def pair_kernel(z, own, *refs):
+    *other, out = refs
+    products, sums = joined(z, [own[...], jnp.concatenate([ref[...].astype(F32) for ref in other], axis=0)])
     out[:z.group_each, :] = products.astype(BF16)
     sums = jnp.broadcast_to(sums, (EXTRA, 2 * z.half))
     out[z.group_each:, :] = split_sums(sums, 2 * z.half).astype(BF16)
@@ -289,27 +295,13 @@
         low += out.shape[0]
 
 
-def near_back_kernel(z, *refs):
-    *blocks, out = refs
-    values = [ref[...].astype(F32)[-z.piece:] for ref in blocks]
-    out[...] = jnp.concatenate(values, axis=0).astype(BF16)
+def second_kernel(z, pair_ref, out):
+    out[...] = pair_ref[...].astype(F32)[z.piece:].astype(BF16)
 
 
 def combine_kernel(z, tick, last, weight_ref, rows_ref, kept_ref, *refs):
-    if z.pairs:
-        near = refs[0][...].astype(F32)
-        near = [near[low:low + z.piece] for low in range(0, near.shape[0], z.piece)]
-        returned, refs = [], refs[1:]
-        for group in range(z.groups):
-            if group < z.pairs:
-                values, refs = [ref[...].astype(F32)[:z.piece] for ref in refs[:2]], refs[2:]
-                returned += [values[0], near[group], values[1], near[z.groups + group]]
-            else:
-                values, refs = [ref[...].astype(F32) for ref in refs[:3]], refs[3:]
-                returned += [values[0], near[group], values[1], values[2]]
-    else:
-        count = z.groups * z.pieces
-        returned, refs = [ref[...].astype(F32) for ref in refs[:count]], refs[count:]
+    count = z.groups * z.pieces
+    returned, refs = [ref[...].astype(F32)[:z.piece] for ref in refs[:count]], refs[count:]
     stacked = []
     for piece in range(z.pieces):
         values = [returned[group * z.pieces + piece] for group in range(z.groups)]
@@ -324,7 +316,7 @@
     routes_ref, out, outs = refs[0], refs[1], refs[2:]
     out[...] = jnp.where(lax.axis_index("section") == tick, value, kept_ref[...])
     hits, _, _ = slot_hits(z, routes_ref)
-    send_rows(z, hits, value, outs, z.near)
+    send_rows(z, hits, value, outs, [z.near])
 
 
 def after_waits(waits, kernel, *refs):
@@ -371,34 +363,26 @@
         return lax.ppermute(value, "expert", [(i, i ^ step) for i in range(z.peers)])
 
     def sent_back(pieces, group):
-        if not z.pairs:
+        if group >= z.pairs:
             return exchanged(pieces)
-        own, near, *far = pieces
-        return [own, near] + [across(value, 2 + step) for step, value in enumerate(far)]
-
-    def near_back(returned):
-        if not z.pairs:
-            return sum(returned, [])
-        blocks = [pieces[1] for pieces in returned] + [pieces[2] for pieces in returned[:z.pairs]]
-        rows = shape((len(blocks) * z.piece, z.width), BF16)
-        joint = call(near_back_kernel, (z,), 4, [rows], [VMEM] * len(blocks), [], *blocks)[0]
-        return [across(joint, 1)] + sum([pieces[:1] + pieces[2:] for pieces in returned], [])
+        own, near, far = pieces
+        far = across(far, 2)
+        second = call(second_kernel, (z,), 2, [pay], [VMEM], [], far)[0]
+        return [own, across(near, 1), far, across(second, 1)]
 
     def relayed(pieces, kept, tick):
         hop = [(tick, tick + 1)]
         rows = lax.ppermute(kept, "section", hop)
         if z.pieces == 1:
             return rows, [lax.ppermute(exchanged(pieces)[0], "section", hop)]
-        far = {}
-        for step in steps:
-            if step >= z.near:
-                pairs = [(tick * z.peers + i, (tick + 1) * z.peers + (i ^ step)) for i in range(z.peers)]
-                far[step] = lax.ppermute(pieces[step - z.near], ("section", "expert"), pairs)
-        result = call(near_kernel, (z,), 4, [all_pay] * z.near, [VMEM] * 2, [], routes, rows)
-        for step in range(1, z.near):
-            pairs = [(i, i ^ step) for i in range(z.peers)]
-            result[step] = lax.ppermute(result[step], "expert", pairs)
-        return rows, result + [far[step] for step in range(z.near, z.peers)]
+        pairs = [(tick * z.peers + i, (tick + 1) * z.peers + (i ^ z.near)) for i in range(z.peers)]
+        far = lax.ppermute(pieces[0], ("section", "expert"), pairs)
+        result = call(repack_kernel, (z,), 4, [all_pay] * (z.pieces - 1), [VMEM] * 2, [], routes, rows)
+        result.insert(z.near, far)
+        for step in steps[:-1]:
+            if step != z.near:
+                result[step] = across(result[step], step)
+        return rows, result
 
     def load_down(group, after):
         return call(
@@ -408,9 +392,9 @@
         )
 
     def products(received, group, waits):
-        own, sent = call(
+        own, *sent = call(
             up_kernel, (z, group), 6,
-            [shape(z.partial, F32), shape(z.partial, BF16)],
+            [shape(z.partial, F32)] + [shape((z.partial[0] // CUTS, z.partial[1]), BF16)] * CUTS,
             [VMEM] * (z.members + z.pieces),
             [
                 pltpu.VMEM((z.members, 2 * z.each, 2 * z.width), BF16),
@@ -419,11 +403,11 @@
             *wide[group * z.members:(group + 1) * z.members], *received,
             waits=waits if group else tall[0][:1],
         )
-        return own, swap(sent, 1)
+        return own, [swap(value, 1) for value in sent]
 
     def pair_sums(own, other, waits):
         pair = call(
-            pair_kernel, (z,), 2, [shape(z.partial, BF16)], [VMEM] * 2, [], own, other, waits=waits
+            pair_kernel, (z,), 2, [shape(z.partial, BF16)], [VMEM] * (1 + CUTS), [], own, *other, waits=waits
         )[0]
         return [pair] + [swap(pair, step) for step in range(2, z.splits, 2)]
 
@@ -486,7 +470,6 @@
                 early = tall[-1][:1]
             if group == 0:
                 halves = activated(sums[0], early)
-                waits = list(halves[0][:1])
         for group in groups:
             if group:
                 halves = activated(sums[group], outgoing[:1])
@@ -496,10 +479,10 @@
                 pairs = [(i + 1, i) for i in range(sections - 1)]
                 following = lax.ppermute(outgoing.pop(), "section", pairs)
             returned.append(sent_back(outgoing, group))
-        returned = near_back(returned)
+        returned = sum(returned, [])
         kept, *sent = call(
             combine_kernel, (z, tick, last), 4,
-            [whole] if last else [whole] + [all_pay] * (z.pieces - z.near),
+            [whole] if last else [whole, all_pay],
             [VMEM] * (3 + len(returned) + (not last)), [],
             weight, rows, kept, *returned, *([] if last else [following]),
         )

time: 121 us -> 115 us (0.950); the launches traced: 119 us -> 115 us
  waiting for transfers between devices: 43.4 us -> 37 us
  starting transfers between devices: 35.2 us -> 37.3 us
    ppermute x8, waiting for transfers between devices: 22.1 us -> 12.2 us  [across(): lax.ppermute(value, 'expert', [(i, i ^ step) for i in range(z.peers)])]
    ppermute x3 -> x9, starting transfers between devices: 4.45 us -> 13.4 us  [exchanged(): result[step] = lax.ppermute(pieces[step], 'expert', pairs)]
    ppermute x3 -> x9, waiting for transfers between devices: 0.01 us -> 5.82 us  [exchanged(): result[step] = lax.ppermute(pieces[step], 'expert', pairs)]
    ppermute x3 -> x1, waiting for transfers between devices: 6.16 us -> 0.5 us  [relayed(): far = lax.ppermute(pieces[0], ('section', 'expert'), pairs)]
    ppermute x8, starting transfers between devices: 16.9 us -> 11.8 us  [across(): lax.ppermute(value, 'expert', [(i, i ^ step) for i in range(z.peers)])]
    ppermute x3 -> x1, starting transfers between devices: 4.79 us -> 1.47 us  [relayed(): far = lax.ppermute(pieces[0], ('section', 'expert'), pairs)]
    ppermute x1, waiting for transfers between devices: 4.5 us -> 6.97 us  [relayed(): rows = lax.ppermute(kept, 'section', hop)]
    ppermute x12 -> x16, starting transfers between devices: 5.33 us -> 6.94 us  [swap(): return lax.ppermute(value, 'hidden', pairs)]
  transfers between devices with their start and end apart: 28 -> 36, of which waited for: 17 -> 24; matrix products, arithmetic and copies ran while one was open for 0% -> 0% of each run, Pallas kernels for 25% -> 26%
where the time goes in v2:
time: 115 us
  Pallas kernels  40.1 us (35%)
  starting transfers between devices  37.3 us (32%)
  waiting for transfers between devices  37 us (32%)
    pallas_call x29, Pallas kernels, call(): pl.pallas_call(functools.partial(after_waits, len(waits), functools.parti...  40.1 us
    ppermute x9, starting transfers between devices, exchanged(): result[step] = lax.ppermute(pieces[step], 'expert', pairs)  13.4 us
    ppermute x8, waiting for transfers between devices, across(): lax.ppermute(value, 'expert', [(i, i ^ step) for i in range(z.peers)])  12.2 us
    ppermute x8, starting transfers between devices, across(): lax.ppermute(value, 'expert', [(i, i ^ step) for i in range(z.peers)])  11.8 us
    ppermute x16, waiting for transfers between devices, swap(): return lax.ppermute(value, 'hidden', pairs)  10.2 us
    ppermute x1, waiting for transfers between devices, relayed(): rows = lax.ppermute(kept, 'section', hop)  6.97 us
    ppermute x16, starting transfers between devices, swap(): return lax.ppermute(value, 'hidden', pairs)  6.94 us
    ppermute x9, waiting for transfers between devices, exchanged(): result[step] = lax.ppermute(pieces[step], 'expert', pairs)  5.82 us
  transfers between devices with their start and end apart: 36, of which 24 were waited for; matrix products, arithmetic and copies ran while one was open for 0% of the time, Pallas kernels for 26%

profile of v2, /device:TPU:2, one launch (start us, length us, event | category | flops | bytes accessed | tf_op | source)
XLA Modules:
  0.0 114.7 jit_solution(5823721371600671855)
XLA Ops:
  0.0 1.6 %shard_map.55 = (bf16[48,1792]{1,0:T(8,128)(2,1)S(1)}, bf16[48,1792]{1,0:T(8,128)(2,1)S(1)}, bf16[48,1792]{1,0:T(8,128)(2,1)S(1)}, bf16[48,1792]{1,0:T(8,128)(2,1)S(1)}, bf16[192,64]{1,0:T(8,128)(2,1)S(1)}) custom-call(s32[4,2,16]{2,1,0:T(2,128)} %bitcast.11, bf16[4,2,16]{2,1,0:T(2,128)(2,1)} %bitcast.14, bf16[64,1792]{1,0:T(8,128)(2,1)} %bitcast.8), custom_call_target="tpu_custom_call" | custom-call | tf_op jit(solution)/shard_map/pallas_call | solution.py:327
  1.6 1.6 %collective-permute-start = (bf16[48,1792]{1,0:T(8,128)(2,1)S(1)}, bf16[48,1792]{1,0:T(8,128)(2,1)S(1)}, u32[]{:S(2)}, u32[]{:S(2)}) collective-permute-start(bf16[48,1792]{1,0:T(8,128)(2,1)S(1)} %get-tuple-element.57), channel_id=1, source_target_pairs={{0,4},{4,0},{8,12},{12,8},{1,5},{5,1},{9,13},{13,9},{2,6},{6,2},{1... | collective-permute-start | bytes 516104 | tf_op jit(solution)/shard_map/ppermute | solution.py:359
  3.3 2.6 %collective-permute-start.1 = (bf16[48,1792]{1,0:T(8,128)(2,1)S(1)}, bf16[48,1792]{1,0:T(8,128)(2,1)S(1)}, u32[]{:S(2)}, u32[]{:S(2)}) collective-permute-start(bf16[48,1792]{1,0:T(8,128)(2,1)S(1)} %get-tuple-element.58), channel_id=1, source_target_pairs={{0,8},{4,12},{8,0},{12,4},{1,9},{5,13},{9,1},{13,5},{2,10},{6,14},... | collective-permute-start | bytes 516104 | tf_op jit(solution)/shard_map/ppermute | solution.py:359
  6.1 9.6 %shard_map.56 = (bf16[3584,1024]{1,0:T(8,128)(2,1)S(1)}, bf16[3584,1024]{1,0:T(8,128)(2,1)S(1)}, bf16[3584,1024]{1,0:T(8,128)(2,1)S(1)}, bf16[3584,1024]{1,0:T(8,128)(2,1)S(1)}) custom-call(bf16[192,64]{1,0:T(8,128)(2,1)S(1)} %get-tuple-element.50.refs_0_, bf16[1,1792,2,4096]{3,2,1,0:T(2,128)(2,1)} %refs_1_.3), custom_call_target="tpu_custom_call" | custom-call | tf_op jit(solution)/shard_map/pallas_call | solution.py:327
  15.7 3.2 %shard_map.57 = (bf16[1024,1792]{1,0:T(8,128)(2,1)S(1)}, bf16[1024,1792]{1,0:T(8,128)(2,1)S(1)}) custom-call(bf16[3584,1024]{1,0:T(8,128)(2,1)S(1)} %get-tuple-element.51.refs_0_.refs_2_, bf16[1,4096,1792]{2,1,0:T(8,128)(2,1)} %refs_1_.5), custom_call_target="tpu_custom_call" | custom-call | tf_op jit(solution)/shard_map/pallas_call | solution.py:327
  19.0 3.2 %shard_map.58 = (f32[112,1024]{1,0:T(8,128)S(1)}, bf16[56,1024]{1,0:T(8,128)(2,1)S(1)}, bf16[56,1024]{1,0:T(8,128)(2,1)S(1)}) custom-call(bf16[1024,1792]{1,0:T(8,128)(2,1)S(1)} %get-tuple-element.52.refs_0_, bf16[3584,1024]{1,0:T(8,128)(2,1)S(1)} %get-tuple-element.54.refs_1_, bf16[3584,1024]{1,0:T(8,128)(2,1)S(1)} %get-tuple-element.55.refs_2_, ...), custom_call_target="tpu_custom_call" | custom-call | tf_op jit(solution)/shard_map/pallas_call | solution.py:327
  25.3 3.2 %shard_map.65 = (f32[112,1024]{1,0:T(8,128)S(1)}, bf16[56,1024]{1,0:T(8,128)(2,1)S(1)}, bf16[56,1024]{1,0:T(8,128)(2,1)S(1)}) custom-call(bf16[112,1024]{1,0:T(8,128)(2,1)S(1)} %shard_map.59.refs_0_.refs_1_, bf16[3584,1024]{1,0:T(8,128)(2,1)S(1)} %get-tuple-element.68.refs_1_, bf16[3584,1024]{1,0:T(8,128)(2,1)S(1)} %get-tuple-element.51.refs_0_.refs_2_, ...), custom_call_target="tpu_custom_call" | custom-call | tf_op jit(solution)/shard_map/pallas_call | solution.py:327
  30.7 3.2 %shard_map.60 = (bf16[1024,1792]{1,0:T(8,128)(2,1)S(1)}, bf16[1024,1792]{1,0:T(8,128)(2,1)S(1)}) custom-call(bf16[112,1024]{1,0:T(8,128)(2,1)S(1)} %shard_map.59.refs_0_.refs_1_, bf16[1,4096,1792]{2,1,0:T(8,128)(2,1)} %refs_1_.5), custom_call_target="tpu_custom_call" | custom-call | tf_op jit(solution)/shard_map/pallas_call | solution.py:327
  36.4 3.8 %collective-permute-start.8 = (bf16[48,1792]{1,0:T(8,128)(2,1)S(1)}, bf16[48,1792]{1,0:T(8,128)(2,1)S(1)}, u32[]{:S(2)}, u32[]{:S(2)}) collective-permute-start(bf16[48,1792]{1,0:T(8,128)(2,1)S(1)} %get-tuple-element.66), channel_id=1, source_target_pairs={{0,8},{4,12},{8,0},{12,4},{1,9},{5,13},{9,1},{13,5},{2,10},{6,14},... | collective-permute-start | bytes 516104 | tf_op jit(solution)/shard_map/ppermute | solution.py:363
  47.3 2.0 %collective-permute-done.8.refs_0_.refs_5_ = bf16[48,1792]{1,0:T(8,128)(2,1)S(1)} collective-permute-done((bf16[48,1792]{1,0:T(8,128)(2,1)S(1)}, bf16[48,1792]{1,0:T(8,128)(2,1)S(1)}, u32[]{:S(2)}, u32[]{:S(2)}) %collective-permute-start.8) | collective-permute-done | bytes 172064 | tf_op jit(solution)/shard_map/ppermute | solution.py:363
  49.3 2.4 %collective-permute-start.17 = (s32[4,2,16]{2,1,0:T(2,128)S(1)}, s32[4,2,16]{2,1,0:T(2,128)S(1)}, u32[]{:S(2)}, u32[]{:S(2)}) collective-permute-start(s32[4,2,16]{2,1,0:T(2,128)S(1)} %get-tuple-element.76), channel_id=1, source_target_pairs={{16,0},{17,1},{18,2},{19,3},{20,4},{21,5},{22,6},{23,7},{24,8},{25... | collective-permute-start | bytes 1544 | tf_op jit(solution)/shard_map/ppermute | solution.py:480
  58.8 7.0 %collective-permute-done.18.refs_1_ = bf16[64,1792]{1,0:T(8,128)(2,1)S(1)} collective-permute-done((bf16[64,1792]{1,0:T(8,128)(2,1)S(1)}, bf16[64,1792]{1,0:T(8,128)(2,1)S(1)}, u32[]{:S(2)}, u32[]{:S(2)}) %collective-permute-start.18) | collective-permute-done | bytes 229408 | tf_op jit(solution)/shard_map/ppermute | solution.py:375
  66.3 4.2 %collective-permute-start.19 = (bf16[48,1792]{1,0:T(8,128)(2,1)S(1)}, bf16[48,1792]{1,0:T(8,128)(2,1)S(1)}, u32[]{:S(2)}, u32[]{:S(2)}) collective-permute-start(bf16[48,1792]{1,0:T(8,128)(2,1)S(1)} %get-tuple-element.79), channel_id=1, source_target_pairs={{0,4},{4,0},{8,12},{12,8},{1,5},{5,1},{9,13},{13,9},{2,6},{6,2},{1... | collective-permute-start | bytes 516104 | tf_op jit(solution)/shard_map/ppermute | solution.py:363
  70.5 2.2 %collective-permute-start.21 = (bf16[48,1792]{1,0:T(8,128)(2,1)S(1)}, bf16[48,1792]{1,0:T(8,128)(2,1)S(1)}, u32[]{:S(2)}, u32[]{:S(2)}) collective-permute-start(bf16[48,1792]{1,0:T(8,128)(2,1)S(1)} %get-tuple-element.81), channel_id=1, source_target_pairs={{0,12},{4,8},{8,4},{12,0},{1,13},{5,9},{9,5},{13,1},{2,14},{6,10},... | collective-permute-start | bytes 516104 | tf_op jit(solution)/shard_map/ppermute | solution.py:363
  73.2 2.3 %collective-permute-done.19.refs_4_ = bf16[48,1792]{1,0:T(8,128)(2,1)S(1)} collective-permute-done((bf16[48,1792]{1,0:T(8,128)(2,1)S(1)}, bf16[48,1792]{1,0:T(8,128)(2,1)S(1)}, u32[]{:S(2)}, u32[]{:S(2)}) %collective-permute-start.19) | collective-permute-done | bytes 172064 | tf_op jit(solution)/shard_map/ppermute | solution.py:363
  75.6 3.2 %collective-permute-done.21.refs_6_ = bf16[48,1792]{1,0:T(8,128)(2,1)S(1)} collective-permute-done((bf16[48,1792]{1,0:T(8,128)(2,1)S(1)}, bf16[48,1792]{1,0:T(8,128)(2,1)S(1)}, u32[]{:S(2)}, u32[]{:S(2)}) %collective-permute-start.21) | collective-permute-done | bytes 172064 | tf_op jit(solution)/shard_map/ppermute | solution.py:363
  78.8 3.2 %shard_map.72 = (f32[112,1024]{1,0:T(8,128)S(1)}, bf16[56,1024]{1,0:T(8,128)(2,1)S(1)}, bf16[56,1024]{1,0:T(8,128)(2,1)S(1)}) custom-call(bf16[1024,1792]{1,0:T(8,128)(2,1)S(1)} %get-tuple-element.52.refs_0_, bf16[3584,1024]{1,0:T(8,128)(2,1)S(1)} %get-tuple-element.54.refs_1_, bf16[3584,1024]{1,0:T(8,128)(2,1)S(1)} %get-tuple-element.55.refs_2_, ...), custom_call_target="tpu_custom_call" | custom-call | tf_op jit(solution)/shard_map/pallas_call | solution.py:327
  85.2 3.2 %shard_map.78 = (f32[112,1024]{1,0:T(8,128)S(1)}, bf16[56,1024]{1,0:T(8,128)(2,1)S(1)}, bf16[56,1024]{1,0:T(8,128)(2,1)S(1)}) custom-call(bf16[112,1024]{1,0:T(8,128)(2,1)S(1)} %shard_map.73.refs_0_, bf16[3584,1024]{1,0:T(8,128)(2,1)S(1)} %get-tuple-element.68.refs_1_, bf16[3584,1024]{1,0:T(8,128)(2,1)S(1)} %get-tuple-element.51.refs_0_.refs_2_, ...), custom_call_target="tpu_custom_call" | custom-call | tf_op jit(solution)/shard_map/pallas_call | solution.py:327
  94.0 3.8 %collective-permute-done.31.refs_2_ = bf16[112,1024]{1,0:T(8,128)(2,1)S(1)} collective-permute-done((bf16[112,1024]{1,0:T(8,128)(2,1)S(1)}, bf16[112,1024]{1,0:T(8,128)(2,1)S(1)}, u32[]{:S(2)}, u32[]{:S(2)}) %collective-permute-start.31) | collective-permute-done | bytes 229408 | tf_op jit(solution)/shard_map/ppermute | solution.py:351
  100.4 1.6 %collective-permute-start.33 = (bf16[24,1792]{1,0:T(8,128)(2,1)S(1)}, bf16[24,1792]{1,0:T(8,128)(2,1)S(1)}, u32[]{:S(2)}, u32[]{:S(2)}) collective-permute-start(bf16[24,1792]{1,0:T(8,128)(2,1)S(1)} %get-tuple-element.92), channel_id=1, source_target_pairs={{0,4},{4,0},{8,12},{12,8},{1,5},{5,1},{9,13},{13,9},{2,6},{6,2},{1... | collective-permute-start | bytes 258056 | tf_op jit(solution)/shard_map/ppermute | solution.py:359
  103.1 1.7 %collective-permute-start.35 = (bf16[24,1792]{1,0:T(8,128)(2,1)S(1)}, bf16[24,1792]{1,0:T(8,128)(2,1)S(1)}, u32[]{:S(2)}, u32[]{:S(2)}) collective-permute-start(bf16[24,1792]{1,0:T(8,128)(2,1)S(1)} %get-tuple-element.94), channel_id=1, source_target_pairs={{0,12},{4,8},{8,4},{12,0},{1,13},{5,9},{9,5},{13,1},{2,14},{6,10},... | collective-permute-start | bytes 258056 | tf_op jit(solution)/shard_map/ppermute | solution.py:359
  105.6 2.1 %collective-permute-done.26.refs_4_ = bf16[24,1792]{1,0:T(8,128)(2,1)S(1)} collective-permute-done((bf16[24,1792]{1,0:T(8,128)(2,1)S(1)}, bf16[24,1792]{1,0:T(8,128)(2,1)S(1)}, u32[]{:S(2)}, u32[]{:S(2)}) %collective-permute-start.26) | collective-permute-done | bytes 86048 | tf_op jit(solution)/shard_map/ppermute | solution.py:363
  107.6 4.3 %collective-permute-done.33.refs_8_ = bf16[24,1792]{1,0:T(8,128)(2,1)S(1)} collective-permute-done((bf16[24,1792]{1,0:T(8,128)(2,1)S(1)}, bf16[24,1792]{1,0:T(8,128)(2,1)S(1)}, u32[]{:S(2)}, u32[]{:S(2)}) %collective-permute-start.33) | collective-permute-done | bytes 86048 | tf_op jit(solution)/shard_map/ppermute | solution.py:359
  112.0 1.8 %collective-permute-done.28.refs_6_ = bf16[24,1792]{1,0:T(8,128)(2,1)S(1)} collective-permute-done((bf16[24,1792]{1,0:T(8,128)(2,1)S(1)}, bf16[24,1792]{1,0:T(8,128)(2,1)S(1)}, u32[]{:S(2)}, u32[]{:S(2)}) %collective-permute-start.28) | collective-permute-done | bytes 86048 | tf_op jit(solution)/shard_map/ppermute | solution.py:363
  (81 shorter events, 37.4 us)
Async XLA Ops:
  1.6 17.3 %collective-permute-start = (bf16[48,1792]{1,0:T(8,128)(2,1)S(1)}, bf16[48,1792]{1,0:T(8,128)(2,1)S(1)}, u32[]{:S(2)}, u32[]{:S(2)}) collective-permute-start(bf16[48,1792]{1,0:T(8,128)(2,1)S(1)} %get-tuple-element.57), channel_id=1, source_target_pairs={{0,4},{4,0},{8,12},{12,8},{1,5},{5,1},{9,13},{13,9},{2,6},{6,2},{1... | collective-permute-start | bytes 516104 | tf_op jit(solution)/shard_map/ppermute | solution.py:359
  3.3 15.7 %collective-permute-start.1 = (bf16[48,1792]{1,0:T(8,128)(2,1)S(1)}, bf16[48,1792]{1,0:T(8,128)(2,1)S(1)}, u32[]{:S(2)}, u32[]{:S(2)}) collective-permute-start(bf16[48,1792]{1,0:T(8,128)(2,1)S(1)} %get-tuple-element.58), channel_id=1, source_target_pairs={{0,8},{4,12},{8,0},{12,4},{1,9},{5,13},{9,1},{13,5},{2,10},{6,14},... | collective-permute-start | bytes 516104 | tf_op jit(solution)/shard_map/ppermute | solution.py:359
  5.9 13.1 %collective-permute-start.2 = (bf16[48,1792]{1,0:T(8,128)(2,1)S(1)}, bf16[48,1792]{1,0:T(8,128)(2,1)S(1)}, u32[]{:S(2)}, u32[]{:S(2)}) collective-permute-start(bf16[48,1792]{1,0:T(8,128)(2,1)S(1)} %get-tuple-element.59), channel_id=1, source_target_pairs={{0,12},{4,8},{8,4},{12,0},{1,13},{5,9},{9,5},{13,1},{2,14},{6,10},... | collective-permute-start | bytes 516104 | tf_op jit(solution)/shard_map/ppermute | solution.py:359
  23.7 10.1 %collective-permute-start.5 = (bf16[112,1024]{1,0:T(8,128)(2,1)S(1)}, bf16[112,1024]{1,0:T(8,128)(2,1)S(1)}, u32[]{:S(2)}, u32[]{:S(2)}) collective-permute-start(bf16[112,1024]{1,0:T(8,128)(2,1)S(1)} %shard_map.59.refs_0_.refs_1_), channel_id=1, source_target_pairs={{0,2},{1,3},{2,0},{3,1},{4,6},{5,7},{6,4},{7,5},{8,10},{9,11},{10,... | collective-permute-start | bytes 688136 | tf_op jit(solution)/shard_map/ppermute | solution.py:351
  30.1 10.0 %collective-permute-start.12 = (bf16[112,1024]{1,0:T(8,128)(2,1)S(1)}, bf16[112,1024]{1,0:T(8,128)(2,1)S(1)}, u32[]{:S(2)}, u32[]{:S(2)}) collective-permute-start(bf16[112,1024]{1,0:T(8,128)(2,1)S(1)} %shard_map.66.refs_1_), channel_id=1, source_target_pairs={{0,2},{1,3},{2,0},{3,1},{4,6},{5,7},{6,4},{7,5},{8,10},{9,11},{10,... | collective-permute-start | bytes 688136 | tf_op jit(solution)/shard_map/ppermute | solution.py:351
  36.4 12.9 %collective-permute-start.8 = (bf16[48,1792]{1,0:T(8,128)(2,1)S(1)}, bf16[48,1792]{1,0:T(8,128)(2,1)S(1)}, u32[]{:S(2)}, u32[]{:S(2)}) collective-permute-start(bf16[48,1792]{1,0:T(8,128)(2,1)S(1)} %get-tuple-element.66), channel_id=1, source_target_pairs={{0,8},{4,12},{8,0},{12,4},{1,9},{5,13},{9,1},{13,5},{2,10},{6,14},... | collective-permute-start | bytes 516104 | tf_op jit(solution)/shard_map/ppermute | solution.py:363
  40.4 8.9 %collective-permute-start.7 = (bf16[24,1792]{1,0:T(8,128)(2,1)S(1)}, bf16[24,1792]{1,0:T(8,128)(2,1)S(1)}, u32[]{:S(2)}, u32[]{:S(2)}) collective-permute-start(bf16[24,1792]{1,0:T(8,128)(2,1)S(1)} %get-tuple-element.65), channel_id=1, source_target_pairs={{0,4},{4,0},{8,12},{12,8},{1,5},{5,1},{9,13},{13,9},{2,6},{6,2},{1... | collective-permute-start | bytes 258056 | tf_op jit(solution)/shard_map/ppermute | solution.py:363
  42.8 10.3 %collective-permute-start.14 = (bf16[24,1792]{1,0:T(8,128)(2,1)S(1)}, bf16[24,1792]{1,0:T(8,128)(2,1)S(1)}, u32[]{:S(2)}, u32[]{:S(2)}) collective-permute-start(bf16[24,1792]{1,0:T(8,128)(2,1)S(1)} %get-tuple-element.73), channel_id=1, source_target_pairs={{0,4},{4,0},{8,12},{12,8},{1,5},{5,1},{9,13},{13,9},{2,6},{6,2},{1... | collective-permute-start | bytes 258056 | tf_op jit(solution)/shard_map/ppermute | solution.py:359
  44.3 10.3 %collective-permute-start.15 = (bf16[24,1792]{1,0:T(8,128)(2,1)S(1)}, bf16[24,1792]{1,0:T(8,128)(2,1)S(1)}, u32[]{:S(2)}, u32[]{:S(2)}) collective-permute-start(bf16[24,1792]{1,0:T(8,128)(2,1)S(1)} %get-tuple-element.74), channel_id=1, source_target_pairs={{0,8},{4,12},{8,0},{12,4},{1,9},{5,13},{9,1},{13,5},{2,10},{6,14},... | collective-permute-start | bytes 258056 | tf_op jit(solution)/shard_map/ppermute | solution.py:359
  45.9 8.7 %collective-permute-start.16 = (bf16[24,1792]{1,0:T(8,128)(2,1)S(1)}, bf16[24,1792]{1,0:T(8,128)(2,1)S(1)}, u32[]{:S(2)}, u32[]{:S(2)}) collective-permute-start(bf16[24,1792]{1,0:T(8,128)(2,1)S(1)} %get-tuple-element.75), channel_id=1, source_target_pairs={{0,12},{4,8},{8,4},{12,0},{1,13},{5,9},{9,5},{13,1},{2,14},{6,10},... | collective-permute-start | bytes 258056 | tf_op jit(solution)/shard_map/ppermute | solution.py:359
  49.3 6.1 %collective-permute-start.9 = (bf16[24,1792]{1,0:T(8,128)(2,1)S(1)}, bf16[24,1792]{1,0:T(8,128)(2,1)S(1)}, u32[]{:S(2)}, u32[]{:S(2)}) collective-permute-start(bf16[24,1792]{1,0:T(8,128)(2,1)S(1)} %shard_map.64), channel_id=1, source_target_pairs={{0,4},{4,0},{8,12},{12,8},{1,5},{5,1},{9,13},{13,9},{2,6},{6,2},{1... | collective-permute-start | bytes 258056 | tf_op jit(solution)/shard_map/ppermute | solution.py:363
  49.3 3.7 %collective-permute-start.17 = (s32[4,2,16]{2,1,0:T(2,128)S(1)}, s32[4,2,16]{2,1,0:T(2,128)S(1)}, u32[]{:S(2)}, u32[]{:S(2)}) collective-permute-start(s32[4,2,16]{2,1,0:T(2,128)S(1)} %get-tuple-element.76), channel_id=1, source_target_pairs={{16,0},{17,1},{18,2},{19,3},{20,4},{21,5},{22,6},{23,7},{24,8},{25... | collective-permute-start | bytes 1544 | tf_op jit(solution)/shard_map/ppermute | solution.py:480
  56.0 9.7 %collective-permute-start.18 = (bf16[64,1792]{1,0:T(8,128)(2,1)S(1)}, bf16[64,1792]{1,0:T(8,128)(2,1)S(1)}, u32[]{:S(2)}, u32[]{:S(2)}) collective-permute-start(bf16[64,1792]{1,0:T(8,128)(2,1)S(1)} %get-tuple-element.77.refs_2_), channel_id=1, source_target_pairs={{0,16},{1,17},{2,18},{3,19},{4,20},{5,21},{6,22},{7,23},{8,24},{9,... | collective-permute-start | bytes 688136 | tf_op jit(solution)/shard_map/ppermute | solution.py:375
  57.3 15.9 %collective-permute-start.20 = (bf16[48,1792]{1,0:T(8,128)(2,1)S(1)}, bf16[48,1792]{1,0:T(8,128)(2,1)S(1)}, u32[]{:S(2)}, u32[]{:S(2)}) collective-permute-start(bf16[48,1792]{1,0:T(8,128)(2,1)S(1)} %get-tuple-element.80), channel_id=1, source_target_pairs={{0,24},{4,28},{8,16},{12,20},{1,25},{5,29},{9,17},{13,21},{2,26},{... | collective-permute-start | bytes 516104 | tf_op jit(solution)/shard_map/ppermute | solution.py:379
  66.3 9.2 %collective-permute-start.19 = (bf16[48,1792]{1,0:T(8,128)(2,1)S(1)}, bf16[48,1792]{1,0:T(8,128)(2,1)S(1)}, u32[]{:S(2)}, u32[]{:S(2)}) collective-permute-start(bf16[48,1792]{1,0:T(8,128)(2,1)S(1)} %get-tuple-element.79), channel_id=1, source_target_pairs={{0,4},{4,0},{8,12},{12,8},{1,5},{5,1},{9,13},{13,9},{2,6},{6,2},{1... | collective-permute-start | bytes 516104 | tf_op jit(solution)/shard_map/ppermute | solution.py:363
  70.5 8.3 %collective-permute-start.21 = (bf16[48,1792]{1,0:T(8,128)(2,1)S(1)}, bf16[48,1792]{1,0:T(8,128)(2,1)S(1)}, u32[]{:S(2)}, u32[]{:S(2)}) collective-permute-start(bf16[48,1792]{1,0:T(8,128)(2,1)S(1)} %get-tuple-element.81), channel_id=1, source_target_pairs={{0,12},{4,8},{8,4},{12,0},{1,13},{5,9},{9,5},{13,1},{2,14},{6,10},... | collective-permute-start | bytes 516104 | tf_op jit(solution)/shard_map/ppermute | solution.py:363
  83.6 7.9 %collective-permute-start.24 = (bf16[112,1024]{1,0:T(8,128)(2,1)S(1)}, bf16[112,1024]{1,0:T(8,128)(2,1)S(1)}, u32[]{:S(2)}, u32[]{:S(2)}) collective-permute-start(bf16[112,1024]{1,0:T(8,128)(2,1)S(1)} %shard_map.73.refs_0_), channel_id=1, source_target_pairs={{0,2},{1,3},{2,0},{3,1},{4,6},{5,7},{6,4},{7,5},{8,10},{9,11},{10,... | collective-permute-start | bytes 688136 | tf_op jit(solution)/shard_map/ppermute | solution.py:351
  90.0 7.9 %collective-permute-start.31 = (bf16[112,1024]{1,0:T(8,128)(2,1)S(1)}, bf16[112,1024]{1,0:T(8,128)(2,1)S(1)}, u32[]{:S(2)}, u32[]{:S(2)}) collective-permute-start(bf16[112,1024]{1,0:T(8,128)(2,1)S(1)} %shard_map.79.refs_1_), channel_id=1, source_target_pairs={{0,2},{1,3},{2,0},{3,1},{4,6},{5,7},{6,4},{7,5},{8,10},{9,11},{10,... | collective-permute-start | bytes 688136 | tf_op jit(solution)/shard_map/ppermute | solution.py:351
  94.0 10.8 %collective-permute-start.27 = (bf16[48,1792]{1,0:T(8,128)(2,1)S(1)}, bf16[48,1792]{1,0:T(8,128)(2,1)S(1)}, u32[]{:S(2)}, u32[]{:S(2)}) collective-permute-start(bf16[48,1792]{1,0:T(8,128)(2,1)S(1)} %get-tuple-element.87), channel_id=1, source_target_pairs={{0,8},{4,12},{8,0},{12,4},{1,9},{5,13},{9,1},{13,5},{2,10},{6,14},... | collective-permute-start | bytes 516104 | tf_op jit(solution)/shard_map/ppermute | solution.py:363
  98.1 9.5 %collective-permute-start.26 = (bf16[24,1792]{1,0:T(8,128)(2,1)S(1)}, bf16[24,1792]{1,0:T(8,128)(2,1)S(1)}, u32[]{:S(2)}, u32[]{:S(2)}) collective-permute-start(bf16[24,1792]{1,0:T(8,128)(2,1)S(1)} %get-tuple-element.86), channel_id=1, source_target_pairs={{0,4},{4,0},{8,12},{12,8},{1,5},{5,1},{9,13},{13,9},{2,6},{6,2},{1... | collective-permute-start | bytes 258056 | tf_op jit(solution)/shard_map/ppermute | solution.py:363
  100.4 11.6 %collective-permute-start.33 = (bf16[24,1792]{1,0:T(8,128)(2,1)S(1)}, bf16[24,1792]{1,0:T(8,128)(2,1)S(1)}, u32[]{:S(2)}, u32[]{:S(2)}) collective-permute-start(bf16[24,1792]{1,0:T(8,128)(2,1)S(1)} %get-tuple-element.92), channel_id=1, source_target_pairs={{0,4},{4,0},{8,12},{12,8},{1,5},{5,1},{9,13},{13,9},{2,6},{6,2},{1... | collective-permute-start | bytes 258056 | tf_op jit(solution)/shard_map/ppermute | solution.py:359
  102.0 10.0 %collective-permute-start.34 = (bf16[24,1792]{1,0:T(8,128)(2,1)S(1)}, bf16[24,1792]{1,0:T(8,128)(2,1)S(1)}, u32[]{:S(2)}, u32[]{:S(2)}) collective-permute-start(bf16[24,1792]{1,0:T(8,128)(2,1)S(1)} %get-tuple-element.93), channel_id=1, source_target_pairs={{0,8},{4,12},{8,0},{12,4},{1,9},{5,13},{9,1},{13,5},{2,10},{6,14},... | collective-permute-start | bytes 258056 | tf_op jit(solution)/shard_map/ppermute | solution.py:359
  103.1 8.9 %collective-permute-start.35 = (bf16[24,1792]{1,0:T(8,128)(2,1)S(1)}, bf16[24,1792]{1,0:T(8,128)(2,1)S(1)}, u32[]{:S(2)}, u32[]{:S(2)}) collective-permute-start(bf16[24,1792]{1,0:T(8,128)(2,1)S(1)} %get-tuple-element.94), channel_id=1, source_target_pairs={{0,12},{4,8},{8,4},{12,0},{1,13},{5,9},{9,5},{13,1},{2,14},{6,10},... | collective-permute-start | bytes 258056 | tf_op jit(solution)/shard_map/ppermute | solution.py:359
  104.8 8.9 %collective-permute-start.28 = (bf16[24,1792]{1,0:T(8,128)(2,1)S(1)}, bf16[24,1792]{1,0:T(8,128)(2,1)S(1)}, u32[]{:S(2)}, u32[]{:S(2)}) collective-permute-start(bf16[24,1792]{1,0:T(8,128)(2,1)S(1)} %shard_map.77), channel_id=1, source_target_pairs={{0,4},{4,0},{8,12},{12,8},{1,5},{5,1},{9,13},{13,9},{2,6},{6,2},{1... | collective-permute-start | bytes 258056 | tf_op jit(solution)/shard_map/ppermute | solution.py:363
  (14 other events, 38.1 us)

commit v3 on v2

--- a/solution.py
+++ b/solution.py
@@ -57,6 +57,7 @@
         self.pieces = peers if peers <= 8 else 1
         self.pairs = self.groups - 1 if self.pieces == 4 else 0
         self.near = self.pieces // 2
+        self.listed = sorted(range(self.pieces), key=lambda step: -step.bit_length())
         self.repacked = [step for step in range(self.pieces) if step != self.near]
         self.group_pay = peers * self.pay
         self.piece = self.group_pay // self.pieces
@@ -159,10 +160,11 @@
     copies = []
     for expert in range(z.local):
         for part in range(parts):
+            rows = pl.ds(part * depth, depth)
             copies.append(
                 pltpu.make_async_copy(
-                    flat.at[pl.ds(part * depth, depth), pl.ds(expert * z.units, z.units)],
-                    outs[expert].at[pl.ds(part * depth, depth)],
+                    flat.at[rows, pl.ds(expert * z.units, z.units)],
+                    outs[expert].at[rows],
                     sems.at[expert * parts + part],
                 )
             )
@@ -172,14 +174,14 @@
         copy.wait()
 
 
-def load_down_kernel(z, group, down_proj, *refs):
-    outs, sems = refs[:z.members], refs[-1]
-    copies = []
-    for index in range(z.members):
-        low = (group * z.members + index) * z.units
-        copies.append(
-            pltpu.make_async_copy(down_proj.at[0, pl.ds(low, z.units), :], outs[index], sems.at[index])
+def load_down_kernel(z, down_proj, *refs):
+    outs, sems = refs[:-1], refs[-1]
+    copies = [
+        pltpu.make_async_copy(
+            down_proj.at[0, pl.ds(expert * z.units, z.units), :], outs[expert], sems.at[expert]
         )
+        for expert in range(z.local)
+    ]
     for copy in copies:
         copy.start()
     for copy in copies:
@@ -198,6 +200,7 @@
 def up_kernel(z, group, *refs):
     weights, refs = refs[:z.members], refs[z.members:]
     received, refs = refs[:z.pieces], refs[z.pieces:]
+    received = [received[z.listed.index(step)] for step in range(z.pieces)]
     own, *sent, spread, staged = refs
     rows = dot(z.order(), group_rows(z, group, received).astype(BF16))
     squares = rows * rows
@@ -295,6 +298,10 @@
         low += out.shape[0]
 
 
+def hand_on_kernel(source, target):
+    target[...] = source[...]
+
+
 def second_kernel(z, pair_ref, out):
     out[...] = pair_ref[...].astype(F32)[z.piece:].astype(BF16)
 
@@ -370,26 +377,24 @@
         second = call(second_kernel, (z,), 2, [pay], [VMEM], [], far)[0]
         return [own, across(near, 1), far, across(second, 1)]
 
+    def within(value, step, section):
+        low = section * z.peers
+        pairs = [(low + i, low + (i ^ step)) for i in range(z.peers)]
+        return lax.ppermute(value, ("section", "expert"), pairs)
+
     def relayed(pieces, kept, tick):
         hop = [(tick, tick + 1)]
         rows = lax.ppermute(kept, "section", hop)
         if z.pieces == 1:
             return rows, [lax.ppermute(exchanged(pieces)[0], "section", hop)]
-        pairs = [(tick * z.peers + i, (tick + 1) * z.peers + (i ^ z.near)) for i in range(z.peers)]
-        far = lax.ppermute(pieces[0], ("section", "expert"), pairs)
+        far = within(pieces[0], z.near, tick)
         result = call(repack_kernel, (z,), 4, [all_pay] * (z.pieces - 1), [VMEM] * 2, [], routes, rows)
-        result.insert(z.near, far)
+        far = call(hand_on_kernel, (), 2, [all_pay], [VMEM], [], far, waits=result[:1])[0]
+        result.insert(z.near, lax.ppermute(far, "section", hop))
         for step in steps[:-1]:
             if step != z.near:
-                result[step] = across(result[step], step)
+                result[step] = within(result[step], step, tick + 1)
         return rows, result
-
-    def load_down(group, after):
-        return call(
-            load_down_kernel, (z, group), 1,
-            [pltpu.VMEM((z.units, z.width), BF16)] * z.members,
-            [HBM], [pltpu.SemaphoreType.DMA((z.members,))], down_proj, waits=[after],
-        )
 
     def products(received, group, waits):
         own, *sent = call(
@@ -400,14 +405,14 @@
                 pltpu.VMEM((z.members, 2 * z.each, 2 * z.width), BF16),
                 pltpu.VMEM((2,) + z.partial, F32),
             ],
-            *wide[group * z.members:(group + 1) * z.members], *received,
-            waits=waits if group else tall[0][:1],
+            *wide[group * z.members:(group + 1) * z.members], *(received[step] for step in z.listed),
+            waits=waits,
         )
         return own, [swap(value, 1) for value in sent]
 
-    def pair_sums(own, other, waits):
+    def pair_sums(own, other):
         pair = call(
-            pair_kernel, (z,), 2, [shape(z.partial, BF16)], [VMEM] * (1 + CUTS), [], own, *other, waits=waits
+            pair_kernel, (z,), 2, [shape(z.partial, BF16)], [VMEM] * (1 + CUTS), [], own, *other
         )[0]
         return [pair] + [swap(pair, step) for step in range(2, z.splits, 2)]
 
@@ -456,20 +461,21 @@
         [pltpu.VMEM((2 * z.width, z.units), BF16)] * z.local,
         [HBM], [pltpu.SemaphoreType.DMA((z.local * parts,))], gate_up, waits=[weight],
     )
-    tall = [load_down(0, wide[-1])]
+    tall = call(
+        load_down_kernel, (z,), 1,
+        [pltpu.VMEM((z.units, z.width), BF16)] * z.local,
+        [HBM], [pltpu.SemaphoreType.DMA((z.local,))], down_proj, waits=wide[-1:],
+    )
+    tall = [tall[group * z.members:(group + 1) * z.members] for group in range(z.groups)]
     groups = range(z.groups)
     for tick in range(sections):
         last = tick == sections - 1
         sums, returned = [], []
-        early, waits = [], []
         for group in groups:
-            own, other = products(received, group, [sums[-1][0]] if group else [])
-            sums.append(pair_sums(own, other, waits))
-            if tick == 0 and group + 1 < z.groups:
-                tall.append(load_down(group + 1, sums[-1][0]))
-                early = tall[-1][:1]
+            own, other = products(received, group, [sums[-1][0]] if group else tall[0][:1])
+            sums.append(pair_sums(own, other))
             if group == 0:
-                halves = activated(sums[0], early)
+                halves = activated(sums[0], [])
         for group in groups:
             if group:
                 halves = activated(sums[group], outgoing[:1])

time: 115 us -> 115 us (level)
  starting transfers between devices: 37.3 us -> 41.1 us
  waiting for transfers between devices: 37 us -> 33.8 us
    ppermute x8 -> x6, waiting for transfers between devices: 12.2 us -> 2.43 us  [across(): lax.ppermute(value, 'expert', [(i, i ^ step) for i in range(z.peers)])]
    ppermute x1 -> x4, starting transfers between devices: 1.47 us -> 9.16 us  [the longest x3 7.68 us: within(): return lax.ppermute(value, ('section', 'expert'), pairs)]
    ppermute x1 -> x4, waiting for transfers between devices: 0.5 us -> 5.82 us  [the longest x3 4.65 us: within(): return lax.ppermute(value, ('section', 'expert'), pairs)]
    ppermute x8 -> x6, starting transfers between devices: 11.8 us -> 8.21 us  [across(): lax.ppermute(value, 'expert', [(i, i ^ step) for i in range(z.peers)])]
    ppermute x9, waiting for transfers between devices: 5.82 us -> 7.14 us  [exchanged(): result[step] = lax.ppermute(pieces[step], 'expert', pairs)]
  transfers between devices with their start and end apart: 36 -> 37, of which waited for: 24 -> 26; matrix products, arithmetic and copies ran while one was open for 0% -> 0% of each run, Pallas kernels for 26% -> 26%
where the time goes in v3:
time: 115 us; the launch traced here: 114 us
  starting transfers between devices  41.1 us (36%)
  Pallas kernels  39 us (34%)
  waiting for transfers between devices  33.8 us (29%)
    pallas_call x29, Pallas kernels, call(): pl.pallas_call(functools.partial(after_waits, len(waits), functools.parti...  39 us
    ppermute x9, starting transfers between devices, exchanged(): result[step] = lax.ppermute(pieces[step], 'expert', pairs)  13.1 us
    ppermute x16, waiting for transfers between devices, swap(): return lax.ppermute(value, 'hidden', pairs)  10 us
    ppermute x6, starting transfers between devices, across(): lax.ppermute(value, 'expert', [(i, i ^ step) for i in range(z.peers)])  8.21 us
    ppermute x3, starting transfers between devices, within(): return lax.ppermute(value, ('section', 'expert'), pairs)  7.68 us
    ppermute x9, waiting for transfers between devices, exchanged(): result[step] = lax.ppermute(pieces[step], 'expert', pairs)  7.14 us
    ppermute x1, waiting for transfers between devices, relayed(): rows = lax.ppermute(kept, 'section', hop)  7.06 us
    ppermute x16, starting transfers between devices, swap(): return lax.ppermute(value, 'hidden', pairs)  6.89 us
  transfers between devices with their start and end apart: 37, of which 26 were waited for; matrix products, arithmetic and copies ran while one was open for 0% of the time, Pallas kernels for 26%

profile of v3, /device:TPU:2, one launch (start us, length us, event | category | flops | bytes accessed | tf_op | source)
XLA Modules:
  0.0 114.3 jit_solution(11553411224108952925)
XLA Ops:
  0.0 1.6 %shard_map.55 = (bf16[48,1792]{1,0:T(8,128)(2,1)S(1)}, bf16[48,1792]{1,0:T(8,128)(2,1)S(1)}, bf16[48,1792]{1,0:T(8,128)(2,1)S(1)}, bf16[48,1792]{1,0:T(8,128)(2,1)S(1)}, bf16[192,64]{1,0:T(8,128)(2,1)S(1)}) custom-call(s32[4,2,16]{2,1,0:T(2,128)} %bitcast.11, bf16[4,2,16]{2,1,0:T(2,128)(2,1)} %bitcast.14, bf16[64,1792]{1,0:T(8,128)(2,1)} %bitcast.8), custom_call_target="tpu_custom_call" | custom-call | tf_op jit(solution)/shard_map/pallas_call | solution.py:334
  1.6 2.7 %collective-permute-start = (bf16[48,1792]{1,0:T(8,128)(2,1)S(1)}, bf16[48,1792]{1,0:T(8,128)(2,1)S(1)}, u32[]{:S(2)}, u32[]{:S(2)}) collective-permute-start(bf16[48,1792]{1,0:T(8,128)(2,1)S(1)} %get-tuple-element.56), channel_id=1, source_target_pairs={{0,8},{4,12},{8,0},{12,4},{1,9},{5,13},{9,1},{13,5},{2,10},{6,14},... | collective-permute-start | bytes 516104 | tf_op jit(solution)/shard_map/ppermute | solution.py:366
  5.9 9.6 %shard_map.56 = (bf16[3584,1024]{1,0:T(8,128)(2,1)S(1)}, bf16[3584,1024]{1,0:T(8,128)(2,1)S(1)}, bf16[3584,1024]{1,0:T(8,128)(2,1)S(1)}, bf16[3584,1024]{1,0:T(8,128)(2,1)S(1)}) custom-call(bf16[192,64]{1,0:T(8,128)(2,1)S(1)} %get-tuple-element.50.refs_0_, bf16[1,1792,2,4096]{3,2,1,0:T(2,128)(2,1)} %refs_1_.2), custom_call_target="tpu_custom_call" | custom-call | tf_op jit(solution)/shard_map/pallas_call | solution.py:334
  15.5 5.3 %shard_map.57 = (bf16[1024,1792]{1,0:T(8,128)(2,1)S(1)}, bf16[1024,1792]{1,0:T(8,128)(2,1)S(1)}, bf16[1024,1792]{1,0:T(8,128)(2,1)S(1)}, bf16[1024,1792]{1,0:T(8,128)(2,1)S(1)}) custom-call(bf16[3584,1024]{1,0:T(8,128)(2,1)S(1)} %get-tuple-element.51.refs_0_.refs_2_, bf16[1,4096,1792]{2,1,0:T(8,128)(2,1)} %refs_1_.3), custom_call_target="tpu_custom_call" | custom-call | tf_op jit(solution)/shard_map/pallas_call | solution.py:334
  20.8 3.2 %shard_map.58 = (f32[112,1024]{1,0:T(8,128)S(1)}, bf16[56,1024]{1,0:T(8,128)(2,1)S(1)}, bf16[56,1024]{1,0:T(8,128)(2,1)S(1)}) custom-call(bf16[1024,1792]{1,0:T(8,128)(2,1)S(1)} %get-tuple-element.52.refs_0_, bf16[3584,1024]{1,0:T(8,128)(2,1)S(1)} %get-tuple-element.54.refs_1_, bf16[3584,1024]{1,0:T(8,128)(2,1)S(1)} %get-tuple-element.55.refs_2_, ...), custom_call_target="tpu_custom_call" | custom-call | tf_op jit(solution)/shard_map/pallas_call | solution.py:334
  25.6 1.6 %collective-permute-start.5 = (bf16[112,1024]{1,0:T(8,128)(2,1)S(1)}, bf16[112,1024]{1,0:T(8,128)(2,1)S(1)}, u32[]{:S(2)}, u32[]{:S(2)}) collective-permute-start(bf16[112,1024]{1,0:T(8,128)(2,1)S(1)} %shard_map.59.refs_0_), channel_id=1, source_target_pairs={{0,2},{1,3},{2,0},{3,1},{4,6},{5,7},{6,4},{7,5},{8,10},{9,11},{10,... | collective-permute-start | bytes 688136 | tf_op jit(solution)/shard_map/ppermute | solution.py:358
  27.2 3.2 %shard_map.64 = (f32[112,1024]{1,0:T(8,128)S(1)}, bf16[56,1024]{1,0:T(8,128)(2,1)S(1)}, bf16[56,1024]{1,0:T(8,128)(2,1)S(1)}) custom-call(bf16[112,1024]{1,0:T(8,128)(2,1)S(1)} %shard_map.59.refs_0_, bf16[3584,1024]{1,0:T(8,128)(2,1)S(1)} %get-tuple-element.68.refs_1_, bf16[3584,1024]{1,0:T(8,128)(2,1)S(1)} %get-tuple-element.51.refs_0_.refs_2_, ...), custom_call_target="tpu_custom_call" | custom-call | tf_op jit(solution)/shard_map/pallas_call | solution.py:334
  36.0 2.9 %collective-permute-start.8 = (bf16[48,1792]{1,0:T(8,128)(2,1)S(1)}, bf16[48,1792]{1,0:T(8,128)(2,1)S(1)}, u32[]{:S(2)}, u32[]{:S(2)}) collective-permute-start(bf16[48,1792]{1,0:T(8,128)(2,1)S(1)} %get-tuple-element.65), channel_id=1, source_target_pairs={{0,8},{4,12},{8,0},{12,4},{1,9},{5,13},{9,1},{13,5},{2,10},{6,14},... | collective-permute-start | bytes 516104 | tf_op jit(solution)/shard_map/ppermute | solution.py:370
  40.2 1.9 %collective-permute-start.7 = (bf16[24,1792]{1,0:T(8,128)(2,1)S(1)}, bf16[24,1792]{1,0:T(8,128)(2,1)S(1)}, u32[]{:S(2)}, u32[]{:S(2)}) collective-permute-start(bf16[24,1792]{1,0:T(8,128)(2,1)S(1)} %get-tuple-element.64), channel_id=1, source_target_pairs={{0,4},{4,0},{8,12},{12,8},{1,5},{5,1},{9,13},{13,9},{2,6},{6,2},{1... | collective-permute-start | bytes 258056 | tf_op jit(solution)/shard_map/ppermute | solution.py:370
  44.3 2.6 %collective-permute-start.15 = (bf16[24,1792]{1,0:T(8,128)(2,1)S(1)}, bf16[24,1792]{1,0:T(8,128)(2,1)S(1)}, u32[]{:S(2)}, u32[]{:S(2)}) collective-permute-start(bf16[24,1792]{1,0:T(8,128)(2,1)S(1)} %get-tuple-element.74), channel_id=1, source_target_pairs={{0,8},{4,12},{8,0},{12,4},{1,9},{5,13},{9,1},{13,5},{2,10},{6,14},... | collective-permute-start | bytes 258056 | tf_op jit(solution)/shard_map/ppermute | solution.py:366
  49.1 2.4 %collective-permute-start.17 = (s32[4,2,16]{2,1,0:T(2,128)S(1)}, s32[4,2,16]{2,1,0:T(2,128)S(1)}, u32[]{:S(2)}, u32[]{:S(2)}) collective-permute-start(s32[4,2,16]{2,1,0:T(2,128)S(1)} %get-tuple-element.76), channel_id=1, source_target_pairs={{16,0},{17,1},{18,2},{19,3},{20,4},{21,5},{22,6},{23,7},{24,8},{25... | collective-permute-start | bytes 1544 | tf_op jit(solution)/shard_map/ppermute | solution.py:486
  57.7 7.1 %collective-permute-done.18.refs_1_ = bf16[64,1792]{1,0:T(8,128)(2,1)S(1)} collective-permute-done((bf16[64,1792]{1,0:T(8,128)(2,1)S(1)}, bf16[64,1792]{1,0:T(8,128)(2,1)S(1)}, u32[]{:S(2)}, u32[]{:S(2)}) %collective-permute-start.18) | collective-permute-done | bytes 229408 | tf_op jit(solution)/shard_map/ppermute | solution.py:387
  65.3 5.1 %collective-permute-start.21 = (bf16[48,1792]{1,0:T(8,128)(2,1)S(1)}, bf16[48,1792]{1,0:T(8,128)(2,1)S(1)}, u32[]{:S(2)}, u32[]{:S(2)}) collective-permute-start(bf16[48,1792]{1,0:T(8,128)(2,1)S(1)} %get-tuple-element.80), channel_id=1, source_target_pairs={{16,28},{20,24},{24,20},{28,16},{17,29},{21,25},{25,21},{29,17},{1... | collective-permute-start | bytes 516104 | tf_op jit(solution)/shard_map/ppermute | solution.py:383
  70.4 1.9 %collective-permute-start.22 = (bf16[48,1792]{1,0:T(8,128)(2,1)S(1)}, bf16[48,1792]{1,0:T(8,128)(2,1)S(1)}, u32[]{:S(2)}, u32[]{:S(2)}) collective-permute-start(bf16[48,1792]{1,0:T(8,128)(2,1)S(1)} %get-tuple-element.81), channel_id=1, source_target_pairs={{16,20},{20,16},{24,28},{28,24},{17,21},{21,17},{25,29},{29,25},{1... | collective-permute-start | bytes 516104 | tf_op jit(solution)/shard_map/ppermute | solution.py:383
  72.4 1.5 %collective-permute-start.20 = (bf16[48,1792]{1,0:T(8,128)(2,1)S(1)}, bf16[48,1792]{1,0:T(8,128)(2,1)S(1)}, u32[]{:S(2)}, u32[]{:S(2)}) collective-permute-start(bf16[48,1792]{1,0:T(8,128)(2,1)S(1)} %shard_map.71), channel_id=1, source_target_pairs={{0,16},{1,17},{2,18},{3,19},{4,20},{5,21},{6,22},{7,23},{8,24},{9,... | collective-permute-start | bytes 516104 | tf_op jit(solution)/shard_map/ppermute | solution.py:393
  73.9 2.2 %collective-permute-done.21.refs_4_ = bf16[48,1792]{1,0:T(8,128)(2,1)S(1)} collective-permute-done((bf16[48,1792]{1,0:T(8,128)(2,1)S(1)}, bf16[48,1792]{1,0:T(8,128)(2,1)S(1)}, u32[]{:S(2)}, u32[]{:S(2)}) %collective-permute-start.21) | collective-permute-done | bytes 172064 | tf_op jit(solution)/shard_map/ppermute | solution.py:383
  76.1 2.5 %collective-permute-done.22.refs_5_ = bf16[48,1792]{1,0:T(8,128)(2,1)S(1)} collective-permute-done((bf16[48,1792]{1,0:T(8,128)(2,1)S(1)}, bf16[48,1792]{1,0:T(8,128)(2,1)S(1)}, u32[]{:S(2)}, u32[]{:S(2)}) %collective-permute-start.22) | collective-permute-done | bytes 172064 | tf_op jit(solution)/shard_map/ppermute | solution.py:383
  79.7 3.2 %shard_map.72 = (f32[112,1024]{1,0:T(8,128)S(1)}, bf16[56,1024]{1,0:T(8,128)(2,1)S(1)}, bf16[56,1024]{1,0:T(8,128)(2,1)S(1)}) custom-call(bf16[1024,1792]{1,0:T(8,128)(2,1)S(1)} %get-tuple-element.52.refs_0_, bf16[3584,1024]{1,0:T(8,128)(2,1)S(1)} %get-tuple-element.54.refs_1_, bf16[3584,1024]{1,0:T(8,128)(2,1)S(1)} %get-tuple-element.55.refs_2_, ...), custom_call_target="tpu_custom_call" | custom-call | tf_op jit(solution)/shard_map/pallas_call | solution.py:334
  85.5 3.2 %shard_map.78 = (f32[112,1024]{1,0:T(8,128)S(1)}, bf16[56,1024]{1,0:T(8,128)(2,1)S(1)}, bf16[56,1024]{1,0:T(8,128)(2,1)S(1)}) custom-call(bf16[112,1024]{1,0:T(8,128)(2,1)S(1)} %shard_map.73.refs_0_, bf16[3584,1024]{1,0:T(8,128)(2,1)S(1)} %get-tuple-element.68.refs_1_, bf16[3584,1024]{1,0:T(8,128)(2,1)S(1)} %get-tuple-element.51.refs_0_.refs_2_, ...), custom_call_target="tpu_custom_call" | custom-call | tf_op jit(solution)/shard_map/pallas_call | solution.py:334
  96.1 2.1 %collective-permute-done.32.refs_2_ = bf16[112,1024]{1,0:T(8,128)(2,1)S(1)} collective-permute-done((bf16[112,1024]{1,0:T(8,128)(2,1)S(1)}, bf16[112,1024]{1,0:T(8,128)(2,1)S(1)}, u32[]{:S(2)}, u32[]{:S(2)}) %collective-permute-start.32) | collective-permute-done | bytes 229408 | tf_op jit(solution)/shard_map/ppermute | solution.py:358
  98.4 2.1 %collective-permute-start.27 = (bf16[24,1792]{1,0:T(8,128)(2,1)S(1)}, bf16[24,1792]{1,0:T(8,128)(2,1)S(1)}, u32[]{:S(2)}, u32[]{:S(2)}) collective-permute-start(bf16[24,1792]{1,0:T(8,128)(2,1)S(1)} %get-tuple-element.86), channel_id=1, source_target_pairs={{0,4},{4,0},{8,12},{12,8},{1,5},{5,1},{9,13},{13,9},{2,6},{6,2},{1... | collective-permute-start | bytes 258056 | tf_op jit(solution)/shard_map/ppermute | solution.py:370
  103.9 2.8 %collective-permute-start.36 = (bf16[24,1792]{1,0:T(8,128)(2,1)S(1)}, bf16[24,1792]{1,0:T(8,128)(2,1)S(1)}, u32[]{:S(2)}, u32[]{:S(2)}) collective-permute-start(bf16[24,1792]{1,0:T(8,128)(2,1)S(1)} %get-tuple-element.94), channel_id=1, source_target_pairs={{0,12},{4,8},{8,4},{12,0},{1,13},{5,9},{9,5},{13,1},{2,14},{6,10},... | collective-permute-start | bytes 258056 | tf_op jit(solution)/shard_map/ppermute | solution.py:366
  106.8 2.5 %collective-permute-done.34.refs_8_ = bf16[24,1792]{1,0:T(8,128)(2,1)S(1)} collective-permute-done((bf16[24,1792]{1,0:T(8,128)(2,1)S(1)}, bf16[24,1792]{1,0:T(8,128)(2,1)S(1)}, u32[]{:S(2)}, u32[]{:S(2)}) %collective-permute-start.34) | collective-permute-done | bytes 86048 | tf_op jit(solution)/shard_map/ppermute | solution.py:366
  109.3 3.3 %collective-permute-done.35.refs_9_ = bf16[24,1792]{1,0:T(8,128)(2,1)S(1)} collective-permute-done((bf16[24,1792]{1,0:T(8,128)(2,1)S(1)}, bf16[24,1792]{1,0:T(8,128)(2,1)S(1)}, u32[]{:S(2)}, u32[]{:S(2)}) %collective-permute-start.35) | collective-permute-done | bytes 86048 | tf_op jit(solution)/shard_map/ppermute | solution.py:366
  (83 shorter events, 37.8 us)
Async XLA Ops:
  1.6 19.2 %collective-permute-start = (bf16[48,1792]{1,0:T(8,128)(2,1)S(1)}, bf16[48,1792]{1,0:T(8,128)(2,1)S(1)}, u32[]{:S(2)}, u32[]{:S(2)}) collective-permute-start(bf16[48,1792]{1,0:T(8,128)(2,1)S(1)} %get-tuple-element.56), channel_id=1, source_target_pairs={{0,8},{4,12},{8,0},{12,4},{1,9},{5,13},{9,1},{13,5},{2,10},{6,14},... | collective-permute-start | bytes 516104 | tf_op jit(solution)/shard_map/ppermute | solution.py:366
  4.3 16.5 %collective-permute-start.1 = (bf16[48,1792]{1,0:T(8,128)(2,1)S(1)}, bf16[48,1792]{1,0:T(8,128)(2,1)S(1)}, u32[]{:S(2)}, u32[]{:S(2)}) collective-permute-start(bf16[48,1792]{1,0:T(8,128)(2,1)S(1)} %get-tuple-element.57), channel_id=1, source_target_pairs={{0,12},{4,8},{8,4},{12,0},{1,13},{5,9},{9,5},{13,1},{2,14},{6,10},... | collective-permute-start | bytes 516104 | tf_op jit(solution)/shard_map/ppermute | solution.py:366
  5.6 15.2 %collective-permute-start.2 = (bf16[48,1792]{1,0:T(8,128)(2,1)S(1)}, bf16[48,1792]{1,0:T(8,128)(2,1)S(1)}, u32[]{:S(2)}, u32[]{:S(2)}) collective-permute-start(bf16[48,1792]{1,0:T(8,128)(2,1)S(1)} %get-tuple-element.58), channel_id=1, source_target_pairs={{0,4},{4,0},{8,12},{12,8},{1,5},{5,1},{9,13},{13,9},{2,6},{6,2},{1... | collective-permute-start | bytes 516104 | tf_op jit(solution)/shard_map/ppermute | solution.py:366
  25.6 7.9 %collective-permute-start.5 = (bf16[112,1024]{1,0:T(8,128)(2,1)S(1)}, bf16[112,1024]{1,0:T(8,128)(2,1)S(1)}, u32[]{:S(2)}, u32[]{:S(2)}) collective-permute-start(bf16[112,1024]{1,0:T(8,128)(2,1)S(1)} %shard_map.59.refs_0_), channel_id=1, source_target_pairs={{0,2},{1,3},{2,0},{3,1},{4,6},{5,7},{6,4},{7,5},{8,10},{9,11},{10,... | collective-permute-start | bytes 688136 | tf_op jit(solution)/shard_map/ppermute | solution.py:358
  32.0 7.9 %collective-permute-start.12 = (bf16[112,1024]{1,0:T(8,128)(2,1)S(1)}, bf16[112,1024]{1,0:T(8,128)(2,1)S(1)}, u32[]{:S(2)}, u32[]{:S(2)}) collective-permute-start(bf16[112,1024]{1,0:T(8,128)(2,1)S(1)} %shard_map.65.refs_1_), channel_id=1, source_target_pairs={{0,2},{1,3},{2,0},{3,1},{4,6},{5,7},{6,4},{7,5},{8,10},{9,11},{10,... | collective-permute-start | bytes 688136 | tf_op jit(solution)/shard_map/ppermute | solution.py:358
  36.0 12.2 %collective-permute-start.8 = (bf16[48,1792]{1,0:T(8,128)(2,1)S(1)}, bf16[48,1792]{1,0:T(8,128)(2,1)S(1)}, u32[]{:S(2)}, u32[]{:S(2)}) collective-permute-start(bf16[48,1792]{1,0:T(8,128)(2,1)S(1)} %get-tuple-element.65), channel_id=1, source_target_pairs={{0,8},{4,12},{8,0},{12,4},{1,9},{5,13},{9,1},{13,5},{2,10},{6,14},... | collective-permute-start | bytes 516104 | tf_op jit(solution)/shard_map/ppermute | solution.py:370
  40.2 8.9 %collective-permute-start.7 = (bf16[24,1792]{1,0:T(8,128)(2,1)S(1)}, bf16[24,1792]{1,0:T(8,128)(2,1)S(1)}, u32[]{:S(2)}, u32[]{:S(2)}) collective-permute-start(bf16[24,1792]{1,0:T(8,128)(2,1)S(1)} %get-tuple-element.64), channel_id=1, source_target_pairs={{0,4},{4,0},{8,12},{12,8},{1,5},{5,1},{9,13},{13,9},{2,6},{6,2},{1... | collective-permute-start | bytes 258056 | tf_op jit(solution)/shard_map/ppermute | solution.py:370
  43.8 9.0 %collective-permute-start.14 = (bf16[24,1792]{1,0:T(8,128)(2,1)S(1)}, bf16[24,1792]{1,0:T(8,128)(2,1)S(1)}, u32[]{:S(2)}, u32[]{:S(2)}) collective-permute-start(bf16[24,1792]{1,0:T(8,128)(2,1)S(1)} %get-tuple-element.73), channel_id=1, source_target_pairs={{0,4},{4,0},{8,12},{12,8},{1,5},{5,1},{9,13},{13,9},{2,6},{6,2},{1... | collective-permute-start | bytes 258056 | tf_op jit(solution)/shard_map/ppermute | solution.py:366
  44.3 9.7 %collective-permute-start.15 = (bf16[24,1792]{1,0:T(8,128)(2,1)S(1)}, bf16[24,1792]{1,0:T(8,128)(2,1)S(1)}, u32[]{:S(2)}, u32[]{:S(2)}) collective-permute-start(bf16[24,1792]{1,0:T(8,128)(2,1)S(1)} %get-tuple-element.74), channel_id=1, source_target_pairs={{0,8},{4,12},{8,0},{12,4},{1,9},{5,13},{9,1},{13,5},{2,10},{6,14},... | collective-permute-start | bytes 258056 | tf_op jit(solution)/shard_map/ppermute | solution.py:366
  46.9 7.3 %collective-permute-start.16 = (bf16[24,1792]{1,0:T(8,128)(2,1)S(1)}, bf16[24,1792]{1,0:T(8,128)(2,1)S(1)}, u32[]{:S(2)}, u32[]{:S(2)}) collective-permute-start(bf16[24,1792]{1,0:T(8,128)(2,1)S(1)} %get-tuple-element.75), channel_id=1, source_target_pairs={{0,12},{4,8},{8,4},{12,0},{1,13},{5,9},{9,5},{13,1},{2,14},{6,10},... | collective-permute-start | bytes 258056 | tf_op jit(solution)/shard_map/ppermute | solution.py:366
  48.2 6.8 %collective-permute-start.9 = (bf16[24,1792]{1,0:T(8,128)(2,1)S(1)}, bf16[24,1792]{1,0:T(8,128)(2,1)S(1)}, u32[]{:S(2)}, u32[]{:S(2)}) collective-permute-start(bf16[24,1792]{1,0:T(8,128)(2,1)S(1)} %shard_map.63), channel_id=1, source_target_pairs={{0,4},{4,0},{8,12},{12,8},{1,5},{5,1},{9,13},{13,9},{2,6},{6,2},{1... | collective-permute-start | bytes 258056 | tf_op jit(solution)/shard_map/ppermute | solution.py:370
  55.7 9.0 %collective-permute-start.18 = (bf16[64,1792]{1,0:T(8,128)(2,1)S(1)}, bf16[64,1792]{1,0:T(8,128)(2,1)S(1)}, u32[]{:S(2)}, u32[]{:S(2)}) collective-permute-start(bf16[64,1792]{1,0:T(8,128)(2,1)S(1)} %get-tuple-element.77.refs_2_), channel_id=1, source_target_pairs={{0,16},{1,17},{2,18},{3,19},{4,20},{5,21},{6,22},{7,23},{8,24},{9,... | collective-permute-start | bytes 688136 | tf_op jit(solution)/shard_map/ppermute | solution.py:387
  57.0 15.3 %collective-permute-start.19 = (bf16[48,1792]{1,0:T(8,128)(2,1)S(1)}, bf16[48,1792]{1,0:T(8,128)(2,1)S(1)}, u32[]{:S(2)}, u32[]{:S(2)}) collective-permute-start(bf16[48,1792]{1,0:T(8,128)(2,1)S(1)} %get-tuple-element.79), channel_id=1, source_target_pairs={{0,8},{4,12},{8,0},{12,4},{1,9},{5,13},{9,1},{13,5},{2,10},{6,14},... | collective-permute-start | bytes 516104 | tf_op jit(solution)/shard_map/ppermute | solution.py:383
  65.3 10.7 %collective-permute-start.21 = (bf16[48,1792]{1,0:T(8,128)(2,1)S(1)}, bf16[48,1792]{1,0:T(8,128)(2,1)S(1)}, u32[]{:S(2)}, u32[]{:S(2)}) collective-permute-start(bf16[48,1792]{1,0:T(8,128)(2,1)S(1)} %get-tuple-element.80), channel_id=1, source_target_pairs={{16,28},{20,24},{24,20},{28,16},{17,29},{21,25},{25,21},{29,17},{1... | collective-permute-start | bytes 516104 | tf_op jit(solution)/shard_map/ppermute | solution.py:383
  70.4 8.1 %collective-permute-start.22 = (bf16[48,1792]{1,0:T(8,128)(2,1)S(1)}, bf16[48,1792]{1,0:T(8,128)(2,1)S(1)}, u32[]{:S(2)}, u32[]{:S(2)}) collective-permute-start(bf16[48,1792]{1,0:T(8,128)(2,1)S(1)} %get-tuple-element.81), channel_id=1, source_target_pairs={{16,20},{20,16},{24,28},{28,24},{17,21},{21,17},{25,29},{29,25},{1... | collective-permute-start | bytes 516104 | tf_op jit(solution)/shard_map/ppermute | solution.py:383
  72.4 7.3 %collective-permute-start.20 = (bf16[48,1792]{1,0:T(8,128)(2,1)S(1)}, bf16[48,1792]{1,0:T(8,128)(2,1)S(1)}, u32[]{:S(2)}, u32[]{:S(2)}) collective-permute-start(bf16[48,1792]{1,0:T(8,128)(2,1)S(1)} %shard_map.71), channel_id=1, source_target_pairs={{0,16},{1,17},{2,18},{3,19},{4,20},{5,21},{6,22},{7,23},{8,24},{9,... | collective-permute-start | bytes 516104 | tf_op jit(solution)/shard_map/ppermute | solution.py:393
  84.5 7.9 %collective-permute-start.25 = (bf16[112,1024]{1,0:T(8,128)(2,1)S(1)}, bf16[112,1024]{1,0:T(8,128)(2,1)S(1)}, u32[]{:S(2)}, u32[]{:S(2)}) collective-permute-start(bf16[112,1024]{1,0:T(8,128)(2,1)S(1)} %shard_map.73.refs_0_), channel_id=1, source_target_pairs={{0,2},{1,3},{2,0},{3,1},{4,6},{5,7},{6,4},{7,5},{8,10},{9,11},{10,... | collective-permute-start | bytes 688136 | tf_op jit(solution)/shard_map/ppermute | solution.py:358
  90.3 7.9 %collective-permute-start.32 = (bf16[112,1024]{1,0:T(8,128)(2,1)S(1)}, bf16[112,1024]{1,0:T(8,128)(2,1)S(1)}, u32[]{:S(2)}, u32[]{:S(2)}) collective-permute-start(bf16[112,1024]{1,0:T(8,128)(2,1)S(1)} %shard_map.79.refs_1_), channel_id=1, source_target_pairs={{0,2},{1,3},{2,0},{3,1},{4,6},{5,7},{6,4},{7,5},{8,10},{9,11},{10,... | collective-permute-start | bytes 688136 | tf_op jit(solution)/shard_map/ppermute | solution.py:358
  94.9 11.8 %collective-permute-start.28 = (bf16[48,1792]{1,0:T(8,128)(2,1)S(1)}, bf16[48,1792]{1,0:T(8,128)(2,1)S(1)}, u32[]{:S(2)}, u32[]{:S(2)}) collective-permute-start(bf16[48,1792]{1,0:T(8,128)(2,1)S(1)} %get-tuple-element.87), channel_id=1, source_target_pairs={{0,8},{4,12},{8,0},{12,4},{1,9},{5,13},{9,1},{13,5},{2,10},{6,14},... | collective-permute-start | bytes 516104 | tf_op jit(solution)/shard_map/ppermute | solution.py:370
  98.4 8.3 %collective-permute-start.27 = (bf16[24,1792]{1,0:T(8,128)(2,1)S(1)}, bf16[24,1792]{1,0:T(8,128)(2,1)S(1)}, u32[]{:S(2)}, u32[]{:S(2)}) collective-permute-start(bf16[24,1792]{1,0:T(8,128)(2,1)S(1)} %get-tuple-element.86), channel_id=1, source_target_pairs={{0,4},{4,0},{8,12},{12,8},{1,5},{5,1},{9,13},{13,9},{2,6},{6,2},{1... | collective-permute-start | bytes 258056 | tf_op jit(solution)/shard_map/ppermute | solution.py:370
  102.2 7.1 %collective-permute-start.34 = (bf16[24,1792]{1,0:T(8,128)(2,1)S(1)}, bf16[24,1792]{1,0:T(8,128)(2,1)S(1)}, u32[]{:S(2)}, u32[]{:S(2)}) collective-permute-start(bf16[24,1792]{1,0:T(8,128)(2,1)S(1)} %get-tuple-element.92), channel_id=1, source_target_pairs={{0,4},{4,0},{8,12},{12,8},{1,5},{5,1},{9,13},{13,9},{2,6},{6,2},{1... | collective-permute-start | bytes 258056 | tf_op jit(solution)/shard_map/ppermute | solution.py:366
  102.7 9.8 %collective-permute-start.35 = (bf16[24,1792]{1,0:T(8,128)(2,1)S(1)}, bf16[24,1792]{1,0:T(8,128)(2,1)S(1)}, u32[]{:S(2)}, u32[]{:S(2)}) collective-permute-start(bf16[24,1792]{1,0:T(8,128)(2,1)S(1)} %get-tuple-element.93), channel_id=1, source_target_pairs={{0,8},{4,12},{8,0},{12,4},{1,9},{5,13},{9,1},{13,5},{2,10},{6,14},... | collective-permute-start | bytes 258056 | tf_op jit(solution)/shard_map/ppermute | solution.py:366
  103.9 8.7 %collective-permute-start.36 = (bf16[24,1792]{1,0:T(8,128)(2,1)S(1)}, bf16[24,1792]{1,0:T(8,128)(2,1)S(1)}, u32[]{:S(2)}, u32[]{:S(2)}) collective-permute-start(bf16[24,1792]{1,0:T(8,128)(2,1)S(1)} %get-tuple-element.94), channel_id=1, source_target_pairs={{0,12},{4,8},{8,4},{12,0},{1,13},{5,9},{9,5},{13,1},{2,14},{6,10},... | collective-permute-start | bytes 258056 | tf_op jit(solution)/shard_map/ppermute | solution.py:366
  106.7 6.6 %collective-permute-start.29 = (bf16[24,1792]{1,0:T(8,128)(2,1)S(1)}, bf16[24,1792]{1,0:T(8,128)(2,1)S(1)}, u32[]{:S(2)}, u32[]{:S(2)}) collective-permute-start(bf16[24,1792]{1,0:T(8,128)(2,1)S(1)} %shard_map.77), channel_id=1, source_target_pairs={{0,4},{4,0},{8,12},{12,8},{1,5},{5,1},{9,13},{13,9},{2,6},{6,2},{1... | collective-permute-start | bytes 258056 | tf_op jit(solution)/shard_map/ppermute | solution.py:370
  (15 other events, 44.7 us)

commit v4 on v3

--- a/solution.py
+++ b/solution.py
@@ -298,10 +298,6 @@
         low += out.shape[0]
 
 
-def hand_on_kernel(source, target):
-    target[...] = source[...]
-
-
 def second_kernel(z, pair_ref, out):
     out[...] = pair_ref[...].astype(F32)[z.piece:].astype(BF16)
 
@@ -387,10 +383,10 @@
         rows = lax.ppermute(kept, "section", hop)
         if z.pieces == 1:
             return rows, [lax.ppermute(exchanged(pieces)[0], "section", hop)]
-        far = within(pieces[0], z.near, tick)
+        pairs = [(tick * z.peers + i, (tick + 1) * z.peers + (i ^ z.near)) for i in range(z.peers)]
+        far = lax.ppermute(pieces[0], ("section", "expert"), pairs)
         result = call(repack_kernel, (z,), 4, [all_pay] * (z.pieces - 1), [VMEM] * 2, [], routes, rows)
-        far = call(hand_on_kernel, (), 2, [all_pay], [VMEM], [], far, waits=result[:1])[0]
-        result.insert(z.near, lax.ppermute(far, "section", hop))
+        result.insert(z.near, far)
         for step in steps[:-1]:
             if step != z.near:
                 result[step] = within(result[step], step, tick + 1)

time: 115 us -> 114 us (level)
    ppermute x6, waiting for transfers between devices: 2.43 us -> 4.61 us  [across(): lax.ppermute(value, 'expert', [(i, i ^ step) for i in range(z.peers)])]
    ppermute x9, waiting for transfers between devices: 7.14 us -> 5.81 us  [exchanged(): result[step] = lax.ppermute(pieces[step], 'expert', pairs)]
    ppermute x1, waiting for transfers between devices: 1.17 us -> 0.01 us  [relayed(): far = lax.ppermute(pieces[0], ('section', 'expert'), pairs)]
    ppermute x3 -> x2, starting transfers between devices: 7.68 us -> 8.66 us  [within(): return lax.ppermute(value, ('section', 'expert'), pairs)]
    ppermute x3 -> x2, waiting for transfers between devices: 4.65 us -> 4.07 us  [within(): return lax.ppermute(value, ('section', 'expert'), pairs)]
    pallas_call x29 -> x28, Pallas kernels: 39 us -> 39 us  [call(): pl.pallas_call(functools.partial(after_waits, len(waits), functools.parti...]
  transfers between devices with their start and end apart: 37 -> 36, of which waited for: 26 -> 25; matrix products, arithmetic and copies ran while one was open for 0% -> 0% of each run, Pallas kernels for 26% -> 26%
where the time goes in v4:
time: 114 us
  starting transfers between devices  41.5 us (36%)
  Pallas kernels  39 us (34%)
  waiting for transfers between devices  33.3 us (29%)
    pallas_call x28, Pallas kernels, call(): pl.pallas_call(functools.partial(after_waits, len(waits), functools.parti...  39 us
    ppermute x9, starting transfers between devices, exchanged(): result[step] = lax.ppermute(pieces[step], 'expert', pairs)  13.1 us
    ppermute x16, waiting for transfers between devices, swap(): return lax.ppermute(value, 'hidden', pairs)  10.1 us
    ppermute x2, starting transfers between devices, within(): return lax.ppermute(value, ('section', 'expert'), pairs)  8.66 us
    ppermute x6, starting transfers between devices, across(): lax.ppermute(value, 'expert', [(i, i ^ step) for i in range(z.peers)])  7.83 us
    ppermute x1, waiting for transfers between devices, relayed(): rows = lax.ppermute(kept, 'section', hop)  7.37 us
    ppermute x16, starting transfers between devices, swap(): return lax.ppermute(value, 'hidden', pairs)  6.88 us
    ppermute x9, waiting for transfers between devices, exchanged(): result[step] = lax.ppermute(pieces[step], 'expert', pairs)  5.81 us
  transfers between devices with their start and end apart: 36, of which 25 were waited for; matrix products, arithmetic and copies ran while one was open for 0% of the time, Pallas kernels for 26%

profile of v4, /device:TPU:2, one launch (start us, length us, event | category | flops | bytes accessed | tf_op | source)
XLA Modules:
  0.0 114.2 jit_solution(5591483024333270983)
XLA Ops:
  0.0 1.6 %shard_map.55 = (bf16[48,1792]{1,0:T(8,128)(2,1)S(1)}, bf16[48,1792]{1,0:T(8,128)(2,1)S(1)}, bf16[48,1792]{1,0:T(8,128)(2,1)S(1)}, bf16[48,1792]{1,0:T(8,128)(2,1)S(1)}, bf16[192,64]{1,0:T(8,128)(2,1)S(1)}) custom-call(s32[4,2,16]{2,1,0:T(2,128)} %bitcast.11, bf16[4,2,16]{2,1,0:T(2,128)(2,1)} %bitcast.14, bf16[64,1792]{1,0:T(8,128)(2,1)} %bitcast.8), custom_call_target="tpu_custom_call" | custom-call | tf_op jit(solution)/shard_map/pallas_call | solution.py:330
  1.6 2.7 %collective-permute-start = (bf16[48,1792]{1,0:T(8,128)(2,1)S(1)}, bf16[48,1792]{1,0:T(8,128)(2,1)S(1)}, u32[]{:S(2)}, u32[]{:S(2)}) collective-permute-start(bf16[48,1792]{1,0:T(8,128)(2,1)S(1)} %get-tuple-element.56), channel_id=1, source_target_pairs={{0,8},{4,12},{8,0},{12,4},{1,9},{5,13},{9,1},{13,5},{2,10},{6,14},... | collective-permute-start | bytes 516104 | tf_op jit(solution)/shard_map/ppermute | solution.py:362
  5.9 9.6 %shard_map.56 = (bf16[3584,1024]{1,0:T(8,128)(2,1)S(1)}, bf16[3584,1024]{1,0:T(8,128)(2,1)S(1)}, bf16[3584,1024]{1,0:T(8,128)(2,1)S(1)}, bf16[3584,1024]{1,0:T(8,128)(2,1)S(1)}) custom-call(bf16[192,64]{1,0:T(8,128)(2,1)S(1)} %get-tuple-element.50.refs_0_, bf16[1,1792,2,4096]{3,2,1,0:T(2,128)(2,1)} %refs_1_.2), custom_call_target="tpu_custom_call" | custom-call | tf_op jit(solution)/shard_map/pallas_call | solution.py:330
  15.5 5.3 %shard_map.57 = (bf16[1024,1792]{1,0:T(8,128)(2,1)S(1)}, bf16[1024,1792]{1,0:T(8,128)(2,1)S(1)}, bf16[1024,1792]{1,0:T(8,128)(2,1)S(1)}, bf16[1024,1792]{1,0:T(8,128)(2,1)S(1)}) custom-call(bf16[3584,1024]{1,0:T(8,128)(2,1)S(1)} %get-tuple-element.51.refs_0_.refs_2_, bf16[1,4096,1792]{2,1,0:T(8,128)(2,1)} %refs_1_.3), custom_call_target="tpu_custom_call" | custom-call | tf_op jit(solution)/shard_map/pallas_call | solution.py:330
  20.8 3.2 %shard_map.58 = (f32[112,1024]{1,0:T(8,128)S(1)}, bf16[56,1024]{1,0:T(8,128)(2,1)S(1)}, bf16[56,1024]{1,0:T(8,128)(2,1)S(1)}) custom-call(bf16[1024,1792]{1,0:T(8,128)(2,1)S(1)} %get-tuple-element.52.refs_0_, bf16[3584,1024]{1,0:T(8,128)(2,1)S(1)} %get-tuple-element.54.refs_1_, bf16[3584,1024]{1,0:T(8,128)(2,1)S(1)} %get-tuple-element.55.refs_2_, ...), custom_call_target="tpu_custom_call" | custom-call | tf_op jit(solution)/shard_map/pallas_call | solution.py:330
  25.6 1.6 %collective-permute-start.5 = (bf16[112,1024]{1,0:T(8,128)(2,1)S(1)}, bf16[112,1024]{1,0:T(8,128)(2,1)S(1)}, u32[]{:S(2)}, u32[]{:S(2)}) collective-permute-start(bf16[112,1024]{1,0:T(8,128)(2,1)S(1)} %shard_map.59.refs_0_), channel_id=1, source_target_pairs={{0,2},{1,3},{2,0},{3,1},{4,6},{5,7},{6,4},{7,5},{8,10},{9,11},{10,... | collective-permute-start | bytes 688136 | tf_op jit(solution)/shard_map/ppermute | solution.py:354
  27.2 3.2 %shard_map.64 = (f32[112,1024]{1,0:T(8,128)S(1)}, bf16[56,1024]{1,0:T(8,128)(2,1)S(1)}, bf16[56,1024]{1,0:T(8,128)(2,1)S(1)}) custom-call(bf16[112,1024]{1,0:T(8,128)(2,1)S(1)} %shard_map.59.refs_0_, bf16[3584,1024]{1,0:T(8,128)(2,1)S(1)} %get-tuple-element.68.refs_1_, bf16[3584,1024]{1,0:T(8,128)(2,1)S(1)} %get-tuple-element.51.refs_0_.refs_2_, ...), custom_call_target="tpu_custom_call" | custom-call | tf_op jit(solution)/shard_map/pallas_call | solution.py:330
  36.0 2.9 %collective-permute-start.8 = (bf16[48,1792]{1,0:T(8,128)(2,1)S(1)}, bf16[48,1792]{1,0:T(8,128)(2,1)S(1)}, u32[]{:S(2)}, u32[]{:S(2)}) collective-permute-start(bf16[48,1792]{1,0:T(8,128)(2,1)S(1)} %get-tuple-element.65), channel_id=1, source_target_pairs={{0,8},{4,12},{8,0},{12,4},{1,9},{5,13},{9,1},{13,5},{2,10},{6,14},... | collective-permute-start | bytes 516104 | tf_op jit(solution)/shard_map/ppermute | solution.py:366
  40.2 1.9 %collective-permute-start.7 = (bf16[24,1792]{1,0:T(8,128)(2,1)S(1)}, bf16[24,1792]{1,0:T(8,128)(2,1)S(1)}, u32[]{:S(2)}, u32[]{:S(2)}) collective-permute-start(bf16[24,1792]{1,0:T(8,128)(2,1)S(1)} %get-tuple-element.64), channel_id=1, source_target_pairs={{0,4},{4,0},{8,12},{12,8},{1,5},{5,1},{9,13},{13,9},{2,6},{6,2},{1... | collective-permute-start | bytes 258056 | tf_op jit(solution)/shard_map/ppermute | solution.py:366
  44.3 2.6 %collective-permute-start.15 = (bf16[24,1792]{1,0:T(8,128)(2,1)S(1)}, bf16[24,1792]{1,0:T(8,128)(2,1)S(1)}, u32[]{:S(2)}, u32[]{:S(2)}) collective-permute-start(bf16[24,1792]{1,0:T(8,128)(2,1)S(1)} %get-tuple-element.74), channel_id=1, source_target_pairs={{0,8},{4,12},{8,0},{12,4},{1,9},{5,13},{9,1},{13,5},{2,10},{6,14},... | collective-permute-start | bytes 258056 | tf_op jit(solution)/shard_map/ppermute | solution.py:362
  49.1 2.4 %collective-permute-start.17 = (s32[4,2,16]{2,1,0:T(2,128)S(1)}, s32[4,2,16]{2,1,0:T(2,128)S(1)}, u32[]{:S(2)}, u32[]{:S(2)}) collective-permute-start(s32[4,2,16]{2,1,0:T(2,128)S(1)} %get-tuple-element.76), channel_id=1, source_target_pairs={{16,0},{17,1},{18,2},{19,3},{20,4},{21,5},{22,6},{23,7},{24,8},{25... | collective-permute-start | bytes 1544 | tf_op jit(solution)/shard_map/ppermute | solution.py:482
  58.3 7.4 %collective-permute-done.18.refs_1_ = bf16[64,1792]{1,0:T(8,128)(2,1)S(1)} collective-permute-done((bf16[64,1792]{1,0:T(8,128)(2,1)S(1)}, bf16[64,1792]{1,0:T(8,128)(2,1)S(1)}, u32[]{:S(2)}, u32[]{:S(2)}) %collective-permute-start.18) | collective-permute-done | bytes 229408 | tf_op jit(solution)/shard_map/ppermute | solution.py:383
  66.3 4.3 %collective-permute-start.20 = (bf16[48,1792]{1,0:T(8,128)(2,1)S(1)}, bf16[48,1792]{1,0:T(8,128)(2,1)S(1)}, u32[]{:S(2)}, u32[]{:S(2)}) collective-permute-start(bf16[48,1792]{1,0:T(8,128)(2,1)S(1)} %get-tuple-element.79), channel_id=1, source_target_pairs={{16,28},{20,24},{24,20},{28,16},{17,29},{21,25},{25,21},{29,17},{1... | collective-permute-start | bytes 516104 | tf_op jit(solution)/shard_map/ppermute | solution.py:379
  70.5 4.4 %collective-permute-start.21 = (bf16[48,1792]{1,0:T(8,128)(2,1)S(1)}, bf16[48,1792]{1,0:T(8,128)(2,1)S(1)}, u32[]{:S(2)}, u32[]{:S(2)}) collective-permute-start(bf16[48,1792]{1,0:T(8,128)(2,1)S(1)} %get-tuple-element.80), channel_id=1, source_target_pairs={{16,20},{20,16},{24,28},{28,24},{17,21},{21,17},{25,29},{29,25},{1... | collective-permute-start | bytes 516104 | tf_op jit(solution)/shard_map/ppermute | solution.py:379
  74.9 2.1 %collective-permute-done.20.refs_4_ = bf16[48,1792]{1,0:T(8,128)(2,1)S(1)} collective-permute-done((bf16[48,1792]{1,0:T(8,128)(2,1)S(1)}, bf16[48,1792]{1,0:T(8,128)(2,1)S(1)}, u32[]{:S(2)}, u32[]{:S(2)}) %collective-permute-start.20) | collective-permute-done | bytes 172064 | tf_op jit(solution)/shard_map/ppermute | solution.py:379
  77.0 2.0 %collective-permute-done.21.refs_5_ = bf16[48,1792]{1,0:T(8,128)(2,1)S(1)} collective-permute-done((bf16[48,1792]{1,0:T(8,128)(2,1)S(1)}, bf16[48,1792]{1,0:T(8,128)(2,1)S(1)}, u32[]{:S(2)}, u32[]{:S(2)}) %collective-permute-start.21) | collective-permute-done | bytes 172064 | tf_op jit(solution)/shard_map/ppermute | solution.py:379
  79.0 3.2 %shard_map.71 = (f32[112,1024]{1,0:T(8,128)S(1)}, bf16[56,1024]{1,0:T(8,128)(2,1)S(1)}, bf16[56,1024]{1,0:T(8,128)(2,1)S(1)}) custom-call(bf16[1024,1792]{1,0:T(8,128)(2,1)S(1)} %get-tuple-element.52.refs_0_, bf16[3584,1024]{1,0:T(8,128)(2,1)S(1)} %get-tuple-element.54.refs_1_, bf16[3584,1024]{1,0:T(8,128)(2,1)S(1)} %get-tuple-element.55.refs_2_, ...), custom_call_target="tpu_custom_call" | custom-call | tf_op jit(solution)/shard_map/pallas_call | solution.py:330
  84.9 3.2 %shard_map.77 = (f32[112,1024]{1,0:T(8,128)S(1)}, bf16[56,1024]{1,0:T(8,128)(2,1)S(1)}, bf16[56,1024]{1,0:T(8,128)(2,1)S(1)}) custom-call(bf16[112,1024]{1,0:T(8,128)(2,1)S(1)} %shard_map.72.refs_0_, bf16[3584,1024]{1,0:T(8,128)(2,1)S(1)} %get-tuple-element.68.refs_1_, bf16[3584,1024]{1,0:T(8,128)(2,1)S(1)} %get-tuple-element.51.refs_0_.refs_2_, ...), custom_call_target="tpu_custom_call" | custom-call | tf_op jit(solution)/shard_map/pallas_call | solution.py:330
  95.4 2.2 %collective-permute-done.31.refs_2_ = bf16[112,1024]{1,0:T(8,128)(2,1)S(1)} collective-permute-done((bf16[112,1024]{1,0:T(8,128)(2,1)S(1)}, bf16[112,1024]{1,0:T(8,128)(2,1)S(1)}, u32[]{:S(2)}, u32[]{:S(2)}) %collective-permute-start.31) | collective-permute-done | bytes 229408 | tf_op jit(solution)/shard_map/ppermute | solution.py:354
  97.9 1.7 %collective-permute-start.26 = (bf16[24,1792]{1,0:T(8,128)(2,1)S(1)}, bf16[24,1792]{1,0:T(8,128)(2,1)S(1)}, u32[]{:S(2)}, u32[]{:S(2)}) collective-permute-start(bf16[24,1792]{1,0:T(8,128)(2,1)S(1)} %get-tuple-element.86), channel_id=1, source_target_pairs={{0,4},{4,0},{8,12},{12,8},{1,5},{5,1},{9,13},{13,9},{2,6},{6,2},{1... | collective-permute-start | bytes 258056 | tf_op jit(solution)/shard_map/ppermute | solution.py:366
  103.0 2.7 %collective-permute-start.35 = (bf16[24,1792]{1,0:T(8,128)(2,1)S(1)}, bf16[24,1792]{1,0:T(8,128)(2,1)S(1)}, u32[]{:S(2)}, u32[]{:S(2)}) collective-permute-start(bf16[24,1792]{1,0:T(8,128)(2,1)S(1)} %get-tuple-element.94), channel_id=1, source_target_pairs={{0,12},{4,8},{8,4},{12,0},{1,13},{5,9},{9,5},{13,1},{2,14},{6,10},... | collective-permute-start | bytes 258056 | tf_op jit(solution)/shard_map/ppermute | solution.py:362
  105.8 1.5 %collective-permute-done.26.refs_4_ = bf16[24,1792]{1,0:T(8,128)(2,1)S(1)} collective-permute-done((bf16[24,1792]{1,0:T(8,128)(2,1)S(1)}, bf16[24,1792]{1,0:T(8,128)(2,1)S(1)}, u32[]{:S(2)}, u32[]{:S(2)}) %collective-permute-start.26) | collective-permute-done | bytes 86048 | tf_op jit(solution)/shard_map/ppermute | solution.py:366
  107.4 4.5 %collective-permute-done.33.refs_8_ = bf16[24,1792]{1,0:T(8,128)(2,1)S(1)} collective-permute-done((bf16[24,1792]{1,0:T(8,128)(2,1)S(1)}, bf16[24,1792]{1,0:T(8,128)(2,1)S(1)}, u32[]{:S(2)}, u32[]{:S(2)}) %collective-permute-start.33) | collective-permute-done | bytes 86048 | tf_op jit(solution)/shard_map/ppermute | solution.py:362
  111.8 1.4 %collective-permute-done.28.refs_6_ = bf16[24,1792]{1,0:T(8,128)(2,1)S(1)} collective-permute-done((bf16[24,1792]{1,0:T(8,128)(2,1)S(1)}, bf16[24,1792]{1,0:T(8,128)(2,1)S(1)}, u32[]{:S(2)}, u32[]{:S(2)}) %collective-permute-start.28) | collective-permute-done | bytes 86048 | tf_op jit(solution)/shard_map/ppermute | solution.py:366
  (80 shorter events, 36.5 us)
Async XLA Ops:
  1.6 19.2 %collective-permute-start = (bf16[48,1792]{1,0:T(8,128)(2,1)S(1)}, bf16[48,1792]{1,0:T(8,128)(2,1)S(1)}, u32[]{:S(2)}, u32[]{:S(2)}) collective-permute-start(bf16[48,1792]{1,0:T(8,128)(2,1)S(1)} %get-tuple-element.56), channel_id=1, source_target_pairs={{0,8},{4,12},{8,0},{12,4},{1,9},{5,13},{9,1},{13,5},{2,10},{6,14},... | collective-permute-start | bytes 516104 | tf_op jit(solution)/shard_map/ppermute | solution.py:362
  4.3 16.5 %collective-permute-start.1 = (bf16[48,1792]{1,0:T(8,128)(2,1)S(1)}, bf16[48,1792]{1,0:T(8,128)(2,1)S(1)}, u32[]{:S(2)}, u32[]{:S(2)}) collective-permute-start(bf16[48,1792]{1,0:T(8,128)(2,1)S(1)} %get-tuple-element.57), channel_id=1, source_target_pairs={{0,12},{4,8},{8,4},{12,0},{1,13},{5,9},{9,5},{13,1},{2,14},{6,10},... | collective-permute-start | bytes 516104 | tf_op jit(solution)/shard_map/ppermute | solution.py:362
  5.6 15.2 %collective-permute-start.2 = (bf16[48,1792]{1,0:T(8,128)(2,1)S(1)}, bf16[48,1792]{1,0:T(8,128)(2,1)S(1)}, u32[]{:S(2)}, u32[]{:S(2)}) collective-permute-start(bf16[48,1792]{1,0:T(8,128)(2,1)S(1)} %get-tuple-element.58), channel_id=1, source_target_pairs={{0,4},{4,0},{8,12},{12,8},{1,5},{5,1},{9,13},{13,9},{2,6},{6,2},{1... | collective-permute-start | bytes 516104 | tf_op jit(solution)/shard_map/ppermute | solution.py:362
  25.6 7.9 %collective-permute-start.5 = (bf16[112,1024]{1,0:T(8,128)(2,1)S(1)}, bf16[112,1024]{1,0:T(8,128)(2,1)S(1)}, u32[]{:S(2)}, u32[]{:S(2)}) collective-permute-start(bf16[112,1024]{1,0:T(8,128)(2,1)S(1)} %shard_map.59.refs_0_), channel_id=1, source_target_pairs={{0,2},{1,3},{2,0},{3,1},{4,6},{5,7},{6,4},{7,5},{8,10},{9,11},{10,... | collective-permute-start | bytes 688136 | tf_op jit(solution)/shard_map/ppermute | solution.py:354
  32.0 7.9 %collective-permute-start.12 = (bf16[112,1024]{1,0:T(8,128)(2,1)S(1)}, bf16[112,1024]{1,0:T(8,128)(2,1)S(1)}, u32[]{:S(2)}, u32[]{:S(2)}) collective-permute-start(bf16[112,1024]{1,0:T(8,128)(2,1)S(1)} %shard_map.65.refs_1_), channel_id=1, source_target_pairs={{0,2},{1,3},{2,0},{3,1},{4,6},{5,7},{6,4},{7,5},{8,10},{9,11},{10,... | collective-permute-start | bytes 688136 | tf_op jit(solution)/shard_map/ppermute | solution.py:354
  36.0 12.2 %collective-permute-start.8 = (bf16[48,1792]{1,0:T(8,128)(2,1)S(1)}, bf16[48,1792]{1,0:T(8,128)(2,1)S(1)}, u32[]{:S(2)}, u32[]{:S(2)}) collective-permute-start(bf16[48,1792]{1,0:T(8,128)(2,1)S(1)} %get-tuple-element.65), channel_id=1, source_target_pairs={{0,8},{4,12},{8,0},{12,4},{1,9},{5,13},{9,1},{13,5},{2,10},{6,14},... | collective-permute-start | bytes 516104 | tf_op jit(solution)/shard_map/ppermute | solution.py:366
  40.2 8.9 %collective-permute-start.7 = (bf16[24,1792]{1,0:T(8,128)(2,1)S(1)}, bf16[24,1792]{1,0:T(8,128)(2,1)S(1)}, u32[]{:S(2)}, u32[]{:S(2)}) collective-permute-start(bf16[24,1792]{1,0:T(8,128)(2,1)S(1)} %get-tuple-element.64), channel_id=1, source_target_pairs={{0,4},{4,0},{8,12},{12,8},{1,5},{5,1},{9,13},{13,9},{2,6},{6,2},{1... | collective-permute-start | bytes 258056 | tf_op jit(solution)/shard_map/ppermute | solution.py:366
  43.8 9.0 %collective-permute-start.14 = (bf16[24,1792]{1,0:T(8,128)(2,1)S(1)}, bf16[24,1792]{1,0:T(8,128)(2,1)S(1)}, u32[]{:S(2)}, u32[]{:S(2)}) collective-permute-start(bf16[24,1792]{1,0:T(8,128)(2,1)S(1)} %get-tuple-element.73), channel_id=1, source_target_pairs={{0,4},{4,0},{8,12},{12,8},{1,5},{5,1},{9,13},{13,9},{2,6},{6,2},{1... | collective-permute-start | bytes 258056 | tf_op jit(solution)/shard_map/ppermute | solution.py:362
  44.3 9.7 %collective-permute-start.15 = (bf16[24,1792]{1,0:T(8,128)(2,1)S(1)}, bf16[24,1792]{1,0:T(8,128)(2,1)S(1)}, u32[]{:S(2)}, u32[]{:S(2)}) collective-permute-start(bf16[24,1792]{1,0:T(8,128)(2,1)S(1)} %get-tuple-element.74), channel_id=1, source_target_pairs={{0,8},{4,12},{8,0},{12,4},{1,9},{5,13},{9,1},{13,5},{2,10},{6,14},... | collective-permute-start | bytes 258056 | tf_op jit(solution)/shard_map/ppermute | solution.py:362
  46.9 7.3 %collective-permute-start.16 = (bf16[24,1792]{1,0:T(8,128)(2,1)S(1)}, bf16[24,1792]{1,0:T(8,128)(2,1)S(1)}, u32[]{:S(2)}, u32[]{:S(2)}) collective-permute-start(bf16[24,1792]{1,0:T(8,128)(2,1)S(1)} %get-tuple-element.75), channel_id=1, source_target_pairs={{0,12},{4,8},{8,4},{12,0},{1,13},{5,9},{9,5},{13,1},{2,14},{6,10},... | collective-permute-start | bytes 258056 | tf_op jit(solution)/shard_map/ppermute | solution.py:362
  48.2 6.8 %collective-permute-start.9 = (bf16[24,1792]{1,0:T(8,128)(2,1)S(1)}, bf16[24,1792]{1,0:T(8,128)(2,1)S(1)}, u32[]{:S(2)}, u32[]{:S(2)}) collective-permute-start(bf16[24,1792]{1,0:T(8,128)(2,1)S(1)} %shard_map.63), channel_id=1, source_target_pairs={{0,4},{4,0},{8,12},{12,8},{1,5},{5,1},{9,13},{13,9},{2,6},{6,2},{1... | collective-permute-start | bytes 258056 | tf_op jit(solution)/shard_map/ppermute | solution.py:366
  49.1 3.7 %collective-permute-start.17 = (s32[4,2,16]{2,1,0:T(2,128)S(1)}, s32[4,2,16]{2,1,0:T(2,128)S(1)}, u32[]{:S(2)}, u32[]{:S(2)}) collective-permute-start(s32[4,2,16]{2,1,0:T(2,128)S(1)} %get-tuple-element.76), channel_id=1, source_target_pairs={{16,0},{17,1},{18,2},{19,3},{20,4},{21,5},{22,6},{23,7},{24,8},{25... | collective-permute-start | bytes 1544 | tf_op jit(solution)/shard_map/ppermute | solution.py:482
  55.7 10.0 %collective-permute-start.18 = (bf16[64,1792]{1,0:T(8,128)(2,1)S(1)}, bf16[64,1792]{1,0:T(8,128)(2,1)S(1)}, u32[]{:S(2)}, u32[]{:S(2)}) collective-permute-start(bf16[64,1792]{1,0:T(8,128)(2,1)S(1)} %get-tuple-element.77.refs_2_), channel_id=1, source_target_pairs={{0,16},{1,17},{2,18},{3,19},{4,20},{5,21},{6,22},{7,23},{8,24},{9,... | collective-permute-start | bytes 688136 | tf_op jit(solution)/shard_map/ppermute | solution.py:383
  57.0 17.9 %collective-permute-start.19 = (bf16[48,1792]{1,0:T(8,128)(2,1)S(1)}, bf16[48,1792]{1,0:T(8,128)(2,1)S(1)}, u32[]{:S(2)}, u32[]{:S(2)}) collective-permute-start(bf16[48,1792]{1,0:T(8,128)(2,1)S(1)} %get-tuple-element.78), channel_id=1, source_target_pairs={{0,24},{4,28},{8,16},{12,20},{1,25},{5,29},{9,17},{13,21},{2,26},{... | collective-permute-start | bytes 516104 | tf_op jit(solution)/shard_map/ppermute | solution.py:387
  66.3 10.8 %collective-permute-start.20 = (bf16[48,1792]{1,0:T(8,128)(2,1)S(1)}, bf16[48,1792]{1,0:T(8,128)(2,1)S(1)}, u32[]{:S(2)}, u32[]{:S(2)}) collective-permute-start(bf16[48,1792]{1,0:T(8,128)(2,1)S(1)} %get-tuple-element.79), channel_id=1, source_target_pairs={{16,28},{20,24},{24,20},{28,16},{17,29},{21,25},{25,21},{29,17},{1... | collective-permute-start | bytes 516104 | tf_op jit(solution)/shard_map/ppermute | solution.py:379
  70.5 8.5 %collective-permute-start.21 = (bf16[48,1792]{1,0:T(8,128)(2,1)S(1)}, bf16[48,1792]{1,0:T(8,128)(2,1)S(1)}, u32[]{:S(2)}, u32[]{:S(2)}) collective-permute-start(bf16[48,1792]{1,0:T(8,128)(2,1)S(1)} %get-tuple-element.80), channel_id=1, source_target_pairs={{16,20},{20,16},{24,28},{28,24},{17,21},{21,17},{25,29},{29,25},{1... | collective-permute-start | bytes 516104 | tf_op jit(solution)/shard_map/ppermute | solution.py:379
  83.8 7.9 %collective-permute-start.24 = (bf16[112,1024]{1,0:T(8,128)(2,1)S(1)}, bf16[112,1024]{1,0:T(8,128)(2,1)S(1)}, u32[]{:S(2)}, u32[]{:S(2)}) collective-permute-start(bf16[112,1024]{1,0:T(8,128)(2,1)S(1)} %shard_map.72.refs_0_), channel_id=1, source_target_pairs={{0,2},{1,3},{2,0},{3,1},{4,6},{5,7},{6,4},{7,5},{8,10},{9,11},{10,... | collective-permute-start | bytes 688136 | tf_op jit(solution)/shard_map/ppermute | solution.py:354
  89.7 7.9 %collective-permute-start.31 = (bf16[112,1024]{1,0:T(8,128)(2,1)S(1)}, bf16[112,1024]{1,0:T(8,128)(2,1)S(1)}, u32[]{:S(2)}, u32[]{:S(2)}) collective-permute-start(bf16[112,1024]{1,0:T(8,128)(2,1)S(1)} %shard_map.78.refs_1_), channel_id=1, source_target_pairs={{0,2},{1,3},{2,0},{3,1},{4,6},{5,7},{6,4},{7,5},{8,10},{9,11},{10,... | collective-permute-start | bytes 688136 | tf_op jit(solution)/shard_map/ppermute | solution.py:354
  94.2 11.5 %collective-permute-start.27 = (bf16[48,1792]{1,0:T(8,128)(2,1)S(1)}, bf16[48,1792]{1,0:T(8,128)(2,1)S(1)}, u32[]{:S(2)}, u32[]{:S(2)}) collective-permute-start(bf16[48,1792]{1,0:T(8,128)(2,1)S(1)} %get-tuple-element.87), channel_id=1, source_target_pairs={{0,8},{4,12},{8,0},{12,4},{1,9},{5,13},{9,1},{13,5},{2,10},{6,14},... | collective-permute-start | bytes 516104 | tf_op jit(solution)/shard_map/ppermute | solution.py:366
  97.9 9.5 %collective-permute-start.26 = (bf16[24,1792]{1,0:T(8,128)(2,1)S(1)}, bf16[24,1792]{1,0:T(8,128)(2,1)S(1)}, u32[]{:S(2)}, u32[]{:S(2)}) collective-permute-start(bf16[24,1792]{1,0:T(8,128)(2,1)S(1)} %get-tuple-element.86), channel_id=1, source_target_pairs={{0,4},{4,0},{8,12},{12,8},{1,5},{5,1},{9,13},{13,9},{2,6},{6,2},{1... | collective-permute-start | bytes 258056 | tf_op jit(solution)/shard_map/ppermute | solution.py:366
  101.3 10.5 %collective-permute-start.33 = (bf16[24,1792]{1,0:T(8,128)(2,1)S(1)}, bf16[24,1792]{1,0:T(8,128)(2,1)S(1)}, u32[]{:S(2)}, u32[]{:S(2)}) collective-permute-start(bf16[24,1792]{1,0:T(8,128)(2,1)S(1)} %get-tuple-element.92), channel_id=1, source_target_pairs={{0,4},{4,0},{8,12},{12,8},{1,5},{5,1},{9,13},{13,9},{2,6},{6,2},{1... | collective-permute-start | bytes 258056 | tf_op jit(solution)/shard_map/ppermute | solution.py:362
  101.8 10.0 %collective-permute-start.34 = (bf16[24,1792]{1,0:T(8,128)(2,1)S(1)}, bf16[24,1792]{1,0:T(8,128)(2,1)S(1)}, u32[]{:S(2)}, u32[]{:S(2)}) collective-permute-start(bf16[24,1792]{1,0:T(8,128)(2,1)S(1)} %get-tuple-element.93), channel_id=1, source_target_pairs={{0,8},{4,12},{8,0},{12,4},{1,9},{5,13},{9,1},{13,5},{2,10},{6,14},... | collective-permute-start | bytes 258056 | tf_op jit(solution)/shard_map/ppermute | solution.py:362
  103.0 8.8 %collective-permute-start.35 = (bf16[24,1792]{1,0:T(8,128)(2,1)S(1)}, bf16[24,1792]{1,0:T(8,128)(2,1)S(1)}, u32[]{:S(2)}, u32[]{:S(2)}) collective-permute-start(bf16[24,1792]{1,0:T(8,128)(2,1)S(1)} %get-tuple-element.94), channel_id=1, source_target_pairs={{0,12},{4,8},{8,4},{12,0},{1,13},{5,9},{9,5},{13,1},{2,14},{6,10},... | collective-permute-start | bytes 258056 | tf_op jit(solution)/shard_map/ppermute | solution.py:362
  105.8 7.5 %collective-permute-start.28 = (bf16[24,1792]{1,0:T(8,128)(2,1)S(1)}, bf16[24,1792]{1,0:T(8,128)(2,1)S(1)}, u32[]{:S(2)}, u32[]{:S(2)}) collective-permute-start(bf16[24,1792]{1,0:T(8,128)(2,1)S(1)} %shard_map.76), channel_id=1, source_target_pairs={{0,4},{4,0},{8,12},{12,8},{1,5},{5,1},{9,13},{13,9},{2,6},{6,2},{1... | collective-permute-start | bytes 258056 | tf_op jit(solution)/shard_map/ppermute | solution.py:366
  (14 other events, 40.6 us)

commit v5 on v4

--- a/solution.py
+++ b/solution.py
@@ -58,7 +58,6 @@
         self.pairs = self.groups - 1 if self.pieces == 4 else 0
         self.near = self.pieces // 2
         self.listed = sorted(range(self.pieces), key=lambda step: -step.bit_length())
-        self.repacked = [step for step in range(self.pieces) if step != self.near]
         self.group_pay = peers * self.pay
         self.piece = self.group_pay // self.pieces
         self.all_pay = self.groups * self.group_pay
@@ -120,9 +119,9 @@
         out[...] = value[index * z.all_piece:(index + 1) * z.all_piece].astype(BF16)
 
 
-def repack_kernel(z, routes_ref, rows_ref, *outs):
+def near_kernel(z, routes_ref, rows_ref, *outs):
     hits, _, _ = slot_hits(z, routes_ref)
-    send_rows(z, hits, rows_ref[...], outs, z.repacked)
+    send_rows(z, hits, rows_ref[...], outs, range(z.near))
 
 
 def group_rows(z, group, pieces):
@@ -319,7 +318,7 @@
     routes_ref, out, outs = refs[0], refs[1], refs[2:]
     out[...] = jnp.where(lax.axis_index("section") == tick, value, kept_ref[...])
     hits, _, _ = slot_hits(z, routes_ref)
-    send_rows(z, hits, value, outs, [z.near])
+    send_rows(z, hits, value, outs, range(z.near, z.pieces))
 
 
 def after_waits(waits, kernel, *refs):
@@ -383,14 +382,15 @@
         rows = lax.ppermute(kept, "section", hop)
         if z.pieces == 1:
             return rows, [lax.ppermute(exchanged(pieces)[0], "section", hop)]
-        pairs = [(tick * z.peers + i, (tick + 1) * z.peers + (i ^ z.near)) for i in range(z.peers)]
-        far = lax.ppermute(pieces[0], ("section", "expert"), pairs)
-        result = call(repack_kernel, (z,), 4, [all_pay] * (z.pieces - 1), [VMEM] * 2, [], routes, rows)
-        result.insert(z.near, far)
-        for step in steps[:-1]:
-            if step != z.near:
-                result[step] = within(result[step], step, tick + 1)
-        return rows, result
+        far = {}
+        for step in steps:
+            if step >= z.near:
+                pairs = [(tick * z.peers + i, (tick + 1) * z.peers + (i ^ step)) for i in range(z.peers)]
+                far[step] = lax.ppermute(pieces[step - z.near], ("section", "expert"), pairs)
+        result = call(near_kernel, (z,), 4, [all_pay] * z.near, [VMEM] * 2, [], routes, rows)
+        for step in range(1, z.near):
+            result[step] = within(result[step], step, tick + 1)
+        return rows, result + [far[step] for step in range(z.near, z.pieces)]
 
     def products(received, group, waits):
         own, *sent = call(
@@ -484,7 +484,7 @@
         returned = sum(returned, [])
         kept, *sent = call(
             combine_kernel, (z, tick, last), 4,
-            [whole] if last else [whole, all_pay],
+            [whole] if last else [whole] + [all_pay] * (z.pieces - z.near),
             [VMEM] * (3 + len(returned) + (not last)), [],
             weight, rows, kept, *returned, *([] if last else [following]),
         )

time: 114 us -> 112 us (0.982)
  waiting for transfers between devices: 33.3 us -> 28.9 us
  starting transfers between devices: 41.5 us -> 43.1 us
    ppermute x6, starting transfers between devices: 7.83 us -> 11.9 us  [across(): lax.ppermute(value, 'expert', [(i, i ^ step) for i in range(z.peers)])]
    ppermute x2 -> x1, waiting for transfers between devices: 4.07 us -> 0.01 us  [within(): return lax.ppermute(value, ('section', 'expert'), pairs)]
    ppermute x1 -> x2, waiting for transfers between devices: 0.01 us -> 3.97 us  [relayed(): lax.ppermute(pieces[step - z.near], ('section', 'expert'), pairs)]
    ppermute x2 -> x1, starting transfers between devices: 8.66 us -> 4.81 us  [within(): return lax.ppermute(value, ('section', 'expert'), pairs)]
    ppermute x6, waiting for transfers between devices: 4.61 us -> 2.42 us  [across(): lax.ppermute(value, 'expert', [(i, i ^ step) for i in range(z.peers)])]
    ppermute x16, waiting for transfers between devices: 10.1 us -> 7.95 us  [swap(): return lax.ppermute(value, 'hidden', pairs)]
    ppermute x9, waiting for transfers between devices: 5.81 us -> 7.16 us  [exchanged(): result[step] = lax.ppermute(pieces[step], 'expert', pairs)]
    ppermute x1, waiting for transfers between devices: 7.37 us -> 6.07 us  [relayed(): rows = lax.ppermute(kept, 'section', hop)]
  transfers between devices with their start and end apart: 36 -> 36, of which waited for: 25 -> 23; matrix products, arithmetic and copies ran while one was open for 0% -> 0% of each run, Pallas kernels for 26% -> 26%
where the time goes in v5:
time: 112 us; the launch traced here: 111 us
  starting transfers between devices  43.1 us (38%)
  Pallas kernels  39 us (35%)
  waiting for transfers between devices  28.9 us (26%)
    pallas_call x28, Pallas kernels, call(): pl.pallas_call(functools.partial(after_waits, len(waits), functools.parti...  39 us
    ppermute x9, starting transfers between devices, exchanged(): result[step] = lax.ppermute(pieces[step], 'expert', pairs)  13.1 us
    ppermute x6, starting transfers between devices, across(): lax.ppermute(value, 'expert', [(i, i ^ step) for i in range(z.peers)])  11.9 us
    ppermute x16, waiting for transfers between devices, swap(): return lax.ppermute(value, 'hidden', pairs)  7.95 us
    ppermute x9, waiting for transfers between devices, exchanged(): result[step] = lax.ppermute(pieces[step], 'expert', pairs)  7.16 us
    ppermute x16, starting transfers between devices, swap(): return lax.ppermute(value, 'hidden', pairs)  6.89 us
    ppermute x1, waiting for transfers between devices, relayed(): rows = lax.ppermute(kept, 'section', hop)  6.07 us
    ppermute x1, starting transfers between devices, within(): return lax.ppermute(value, ('section', 'expert'), pairs)  4.81 us
  transfers between devices with their start and end apart: 36, of which 23 were waited for; matrix products, arithmetic and copies ran while one was open for 0% of the time, Pallas kernels for 26%

profile of v5, /device:TPU:2, one launch (start us, length us, event | category | flops | bytes accessed | tf_op | source)
XLA Modules:
  0.0 111.3 jit_solution(17838979810910932816)
XLA Ops:
  0.0 1.6 %shard_map.55 = (bf16[48,1792]{1,0:T(8,128)(2,1)S(1)}, bf16[48,1792]{1,0:T(8,128)(2,1)S(1)}, bf16[48,1792]{1,0:T(8,128)(2,1)S(1)}, bf16[48,1792]{1,0:T(8,128)(2,1)S(1)}, bf16[192,64]{1,0:T(8,128)(2,1)S(1)}) custom-call(s32[4,2,16]{2,1,0:T(2,128)} %bitcast.11, bf16[4,2,16]{2,1,0:T(2,128)(2,1)} %bitcast.14, bf16[64,1792]{1,0:T(8,128)(2,1)} %bitcast.8), custom_call_target="tpu_custom_call" | custom-call | tf_op jit(solution)/shard_map/pallas_call | solution.py:329
  1.6 2.7 %collective-permute-start = (bf16[48,1792]{1,0:T(8,128)(2,1)S(1)}, bf16[48,1792]{1,0:T(8,128)(2,1)S(1)}, u32[]{:S(2)}, u32[]{:S(2)}) collective-permute-start(bf16[48,1792]{1,0:T(8,128)(2,1)S(1)} %get-tuple-element.56), channel_id=1, source_target_pairs={{0,8},{4,12},{8,0},{12,4},{1,9},{5,13},{9,1},{13,5},{2,10},{6,14},... | collective-permute-start | bytes 516104 | tf_op jit(solution)/shard_map/ppermute | solution.py:361
  4.3 1.3 %collective-permute-start.1 = (bf16[48,1792]{1,0:T(8,128)(2,1)S(1)}, bf16[48,1792]{1,0:T(8,128)(2,1)S(1)}, u32[]{:S(2)}, u32[]{:S(2)}) collective-permute-start(bf16[48,1792]{1,0:T(8,128)(2,1)S(1)} %get-tuple-element.57), channel_id=1, source_target_pairs={{0,12},{4,8},{8,4},{12,0},{1,13},{5,9},{9,5},{13,1},{2,14},{6,10},... | collective-permute-start | bytes 516104 | tf_op jit(solution)/shard_map/ppermute | solution.py:361
  5.9 9.6 %shard_map.56 = (bf16[3584,1024]{1,0:T(8,128)(2,1)S(1)}, bf16[3584,1024]{1,0:T(8,128)(2,1)S(1)}, bf16[3584,1024]{1,0:T(8,128)(2,1)S(1)}, bf16[3584,1024]{1,0:T(8,128)(2,1)S(1)}) custom-call(bf16[192,64]{1,0:T(8,128)(2,1)S(1)} %get-tuple-element.50.refs_0_, bf16[1,1792,2,4096]{3,2,1,0:T(2,128)(2,1)} %refs_1_.2), custom_call_target="tpu_custom_call" | custom-call | tf_op jit(solution)/shard_map/pallas_call | solution.py:329
  15.5 5.3 %shard_map.57 = (bf16[1024,1792]{1,0:T(8,128)(2,1)S(1)}, bf16[1024,1792]{1,0:T(8,128)(2,1)S(1)}, bf16[1024,1792]{1,0:T(8,128)(2,1)S(1)}, bf16[1024,1792]{1,0:T(8,128)(2,1)S(1)}) custom-call(bf16[3584,1024]{1,0:T(8,128)(2,1)S(1)} %get-tuple-element.51.refs_0_.refs_2_, bf16[1,4096,1792]{2,1,0:T(8,128)(2,1)} %refs_1_.3), custom_call_target="tpu_custom_call" | custom-call | tf_op jit(solution)/shard_map/pallas_call | solution.py:329
  20.8 3.2 %shard_map.58 = (f32[112,1024]{1,0:T(8,128)S(1)}, bf16[56,1024]{1,0:T(8,128)(2,1)S(1)}, bf16[56,1024]{1,0:T(8,128)(2,1)S(1)}) custom-call(bf16[1024,1792]{1,0:T(8,128)(2,1)S(1)} %get-tuple-element.52.refs_0_, bf16[3584,1024]{1,0:T(8,128)(2,1)S(1)} %get-tuple-element.54.refs_1_, bf16[3584,1024]{1,0:T(8,128)(2,1)S(1)} %get-tuple-element.55.refs_2_, ...), custom_call_target="tpu_custom_call" | custom-call | tf_op jit(solution)/shard_map/pallas_call | solution.py:329
  25.6 1.6 %collective-permute-start.5 = (bf16[112,1024]{1,0:T(8,128)(2,1)S(1)}, bf16[112,1024]{1,0:T(8,128)(2,1)S(1)}, u32[]{:S(2)}, u32[]{:S(2)}) collective-permute-start(bf16[112,1024]{1,0:T(8,128)(2,1)S(1)} %shard_map.59.refs_0_), channel_id=1, source_target_pairs={{0,2},{1,3},{2,0},{3,1},{4,6},{5,7},{6,4},{7,5},{8,10},{9,11},{10,... | collective-permute-start | bytes 688136 | tf_op jit(solution)/shard_map/ppermute | solution.py:353
  27.2 3.2 %shard_map.64 = (f32[112,1024]{1,0:T(8,128)S(1)}, bf16[56,1024]{1,0:T(8,128)(2,1)S(1)}, bf16[56,1024]{1,0:T(8,128)(2,1)S(1)}) custom-call(bf16[112,1024]{1,0:T(8,128)(2,1)S(1)} %shard_map.59.refs_0_, bf16[3584,1024]{1,0:T(8,128)(2,1)S(1)} %get-tuple-element.68.refs_1_, bf16[3584,1024]{1,0:T(8,128)(2,1)S(1)} %get-tuple-element.51.refs_0_.refs_2_, ...), custom_call_target="tpu_custom_call" | custom-call | tf_op jit(solution)/shard_map/pallas_call | solution.py:329
  36.0 2.9 %collective-permute-start.8 = (bf16[48,1792]{1,0:T(8,128)(2,1)S(1)}, bf16[48,1792]{1,0:T(8,128)(2,1)S(1)}, u32[]{:S(2)}, u32[]{:S(2)}) collective-permute-start(bf16[48,1792]{1,0:T(8,128)(2,1)S(1)} %get-tuple-element.65), channel_id=1, source_target_pairs={{0,8},{4,12},{8,0},{12,4},{1,9},{5,13},{9,1},{13,5},{2,10},{6,14},... | collective-permute-start | bytes 516104 | tf_op jit(solution)/shard_map/ppermute | solution.py:365
  40.2 1.9 %collective-permute-start.7 = (bf16[24,1792]{1,0:T(8,128)(2,1)S(1)}, bf16[24,1792]{1,0:T(8,128)(2,1)S(1)}, u32[]{:S(2)}, u32[]{:S(2)}) collective-permute-start(bf16[24,1792]{1,0:T(8,128)(2,1)S(1)} %get-tuple-element.64), channel_id=1, source_target_pairs={{0,4},{4,0},{8,12},{12,8},{1,5},{5,1},{9,13},{13,9},{2,6},{6,2},{1... | collective-permute-start | bytes 258056 | tf_op jit(solution)/shard_map/ppermute | solution.py:365
  44.3 2.6 %collective-permute-start.15 = (bf16[24,1792]{1,0:T(8,128)(2,1)S(1)}, bf16[24,1792]{1,0:T(8,128)(2,1)S(1)}, u32[]{:S(2)}, u32[]{:S(2)}) collective-permute-start(bf16[24,1792]{1,0:T(8,128)(2,1)S(1)} %get-tuple-element.74), channel_id=1, source_target_pairs={{0,8},{4,12},{8,0},{12,4},{1,9},{5,13},{9,1},{13,5},{2,10},{6,14},... | collective-permute-start | bytes 258056 | tf_op jit(solution)/shard_map/ppermute | solution.py:361
  46.9 1.3 %collective-permute-start.16 = (bf16[24,1792]{1,0:T(8,128)(2,1)S(1)}, bf16[24,1792]{1,0:T(8,128)(2,1)S(1)}, u32[]{:S(2)}, u32[]{:S(2)}) collective-permute-start(bf16[24,1792]{1,0:T(8,128)(2,1)S(1)} %get-tuple-element.75), channel_id=1, source_target_pairs={{0,12},{4,8},{8,4},{12,0},{1,13},{5,9},{9,5},{13,1},{2,14},{6,10},... | collective-permute-start | bytes 258056 | tf_op jit(solution)/shard_map/ppermute | solution.py:361
  49.1 2.4 %collective-permute-start.17 = (s32[4,2,16]{2,1,0:T(2,128)S(1)}, s32[4,2,16]{2,1,0:T(2,128)S(1)}, u32[]{:S(2)}, u32[]{:S(2)}) collective-permute-start(s32[4,2,16]{2,1,0:T(2,128)S(1)} %get-tuple-element.76), channel_id=1, source_target_pairs={{16,0},{17,1},{18,2},{19,3},{20,4},{21,5},{22,6},{23,7},{24,8},{25... | collective-permute-start | bytes 1544 | tf_op jit(solution)/shard_map/ppermute | solution.py:482
  59.7 6.1 %collective-permute-done.18.refs_1_ = bf16[64,1792]{1,0:T(8,128)(2,1)S(1)} collective-permute-done((bf16[64,1792]{1,0:T(8,128)(2,1)S(1)}, bf16[64,1792]{1,0:T(8,128)(2,1)S(1)}, u32[]{:S(2)}, u32[]{:S(2)}) %collective-permute-start.18) | collective-permute-done | bytes 229408 | tf_op jit(solution)/shard_map/ppermute | solution.py:382
  66.3 4.8 %collective-permute-start.21 = (bf16[48,1792]{1,0:T(8,128)(2,1)S(1)}, bf16[48,1792]{1,0:T(8,128)(2,1)S(1)}, u32[]{:S(2)}, u32[]{:S(2)}) collective-permute-start(bf16[48,1792]{1,0:T(8,128)(2,1)S(1)} %get-tuple-element.80), channel_id=1, source_target_pairs={{16,20},{20,16},{24,28},{28,24},{17,21},{21,17},{25,29},{29,25},{1... | collective-permute-start | bytes 516104 | tf_op jit(solution)/shard_map/ppermute | solution.py:378
  71.1 4.0 %collective-permute-done.19.refs_3_ = bf16[48,1792]{1,0:T(8,128)(2,1)S(1)} collective-permute-done((bf16[48,1792]{1,0:T(8,128)(2,1)S(1)}, bf16[48,1792]{1,0:T(8,128)(2,1)S(1)}, u32[]{:S(2)}, u32[]{:S(2)}) %collective-permute-start.19) | collective-permute-done | bytes 172064 | tf_op jit(solution)/shard_map/ppermute | solution.py:389
  75.0 3.2 %shard_map.71 = (f32[112,1024]{1,0:T(8,128)S(1)}, bf16[56,1024]{1,0:T(8,128)(2,1)S(1)}, bf16[56,1024]{1,0:T(8,128)(2,1)S(1)}) custom-call(bf16[1024,1792]{1,0:T(8,128)(2,1)S(1)} %get-tuple-element.52.refs_0_, bf16[3584,1024]{1,0:T(8,128)(2,1)S(1)} %get-tuple-element.54.refs_1_, bf16[3584,1024]{1,0:T(8,128)(2,1)S(1)} %get-tuple-element.55.refs_2_, ...), custom_call_target="tpu_custom_call" | custom-call | tf_op jit(solution)/shard_map/pallas_call | solution.py:329
  80.8 3.2 %shard_map.77 = (f32[112,1024]{1,0:T(8,128)S(1)}, bf16[56,1024]{1,0:T(8,128)(2,1)S(1)}, bf16[56,1024]{1,0:T(8,128)(2,1)S(1)}) custom-call(bf16[112,1024]{1,0:T(8,128)(2,1)S(1)} %shard_map.72.refs_0_, bf16[3584,1024]{1,0:T(8,128)(2,1)S(1)} %get-tuple-element.68.refs_1_, bf16[3584,1024]{1,0:T(8,128)(2,1)S(1)} %get-tuple-element.51.refs_0_.refs_2_, ...), custom_call_target="tpu_custom_call" | custom-call | tf_op jit(solution)/shard_map/pallas_call | solution.py:329
  90.2 4.1 %collective-permute-start.27 = (bf16[48,1792]{1,0:T(8,128)(2,1)S(1)}, bf16[48,1792]{1,0:T(8,128)(2,1)S(1)}, u32[]{:S(2)}, u32[]{:S(2)}) collective-permute-start(bf16[48,1792]{1,0:T(8,128)(2,1)S(1)} %get-tuple-element.87), channel_id=1, source_target_pairs={{0,8},{4,12},{8,0},{12,4},{1,9},{5,13},{9,1},{13,5},{2,10},{6,14},... | collective-permute-start | bytes 516104 | tf_op jit(solution)/shard_map/ppermute | solution.py:365
  94.6 2.9 %collective-permute-start.26 = (bf16[24,1792]{1,0:T(8,128)(2,1)S(1)}, bf16[24,1792]{1,0:T(8,128)(2,1)S(1)}, u32[]{:S(2)}, u32[]{:S(2)}) collective-permute-start(bf16[24,1792]{1,0:T(8,128)(2,1)S(1)} %get-tuple-element.86), channel_id=1, source_target_pairs={{0,4},{4,0},{8,12},{12,8},{1,5},{5,1},{9,13},{13,9},{2,6},{6,2},{1... | collective-permute-start | bytes 258056 | tf_op jit(solution)/shard_map/ppermute | solution.py:365
  99.8 2.6 %collective-permute-start.34 = (bf16[24,1792]{1,0:T(8,128)(2,1)S(1)}, bf16[24,1792]{1,0:T(8,128)(2,1)S(1)}, u32[]{:S(2)}, u32[]{:S(2)}) collective-permute-start(bf16[24,1792]{1,0:T(8,128)(2,1)S(1)} %get-tuple-element.93), channel_id=1, source_target_pairs={{0,8},{4,12},{8,0},{12,4},{1,9},{5,13},{9,1},{13,5},{2,10},{6,14},... | collective-permute-start | bytes 258056 | tf_op jit(solution)/shard_map/ppermute | solution.py:361
  102.3 1.3 %collective-permute-start.35 = (bf16[24,1792]{1,0:T(8,128)(2,1)S(1)}, bf16[24,1792]{1,0:T(8,128)(2,1)S(1)}, u32[]{:S(2)}, u32[]{:S(2)}) collective-permute-start(bf16[24,1792]{1,0:T(8,128)(2,1)S(1)} %get-tuple-element.94), channel_id=1, source_target_pairs={{0,12},{4,8},{8,4},{12,0},{1,13},{5,9},{9,5},{13,1},{2,14},{6,10},... | collective-permute-start | bytes 258056 | tf_op jit(solution)/shard_map/ppermute | solution.py:361
  103.8 2.4 %collective-permute-done.33.refs_8_ = bf16[24,1792]{1,0:T(8,128)(2,1)S(1)} collective-permute-done((bf16[24,1792]{1,0:T(8,128)(2,1)S(1)}, bf16[24,1792]{1,0:T(8,128)(2,1)S(1)}, u32[]{:S(2)}, u32[]{:S(2)}) %collective-permute-start.33) | collective-permute-done | bytes 86048 | tf_op jit(solution)/shard_map/ppermute | solution.py:361
  106.2 3.4 %collective-permute-done.34.refs_9_ = bf16[24,1792]{1,0:T(8,128)(2,1)S(1)} collective-permute-done((bf16[24,1792]{1,0:T(8,128)(2,1)S(1)}, bf16[24,1792]{1,0:T(8,128)(2,1)S(1)}, u32[]{:S(2)}, u32[]{:S(2)}) %collective-permute-start.34) | collective-permute-done | bytes 86048 | tf_op jit(solution)/shard_map/ppermute | solution.py:361
  (80 shorter events, 33.4 us)
Async XLA Ops:
  1.6 19.2 %collective-permute-start = (bf16[48,1792]{1,0:T(8,128)(2,1)S(1)}, bf16[48,1792]{1,0:T(8,128)(2,1)S(1)}, u32[]{:S(2)}, u32[]{:S(2)}) collective-permute-start(bf16[48,1792]{1,0:T(8,128)(2,1)S(1)} %get-tuple-element.56), channel_id=1, source_target_pairs={{0,8},{4,12},{8,0},{12,4},{1,9},{5,13},{9,1},{13,5},{2,10},{6,14},... | collective-permute-start | bytes 516104 | tf_op jit(solution)/shard_map/ppermute | solution.py:361
  4.3 16.5 %collective-permute-start.1 = (bf16[48,1792]{1,0:T(8,128)(2,1)S(1)}, bf16[48,1792]{1,0:T(8,128)(2,1)S(1)}, u32[]{:S(2)}, u32[]{:S(2)}) collective-permute-start(bf16[48,1792]{1,0:T(8,128)(2,1)S(1)} %get-tuple-element.57), channel_id=1, source_target_pairs={{0,12},{4,8},{8,4},{12,0},{1,13},{5,9},{9,5},{13,1},{2,14},{6,10},... | collective-permute-start | bytes 516104 | tf_op jit(solution)/shard_map/ppermute | solution.py:361
  5.6 15.2 %collective-permute-start.2 = (bf16[48,1792]{1,0:T(8,128)(2,1)S(1)}, bf16[48,1792]{1,0:T(8,128)(2,1)S(1)}, u32[]{:S(2)}, u32[]{:S(2)}) collective-permute-start(bf16[48,1792]{1,0:T(8,128)(2,1)S(1)} %get-tuple-element.58), channel_id=1, source_target_pairs={{0,4},{4,0},{8,12},{12,8},{1,5},{5,1},{9,13},{13,9},{2,6},{6,2},{1... | collective-permute-start | bytes 516104 | tf_op jit(solution)/shard_map/ppermute | solution.py:361
  25.6 7.9 %collective-permute-start.5 = (bf16[112,1024]{1,0:T(8,128)(2,1)S(1)}, bf16[112,1024]{1,0:T(8,128)(2,1)S(1)}, u32[]{:S(2)}, u32[]{:S(2)}) collective-permute-start(bf16[112,1024]{1,0:T(8,128)(2,1)S(1)} %shard_map.59.refs_0_), channel_id=1, source_target_pairs={{0,2},{1,3},{2,0},{3,1},{4,6},{5,7},{6,4},{7,5},{8,10},{9,11},{10,... | collective-permute-start | bytes 688136 | tf_op jit(solution)/shard_map/ppermute | solution.py:353
  32.0 7.9 %collective-permute-start.12 = (bf16[112,1024]{1,0:T(8,128)(2,1)S(1)}, bf16[112,1024]{1,0:T(8,128)(2,1)S(1)}, u32[]{:S(2)}, u32[]{:S(2)}) collective-permute-start(bf16[112,1024]{1,0:T(8,128)(2,1)S(1)} %shard_map.65.refs_1_), channel_id=1, source_target_pairs={{0,2},{1,3},{2,0},{3,1},{4,6},{5,7},{6,4},{7,5},{8,10},{9,11},{10,... | collective-permute-start | bytes 688136 | tf_op jit(solution)/shard_map/ppermute | solution.py:353
  36.0 12.2 %collective-permute-start.8 = (bf16[48,1792]{1,0:T(8,128)(2,1)S(1)}, bf16[48,1792]{1,0:T(8,128)(2,1)S(1)}, u32[]{:S(2)}, u32[]{:S(2)}) collective-permute-start(bf16[48,1792]{1,0:T(8,128)(2,1)S(1)} %get-tuple-element.65), channel_id=1, source_target_pairs={{0,8},{4,12},{8,0},{12,4},{1,9},{5,13},{9,1},{13,5},{2,10},{6,14},... | collective-permute-start | bytes 516104 | tf_op jit(solution)/shard_map/ppermute | solution.py:365
  40.2 8.9 %collective-permute-start.7 = (bf16[24,1792]{1,0:T(8,128)(2,1)S(1)}, bf16[24,1792]{1,0:T(8,128)(2,1)S(1)}, u32[]{:S(2)}, u32[]{:S(2)}) collective-permute-start(bf16[24,1792]{1,0:T(8,128)(2,1)S(1)} %get-tuple-element.64), channel_id=1, source_target_pairs={{0,4},{4,0},{8,12},{12,8},{1,5},{5,1},{9,13},{13,9},{2,6},{6,2},{1... | collective-permute-start | bytes 258056 | tf_op jit(solution)/shard_map/ppermute | solution.py:365
  43.8 9.0 %collective-permute-start.14 = (bf16[24,1792]{1,0:T(8,128)(2,1)S(1)}, bf16[24,1792]{1,0:T(8,128)(2,1)S(1)}, u32[]{:S(2)}, u32[]{:S(2)}) collective-permute-start(bf16[24,1792]{1,0:T(8,128)(2,1)S(1)} %get-tuple-element.73), channel_id=1, source_target_pairs={{0,4},{4,0},{8,12},{12,8},{1,5},{5,1},{9,13},{13,9},{2,6},{6,2},{1... | collective-permute-start | bytes 258056 | tf_op jit(solution)/shard_map/ppermute | solution.py:361
  44.3 9.7 %collective-permute-start.15 = (bf16[24,1792]{1,0:T(8,128)(2,1)S(1)}, bf16[24,1792]{1,0:T(8,128)(2,1)S(1)}, u32[]{:S(2)}, u32[]{:S(2)}) collective-permute-start(bf16[24,1792]{1,0:T(8,128)(2,1)S(1)} %get-tuple-element.74), channel_id=1, source_target_pairs={{0,8},{4,12},{8,0},{12,4},{1,9},{5,13},{9,1},{13,5},{2,10},{6,14},... | collective-permute-start | bytes 258056 | tf_op jit(solution)/shard_map/ppermute | solution.py:361
  46.9 7.3 %collective-permute-start.16 = (bf16[24,1792]{1,0:T(8,128)(2,1)S(1)}, bf16[24,1792]{1,0:T(8,128)(2,1)S(1)}, u32[]{:S(2)}, u32[]{:S(2)}) collective-permute-start(bf16[24,1792]{1,0:T(8,128)(2,1)S(1)} %get-tuple-element.75), channel_id=1, source_target_pairs={{0,12},{4,8},{8,4},{12,0},{1,13},{5,9},{9,5},{13,1},{2,14},{6,10},... | collective-permute-start | bytes 258056 | tf_op jit(solution)/shard_map/ppermute | solution.py:361
  48.2 6.8 %collective-permute-start.9 = (bf16[24,1792]{1,0:T(8,128)(2,1)S(1)}, bf16[24,1792]{1,0:T(8,128)(2,1)S(1)}, u32[]{:S(2)}, u32[]{:S(2)}) collective-permute-start(bf16[24,1792]{1,0:T(8,128)(2,1)S(1)} %shard_map.63), channel_id=1, source_target_pairs={{0,4},{4,0},{8,12},{12,8},{1,5},{5,1},{9,13},{13,9},{2,6},{6,2},{1... | collective-permute-start | bytes 258056 | tf_op jit(solution)/shard_map/ppermute | solution.py:365
  55.8 10.0 %collective-permute-start.18 = (bf16[64,1792]{1,0:T(8,128)(2,1)S(1)}, bf16[64,1792]{1,0:T(8,128)(2,1)S(1)}, u32[]{:S(2)}, u32[]{:S(2)}) collective-permute-start(bf16[64,1792]{1,0:T(8,128)(2,1)S(1)} %get-tuple-element.77.refs_2_), channel_id=1, source_target_pairs={{0,16},{1,17},{2,18},{3,19},{4,20},{5,21},{6,22},{7,23},{8,24},{9,... | collective-permute-start | bytes 688136 | tf_op jit(solution)/shard_map/ppermute | solution.py:382
  57.1 18.0 %collective-permute-start.19 = (bf16[48,1792]{1,0:T(8,128)(2,1)S(1)}, bf16[48,1792]{1,0:T(8,128)(2,1)S(1)}, u32[]{:S(2)}, u32[]{:S(2)}) collective-permute-start(bf16[48,1792]{1,0:T(8,128)(2,1)S(1)} %get-tuple-element.78), channel_id=1, source_target_pairs={{0,24},{4,28},{8,16},{12,20},{1,25},{5,29},{9,17},{13,21},{2,26},{... | collective-permute-start | bytes 516104 | tf_op jit(solution)/shard_map/ppermute | solution.py:389
  58.4 16.7 %collective-permute-start.20 = (bf16[48,1792]{1,0:T(8,128)(2,1)S(1)}, bf16[48,1792]{1,0:T(8,128)(2,1)S(1)}, u32[]{:S(2)}, u32[]{:S(2)}) collective-permute-start(bf16[48,1792]{1,0:T(8,128)(2,1)S(1)} %get-tuple-element.79), channel_id=1, source_target_pairs={{0,28},{4,24},{8,20},{12,16},{1,29},{5,25},{9,21},{13,17},{2,30},{... | collective-permute-start | bytes 516104 | tf_op jit(solution)/shard_map/ppermute | solution.py:389
  66.3 8.8 %collective-permute-start.21 = (bf16[48,1792]{1,0:T(8,128)(2,1)S(1)}, bf16[48,1792]{1,0:T(8,128)(2,1)S(1)}, u32[]{:S(2)}, u32[]{:S(2)}) collective-permute-start(bf16[48,1792]{1,0:T(8,128)(2,1)S(1)} %get-tuple-element.80), channel_id=1, source_target_pairs={{16,20},{20,16},{24,28},{28,24},{17,21},{21,17},{25,29},{29,25},{1... | collective-permute-start | bytes 516104 | tf_op jit(solution)/shard_map/ppermute | solution.py:378
  79.8 7.9 %collective-permute-start.24 = (bf16[112,1024]{1,0:T(8,128)(2,1)S(1)}, bf16[112,1024]{1,0:T(8,128)(2,1)S(1)}, u32[]{:S(2)}, u32[]{:S(2)}) collective-permute-start(bf16[112,1024]{1,0:T(8,128)(2,1)S(1)} %shard_map.72.refs_0_), channel_id=1, source_target_pairs={{0,2},{1,3},{2,0},{3,1},{4,6},{5,7},{6,4},{7,5},{8,10},{9,11},{10,... | collective-permute-start | bytes 688136 | tf_op jit(solution)/shard_map/ppermute | solution.py:353
  85.6 8.7 %collective-permute-start.31 = (bf16[112,1024]{1,0:T(8,128)(2,1)S(1)}, bf16[112,1024]{1,0:T(8,128)(2,1)S(1)}, u32[]{:S(2)}, u32[]{:S(2)}) collective-permute-start(bf16[112,1024]{1,0:T(8,128)(2,1)S(1)} %shard_map.78.refs_1_), channel_id=1, source_target_pairs={{0,2},{1,3},{2,0},{3,1},{4,6},{5,7},{6,4},{7,5},{8,10},{9,11},{10,... | collective-permute-start | bytes 688136 | tf_op jit(solution)/shard_map/ppermute | solution.py:353
  90.2 13.5 %collective-permute-start.27 = (bf16[48,1792]{1,0:T(8,128)(2,1)S(1)}, bf16[48,1792]{1,0:T(8,128)(2,1)S(1)}, u32[]{:S(2)}, u32[]{:S(2)}) collective-permute-start(bf16[48,1792]{1,0:T(8,128)(2,1)S(1)} %get-tuple-element.87), channel_id=1, source_target_pairs={{0,8},{4,12},{8,0},{12,4},{1,9},{5,13},{9,1},{13,5},{2,10},{6,14},... | collective-permute-start | bytes 516104 | tf_op jit(solution)/shard_map/ppermute | solution.py:365
  94.5 3.8 %collective-permute-start.32 = (bf16[96,512]{1,0:T(8,128)(2,1)S(1)}, bf16[96,512]{1,0:T(8,128)(2,1)S(1)}, u32[]{:S(2)}, u32[]{:S(2)}) collective-permute-start(bf16[96,512]{1,0:T(8,128)(2,1)S(1)} %shard_map.79.refs_2_), channel_id=1, source_target_pairs={{0,1},{1,0},{2,3},{3,2},{4,5},{5,4},{6,7},{7,6},{8,9},{9,8},{10,11... | collective-permute-start | bytes 294920 | tf_op jit(solution)/shard_map/ppermute | solution.py:353
  94.6 9.2 %collective-permute-start.26 = (bf16[24,1792]{1,0:T(8,128)(2,1)S(1)}, bf16[24,1792]{1,0:T(8,128)(2,1)S(1)}, u32[]{:S(2)}, u32[]{:S(2)}) collective-permute-start(bf16[24,1792]{1,0:T(8,128)(2,1)S(1)} %get-tuple-element.86), channel_id=1, source_target_pairs={{0,4},{4,0},{8,12},{12,8},{1,5},{5,1},{9,13},{13,9},{2,6},{6,2},{1... | collective-permute-start | bytes 258056 | tf_op jit(solution)/shard_map/ppermute | solution.py:365
  99.2 7.0 %collective-permute-start.33 = (bf16[24,1792]{1,0:T(8,128)(2,1)S(1)}, bf16[24,1792]{1,0:T(8,128)(2,1)S(1)}, u32[]{:S(2)}, u32[]{:S(2)}) collective-permute-start(bf16[24,1792]{1,0:T(8,128)(2,1)S(1)} %get-tuple-element.92), channel_id=1, source_target_pairs={{0,4},{4,0},{8,12},{12,8},{1,5},{5,1},{9,13},{13,9},{2,6},{6,2},{1... | collective-permute-start | bytes 258056 | tf_op jit(solution)/shard_map/ppermute | solution.py:361
  99.8 9.9 %collective-permute-start.34 = (bf16[24,1792]{1,0:T(8,128)(2,1)S(1)}, bf16[24,1792]{1,0:T(8,128)(2,1)S(1)}, u32[]{:S(2)}, u32[]{:S(2)}) collective-permute-start(bf16[24,1792]{1,0:T(8,128)(2,1)S(1)} %get-tuple-element.93), channel_id=1, source_target_pairs={{0,8},{4,12},{8,0},{12,4},{1,9},{5,13},{9,1},{13,5},{2,10},{6,14},... | collective-permute-start | bytes 258056 | tf_op jit(solution)/shard_map/ppermute | solution.py:361
  102.3 7.3 %collective-permute-start.35 = (bf16[24,1792]{1,0:T(8,128)(2,1)S(1)}, bf16[24,1792]{1,0:T(8,128)(2,1)S(1)}, u32[]{:S(2)}, u32[]{:S(2)}) collective-permute-start(bf16[24,1792]{1,0:T(8,128)(2,1)S(1)} %get-tuple-element.94), channel_id=1, source_target_pairs={{0,12},{4,8},{8,4},{12,0},{1,13},{5,9},{9,5},{13,1},{2,14},{6,10},... | collective-permute-start | bytes 258056 | tf_op jit(solution)/shard_map/ppermute | solution.py:361
  103.7 6.6 %collective-permute-start.28 = (bf16[24,1792]{1,0:T(8,128)(2,1)S(1)}, bf16[24,1792]{1,0:T(8,128)(2,1)S(1)}, u32[]{:S(2)}, u32[]{:S(2)}) collective-permute-start(bf16[24,1792]{1,0:T(8,128)(2,1)S(1)} %shard_map.76), channel_id=1, source_target_pairs={{0,4},{4,0},{8,12},{12,8},{1,5},{5,1},{9,13},{13,9},{2,6},{6,2},{1... | collective-permute-start | bytes 258056 | tf_op jit(solution)/shard_map/ppermute | solution.py:365
  (14 other events, 41.8 us)

commit v6 on v5

--- a/solution.py
+++ b/solution.py
@@ -143,12 +143,13 @@
     ]
     for copy in copies:
         copy.start()
-    for copy in copies:
-        copy.wait()
+    copies[0].wait()
     hits, first, second = slot_hits(z, routes_ref)
+    copies[1].wait()
     gates = line_up(z, gates_ref)
     weight = jnp.where(first, gates[0:1, :], F32(0.0)) + jnp.where(second, gates[1:2, :], F32(0.0))
     outs[-1][...] = (hits * weight).astype(BF16)
+    copies[2].wait()
     send_rows(z, hits, rows_ref[...], outs[:-1], range(z.pieces))
 
 
@@ -173,14 +174,12 @@
         copy.wait()
 
 
-def load_down_kernel(z, down_proj, *refs):
+def load_down_kernel(z, group, down_proj, *refs):
     outs, sems = refs[:-1], refs[-1]
-    copies = [
-        pltpu.make_async_copy(
-            down_proj.at[0, pl.ds(expert * z.units, z.units), :], outs[expert], sems.at[expert]
-        )
-        for expert in range(z.local)
-    ]
+    copies = []
+    for index in range(z.members):
+        rows = pl.ds((group * z.members + index) * z.units, z.units)
+        copies.append(pltpu.make_async_copy(down_proj.at[0, rows, :], outs[index], sems.at[index]))
     for copy in copies:
         copy.start()
     for copy in copies:
@@ -248,9 +247,8 @@
 def pair_kernel(z, own, *refs):
     *other, out = refs
     products, sums = joined(z, [own[...], jnp.concatenate([ref[...].astype(F32) for ref in other], axis=0)])
-    out[:z.group_each, :] = products.astype(BF16)
-    sums = jnp.broadcast_to(sums, (EXTRA, 2 * z.half))
-    out[z.group_each:, :] = split_sums(sums, 2 * z.half).astype(BF16)
+    sums = split_sums(jnp.broadcast_to(sums, (EXTRA, 2 * z.half)), 2 * z.half)
+    out[...] = jnp.concatenate([products, sums], axis=0).astype(BF16)
 
 
 def act_kernel(z, count, *refs):
@@ -457,12 +455,15 @@
         [pltpu.VMEM((2 * z.width, z.units), BF16)] * z.local,
         [HBM], [pltpu.SemaphoreType.DMA((z.local * parts,))], gate_up, waits=[weight],
     )
-    tall = call(
-        load_down_kernel, (z,), 1,
-        [pltpu.VMEM((z.units, z.width), BF16)] * z.local,
-        [HBM], [pltpu.SemaphoreType.DMA((z.local,))], down_proj, waits=wide[-1:],
-    )
-    tall = [tall[group * z.members:(group + 1) * z.members] for group in range(z.groups)]
+
+    def load_down(group, after):
+        return call(
+            load_down_kernel, (z, group), 1,
+            [pltpu.VMEM((z.units, z.width), BF16)] * z.members,
+            [HBM], [pltpu.SemaphoreType.DMA((z.members,))], down_proj, waits=[after],
+        )
+
+    tall = [load_down(0, wide[-1])]
     groups = range(z.groups)
     for tick in range(sections):
         last = tick == sections - 1
@@ -473,8 +474,10 @@
             if group == 0:
                 halves = activated(sums[0], [])
         for group in groups:
+            if group and tick == 0:
+                tall.append(load_down(group, outgoing[0]))
             if group:
-                halves = activated(sums[group], outgoing[:1])
+                halves = activated(sums[group], tall[group][:1] if tick == 0 else outgoing[:1])
             hand_on = [routes] if tick == 0 and group == z.groups - 1 else []
             outgoing = down(halves, group, hand_on)
             if hand_on:

time: 112 us -> 112 us (level)
    ppermute x6, starting transfers between devices: 11.9 us -> 9.97 us  [across(): lax.ppermute(value, 'expert', [(i, i ^ step) for i in range(z.peers)])]
    ppermute x2, waiting for transfers between devices: 3.97 us -> 2.54 us  [relayed(): lax.ppermute(pieces[step - z.near], ('section', 'expert'), pairs)]
    ppermute x1, starting transfers between devices: 4.81 us -> 6.24 us  [within(): return lax.ppermute(value, ('section', 'expert'), pairs)]
    pallas_call x28 -> x29, Pallas kernels: 39 us -> 40 us  [call(): pl.pallas_call(functools.partial(after_waits, len(waits), functools.parti...]
  transfers between devices with their start and end apart: 36 -> 36, of which waited for: 23 -> 23; matrix products, arithmetic and copies ran while one was open for 0% -> 0% of each run, Pallas kernels for 26% -> 27%
where the time goes in v6:
time: 112 us; the launch traced here: 111 us
  starting transfers between devices  42.5 us (38%)
  Pallas kernels  40 us (36%)
  waiting for transfers between devices  28.4 us (25%)
    pallas_call x29, Pallas kernels, call(): pl.pallas_call(functools.partial(after_waits, len(waits), functools.parti...  40 us
    ppermute x9, starting transfers between devices, exchanged(): result[step] = lax.ppermute(pieces[step], 'expert', pairs)  13.1 us
    ppermute x6, starting transfers between devices, across(): lax.ppermute(value, 'expert', [(i, i ^ step) for i in range(z.peers)])  9.97 us
    ppermute x16, waiting for transfers between devices, swap(): return lax.ppermute(value, 'hidden', pairs)  8.82 us
    ppermute x9, waiting for transfers between devices, exchanged(): result[step] = lax.ppermute(pieces[step], 'expert', pairs)  7.45 us
    ppermute x16, starting transfers between devices, swap(): return lax.ppermute(value, 'hidden', pairs)  6.88 us
    ppermute x1, starting transfers between devices, within(): return lax.ppermute(value, ('section', 'expert'), pairs)  6.24 us
    ppermute x1, waiting for transfers between devices, relayed(): rows = lax.ppermute(kept, 'section', hop)  5.91 us
  transfers between devices with their start and end apart: 36, of which 23 were waited for; matrix products, arithmetic and copies ran while one was open for 0% of the time, Pallas kernels for 27%

profile of v6, /device:TPU:2, one launch (start us, length us, event | category | flops | bytes accessed | tf_op | source)
XLA Modules:
  0.0 111.3 jit_solution(13662269870194974417)
XLA Ops:
  0.0 1.5 %shard_map.55 = (bf16[48,1792]{1,0:T(8,128)(2,1)S(1)}, bf16[48,1792]{1,0:T(8,128)(2,1)S(1)}, bf16[48,1792]{1,0:T(8,128)(2,1)S(1)}, bf16[48,1792]{1,0:T(8,128)(2,1)S(1)}, bf16[192,64]{1,0:T(8,128)(2,1)S(1)}) custom-call(s32[4,2,16]{2,1,0:T(2,128)} %bitcast.11, bf16[4,2,16]{2,1,0:T(2,128)(2,1)} %bitcast.14, bf16[64,1792]{1,0:T(8,128)(2,1)} %bitcast.8), custom_call_target="tpu_custom_call" | custom-call | tf_op jit(solution)/shard_map/pallas_call | solution.py:327
  1.5 2.6 %collective-permute-start = (bf16[48,1792]{1,0:T(8,128)(2,1)S(1)}, bf16[48,1792]{1,0:T(8,128)(2,1)S(1)}, u32[]{:S(2)}, u32[]{:S(2)}) collective-permute-start(bf16[48,1792]{1,0:T(8,128)(2,1)S(1)} %get-tuple-element.56), channel_id=1, source_target_pairs={{0,8},{4,12},{8,0},{12,4},{1,9},{5,13},{9,1},{13,5},{2,10},{6,14},... | collective-permute-start | bytes 516104 | tf_op jit(solution)/shard_map/ppermute | solution.py:359
  5.8 9.6 %shard_map.56 = (bf16[3584,1024]{1,0:T(8,128)(2,1)S(1)}, bf16[3584,1024]{1,0:T(8,128)(2,1)S(1)}, bf16[3584,1024]{1,0:T(8,128)(2,1)S(1)}, bf16[3584,1024]{1,0:T(8,128)(2,1)S(1)}) custom-call(bf16[192,64]{1,0:T(8,128)(2,1)S(1)} %get-tuple-element.50.refs_0_, bf16[1,1792,2,4096]{3,2,1,0:T(2,128)(2,1)} %refs_1_.3), custom_call_target="tpu_custom_call" | custom-call | tf_op jit(solution)/shard_map/pallas_call | solution.py:327
  15.4 3.2 %shard_map.57 = (bf16[1024,1792]{1,0:T(8,128)(2,1)S(1)}, bf16[1024,1792]{1,0:T(8,128)(2,1)S(1)}) custom-call(bf16[3584,1024]{1,0:T(8,128)(2,1)S(1)} %get-tuple-element.51.refs_0_.refs_2_, bf16[1,4096,1792]{2,1,0:T(8,128)(2,1)} %refs_1_.5), custom_call_target="tpu_custom_call" | custom-call | tf_op jit(solution)/shard_map/pallas_call | solution.py:327
  18.6 3.2 %shard_map.58 = (f32[112,1024]{1,0:T(8,128)S(1)}, bf16[56,1024]{1,0:T(8,128)(2,1)S(1)}, bf16[56,1024]{1,0:T(8,128)(2,1)S(1)}) custom-call(bf16[1024,1792]{1,0:T(8,128)(2,1)S(1)} %get-tuple-element.52.refs_0_, bf16[3584,1024]{1,0:T(8,128)(2,1)S(1)} %get-tuple-element.54.refs_1_, bf16[3584,1024]{1,0:T(8,128)(2,1)S(1)} %get-tuple-element.55.refs_2_, ...), custom_call_target="tpu_custom_call" | custom-call | tf_op jit(solution)/shard_map/pallas_call | solution.py:327
  23.4 1.6 %collective-permute-start.5 = (bf16[112,1024]{1,0:T(8,128)(2,1)S(1)}, bf16[112,1024]{1,0:T(8,128)(2,1)S(1)}, u32[]{:S(2)}, u32[]{:S(2)}) collective-permute-start(bf16[112,1024]{1,0:T(8,128)(2,1)S(1)} %shard_map.59.refs_0_), channel_id=1, source_target_pairs={{0,2},{1,3},{2,0},{3,1},{4,6},{5,7},{6,4},{7,5},{8,10},{9,11},{10,... | collective-permute-start | bytes 688136 | tf_op jit(solution)/shard_map/ppermute | solution.py:351
  25.0 3.2 %shard_map.65 = (f32[112,1024]{1,0:T(8,128)S(1)}, bf16[56,1024]{1,0:T(8,128)(2,1)S(1)}, bf16[56,1024]{1,0:T(8,128)(2,1)S(1)}) custom-call(bf16[112,1024]{1,0:T(8,128)(2,1)S(1)} %shard_map.59.refs_0_, bf16[3584,1024]{1,0:T(8,128)(2,1)S(1)} %get-tuple-element.68.refs_1_, bf16[3584,1024]{1,0:T(8,128)(2,1)S(1)} %get-tuple-element.51.refs_0_.refs_2_, ...), custom_call_target="tpu_custom_call" | custom-call | tf_op jit(solution)/shard_map/pallas_call | solution.py:327
  33.8 3.7 %collective-permute-start.8 = (bf16[48,1792]{1,0:T(8,128)(2,1)S(1)}, bf16[48,1792]{1,0:T(8,128)(2,1)S(1)}, u32[]{:S(2)}, u32[]{:S(2)}) collective-permute-start(bf16[48,1792]{1,0:T(8,128)(2,1)S(1)} %get-tuple-element.65), channel_id=1, source_target_pairs={{0,8},{4,12},{8,0},{12,4},{1,9},{5,13},{9,1},{13,5},{2,10},{6,14},... | collective-permute-start | bytes 516104 | tf_op jit(solution)/shard_map/ppermute | solution.py:363
  37.6 3.2 %shard_map.64 = (bf16[1024,1792]{1,0:T(8,128)(2,1)S(1)}, bf16[1024,1792]{1,0:T(8,128)(2,1)S(1)}) custom-call(bf16[24,1792]{1,0:T(8,128)(2,1)S(1)} %get-tuple-element.63.refs_0_.refs_3_, bf16[1,4096,1792]{2,1,0:T(8,128)(2,1)} %refs_1_.5), custom_call_target="tpu_custom_call" | custom-call | tf_op jit(solution)/shard_map/pallas_call | solution.py:327
  43.3 1.6 %collective-permute-start.14 = (bf16[24,1792]{1,0:T(8,128)(2,1)S(1)}, bf16[24,1792]{1,0:T(8,128)(2,1)S(1)}, u32[]{:S(2)}, u32[]{:S(2)}) collective-permute-start(bf16[24,1792]{1,0:T(8,128)(2,1)S(1)} %get-tuple-element.73), channel_id=1, source_target_pairs={{0,4},{4,0},{8,12},{12,8},{1,5},{5,1},{9,13},{13,9},{2,6},{6,2},{1... | collective-permute-start | bytes 258056 | tf_op jit(solution)/shard_map/ppermute | solution.py:359
  45.5 2.2 %collective-permute-start.16 = (bf16[24,1792]{1,0:T(8,128)(2,1)S(1)}, bf16[24,1792]{1,0:T(8,128)(2,1)S(1)}, u32[]{:S(2)}, u32[]{:S(2)}) collective-permute-start(bf16[24,1792]{1,0:T(8,128)(2,1)S(1)} %get-tuple-element.75), channel_id=1, source_target_pairs={{0,12},{4,8},{8,4},{12,0},{1,13},{5,9},{9,5},{13,1},{2,14},{6,10},... | collective-permute-start | bytes 258056 | tf_op jit(solution)/shard_map/ppermute | solution.py:359
  48.5 2.4 %collective-permute-start.17 = (s32[4,2,16]{2,1,0:T(2,128)S(1)}, s32[4,2,16]{2,1,0:T(2,128)S(1)}, u32[]{:S(2)}, u32[]{:S(2)}) collective-permute-start(s32[4,2,16]{2,1,0:T(2,128)S(1)} %get-tuple-element.76), channel_id=1, source_target_pairs={{16,0},{17,1},{18,2},{19,3},{20,4},{21,5},{22,6},{23,7},{24,8},{25... | collective-permute-start | bytes 1544 | tf_op jit(solution)/shard_map/ppermute | solution.py:485
  52.2 1.6 %collective-permute-done.15.refs_9_ = bf16[24,1792]{1,0:T(8,128)(2,1)S(1)} collective-permute-done((bf16[24,1792]{1,0:T(8,128)(2,1)S(1)}, bf16[24,1792]{1,0:T(8,128)(2,1)S(1)}, u32[]{:S(2)}, u32[]{:S(2)}) %collective-permute-start.15) | collective-permute-done | bytes 86048 | tf_op jit(solution)/shard_map/ppermute | solution.py:359
  59.8 5.9 %collective-permute-done.18.refs_1_ = bf16[64,1792]{1,0:T(8,128)(2,1)S(1)} collective-permute-done((bf16[64,1792]{1,0:T(8,128)(2,1)S(1)}, bf16[64,1792]{1,0:T(8,128)(2,1)S(1)}, u32[]{:S(2)}, u32[]{:S(2)}) %collective-permute-start.18) | collective-permute-done | bytes 229408 | tf_op jit(solution)/shard_map/ppermute | solution.py:380
  66.2 6.2 %collective-permute-start.21 = (bf16[48,1792]{1,0:T(8,128)(2,1)S(1)}, bf16[48,1792]{1,0:T(8,128)(2,1)S(1)}, u32[]{:S(2)}, u32[]{:S(2)}) collective-permute-start(bf16[48,1792]{1,0:T(8,128)(2,1)S(1)} %get-tuple-element.80), channel_id=1, source_target_pairs={{16,20},{20,16},{24,28},{28,24},{17,21},{21,17},{25,29},{29,25},{1... | collective-permute-start | bytes 516104 | tf_op jit(solution)/shard_map/ppermute | solution.py:376
  72.4 2.5 %collective-permute-done.19.refs_3_ = bf16[48,1792]{1,0:T(8,128)(2,1)S(1)} collective-permute-done((bf16[48,1792]{1,0:T(8,128)(2,1)S(1)}, bf16[48,1792]{1,0:T(8,128)(2,1)S(1)}, u32[]{:S(2)}, u32[]{:S(2)}) %collective-permute-start.19) | collective-permute-done | bytes 172064 | tf_op jit(solution)/shard_map/ppermute | solution.py:387
  75.6 3.2 %shard_map.72 = (f32[112,1024]{1,0:T(8,128)S(1)}, bf16[56,1024]{1,0:T(8,128)(2,1)S(1)}, bf16[56,1024]{1,0:T(8,128)(2,1)S(1)}) custom-call(bf16[1024,1792]{1,0:T(8,128)(2,1)S(1)} %get-tuple-element.52.refs_0_, bf16[3584,1024]{1,0:T(8,128)(2,1)S(1)} %get-tuple-element.54.refs_1_, bf16[3584,1024]{1,0:T(8,128)(2,1)S(1)} %get-tuple-element.55.refs_2_, ...), custom_call_target="tpu_custom_call" | custom-call | tf_op jit(solution)/shard_map/pallas_call | solution.py:327
  80.4 1.7 %collective-permute-start.24 = (bf16[112,1024]{1,0:T(8,128)(2,1)S(1)}, bf16[112,1024]{1,0:T(8,128)(2,1)S(1)}, u32[]{:S(2)}, u32[]{:S(2)}) collective-permute-start(bf16[112,1024]{1,0:T(8,128)(2,1)S(1)} %shard_map.73.refs_0_), channel_id=1, source_target_pairs={{0,2},{1,3},{2,0},{3,1},{4,6},{5,7},{6,4},{7,5},{8,10},{9,11},{10,... | collective-permute-start | bytes 688136 | tf_op jit(solution)/shard_map/ppermute | solution.py:351
  82.2 3.2 %shard_map.78 = (f32[112,1024]{1,0:T(8,128)S(1)}, bf16[56,1024]{1,0:T(8,128)(2,1)S(1)}, bf16[56,1024]{1,0:T(8,128)(2,1)S(1)}) custom-call(bf16[112,1024]{1,0:T(8,128)(2,1)S(1)} %shard_map.73.refs_0_, bf16[3584,1024]{1,0:T(8,128)(2,1)S(1)} %get-tuple-element.68.refs_1_, bf16[3584,1024]{1,0:T(8,128)(2,1)S(1)} %get-tuple-element.51.refs_0_.refs_2_, ...), custom_call_target="tpu_custom_call" | custom-call | tf_op jit(solution)/shard_map/pallas_call | solution.py:327
  90.8 2.6 %collective-permute-start.27 = (bf16[48,1792]{1,0:T(8,128)(2,1)S(1)}, bf16[48,1792]{1,0:T(8,128)(2,1)S(1)}, u32[]{:S(2)}, u32[]{:S(2)}) collective-permute-start(bf16[48,1792]{1,0:T(8,128)(2,1)S(1)} %get-tuple-element.87), channel_id=1, source_target_pairs={{0,8},{4,12},{8,0},{12,4},{1,9},{5,13},{9,1},{13,5},{2,10},{6,14},... | collective-permute-start | bytes 516104 | tf_op jit(solution)/shard_map/ppermute | solution.py:363
  93.4 1.4 %collective-permute-done.31.refs_2_ = bf16[112,1024]{1,0:T(8,128)(2,1)S(1)} collective-permute-done((bf16[112,1024]{1,0:T(8,128)(2,1)S(1)}, bf16[112,1024]{1,0:T(8,128)(2,1)S(1)}, u32[]{:S(2)}, u32[]{:S(2)}) %collective-permute-start.31) | collective-permute-done | bytes 229408 | tf_op jit(solution)/shard_map/ppermute | solution.py:351
  95.1 2.7 %collective-permute-start.26 = (bf16[24,1792]{1,0:T(8,128)(2,1)S(1)}, bf16[24,1792]{1,0:T(8,128)(2,1)S(1)}, u32[]{:S(2)}, u32[]{:S(2)}) collective-permute-start(bf16[24,1792]{1,0:T(8,128)(2,1)S(1)} %get-tuple-element.86), channel_id=1, source_target_pairs={{0,4},{4,0},{8,12},{12,8},{1,5},{5,1},{9,13},{13,9},{2,6},{6,2},{1... | collective-permute-start | bytes 258056 | tf_op jit(solution)/shard_map/ppermute | solution.py:363
  101.5 2.5 %collective-permute-start.35 = (bf16[24,1792]{1,0:T(8,128)(2,1)S(1)}, bf16[24,1792]{1,0:T(8,128)(2,1)S(1)}, u32[]{:S(2)}, u32[]{:S(2)}) collective-permute-start(bf16[24,1792]{1,0:T(8,128)(2,1)S(1)} %get-tuple-element.94), channel_id=1, source_target_pairs={{0,12},{4,8},{8,4},{12,0},{1,13},{5,9},{9,5},{13,1},{2,14},{6,10},... | collective-permute-start | bytes 258056 | tf_op jit(solution)/shard_map/ppermute | solution.py:359
  105.1 4.8 %collective-permute-done.34.refs_9_ = bf16[24,1792]{1,0:T(8,128)(2,1)S(1)} collective-permute-done((bf16[24,1792]{1,0:T(8,128)(2,1)S(1)}, bf16[24,1792]{1,0:T(8,128)(2,1)S(1)}, u32[]{:S(2)}, u32[]{:S(2)}) %collective-permute-start.34) | collective-permute-done | bytes 86048 | tf_op jit(solution)/shard_map/ppermute | solution.py:359
  (81 shorter events, 34.4 us)
Async XLA Ops:
  1.5 17.1 %collective-permute-start = (bf16[48,1792]{1,0:T(8,128)(2,1)S(1)}, bf16[48,1792]{1,0:T(8,128)(2,1)S(1)}, u32[]{:S(2)}, u32[]{:S(2)}) collective-permute-start(bf16[48,1792]{1,0:T(8,128)(2,1)S(1)} %get-tuple-element.56), channel_id=1, source_target_pairs={{0,8},{4,12},{8,0},{12,4},{1,9},{5,13},{9,1},{13,5},{2,10},{6,14},... | collective-permute-start | bytes 516104 | tf_op jit(solution)/shard_map/ppermute | solution.py:359
  4.2 14.4 %collective-permute-start.1 = (bf16[48,1792]{1,0:T(8,128)(2,1)S(1)}, bf16[48,1792]{1,0:T(8,128)(2,1)S(1)}, u32[]{:S(2)}, u32[]{:S(2)}) collective-permute-start(bf16[48,1792]{1,0:T(8,128)(2,1)S(1)} %get-tuple-element.57), channel_id=1, source_target_pairs={{0,12},{4,8},{8,4},{12,0},{1,13},{5,9},{9,5},{13,1},{2,14},{6,10},... | collective-permute-start | bytes 516104 | tf_op jit(solution)/shard_map/ppermute | solution.py:359
  5.5 13.1 %collective-permute-start.2 = (bf16[48,1792]{1,0:T(8,128)(2,1)S(1)}, bf16[48,1792]{1,0:T(8,128)(2,1)S(1)}, u32[]{:S(2)}, u32[]{:S(2)}) collective-permute-start(bf16[48,1792]{1,0:T(8,128)(2,1)S(1)} %get-tuple-element.58), channel_id=1, source_target_pairs={{0,4},{4,0},{8,12},{12,8},{1,5},{5,1},{9,13},{13,9},{2,6},{6,2},{1... | collective-permute-start | bytes 516104 | tf_op jit(solution)/shard_map/ppermute | solution.py:359
  23.4 7.9 %collective-permute-start.5 = (bf16[112,1024]{1,0:T(8,128)(2,1)S(1)}, bf16[112,1024]{1,0:T(8,128)(2,1)S(1)}, u32[]{:S(2)}, u32[]{:S(2)}) collective-permute-start(bf16[112,1024]{1,0:T(8,128)(2,1)S(1)} %shard_map.59.refs_0_), channel_id=1, source_target_pairs={{0,2},{1,3},{2,0},{3,1},{4,6},{5,7},{6,4},{7,5},{8,10},{9,11},{10,... | collective-permute-start | bytes 688136 | tf_op jit(solution)/shard_map/ppermute | solution.py:351
  29.8 11.0 %collective-permute-start.12 = (bf16[112,1024]{1,0:T(8,128)(2,1)S(1)}, bf16[112,1024]{1,0:T(8,128)(2,1)S(1)}, u32[]{:S(2)}, u32[]{:S(2)}) collective-permute-start(bf16[112,1024]{1,0:T(8,128)(2,1)S(1)} %shard_map.66.refs_1_), channel_id=1, source_target_pairs={{0,2},{1,3},{2,0},{3,1},{4,6},{5,7},{6,4},{7,5},{8,10},{9,11},{10,... | collective-permute-start | bytes 688136 | tf_op jit(solution)/shard_map/ppermute | solution.py:351
  33.8 13.9 %collective-permute-start.8 = (bf16[48,1792]{1,0:T(8,128)(2,1)S(1)}, bf16[48,1792]{1,0:T(8,128)(2,1)S(1)}, u32[]{:S(2)}, u32[]{:S(2)}) collective-permute-start(bf16[48,1792]{1,0:T(8,128)(2,1)S(1)} %get-tuple-element.65), channel_id=1, source_target_pairs={{0,8},{4,12},{8,0},{12,4},{1,9},{5,13},{9,1},{13,5},{2,10},{6,14},... | collective-permute-start | bytes 516104 | tf_op jit(solution)/shard_map/ppermute | solution.py:363
  41.0 7.4 %collective-permute-start.7 = (bf16[24,1792]{1,0:T(8,128)(2,1)S(1)}, bf16[24,1792]{1,0:T(8,128)(2,1)S(1)}, u32[]{:S(2)}, u32[]{:S(2)}) collective-permute-start(bf16[24,1792]{1,0:T(8,128)(2,1)S(1)} %get-tuple-element.64), channel_id=1, source_target_pairs={{0,4},{4,0},{8,12},{12,8},{1,5},{5,1},{9,13},{13,9},{2,6},{6,2},{1... | collective-permute-start | bytes 258056 | tf_op jit(solution)/shard_map/ppermute | solution.py:363
  43.3 9.0 %collective-permute-start.14 = (bf16[24,1792]{1,0:T(8,128)(2,1)S(1)}, bf16[24,1792]{1,0:T(8,128)(2,1)S(1)}, u32[]{:S(2)}, u32[]{:S(2)}) collective-permute-start(bf16[24,1792]{1,0:T(8,128)(2,1)S(1)} %get-tuple-element.73), channel_id=1, source_target_pairs={{0,4},{4,0},{8,12},{12,8},{1,5},{5,1},{9,13},{13,9},{2,6},{6,2},{1... | collective-permute-start | bytes 258056 | tf_op jit(solution)/shard_map/ppermute | solution.py:359
  44.9 9.0 %collective-permute-start.15 = (bf16[24,1792]{1,0:T(8,128)(2,1)S(1)}, bf16[24,1792]{1,0:T(8,128)(2,1)S(1)}, u32[]{:S(2)}, u32[]{:S(2)}) collective-permute-start(bf16[24,1792]{1,0:T(8,128)(2,1)S(1)} %get-tuple-element.74), channel_id=1, source_target_pairs={{0,8},{4,12},{8,0},{12,4},{1,9},{5,13},{9,1},{13,5},{2,10},{6,14},... | collective-permute-start | bytes 258056 | tf_op jit(solution)/shard_map/ppermute | solution.py:359
  45.5 8.3 %collective-permute-start.16 = (bf16[24,1792]{1,0:T(8,128)(2,1)S(1)}, bf16[24,1792]{1,0:T(8,128)(2,1)S(1)}, u32[]{:S(2)}, u32[]{:S(2)}) collective-permute-start(bf16[24,1792]{1,0:T(8,128)(2,1)S(1)} %get-tuple-element.75), channel_id=1, source_target_pairs={{0,12},{4,8},{8,4},{12,0},{1,13},{5,9},{9,5},{13,1},{2,14},{6,10},... | collective-permute-start | bytes 258056 | tf_op jit(solution)/shard_map/ppermute | solution.py:359
  47.7 7.4 %collective-permute-start.9 = (bf16[24,1792]{1,0:T(8,128)(2,1)S(1)}, bf16[24,1792]{1,0:T(8,128)(2,1)S(1)}, u32[]{:S(2)}, u32[]{:S(2)}) collective-permute-start(bf16[24,1792]{1,0:T(8,128)(2,1)S(1)} %shard_map.63), channel_id=1, source_target_pairs={{0,4},{4,0},{8,12},{12,8},{1,5},{5,1},{9,13},{13,9},{2,6},{6,2},{1... | collective-permute-start | bytes 258056 | tf_op jit(solution)/shard_map/ppermute | solution.py:363
  48.5 3.7 %collective-permute-start.17 = (s32[4,2,16]{2,1,0:T(2,128)S(1)}, s32[4,2,16]{2,1,0:T(2,128)S(1)}, u32[]{:S(2)}, u32[]{:S(2)}) collective-permute-start(s32[4,2,16]{2,1,0:T(2,128)S(1)} %get-tuple-element.76), channel_id=1, source_target_pairs={{16,0},{17,1},{18,2},{19,3},{20,4},{21,5},{22,6},{23,7},{24,8},{25... | collective-permute-start | bytes 1544 | tf_op jit(solution)/shard_map/ppermute | solution.py:485
  55.9 9.8 %collective-permute-start.18 = (bf16[64,1792]{1,0:T(8,128)(2,1)S(1)}, bf16[64,1792]{1,0:T(8,128)(2,1)S(1)}, u32[]{:S(2)}, u32[]{:S(2)}) collective-permute-start(bf16[64,1792]{1,0:T(8,128)(2,1)S(1)} %get-tuple-element.77.refs_2_), channel_id=1, source_target_pairs={{0,16},{1,17},{2,18},{3,19},{4,20},{5,21},{6,22},{7,23},{8,24},{9,... | collective-permute-start | bytes 688136 | tf_op jit(solution)/shard_map/ppermute | solution.py:380
  57.2 17.8 %collective-permute-start.19 = (bf16[48,1792]{1,0:T(8,128)(2,1)S(1)}, bf16[48,1792]{1,0:T(8,128)(2,1)S(1)}, u32[]{:S(2)}, u32[]{:S(2)}) collective-permute-start(bf16[48,1792]{1,0:T(8,128)(2,1)S(1)} %get-tuple-element.78), channel_id=1, source_target_pairs={{0,24},{4,28},{8,16},{12,20},{1,25},{5,29},{9,17},{13,21},{2,26},{... | collective-permute-start | bytes 516104 | tf_op jit(solution)/shard_map/ppermute | solution.py:387
  58.5 16.5 %collective-permute-start.20 = (bf16[48,1792]{1,0:T(8,128)(2,1)S(1)}, bf16[48,1792]{1,0:T(8,128)(2,1)S(1)}, u32[]{:S(2)}, u32[]{:S(2)}) collective-permute-start(bf16[48,1792]{1,0:T(8,128)(2,1)S(1)} %get-tuple-element.79), channel_id=1, source_target_pairs={{0,28},{4,24},{8,20},{12,16},{1,29},{5,25},{9,21},{13,17},{2,30},{... | collective-permute-start | bytes 516104 | tf_op jit(solution)/shard_map/ppermute | solution.py:387
  66.2 9.4 %collective-permute-start.21 = (bf16[48,1792]{1,0:T(8,128)(2,1)S(1)}, bf16[48,1792]{1,0:T(8,128)(2,1)S(1)}, u32[]{:S(2)}, u32[]{:S(2)}) collective-permute-start(bf16[48,1792]{1,0:T(8,128)(2,1)S(1)} %get-tuple-element.80), channel_id=1, source_target_pairs={{16,20},{20,16},{24,28},{28,24},{17,21},{21,17},{25,29},{29,25},{1... | collective-permute-start | bytes 516104 | tf_op jit(solution)/shard_map/ppermute | solution.py:376
  80.4 7.9 %collective-permute-start.24 = (bf16[112,1024]{1,0:T(8,128)(2,1)S(1)}, bf16[112,1024]{1,0:T(8,128)(2,1)S(1)}, u32[]{:S(2)}, u32[]{:S(2)}) collective-permute-start(bf16[112,1024]{1,0:T(8,128)(2,1)S(1)} %shard_map.73.refs_0_), channel_id=1, source_target_pairs={{0,2},{1,3},{2,0},{3,1},{4,6},{5,7},{6,4},{7,5},{8,10},{9,11},{10,... | collective-permute-start | bytes 688136 | tf_op jit(solution)/shard_map/ppermute | solution.py:351
  87.0 7.9 %collective-permute-start.31 = (bf16[112,1024]{1,0:T(8,128)(2,1)S(1)}, bf16[112,1024]{1,0:T(8,128)(2,1)S(1)}, u32[]{:S(2)}, u32[]{:S(2)}) collective-permute-start(bf16[112,1024]{1,0:T(8,128)(2,1)S(1)} %shard_map.79.refs_1_), channel_id=1, source_target_pairs={{0,2},{1,3},{2,0},{3,1},{4,6},{5,7},{6,4},{7,5},{8,10},{9,11},{10,... | collective-permute-start | bytes 688136 | tf_op jit(solution)/shard_map/ppermute | solution.py:351
  90.8 13.2 %collective-permute-start.27 = (bf16[48,1792]{1,0:T(8,128)(2,1)S(1)}, bf16[48,1792]{1,0:T(8,128)(2,1)S(1)}, u32[]{:S(2)}, u32[]{:S(2)}) collective-permute-start(bf16[48,1792]{1,0:T(8,128)(2,1)S(1)} %get-tuple-element.87), channel_id=1, source_target_pairs={{0,8},{4,12},{8,0},{12,4},{1,9},{5,13},{9,1},{13,5},{2,10},{6,14},... | collective-permute-start | bytes 516104 | tf_op jit(solution)/shard_map/ppermute | solution.py:363
  95.1 8.9 %collective-permute-start.26 = (bf16[24,1792]{1,0:T(8,128)(2,1)S(1)}, bf16[24,1792]{1,0:T(8,128)(2,1)S(1)}, u32[]{:S(2)}, u32[]{:S(2)}) collective-permute-start(bf16[24,1792]{1,0:T(8,128)(2,1)S(1)} %get-tuple-element.86), channel_id=1, source_target_pairs={{0,4},{4,0},{8,12},{12,8},{1,5},{5,1},{9,13},{13,9},{2,6},{6,2},{1... | collective-permute-start | bytes 258056 | tf_op jit(solution)/shard_map/ppermute | solution.py:363
  99.5 5.6 %collective-permute-start.33 = (bf16[24,1792]{1,0:T(8,128)(2,1)S(1)}, bf16[24,1792]{1,0:T(8,128)(2,1)S(1)}, u32[]{:S(2)}, u32[]{:S(2)}) collective-permute-start(bf16[24,1792]{1,0:T(8,128)(2,1)S(1)} %get-tuple-element.92), channel_id=1, source_target_pairs={{0,4},{4,0},{8,12},{12,8},{1,5},{5,1},{9,13},{13,9},{2,6},{6,2},{1... | collective-permute-start | bytes 258056 | tf_op jit(solution)/shard_map/ppermute | solution.py:359
  100.1 9.8 %collective-permute-start.34 = (bf16[24,1792]{1,0:T(8,128)(2,1)S(1)}, bf16[24,1792]{1,0:T(8,128)(2,1)S(1)}, u32[]{:S(2)}, u32[]{:S(2)}) collective-permute-start(bf16[24,1792]{1,0:T(8,128)(2,1)S(1)} %get-tuple-element.93), channel_id=1, source_target_pairs={{0,8},{4,12},{8,0},{12,4},{1,9},{5,13},{9,1},{13,5},{2,10},{6,14},... | collective-permute-start | bytes 258056 | tf_op jit(solution)/shard_map/ppermute | solution.py:359
  101.5 8.4 %collective-permute-start.35 = (bf16[24,1792]{1,0:T(8,128)(2,1)S(1)}, bf16[24,1792]{1,0:T(8,128)(2,1)S(1)}, u32[]{:S(2)}, u32[]{:S(2)}) collective-permute-start(bf16[24,1792]{1,0:T(8,128)(2,1)S(1)} %get-tuple-element.94), channel_id=1, source_target_pairs={{0,12},{4,8},{8,4},{12,0},{1,13},{5,9},{9,5},{13,1},{2,14},{6,10},... | collective-permute-start | bytes 258056 | tf_op jit(solution)/shard_map/ppermute | solution.py:359
  104.0 6.3 %collective-permute-start.28 = (bf16[24,1792]{1,0:T(8,128)(2,1)S(1)}, bf16[24,1792]{1,0:T(8,128)(2,1)S(1)}, u32[]{:S(2)}, u32[]{:S(2)}) collective-permute-start(bf16[24,1792]{1,0:T(8,128)(2,1)S(1)} %shard_map.77), channel_id=1, source_target_pairs={{0,4},{4,0},{8,12},{12,8},{1,5},{5,1},{9,13},{13,9},{2,6},{6,2},{1... | collective-permute-start | bytes 258056 | tf_op jit(solution)/shard_map/ppermute | solution.py:363
  (14 other events, 34.6 us)

commit v7 on v6

--- a/solution.py
+++ b/solution.py
@@ -281,14 +281,13 @@
     out[...] = half_products(z, weights, units_ref, lax.axis_index("hidden") & 1)
 
 
-def down_kernel(z, hands_on, *refs):
+def down_kernel(z, nears, *refs):
     weights, refs = refs[:z.members], refs[z.members:]
-    units_ref, own_ref, outs = refs[:1], refs[1], refs[2:]
-    if hands_on:
-        outs[-1][...] = outs[0][...]
-        outs = outs[1:-1]
+    units_ref, own_ref, refs = refs[:1], refs[1], refs[2:]
+    near, outs = [ref[...].astype(F32) for ref in refs[:nears]], refs[nears:]
     total = own_ref[...] + half_products(z, weights, units_ref, 1 - (lax.axis_index("hidden") & 1))
     value = dot(z.order(), total.astype(BF16), DOWN)
+    value = jnp.concatenate([value[:z.piece], *near, value[z.piece:]], axis=0) if near else value
     low = 0
     for out in outs:
         out[...] = value[low:low + out.shape[0]].astype(BF16)
@@ -300,8 +299,17 @@
 
 
 def combine_kernel(z, tick, last, weight_ref, rows_ref, kept_ref, *refs):
-    count = z.groups * z.pieces
-    returned, refs = [ref[...].astype(F32)[:z.piece] for ref in refs[:count]], refs[count:]
+    returned = []
+    if z.pairs:
+        count = z.groups * z.pieces
+        values, refs = [ref[...].astype(F32) for ref in refs[:count]], refs[count:]
+        near = values[-z.groups:]
+        for group in range(z.groups):
+            own, *far = values[3 * group:3 * group + 3]
+            returned += [own, near[group], far[0][:z.piece], far[1]]
+    else:
+        count = z.groups * z.pieces
+        returned, refs = [ref[...].astype(F32) for ref in refs[:count]], refs[count:]
     stacked = []
     for piece in range(z.pieces):
         values = [returned[group * z.pieces + piece] for group in range(z.groups)]
@@ -342,6 +350,7 @@
     shape = jax.ShapeDtypeStruct
     pay = shape((z.piece, z.width), BF16)
     all_pay = shape((z.all_piece, z.width), BF16)
+    joined_near = [pay] * (z.groups + 3)
     merged = [pay, pay, shape((2 * z.piece, z.width), BF16)]
     whole = shape((z.rows, z.width), BF16)
     steps = sorted(range(z.peers), key=lambda step: -step.bit_length())
@@ -363,12 +372,16 @@
         return lax.ppermute(value, "expert", [(i, i ^ step) for i in range(z.peers)])
 
     def sent_back(pieces, group):
-        if group >= z.pairs:
+        if not z.pairs:
             return exchanged(pieces)
-        own, near, far = pieces
-        far = across(far, 2)
-        second = call(second_kernel, (z,), 2, [pay], [VMEM], [], far)[0]
-        return [own, across(near, 1), far, across(second, 1)]
+        if group < z.pairs:
+            return [pieces[0], across(pieces[2], 2)]
+        own, *near, two, three = pieces
+        two, three = across(two, 2), across(three, 3)
+        return [own, two, three, *(across(value, 1) for value in near)]
+
+    def sent_on(pair, waits):
+        return across(call(second_kernel, (z,), 2, [pay], [VMEM], [], pair, waits=waits)[0], 1)
 
     def within(value, step, section):
         low = section * z.peers
@@ -418,17 +431,16 @@
         )
         return units, [swap(part, 1) for part in units]
 
-    def down(halves, group, hand_on):
+    def down(halves, group, nears):
         own = call(
             own_down_kernel, (z,), 4, [shape((z.group_each, z.width), F32)],
             [VMEM] * (z.members + len(halves[0])), [], *tall[group], *halves[0],
         )[0]
         return call(
-            down_kernel, (z, len(hand_on)), 4,
-            (merged if group < z.pairs else [pay] * z.pieces)
-            + [shape(value.shape, value.dtype) for value in hand_on],
-            [VMEM] * (z.members + 1 + len(halves[1]) + len(hand_on)), [],
-            *tall[group], *halves[1], own, *hand_on,
+            down_kernel, (z, len(nears)), 4,
+            merged if group < z.pairs else joined_near if nears else [pay] * z.pieces,
+            [VMEM] * (z.members + 1 + len(halves[1]) + len(nears)), [],
+            *tall[group], *halves[1], own, *nears,
         )
 
     routes = routes[0].transpose(0, 2, 1)
@@ -465,9 +477,10 @@
 
     tall = [load_down(0, wide[-1])]
     groups = range(z.groups)
+    following = lax.ppermute(routes, "section", [(i + 1, i) for i in range(sections - 1)])
     for tick in range(sections):
         last = tick == sections - 1
-        sums, returned = [], []
+        sums, returned, nears = [], [], []
         for group in groups:
             own, other = products(received, group, [sums[-1][0]] if group else tall[0][:1])
             sums.append(pair_sums(own, other))
@@ -477,13 +490,12 @@
             if group and tick == 0:
                 tall.append(load_down(group, outgoing[0]))
             if group:
-                halves = activated(sums[group], tall[group][:1] if tick == 0 else outgoing[:1])
-            hand_on = [routes] if tick == 0 and group == z.groups - 1 else []
-            outgoing = down(halves, group, hand_on)
-            if hand_on:
-                pairs = [(i + 1, i) for i in range(sections - 1)]
-                following = lax.ppermute(outgoing.pop(), "section", pairs)
+                halves = activated(sums[group], tall[group][:1] + [following] if tick == 0 else outgoing[:1])
+            outgoing = down(halves, group, nears if group >= z.pairs else [])
+            nears += outgoing[1:2] if group < z.pairs else []
             returned.append(sent_back(outgoing, group))
+        for group in range(z.pairs):
+            returned[group].append(sent_on(returned[group][1], outgoing[:1]))
         returned = sum(returned, [])
         kept, *sent = call(
             combine_kernel, (z, tick, last), 4,

time: 112 us -> 118 us (1.054)
  waiting for transfers between devices: 28.4 us -> 33.2 us
  starting transfers between devices: 42.5 us -> 44 us
    ppermute x6 -> x12, waiting for transfers between devices: 1.7 us -> 16.8 us  [across(): lax.ppermute(value, 'expert', [(i, i ^ step) for i in range(z.peers)])]
    ppermute x6 -> x12, starting transfers between devices: 9.97 us -> 21.3 us  [across(): lax.ppermute(value, 'expert', [(i, i ^ step) for i in range(z.peers)])]
    ppermute x9 -> x3, starting transfers between devices: 13.1 us -> 4.23 us  [exchanged(): result[step] = lax.ppermute(pieces[step], 'expert', pairs)]
    ppermute x9 -> x3, waiting for transfers between devices: 7.45 us -> 0.01 us  [exchanged(): result[step] = lax.ppermute(pieces[step], 'expert', pairs)]
    ppermute x1, waiting for transfers between devices: 1.31 us -> 0.01 us  [on_device(): lax.ppermute(routes, 'section', [(i + 1, i) for i in range(sections - 1)])]
  transfers between devices with their start and end apart: 36 -> 36, of which waited for: 23 -> 26; matrix products, arithmetic and copies ran while one was open for 0% -> 0% of each run, Pallas kernels for 27% -> 26%
where the time goes in v7:
time: 118 us; the launch traced here: 117 us
  starting transfers between devices  44 us (37%)
  Pallas kernels  40 us (34%)
  waiting for transfers between devices  33.2 us (28%)
    pallas_call x29, Pallas kernels, call(): pl.pallas_call(functools.partial(after_waits, len(waits), functools.parti...  40 us
    ppermute x12, starting transfers between devices, across(): lax.ppermute(value, 'expert', [(i, i ^ step) for i in range(z.peers)])  21.3 us
    ppermute x12, waiting for transfers between devices, across(): lax.ppermute(value, 'expert', [(i, i ^ step) for i in range(z.peers)])  16.8 us
    ppermute x16, waiting for transfers between devices, swap(): return lax.ppermute(value, 'hidden', pairs)  7.99 us
    ppermute x16, starting transfers between devices, swap(): return lax.ppermute(value, 'hidden', pairs)  6.88 us
    ppermute x1, starting transfers between devices, within(): return lax.ppermute(value, ('section', 'expert'), pairs)  5.22 us
    ppermute x1, waiting for transfers between devices, relayed(): rows = lax.ppermute(kept, 'section', hop)  5.17 us
    ppermute x3, starting transfers between devices, exchanged(): result[step] = lax.ppermute(pieces[step], 'expert', pairs)  4.23 us
  transfers between devices with their start and end apart: 36, of which 26 were waited for; matrix products, arithmetic and copies ran while one was open for 0% of the time, Pallas kernels for 26%

profile of v7, /device:TPU:2, one launch (start us, length us, event | category | flops | bytes accessed | tf_op | source)
XLA Modules:
  0.0 117.5 jit_solution(11214319906476366897)
XLA Ops:
  1.5 2.6 %collective-permute-start = (bf16[48,1792]{1,0:T(8,128)(2,1)S(1)}, bf16[48,1792]{1,0:T(8,128)(2,1)S(1)}, u32[]{:S(2)}, u32[]{:S(2)}) collective-permute-start(bf16[48,1792]{1,0:T(8,128)(2,1)S(1)} %get-tuple-element.57), channel_id=1, source_target_pairs={{0,8},{4,12},{8,0},{12,4},{1,9},{5,13},{9,1},{13,5},{2,10},{6,14},... | collective-permute-start | bytes 516104 | tf_op jit(solution)/shard_map/ppermute | solution.py:368
  5.8 9.6 %shard_map.56 = (bf16[3584,1024]{1,0:T(8,128)(2,1)S(1)}, bf16[3584,1024]{1,0:T(8,128)(2,1)S(1)}, bf16[3584,1024]{1,0:T(8,128)(2,1)S(1)}, bf16[3584,1024]{1,0:T(8,128)(2,1)S(1)}) custom-call(bf16[192,64]{1,0:T(8,128)(2,1)S(1)} %get-tuple-element.51.refs_0_, bf16[1,1792,2,4096]{3,2,1,0:T(2,128)(2,1)} %refs_1_.3), custom_call_target="tpu_custom_call" | custom-call | tf_op jit(solution)/shard_map/pallas_call | solution.py:335
  15.4 3.2 %shard_map.57 = (bf16[1024,1792]{1,0:T(8,128)(2,1)S(1)}, bf16[1024,1792]{1,0:T(8,128)(2,1)S(1)}) custom-call(bf16[3584,1024]{1,0:T(8,128)(2,1)S(1)} %get-tuple-element.52.refs_0_.refs_2_, bf16[1,4096,1792]{2,1,0:T(8,128)(2,1)} %refs_1_.5), custom_call_target="tpu_custom_call" | custom-call | tf_op jit(solution)/shard_map/pallas_call | solution.py:335
  18.6 3.2 %shard_map.58 = (f32[112,1024]{1,0:T(8,128)S(1)}, bf16[56,1024]{1,0:T(8,128)(2,1)S(1)}, bf16[56,1024]{1,0:T(8,128)(2,1)S(1)}) custom-call(bf16[1024,1792]{1,0:T(8,128)(2,1)S(1)} %get-tuple-element.53.refs_0_, bf16[3584,1024]{1,0:T(8,128)(2,1)S(1)} %get-tuple-element.55.refs_1_, bf16[3584,1024]{1,0:T(8,128)(2,1)S(1)} %get-tuple-element.56.refs_2_, ...), custom_call_target="tpu_custom_call" | custom-call | tf_op jit(solution)/shard_map/pallas_call | solution.py:335
  25.0 3.2 %shard_map.64 = (f32[112,1024]{1,0:T(8,128)S(1)}, bf16[56,1024]{1,0:T(8,128)(2,1)S(1)}, bf16[56,1024]{1,0:T(8,128)(2,1)S(1)}) custom-call(bf16[112,1024]{1,0:T(8,128)(2,1)S(1)} %shard_map.59.refs_0_, bf16[3584,1024]{1,0:T(8,128)(2,1)S(1)} %get-tuple-element.68.refs_1_, bf16[3584,1024]{1,0:T(8,128)(2,1)S(1)} %get-tuple-element.52.refs_0_.refs_2_, ...), custom_call_target="tpu_custom_call" | custom-call | tf_op jit(solution)/shard_map/pallas_call | solution.py:335
  33.8 3.7 %collective-permute-start.7 = (bf16[48,1792]{1,0:T(8,128)(2,1)S(1)}, bf16[48,1792]{1,0:T(8,128)(2,1)S(1)}, u32[]{:S(2)}, u32[]{:S(2)}) collective-permute-start(bf16[48,1792]{1,0:T(8,128)(2,1)S(1)} %get-tuple-element.65), channel_id=1, source_target_pairs={{0,8},{4,12},{8,0},{12,4},{1,9},{5,13},{9,1},{13,5},{2,10},{6,14},... | collective-permute-start | bytes 516104 | tf_op jit(solution)/shard_map/ppermute | solution.py:372
  37.6 2.4 %collective-permute-start.8 = (s32[4,2,16]{2,1,0:T(2,128)S(1)}, s32[4,2,16]{2,1,0:T(2,128)S(1)}, u32[]{:S(2)}, u32[]{:S(2)}) collective-permute-start(s32[4,2,16]{2,1,0:T(2,128)S(1)} %bitcast.12), channel_id=1, source_target_pairs={{16,0},{17,1},{18,2},{19,3},{20,4},{21,5},{22,6},{23,7},{24,8},{25... | collective-permute-start | bytes 1544 | tf_op jit(solution)/shard_map/ppermute | solution.py:480
  40.0 3.2 %shard_map.63 = (bf16[1024,1792]{1,0:T(8,128)(2,1)S(1)}, bf16[1024,1792]{1,0:T(8,128)(2,1)S(1)}) custom-call(bf16[24,1792]{1,0:T(8,128)(2,1)S(1)} %get-tuple-element.64.refs_0_.refs_3_, bf16[1,4096,1792]{2,1,0:T(8,128)(2,1)} %refs_1_.5), custom_call_target="tpu_custom_call" | custom-call | tf_op jit(solution)/shard_map/pallas_call | solution.py:335
  45.8 2.1 %collective-permute-start.15 = (bf16[24,1792]{1,0:T(8,128)(2,1)S(1)}, bf16[24,1792]{1,0:T(8,128)(2,1)S(1)}, u32[]{:S(2)}, u32[]{:S(2)}) collective-permute-start(bf16[24,1792]{1,0:T(8,128)(2,1)S(1)} %get-tuple-element.75), channel_id=1, source_target_pairs={{0,12},{4,8},{8,4},{12,0},{1,13},{5,9},{9,5},{13,1},{2,14},{6,10},... | collective-permute-start | bytes 258056 | tf_op jit(solution)/shard_map/ppermute | solution.py:372
  51.4 2.9 %collective-permute-done.14.refs_7_ = bf16[24,1792]{1,0:T(8,128)(2,1)S(1)} collective-permute-done((bf16[24,1792]{1,0:T(8,128)(2,1)S(1)}, bf16[24,1792]{1,0:T(8,128)(2,1)S(1)}, u32[]{:S(2)}, u32[]{:S(2)}) %collective-permute-start.14) | collective-permute-done | bytes 86048 | tf_op jit(solution)/shard_map/ppermute | solution.py:372
  54.3 1.9 %collective-permute-done.16.refs_9_ = bf16[24,1792]{1,0:T(8,128)(2,1)S(1)} collective-permute-done((bf16[24,1792]{1,0:T(8,128)(2,1)S(1)}, bf16[24,1792]{1,0:T(8,128)(2,1)S(1)}, u32[]{:S(2)}, u32[]{:S(2)}) %collective-permute-start.16) | collective-permute-done | bytes 86048 | tf_op jit(solution)/shard_map/ppermute | solution.py:372
  56.1 1.8 %collective-permute-done.17.refs_10_ = bf16[24,1792]{1,0:T(8,128)(2,1)S(1)} collective-permute-done((bf16[24,1792]{1,0:T(8,128)(2,1)S(1)}, bf16[24,1792]{1,0:T(8,128)(2,1)S(1)}, u32[]{:S(2)}, u32[]{:S(2)}) %collective-permute-start.17) | collective-permute-done | bytes 86048 | tf_op jit(solution)/shard_map/ppermute | solution.py:372
  63.9 5.2 %collective-permute-done.18.refs_1_ = bf16[64,1792]{1,0:T(8,128)(2,1)S(1)} collective-permute-done((bf16[64,1792]{1,0:T(8,128)(2,1)S(1)}, bf16[64,1792]{1,0:T(8,128)(2,1)S(1)}, u32[]{:S(2)}, u32[]{:S(2)}) %collective-permute-start.18) | collective-permute-done | bytes 229408 | tf_op jit(solution)/shard_map/ppermute | solution.py:393
  69.6 5.2 %collective-permute-start.21 = (bf16[48,1792]{1,0:T(8,128)(2,1)S(1)}, bf16[48,1792]{1,0:T(8,128)(2,1)S(1)}, u32[]{:S(2)}, u32[]{:S(2)}) collective-permute-start(bf16[48,1792]{1,0:T(8,128)(2,1)S(1)} %get-tuple-element.81), channel_id=1, source_target_pairs={{16,20},{20,16},{24,28},{28,24},{17,21},{21,17},{25,29},{29,25},{1... | collective-permute-start | bytes 516104 | tf_op jit(solution)/shard_map/ppermute | solution.py:389
  74.8 2.5 %collective-permute-done.19.refs_3_ = bf16[48,1792]{1,0:T(8,128)(2,1)S(1)} collective-permute-done((bf16[48,1792]{1,0:T(8,128)(2,1)S(1)}, bf16[48,1792]{1,0:T(8,128)(2,1)S(1)}, u32[]{:S(2)}, u32[]{:S(2)}) %collective-permute-start.19) | collective-permute-done | bytes 172064 | tf_op jit(solution)/shard_map/ppermute | solution.py:400
  78.0 3.2 %shard_map.72 = (f32[112,1024]{1,0:T(8,128)S(1)}, bf16[56,1024]{1,0:T(8,128)(2,1)S(1)}, bf16[56,1024]{1,0:T(8,128)(2,1)S(1)}) custom-call(bf16[1024,1792]{1,0:T(8,128)(2,1)S(1)} %get-tuple-element.53.refs_0_, bf16[3584,1024]{1,0:T(8,128)(2,1)S(1)} %get-tuple-element.55.refs_1_, bf16[3584,1024]{1,0:T(8,128)(2,1)S(1)} %get-tuple-element.56.refs_2_, ...), custom_call_target="tpu_custom_call" | custom-call | tf_op jit(solution)/shard_map/pallas_call | solution.py:335
  82.8 1.6 %collective-permute-start.24 = (bf16[112,1024]{1,0:T(8,128)(2,1)S(1)}, bf16[112,1024]{1,0:T(8,128)(2,1)S(1)}, u32[]{:S(2)}, u32[]{:S(2)}) collective-permute-start(bf16[112,1024]{1,0:T(8,128)(2,1)S(1)} %shard_map.73.refs_0_), channel_id=1, source_target_pairs={{0,2},{1,3},{2,0},{3,1},{4,6},{5,7},{6,4},{7,5},{8,10},{9,11},{10,... | collective-permute-start | bytes 688136 | tf_op jit(solution)/shard_map/ppermute | solution.py:360
  84.4 3.2 %shard_map.77 = (f32[112,1024]{1,0:T(8,128)S(1)}, bf16[56,1024]{1,0:T(8,128)(2,1)S(1)}, bf16[56,1024]{1,0:T(8,128)(2,1)S(1)}) custom-call(bf16[112,1024]{1,0:T(8,128)(2,1)S(1)} %shard_map.73.refs_0_, bf16[3584,1024]{1,0:T(8,128)(2,1)S(1)} %get-tuple-element.68.refs_1_, bf16[3584,1024]{1,0:T(8,128)(2,1)S(1)} %get-tuple-element.52.refs_0_.refs_2_, ...), custom_call_target="tpu_custom_call" | custom-call | tf_op jit(solution)/shard_map/pallas_call | solution.py:335
  93.2 4.4 %collective-permute-start.26 = (bf16[48,1792]{1,0:T(8,128)(2,1)S(1)}, bf16[48,1792]{1,0:T(8,128)(2,1)S(1)}, u32[]{:S(2)}, u32[]{:S(2)}) collective-permute-start(bf16[48,1792]{1,0:T(8,128)(2,1)S(1)} %get-tuple-element.87), channel_id=1, source_target_pairs={{0,8},{4,12},{8,0},{12,4},{1,9},{5,13},{9,1},{13,5},{2,10},{6,14},... | collective-permute-start | bytes 516104 | tf_op jit(solution)/shard_map/ppermute | solution.py:372
  100.0 3.9 %collective-permute-start.32 = (bf16[24,1792]{1,0:T(8,128)(2,1)S(1)}, bf16[24,1792]{1,0:T(8,128)(2,1)S(1)}, u32[]{:S(2)}, u32[]{:S(2)}) collective-permute-start(bf16[24,1792]{1,0:T(8,128)(2,1)S(1)} %get-tuple-element.93), channel_id=1, source_target_pairs={{0,8},{4,12},{8,0},{12,4},{1,9},{5,13},{9,1},{13,5},{2,10},{6,14},... | collective-permute-start | bytes 258056 | tf_op jit(solution)/shard_map/ppermute | solution.py:372
  105.5 2.0 %collective-permute-start.35 = (bf16[24,1792]{1,0:T(8,128)(2,1)S(1)}, bf16[24,1792]{1,0:T(8,128)(2,1)S(1)}, u32[]{:S(2)}, u32[]{:S(2)}) collective-permute-start(bf16[24,1792]{1,0:T(8,128)(2,1)S(1)} %get-tuple-element.96), channel_id=1, source_target_pairs={{0,4},{4,0},{8,12},{12,8},{1,5},{5,1},{9,13},{13,9},{2,6},{6,2},{1... | collective-permute-start | bytes 258056 | tf_op jit(solution)/shard_map/ppermute | solution.py:372
  107.5 1.8 %collective-permute-done.26.refs_1_.refs_4_ = bf16[48,1792]{1,0:T(8,128)(2,1)S(1)} collective-permute-done((bf16[48,1792]{1,0:T(8,128)(2,1)S(1)}, bf16[48,1792]{1,0:T(8,128)(2,1)S(1)}, u32[]{:S(2)}, u32[]{:S(2)}) %collective-permute-start.26) | collective-permute-done | bytes 172064 | tf_op jit(solution)/shard_map/ppermute | solution.py:372
  109.3 2.6 %collective-permute-done.32.refs_7_ = bf16[24,1792]{1,0:T(8,128)(2,1)S(1)} collective-permute-done((bf16[24,1792]{1,0:T(8,128)(2,1)S(1)}, bf16[24,1792]{1,0:T(8,128)(2,1)S(1)}, u32[]{:S(2)}, u32[]{:S(2)}) %collective-permute-start.32) | collective-permute-done | bytes 86048 | tf_op jit(solution)/shard_map/ppermute | solution.py:372
  113.4 1.8 %collective-permute-done.35.refs_10_ = bf16[24,1792]{1,0:T(8,128)(2,1)S(1)} collective-permute-done((bf16[24,1792]{1,0:T(8,128)(2,1)S(1)}, bf16[24,1792]{1,0:T(8,128)(2,1)S(1)}, u32[]{:S(2)}, u32[]{:S(2)}) %collective-permute-start.35) | collective-permute-done | bytes 86048 | tf_op jit(solution)/shard_map/ppermute | solution.py:372
  (81 shorter events, 39.9 us)
Async XLA Ops:
  1.5 17.1 %collective-permute-start = (bf16[48,1792]{1,0:T(8,128)(2,1)S(1)}, bf16[48,1792]{1,0:T(8,128)(2,1)S(1)}, u32[]{:S(2)}, u32[]{:S(2)}) collective-permute-start(bf16[48,1792]{1,0:T(8,128)(2,1)S(1)} %get-tuple-element.57), channel_id=1, source_target_pairs={{0,8},{4,12},{8,0},{12,4},{1,9},{5,13},{9,1},{13,5},{2,10},{6,14},... | collective-permute-start | bytes 516104 | tf_op jit(solution)/shard_map/ppermute | solution.py:368
  4.2 14.4 %collective-permute-start.1 = (bf16[48,1792]{1,0:T(8,128)(2,1)S(1)}, bf16[48,1792]{1,0:T(8,128)(2,1)S(1)}, u32[]{:S(2)}, u32[]{:S(2)}) collective-permute-start(bf16[48,1792]{1,0:T(8,128)(2,1)S(1)} %get-tuple-element.58), channel_id=1, source_target_pairs={{0,12},{4,8},{8,4},{12,0},{1,13},{5,9},{9,5},{13,1},{2,14},{6,10},... | collective-permute-start | bytes 516104 | tf_op jit(solution)/shard_map/ppermute | solution.py:368
  5.5 13.1 %collective-permute-start.2 = (bf16[48,1792]{1,0:T(8,128)(2,1)S(1)}, bf16[48,1792]{1,0:T(8,128)(2,1)S(1)}, u32[]{:S(2)}, u32[]{:S(2)}) collective-permute-start(bf16[48,1792]{1,0:T(8,128)(2,1)S(1)} %get-tuple-element.59), channel_id=1, source_target_pairs={{0,4},{4,0},{8,12},{12,8},{1,5},{5,1},{9,13},{13,9},{2,6},{6,2},{1... | collective-permute-start | bytes 516104 | tf_op jit(solution)/shard_map/ppermute | solution.py:368
  23.4 7.9 %collective-permute-start.5 = (bf16[112,1024]{1,0:T(8,128)(2,1)S(1)}, bf16[112,1024]{1,0:T(8,128)(2,1)S(1)}, u32[]{:S(2)}, u32[]{:S(2)}) collective-permute-start(bf16[112,1024]{1,0:T(8,128)(2,1)S(1)} %shard_map.59.refs_0_), channel_id=1, source_target_pairs={{0,2},{1,3},{2,0},{3,1},{4,6},{5,7},{6,4},{7,5},{8,10},{9,11},{10,... | collective-permute-start | bytes 688136 | tf_op jit(solution)/shard_map/ppermute | solution.py:360
  29.8 13.4 %collective-permute-start.11 = (bf16[112,1024]{1,0:T(8,128)(2,1)S(1)}, bf16[112,1024]{1,0:T(8,128)(2,1)S(1)}, u32[]{:S(2)}, u32[]{:S(2)}) collective-permute-start(bf16[112,1024]{1,0:T(8,128)(2,1)S(1)} %shard_map.65.refs_2_), channel_id=1, source_target_pairs={{0,2},{1,3},{2,0},{3,1},{4,6},{5,7},{6,4},{7,5},{8,10},{9,11},{10,... | collective-permute-start | bytes 688136 | tf_op jit(solution)/shard_map/ppermute | solution.py:360
  33.8 16.2 %collective-permute-start.7 = (bf16[48,1792]{1,0:T(8,128)(2,1)S(1)}, bf16[48,1792]{1,0:T(8,128)(2,1)S(1)}, u32[]{:S(2)}, u32[]{:S(2)}) collective-permute-start(bf16[48,1792]{1,0:T(8,128)(2,1)S(1)} %get-tuple-element.65), channel_id=1, source_target_pairs={{0,8},{4,12},{8,0},{12,4},{1,9},{5,13},{9,1},{13,5},{2,10},{6,14},... | collective-permute-start | bytes 516104 | tf_op jit(solution)/shard_map/ppermute | solution.py:372
  37.6 5.6 %collective-permute-start.8 = (s32[4,2,16]{2,1,0:T(2,128)S(1)}, s32[4,2,16]{2,1,0:T(2,128)S(1)}, u32[]{:S(2)}, u32[]{:S(2)}) collective-permute-start(s32[4,2,16]{2,1,0:T(2,128)S(1)} %bitcast.12), channel_id=1, source_target_pairs={{16,0},{17,1},{18,2},{19,3},{20,4},{21,5},{22,6},{23,7},{24,8},{25... | collective-permute-start | bytes 1544 | tf_op jit(solution)/shard_map/ppermute | solution.py:480
  45.7 8.6 %collective-permute-start.14 = (bf16[24,1792]{1,0:T(8,128)(2,1)S(1)}, bf16[24,1792]{1,0:T(8,128)(2,1)S(1)}, u32[]{:S(2)}, u32[]{:S(2)}) collective-permute-start(bf16[24,1792]{1,0:T(8,128)(2,1)S(1)} %get-tuple-element.74), channel_id=1, source_target_pairs={{0,8},{4,12},{8,0},{12,4},{1,9},{5,13},{9,1},{13,5},{2,10},{6,14},... | collective-permute-start | bytes 258056 | tf_op jit(solution)/shard_map/ppermute | solution.py:372
  45.8 8.5 %collective-permute-start.15 = (bf16[24,1792]{1,0:T(8,128)(2,1)S(1)}, bf16[24,1792]{1,0:T(8,128)(2,1)S(1)}, u32[]{:S(2)}, u32[]{:S(2)}) collective-permute-start(bf16[24,1792]{1,0:T(8,128)(2,1)S(1)} %get-tuple-element.75), channel_id=1, source_target_pairs={{0,12},{4,8},{8,4},{12,0},{1,13},{5,9},{9,5},{13,1},{2,14},{6,10},... | collective-permute-start | bytes 258056 | tf_op jit(solution)/shard_map/ppermute | solution.py:372
  47.9 8.2 %collective-permute-start.16 = (bf16[24,1792]{1,0:T(8,128)(2,1)S(1)}, bf16[24,1792]{1,0:T(8,128)(2,1)S(1)}, u32[]{:S(2)}, u32[]{:S(2)}) collective-permute-start(bf16[24,1792]{1,0:T(8,128)(2,1)S(1)} %get-tuple-element.76), channel_id=1, source_target_pairs={{0,4},{4,0},{8,12},{12,8},{1,5},{5,1},{9,13},{13,9},{2,6},{6,2},{1... | collective-permute-start | bytes 258056 | tf_op jit(solution)/shard_map/ppermute | solution.py:372
  49.3 8.7 %collective-permute-start.17 = (bf16[24,1792]{1,0:T(8,128)(2,1)S(1)}, bf16[24,1792]{1,0:T(8,128)(2,1)S(1)}, u32[]{:S(2)}, u32[]{:S(2)}) collective-permute-start(bf16[24,1792]{1,0:T(8,128)(2,1)S(1)} %get-tuple-element.77), channel_id=1, source_target_pairs={{0,4},{4,0},{8,12},{12,8},{1,5},{5,1},{9,13},{13,9},{2,6},{6,2},{1... | collective-permute-start | bytes 258056 | tf_op jit(solution)/shard_map/ppermute | solution.py:372
  50.0 9.3 %collective-permute-start.13 = (bf16[24,1792]{1,0:T(8,128)(2,1)S(1)}, bf16[24,1792]{1,0:T(8,128)(2,1)S(1)}, u32[]{:S(2)}, u32[]{:S(2)}) collective-permute-start(bf16[24,1792]{1,0:T(8,128)(2,1)S(1)} %shard_map.69), channel_id=1, source_target_pairs={{0,4},{4,0},{8,12},{12,8},{1,5},{5,1},{9,13},{13,9},{2,6},{6,2},{1... | collective-permute-start | bytes 258056 | tf_op jit(solution)/shard_map/ppermute | solution.py:372
  60.0 9.1 %collective-permute-start.18 = (bf16[64,1792]{1,0:T(8,128)(2,1)S(1)}, bf16[64,1792]{1,0:T(8,128)(2,1)S(1)}, u32[]{:S(2)}, u32[]{:S(2)}) collective-permute-start(bf16[64,1792]{1,0:T(8,128)(2,1)S(1)} %get-tuple-element.78.refs_2_), channel_id=1, source_target_pairs={{0,16},{1,17},{2,18},{3,19},{4,20},{5,21},{6,22},{7,23},{8,24},{9,... | collective-permute-start | bytes 688136 | tf_op jit(solution)/shard_map/ppermute | solution.py:393
  61.3 16.0 %collective-permute-start.19 = (bf16[48,1792]{1,0:T(8,128)(2,1)S(1)}, bf16[48,1792]{1,0:T(8,128)(2,1)S(1)}, u32[]{:S(2)}, u32[]{:S(2)}) collective-permute-start(bf16[48,1792]{1,0:T(8,128)(2,1)S(1)} %get-tuple-element.79), channel_id=1, source_target_pairs={{0,24},{4,28},{8,16},{12,20},{1,25},{5,29},{9,17},{13,21},{2,26},{... | collective-permute-start | bytes 516104 | tf_op jit(solution)/shard_map/ppermute | solution.py:400
  62.6 14.7 %collective-permute-start.20 = (bf16[48,1792]{1,0:T(8,128)(2,1)S(1)}, bf16[48,1792]{1,0:T(8,128)(2,1)S(1)}, u32[]{:S(2)}, u32[]{:S(2)}) collective-permute-start(bf16[48,1792]{1,0:T(8,128)(2,1)S(1)} %get-tuple-element.80), channel_id=1, source_target_pairs={{0,28},{4,24},{8,20},{12,16},{1,29},{5,25},{9,21},{13,17},{2,30},{... | collective-permute-start | bytes 516104 | tf_op jit(solution)/shard_map/ppermute | solution.py:400
  69.6 8.4 %collective-permute-start.21 = (bf16[48,1792]{1,0:T(8,128)(2,1)S(1)}, bf16[48,1792]{1,0:T(8,128)(2,1)S(1)}, u32[]{:S(2)}, u32[]{:S(2)}) collective-permute-start(bf16[48,1792]{1,0:T(8,128)(2,1)S(1)} %get-tuple-element.81), channel_id=1, source_target_pairs={{16,20},{20,16},{24,28},{28,24},{17,21},{21,17},{25,29},{29,25},{1... | collective-permute-start | bytes 516104 | tf_op jit(solution)/shard_map/ppermute | solution.py:389
  82.8 7.9 %collective-permute-start.24 = (bf16[112,1024]{1,0:T(8,128)(2,1)S(1)}, bf16[112,1024]{1,0:T(8,128)(2,1)S(1)}, u32[]{:S(2)}, u32[]{:S(2)}) collective-permute-start(bf16[112,1024]{1,0:T(8,128)(2,1)S(1)} %shard_map.73.refs_0_), channel_id=1, source_target_pairs={{0,2},{1,3},{2,0},{3,1},{4,6},{5,7},{6,4},{7,5},{8,10},{9,11},{10,... | collective-permute-start | bytes 688136 | tf_op jit(solution)/shard_map/ppermute | solution.py:360
  89.1 8.4 %collective-permute-start.29 = (bf16[112,1024]{1,0:T(8,128)(2,1)S(1)}, bf16[112,1024]{1,0:T(8,128)(2,1)S(1)}, u32[]{:S(2)}, u32[]{:S(2)}) collective-permute-start(bf16[112,1024]{1,0:T(8,128)(2,1)S(1)} %shard_map.78.refs_1_), channel_id=1, source_target_pairs={{0,2},{1,3},{2,0},{3,1},{4,6},{5,7},{6,4},{7,5},{8,10},{9,11},{10,... | collective-permute-start | bytes 688136 | tf_op jit(solution)/shard_map/ppermute | solution.py:360
  93.2 16.1 %collective-permute-start.26 = (bf16[48,1792]{1,0:T(8,128)(2,1)S(1)}, bf16[48,1792]{1,0:T(8,128)(2,1)S(1)}, u32[]{:S(2)}, u32[]{:S(2)}) collective-permute-start(bf16[48,1792]{1,0:T(8,128)(2,1)S(1)} %get-tuple-element.87), channel_id=1, source_target_pairs={{0,8},{4,12},{8,0},{12,4},{1,9},{5,13},{9,1},{13,5},{2,10},{6,14},... | collective-permute-start | bytes 516104 | tf_op jit(solution)/shard_map/ppermute | solution.py:372
  100.0 12.0 %collective-permute-start.32 = (bf16[24,1792]{1,0:T(8,128)(2,1)S(1)}, bf16[24,1792]{1,0:T(8,128)(2,1)S(1)}, u32[]{:S(2)}, u32[]{:S(2)}) collective-permute-start(bf16[24,1792]{1,0:T(8,128)(2,1)S(1)} %get-tuple-element.93), channel_id=1, source_target_pairs={{0,8},{4,12},{8,0},{12,4},{1,9},{5,13},{9,1},{13,5},{2,10},{6,14},... | collective-permute-start | bytes 258056 | tf_op jit(solution)/shard_map/ppermute | solution.py:372
  103.9 8.1 %collective-permute-start.33 = (bf16[24,1792]{1,0:T(8,128)(2,1)S(1)}, bf16[24,1792]{1,0:T(8,128)(2,1)S(1)}, u32[]{:S(2)}, u32[]{:S(2)}) collective-permute-start(bf16[24,1792]{1,0:T(8,128)(2,1)S(1)} %get-tuple-element.94), channel_id=1, source_target_pairs={{0,12},{4,8},{8,4},{12,0},{1,13},{5,9},{9,5},{13,1},{2,14},{6,10},... | collective-permute-start | bytes 258056 | tf_op jit(solution)/shard_map/ppermute | solution.py:372
  105.5 8.0 %collective-permute-start.34 = (bf16[24,1792]{1,0:T(8,128)(2,1)S(1)}, bf16[24,1792]{1,0:T(8,128)(2,1)S(1)}, u32[]{:S(2)}, u32[]{:S(2)}) collective-permute-start(bf16[24,1792]{1,0:T(8,128)(2,1)S(1)} %get-tuple-element.95), channel_id=1, source_target_pairs={{0,4},{4,0},{8,12},{12,8},{1,5},{5,1},{9,13},{13,9},{2,6},{6,2},{1... | collective-permute-start | bytes 258056 | tf_op jit(solution)/shard_map/ppermute | solution.py:372
  105.5 9.8 %collective-permute-start.35 = (bf16[24,1792]{1,0:T(8,128)(2,1)S(1)}, bf16[24,1792]{1,0:T(8,128)(2,1)S(1)}, u32[]{:S(2)}, u32[]{:S(2)}) collective-permute-start(bf16[24,1792]{1,0:T(8,128)(2,1)S(1)} %get-tuple-element.96), channel_id=1, source_target_pairs={{0,4},{4,0},{8,12},{12,8},{1,5},{5,1},{9,13},{13,9},{2,6},{6,2},{1... | collective-permute-start | bytes 258056 | tf_op jit(solution)/shard_map/ppermute | solution.py:372
  109.3 7.2 %collective-permute-start.31 = (bf16[24,1792]{1,0:T(8,128)(2,1)S(1)}, bf16[24,1792]{1,0:T(8,128)(2,1)S(1)}, u32[]{:S(2)}, u32[]{:S(2)}) collective-permute-start(bf16[24,1792]{1,0:T(8,128)(2,1)S(1)} %shard_map.82), channel_id=1, source_target_pairs={{0,4},{4,0},{8,12},{12,8},{1,5},{5,1},{9,13},{13,9},{2,6},{6,2},{1... | collective-permute-start | bytes 258056 | tf_op jit(solution)/shard_map/ppermute | solution.py:372
  (14 other events, 38.6 us)

commit v8 on v6

--- a/solution.py
+++ b/solution.py
@@ -174,11 +174,11 @@
         copy.wait()
 
 
-def load_down_kernel(z, group, down_proj, *refs):
+def load_down_kernel(z, experts, down_proj, *refs):
     outs, sems = refs[:-1], refs[-1]
     copies = []
-    for index in range(z.members):
-        rows = pl.ds((group * z.members + index) * z.units, z.units)
+    for index, expert in enumerate(experts):
+        rows = pl.ds(expert * z.units, z.units)
         copies.append(pltpu.make_async_copy(down_proj.at[0, rows, :], outs[index], sems.at[index]))
     for copy in copies:
         copy.start()
@@ -421,14 +421,14 @@
     def down(halves, group, hand_on):
         own = call(
             own_down_kernel, (z,), 4, [shape((z.group_each, z.width), F32)],
-            [VMEM] * (z.members + len(halves[0])), [], *tall[group], *halves[0],
+            [VMEM] * (z.members + len(halves[0])), [], *tall[group * z.members:(group + 1) * z.members], *halves[0],
         )[0]
         return call(
             down_kernel, (z, len(hand_on)), 4,
             (merged if group < z.pairs else [pay] * z.pieces)
             + [shape(value.shape, value.dtype) for value in hand_on],
             [VMEM] * (z.members + 1 + len(halves[1]) + len(hand_on)), [],
-            *tall[group], *halves[1], own, *hand_on,
+            *tall[group * z.members:(group + 1) * z.members], *halves[1], own, *hand_on,
         )
 
     routes = routes[0].transpose(0, 2, 1)
@@ -456,28 +456,29 @@
         [HBM], [pltpu.SemaphoreType.DMA((z.local * parts,))], gate_up, waits=[weight],
     )
 
-    def load_down(group, after):
+    def load_down(experts, after):
         return call(
-            load_down_kernel, (z, group), 1,
-            [pltpu.VMEM((z.units, z.width), BF16)] * z.members,
-            [HBM], [pltpu.SemaphoreType.DMA((z.members,))], down_proj, waits=[after],
+            load_down_kernel, (z, experts), 1,
+            [pltpu.VMEM((z.units, z.width), BF16)] * len(experts),
+            [HBM], [pltpu.SemaphoreType.DMA((len(experts),))], down_proj, waits=[after],
         )
 
-    tall = [load_down(0, wide[-1])]
+    early = z.local if z.groups == 1 else z.members + z.members // 2
+    tall = load_down(range(early), wide[-1])
     groups = range(z.groups)
     for tick in range(sections):
         last = tick == sections - 1
         sums, returned = [], []
         for group in groups:
-            own, other = products(received, group, [sums[-1][0]] if group else tall[0][:1])
+            own, other = products(received, group, [sums[-1][0]] if group else tall[:1])
             sums.append(pair_sums(own, other))
             if group == 0:
                 halves = activated(sums[0], [])
         for group in groups:
             if group and tick == 0:
-                tall.append(load_down(group, outgoing[0]))
+                tall += load_down(range(early, z.local), outgoing[0])
             if group:
-                halves = activated(sums[group], tall[group][:1] if tick == 0 else outgoing[:1])
+                halves = activated(sums[group], tall[-1:] if tick == 0 else outgoing[:1])
             hand_on = [routes] if tick == 0 and group == z.groups - 1 else []
             outgoing = down(halves, group, hand_on)
             if hand_on:

time: 112 us -> 111 us (level)
  waiting for transfers between devices: 28.4 us -> 26.9 us
  starting transfers between devices: 42.5 us -> 43.8 us
    ppermute x16, waiting for transfers between devices: 8.82 us -> 7.04 us  [swap(): return lax.ppermute(value, 'hidden', pairs)]
    ppermute x6, starting transfers between devices: 9.97 us -> 11.7 us  [across(): lax.ppermute(value, 'expert', [(i, i ^ step) for i in range(z.peers)])]
    ppermute x6, waiting for transfers between devices: 1.7 us -> 3.42 us  [across(): lax.ppermute(value, 'expert', [(i, i ^ step) for i in range(z.peers)])]
  transfers between devices with their start and end apart: 36 -> 36, of which waited for: 23 -> 24; matrix products, arithmetic and copies ran while one was open for 0% -> 0% of each run, Pallas kernels for 27% -> 27%
where the time goes in v8:
time: 111 us
  starting transfers between devices  43.8 us (39%)
  Pallas kernels  39.9 us (36%)
  waiting for transfers between devices  26.9 us (24%)
    pallas_call x29, Pallas kernels, call(): pl.pallas_call(functools.partial(after_waits, len(waits), functools.parti...  39.9 us
    ppermute x9, starting transfers between devices, exchanged(): result[step] = lax.ppermute(pieces[step], 'expert', pairs)  13.1 us
    ppermute x6, starting transfers between devices, across(): lax.ppermute(value, 'expert', [(i, i ^ step) for i in range(z.peers)])  11.7 us
    ppermute x16, waiting for transfers between devices, swap(): return lax.ppermute(value, 'hidden', pairs)  7.04 us
    ppermute x16, starting transfers between devices, swap(): return lax.ppermute(value, 'hidden', pairs)  6.89 us
    ppermute x9, waiting for transfers between devices, exchanged(): result[step] = lax.ppermute(pieces[step], 'expert', pairs)  6.67 us
    ppermute x1, starting transfers between devices, within(): return lax.ppermute(value, ('section', 'expert'), pairs)  5.76 us
    ppermute x1, waiting for transfers between devices, relayed(): rows = lax.ppermute(kept, 'section', hop)  5.28 us
  transfers between devices with their start and end apart: 36, of which 24 were waited for; matrix products, arithmetic and copies ran while one was open for 0% of the time, Pallas kernels for 27%

profile of v8, /device:TPU:2, one launch (start us, length us, event | category | flops | bytes accessed | tf_op | source)
XLA Modules:
  0.0 111.0 jit_solution(14010437163197792099)
XLA Ops:
  0.0 1.5 %shard_map.55 = (bf16[48,1792]{1,0:T(8,128)(2,1)S(1)}, bf16[48,1792]{1,0:T(8,128)(2,1)S(1)}, bf16[48,1792]{1,0:T(8,128)(2,1)S(1)}, bf16[48,1792]{1,0:T(8,128)(2,1)S(1)}, bf16[192,64]{1,0:T(8,128)(2,1)S(1)}) custom-call(s32[4,2,16]{2,1,0:T(2,128)} %bitcast.11, bf16[4,2,16]{2,1,0:T(2,128)(2,1)} %bitcast.14, bf16[64,1792]{1,0:T(8,128)(2,1)} %bitcast.8), custom_call_target="tpu_custom_call" | custom-call | tf_op jit(solution)/shard_map/pallas_call | solution.py:327
  1.5 2.6 %collective-permute-start = (bf16[48,1792]{1,0:T(8,128)(2,1)S(1)}, bf16[48,1792]{1,0:T(8,128)(2,1)S(1)}, u32[]{:S(2)}, u32[]{:S(2)}) collective-permute-start(bf16[48,1792]{1,0:T(8,128)(2,1)S(1)} %get-tuple-element.55), channel_id=1, source_target_pairs={{0,8},{4,12},{8,0},{12,4},{1,9},{5,13},{9,1},{13,5},{2,10},{6,14},... | collective-permute-start | bytes 516104 | tf_op jit(solution)/shard_map/ppermute | solution.py:359
  5.8 9.6 %shard_map.56 = (bf16[3584,1024]{1,0:T(8,128)(2,1)S(1)}, bf16[3584,1024]{1,0:T(8,128)(2,1)S(1)}, bf16[3584,1024]{1,0:T(8,128)(2,1)S(1)}, bf16[3584,1024]{1,0:T(8,128)(2,1)S(1)}) custom-call(bf16[192,64]{1,0:T(8,128)(2,1)S(1)} %get-tuple-element.49.refs_0_, bf16[1,1792,2,4096]{3,2,1,0:T(2,128)(2,1)} %refs_1_.3), custom_call_target="tpu_custom_call" | custom-call | tf_op jit(solution)/shard_map/pallas_call | solution.py:327
  15.4 4.2 %shard_map.57 = (bf16[1024,1792]{1,0:T(8,128)(2,1)S(1)}, bf16[1024,1792]{1,0:T(8,128)(2,1)S(1)}, bf16[1024,1792]{1,0:T(8,128)(2,1)S(1)}) custom-call(bf16[3584,1024]{1,0:T(8,128)(2,1)S(1)} %get-tuple-element.50.refs_0_.refs_2_, bf16[1,4096,1792]{2,1,0:T(8,128)(2,1)} %refs_1_.5), custom_call_target="tpu_custom_call" | custom-call | tf_op jit(solution)/shard_map/pallas_call | solution.py:327
  19.7 3.2 %shard_map.58 = (f32[112,1024]{1,0:T(8,128)S(1)}, bf16[56,1024]{1,0:T(8,128)(2,1)S(1)}, bf16[56,1024]{1,0:T(8,128)(2,1)S(1)}) custom-call(bf16[1024,1792]{1,0:T(8,128)(2,1)S(1)} %get-tuple-element.51.refs_0_, bf16[3584,1024]{1,0:T(8,128)(2,1)S(1)} %get-tuple-element.53.refs_1_, bf16[3584,1024]{1,0:T(8,128)(2,1)S(1)} %get-tuple-element.54.refs_2_, ...), custom_call_target="tpu_custom_call" | custom-call | tf_op jit(solution)/shard_map/pallas_call | solution.py:327
  24.5 1.6 %collective-permute-start.5 = (bf16[112,1024]{1,0:T(8,128)(2,1)S(1)}, bf16[112,1024]{1,0:T(8,128)(2,1)S(1)}, u32[]{:S(2)}, u32[]{:S(2)}) collective-permute-start(bf16[112,1024]{1,0:T(8,128)(2,1)S(1)} %shard_map.59.refs_0_), channel_id=1, source_target_pairs={{0,2},{1,3},{2,0},{3,1},{4,6},{5,7},{6,4},{7,5},{8,10},{9,11},{10,... | collective-permute-start | bytes 688136 | tf_op jit(solution)/shard_map/ppermute | solution.py:351
  26.1 3.2 %shard_map.65 = (f32[112,1024]{1,0:T(8,128)S(1)}, bf16[56,1024]{1,0:T(8,128)(2,1)S(1)}, bf16[56,1024]{1,0:T(8,128)(2,1)S(1)}) custom-call(bf16[112,1024]{1,0:T(8,128)(2,1)S(1)} %shard_map.59.refs_0_, bf16[3584,1024]{1,0:T(8,128)(2,1)S(1)} %get-tuple-element.66.refs_1_, bf16[3584,1024]{1,0:T(8,128)(2,1)S(1)} %get-tuple-element.50.refs_0_.refs_2_, ...), custom_call_target="tpu_custom_call" | custom-call | tf_op jit(solution)/shard_map/pallas_call | solution.py:327
  34.9 2.9 %collective-permute-start.8 = (bf16[48,1792]{1,0:T(8,128)(2,1)S(1)}, bf16[48,1792]{1,0:T(8,128)(2,1)S(1)}, u32[]{:S(2)}, u32[]{:S(2)}) collective-permute-start(bf16[48,1792]{1,0:T(8,128)(2,1)S(1)} %get-tuple-element.64), channel_id=1, source_target_pairs={{0,8},{4,12},{8,0},{12,4},{1,9},{5,13},{9,1},{13,5},{2,10},{6,14},... | collective-permute-start | bytes 516104 | tf_op jit(solution)/shard_map/ppermute | solution.py:363
  37.7 2.0 %shard_map.64.refs_0_.refs_1_ = bf16[1024,1792]{1,0:T(8,128)(2,1)S(1)} custom-call(bf16[24,1792]{1,0:T(8,128)(2,1)S(1)} %get-tuple-element.62.refs_0_.refs_3_, bf16[1,4096,1792]{2,1,0:T(8,128)(2,1)} %refs_1_.5), custom_call_target="tpu_custom_call" | custom-call | tf_op jit(solution)/shard_map/pallas_call | solution.py:327
  43.9 1.8 %collective-permute-start.15 = (bf16[24,1792]{1,0:T(8,128)(2,1)S(1)}, bf16[24,1792]{1,0:T(8,128)(2,1)S(1)}, u32[]{:S(2)}, u32[]{:S(2)}) collective-permute-start(bf16[24,1792]{1,0:T(8,128)(2,1)S(1)} %get-tuple-element.72), channel_id=1, source_target_pairs={{0,8},{4,12},{8,0},{12,4},{1,9},{5,13},{9,1},{13,5},{2,10},{6,14},... | collective-permute-start | bytes 258056 | tf_op jit(solution)/shard_map/ppermute | solution.py:359
  47.5 1.4 %collective-permute-done.7.refs_4_ = bf16[24,1792]{1,0:T(8,128)(2,1)S(1)} collective-permute-done((bf16[24,1792]{1,0:T(8,128)(2,1)S(1)}, bf16[24,1792]{1,0:T(8,128)(2,1)S(1)}, u32[]{:S(2)}, u32[]{:S(2)}) %collective-permute-start.7) | collective-permute-done | bytes 86048 | tf_op jit(solution)/shard_map/ppermute | solution.py:363
  48.9 2.4 %collective-permute-start.17 = (s32[4,2,16]{2,1,0:T(2,128)S(1)}, s32[4,2,16]{2,1,0:T(2,128)S(1)}, u32[]{:S(2)}, u32[]{:S(2)}) collective-permute-start(s32[4,2,16]{2,1,0:T(2,128)S(1)} %get-tuple-element.74), channel_id=1, source_target_pairs={{16,0},{17,1},{18,2},{19,3},{20,4},{21,5},{22,6},{23,7},{24,8},{25... | collective-permute-start | bytes 1544 | tf_op jit(solution)/shard_map/ppermute | solution.py:486
  59.5 5.3 %collective-permute-done.18.refs_1_ = bf16[64,1792]{1,0:T(8,128)(2,1)S(1)} collective-permute-done((bf16[64,1792]{1,0:T(8,128)(2,1)S(1)}, bf16[64,1792]{1,0:T(8,128)(2,1)S(1)}, u32[]{:S(2)}, u32[]{:S(2)}) %collective-permute-start.18) | collective-permute-done | bytes 229408 | tf_op jit(solution)/shard_map/ppermute | solution.py:380
  65.3 5.8 %collective-permute-start.21 = (bf16[48,1792]{1,0:T(8,128)(2,1)S(1)}, bf16[48,1792]{1,0:T(8,128)(2,1)S(1)}, u32[]{:S(2)}, u32[]{:S(2)}) collective-permute-start(bf16[48,1792]{1,0:T(8,128)(2,1)S(1)} %get-tuple-element.78), channel_id=1, source_target_pairs={{16,20},{20,16},{24,28},{28,24},{17,21},{21,17},{25,29},{29,25},{1... | collective-permute-start | bytes 516104 | tf_op jit(solution)/shard_map/ppermute | solution.py:376
  71.1 2.8 %collective-permute-done.19.refs_3_ = bf16[48,1792]{1,0:T(8,128)(2,1)S(1)} collective-permute-done((bf16[48,1792]{1,0:T(8,128)(2,1)S(1)}, bf16[48,1792]{1,0:T(8,128)(2,1)S(1)}, u32[]{:S(2)}, u32[]{:S(2)}) %collective-permute-start.19) | collective-permute-done | bytes 172064 | tf_op jit(solution)/shard_map/ppermute | solution.py:387
  74.3 3.2 %shard_map.72 = (f32[112,1024]{1,0:T(8,128)S(1)}, bf16[56,1024]{1,0:T(8,128)(2,1)S(1)}, bf16[56,1024]{1,0:T(8,128)(2,1)S(1)}) custom-call(bf16[1024,1792]{1,0:T(8,128)(2,1)S(1)} %get-tuple-element.51.refs_0_, bf16[3584,1024]{1,0:T(8,128)(2,1)S(1)} %get-tuple-element.53.refs_1_, bf16[3584,1024]{1,0:T(8,128)(2,1)S(1)} %get-tuple-element.54.refs_2_, ...), custom_call_target="tpu_custom_call" | custom-call | tf_op jit(solution)/shard_map/pallas_call | solution.py:327
  79.1 1.8 %collective-permute-start.24 = (bf16[112,1024]{1,0:T(8,128)(2,1)S(1)}, bf16[112,1024]{1,0:T(8,128)(2,1)S(1)}, u32[]{:S(2)}, u32[]{:S(2)}) collective-permute-start(bf16[112,1024]{1,0:T(8,128)(2,1)S(1)} %shard_map.73.refs_0_), channel_id=1, source_target_pairs={{0,2},{1,3},{2,0},{3,1},{4,6},{5,7},{6,4},{7,5},{8,10},{9,11},{10,... | collective-permute-start | bytes 688136 | tf_op jit(solution)/shard_map/ppermute | solution.py:351
  80.8 3.2 %shard_map.78 = (f32[112,1024]{1,0:T(8,128)S(1)}, bf16[56,1024]{1,0:T(8,128)(2,1)S(1)}, bf16[56,1024]{1,0:T(8,128)(2,1)S(1)}) custom-call(bf16[112,1024]{1,0:T(8,128)(2,1)S(1)} %shard_map.73.refs_0_, bf16[3584,1024]{1,0:T(8,128)(2,1)S(1)} %get-tuple-element.66.refs_1_, bf16[3584,1024]{1,0:T(8,128)(2,1)S(1)} %get-tuple-element.50.refs_0_.refs_2_, ...), custom_call_target="tpu_custom_call" | custom-call | tf_op jit(solution)/shard_map/pallas_call | solution.py:327
  89.4 4.0 %collective-permute-start.27 = (bf16[48,1792]{1,0:T(8,128)(2,1)S(1)}, bf16[48,1792]{1,0:T(8,128)(2,1)S(1)}, u32[]{:S(2)}, u32[]{:S(2)}) collective-permute-start(bf16[48,1792]{1,0:T(8,128)(2,1)S(1)} %get-tuple-element.85), channel_id=1, source_target_pairs={{0,8},{4,12},{8,0},{12,4},{1,9},{5,13},{9,1},{13,5},{2,10},{6,14},... | collective-permute-start | bytes 516104 | tf_op jit(solution)/shard_map/ppermute | solution.py:363
  93.8 3.5 %collective-permute-start.26 = (bf16[24,1792]{1,0:T(8,128)(2,1)S(1)}, bf16[24,1792]{1,0:T(8,128)(2,1)S(1)}, u32[]{:S(2)}, u32[]{:S(2)}) collective-permute-start(bf16[24,1792]{1,0:T(8,128)(2,1)S(1)} %get-tuple-element.84), channel_id=1, source_target_pairs={{0,4},{4,0},{8,12},{12,8},{1,5},{5,1},{9,13},{13,9},{2,6},{6,2},{1... | collective-permute-start | bytes 258056 | tf_op jit(solution)/shard_map/ppermute | solution.py:363
  99.6 1.9 %collective-permute-start.34 = (bf16[24,1792]{1,0:T(8,128)(2,1)S(1)}, bf16[24,1792]{1,0:T(8,128)(2,1)S(1)}, u32[]{:S(2)}, u32[]{:S(2)}) collective-permute-start(bf16[24,1792]{1,0:T(8,128)(2,1)S(1)} %get-tuple-element.91), channel_id=1, source_target_pairs={{0,8},{4,12},{8,0},{12,4},{1,9},{5,13},{9,1},{13,5},{2,10},{6,14},... | collective-permute-start | bytes 258056 | tf_op jit(solution)/shard_map/ppermute | solution.py:359
  101.5 2.0 %collective-permute-start.35 = (bf16[24,1792]{1,0:T(8,128)(2,1)S(1)}, bf16[24,1792]{1,0:T(8,128)(2,1)S(1)}, u32[]{:S(2)}, u32[]{:S(2)}) collective-permute-start(bf16[24,1792]{1,0:T(8,128)(2,1)S(1)} %get-tuple-element.92), channel_id=1, source_target_pairs={{0,12},{4,8},{8,4},{12,0},{1,13},{5,9},{9,5},{13,1},{2,14},{6,10},... | collective-permute-start | bytes 258056 | tf_op jit(solution)/shard_map/ppermute | solution.py:359
  103.6 1.4 %collective-permute-done.33.refs_8_ = bf16[24,1792]{1,0:T(8,128)(2,1)S(1)} collective-permute-done((bf16[24,1792]{1,0:T(8,128)(2,1)S(1)}, bf16[24,1792]{1,0:T(8,128)(2,1)S(1)}, u32[]{:S(2)}, u32[]{:S(2)}) %collective-permute-start.33) | collective-permute-done | bytes 86048 | tf_op jit(solution)/shard_map/ppermute | solution.py:359
  105.0 4.4 %collective-permute-done.34.refs_9_ = bf16[24,1792]{1,0:T(8,128)(2,1)S(1)} collective-permute-done((bf16[24,1792]{1,0:T(8,128)(2,1)S(1)}, bf16[24,1792]{1,0:T(8,128)(2,1)S(1)}, u32[]{:S(2)}, u32[]{:S(2)}) %collective-permute-start.34) | collective-permute-done | bytes 86048 | tf_op jit(solution)/shard_map/ppermute | solution.py:359
  (81 shorter events, 34.9 us)
Async XLA Ops:
  1.5 18.1 %collective-permute-start = (bf16[48,1792]{1,0:T(8,128)(2,1)S(1)}, bf16[48,1792]{1,0:T(8,128)(2,1)S(1)}, u32[]{:S(2)}, u32[]{:S(2)}) collective-permute-start(bf16[48,1792]{1,0:T(8,128)(2,1)S(1)} %get-tuple-element.55), channel_id=1, source_target_pairs={{0,8},{4,12},{8,0},{12,4},{1,9},{5,13},{9,1},{13,5},{2,10},{6,14},... | collective-permute-start | bytes 516104 | tf_op jit(solution)/shard_map/ppermute | solution.py:359
  4.2 15.5 %collective-permute-start.1 = (bf16[48,1792]{1,0:T(8,128)(2,1)S(1)}, bf16[48,1792]{1,0:T(8,128)(2,1)S(1)}, u32[]{:S(2)}, u32[]{:S(2)}) collective-permute-start(bf16[48,1792]{1,0:T(8,128)(2,1)S(1)} %get-tuple-element.56), channel_id=1, source_target_pairs={{0,12},{4,8},{8,4},{12,0},{1,13},{5,9},{9,5},{13,1},{2,14},{6,10},... | collective-permute-start | bytes 516104 | tf_op jit(solution)/shard_map/ppermute | solution.py:359
  5.5 14.1 %collective-permute-start.2 = (bf16[48,1792]{1,0:T(8,128)(2,1)S(1)}, bf16[48,1792]{1,0:T(8,128)(2,1)S(1)}, u32[]{:S(2)}, u32[]{:S(2)}) collective-permute-start(bf16[48,1792]{1,0:T(8,128)(2,1)S(1)} %get-tuple-element.57), channel_id=1, source_target_pairs={{0,4},{4,0},{8,12},{12,8},{1,5},{5,1},{9,13},{13,9},{2,6},{6,2},{1... | collective-permute-start | bytes 516104 | tf_op jit(solution)/shard_map/ppermute | solution.py:359
  24.5 7.9 %collective-permute-start.5 = (bf16[112,1024]{1,0:T(8,128)(2,1)S(1)}, bf16[112,1024]{1,0:T(8,128)(2,1)S(1)}, u32[]{:S(2)}, u32[]{:S(2)}) collective-permute-start(bf16[112,1024]{1,0:T(8,128)(2,1)S(1)} %shard_map.59.refs_0_), channel_id=1, source_target_pairs={{0,2},{1,3},{2,0},{3,1},{4,6},{5,7},{6,4},{7,5},{8,10},{9,11},{10,... | collective-permute-start | bytes 688136 | tf_op jit(solution)/shard_map/ppermute | solution.py:351
  30.9 9.0 %collective-permute-start.12 = (bf16[112,1024]{1,0:T(8,128)(2,1)S(1)}, bf16[112,1024]{1,0:T(8,128)(2,1)S(1)}, u32[]{:S(2)}, u32[]{:S(2)}) collective-permute-start(bf16[112,1024]{1,0:T(8,128)(2,1)S(1)} %shard_map.66.refs_1_), channel_id=1, source_target_pairs={{0,2},{1,3},{2,0},{3,1},{4,6},{5,7},{6,4},{7,5},{8,10},{9,11},{10,... | collective-permute-start | bytes 688136 | tf_op jit(solution)/shard_map/ppermute | solution.py:351
  34.9 12.2 %collective-permute-start.8 = (bf16[48,1792]{1,0:T(8,128)(2,1)S(1)}, bf16[48,1792]{1,0:T(8,128)(2,1)S(1)}, u32[]{:S(2)}, u32[]{:S(2)}) collective-permute-start(bf16[48,1792]{1,0:T(8,128)(2,1)S(1)} %get-tuple-element.64), channel_id=1, source_target_pairs={{0,8},{4,12},{8,0},{12,4},{1,9},{5,13},{9,1},{13,5},{2,10},{6,14},... | collective-permute-start | bytes 516104 | tf_op jit(solution)/shard_map/ppermute | solution.py:363
  40.1 8.9 %collective-permute-start.7 = (bf16[24,1792]{1,0:T(8,128)(2,1)S(1)}, bf16[24,1792]{1,0:T(8,128)(2,1)S(1)}, u32[]{:S(2)}, u32[]{:S(2)}) collective-permute-start(bf16[24,1792]{1,0:T(8,128)(2,1)S(1)} %get-tuple-element.63), channel_id=1, source_target_pairs={{0,4},{4,0},{8,12},{12,8},{1,5},{5,1},{9,13},{13,9},{2,6},{6,2},{1... | collective-permute-start | bytes 258056 | tf_op jit(solution)/shard_map/ppermute | solution.py:363
  42.6 10.8 %collective-permute-start.14 = (bf16[24,1792]{1,0:T(8,128)(2,1)S(1)}, bf16[24,1792]{1,0:T(8,128)(2,1)S(1)}, u32[]{:S(2)}, u32[]{:S(2)}) collective-permute-start(bf16[24,1792]{1,0:T(8,128)(2,1)S(1)} %get-tuple-element.71), channel_id=1, source_target_pairs={{0,4},{4,0},{8,12},{12,8},{1,5},{5,1},{9,13},{13,9},{2,6},{6,2},{1... | collective-permute-start | bytes 258056 | tf_op jit(solution)/shard_map/ppermute | solution.py:359
  43.9 9.6 %collective-permute-start.15 = (bf16[24,1792]{1,0:T(8,128)(2,1)S(1)}, bf16[24,1792]{1,0:T(8,128)(2,1)S(1)}, u32[]{:S(2)}, u32[]{:S(2)}) collective-permute-start(bf16[24,1792]{1,0:T(8,128)(2,1)S(1)} %get-tuple-element.72), channel_id=1, source_target_pairs={{0,8},{4,12},{8,0},{12,4},{1,9},{5,13},{9,1},{13,5},{2,10},{6,14},... | collective-permute-start | bytes 258056 | tf_op jit(solution)/shard_map/ppermute | solution.py:359
  45.7 7.8 %collective-permute-start.16 = (bf16[24,1792]{1,0:T(8,128)(2,1)S(1)}, bf16[24,1792]{1,0:T(8,128)(2,1)S(1)}, u32[]{:S(2)}, u32[]{:S(2)}) collective-permute-start(bf16[24,1792]{1,0:T(8,128)(2,1)S(1)} %get-tuple-element.73), channel_id=1, source_target_pairs={{0,12},{4,8},{8,4},{12,0},{1,13},{5,9},{9,5},{13,1},{2,14},{6,10},... | collective-permute-start | bytes 258056 | tf_op jit(solution)/shard_map/ppermute | solution.py:359
  47.1 7.8 %collective-permute-start.9 = (bf16[24,1792]{1,0:T(8,128)(2,1)S(1)}, bf16[24,1792]{1,0:T(8,128)(2,1)S(1)}, u32[]{:S(2)}, u32[]{:S(2)}) collective-permute-start(bf16[24,1792]{1,0:T(8,128)(2,1)S(1)} %shard_map.63), channel_id=1, source_target_pairs={{0,4},{4,0},{8,12},{12,8},{1,5},{5,1},{9,13},{13,9},{2,6},{6,2},{1... | collective-permute-start | bytes 258056 | tf_op jit(solution)/shard_map/ppermute | solution.py:363
  55.6 9.2 %collective-permute-start.18 = (bf16[64,1792]{1,0:T(8,128)(2,1)S(1)}, bf16[64,1792]{1,0:T(8,128)(2,1)S(1)}, u32[]{:S(2)}, u32[]{:S(2)}) collective-permute-start(bf16[64,1792]{1,0:T(8,128)(2,1)S(1)} %get-tuple-element.75.refs_2_), channel_id=1, source_target_pairs={{0,16},{1,17},{2,18},{3,19},{4,20},{5,21},{6,22},{7,23},{8,24},{9,... | collective-permute-start | bytes 688136 | tf_op jit(solution)/shard_map/ppermute | solution.py:380
  56.9 16.9 %collective-permute-start.19 = (bf16[48,1792]{1,0:T(8,128)(2,1)S(1)}, bf16[48,1792]{1,0:T(8,128)(2,1)S(1)}, u32[]{:S(2)}, u32[]{:S(2)}) collective-permute-start(bf16[48,1792]{1,0:T(8,128)(2,1)S(1)} %get-tuple-element.76), channel_id=1, source_target_pairs={{0,24},{4,28},{8,16},{12,20},{1,25},{5,29},{9,17},{13,21},{2,26},{... | collective-permute-start | bytes 516104 | tf_op jit(solution)/shard_map/ppermute | solution.py:387
  58.2 15.6 %collective-permute-start.20 = (bf16[48,1792]{1,0:T(8,128)(2,1)S(1)}, bf16[48,1792]{1,0:T(8,128)(2,1)S(1)}, u32[]{:S(2)}, u32[]{:S(2)}) collective-permute-start(bf16[48,1792]{1,0:T(8,128)(2,1)S(1)} %get-tuple-element.77), channel_id=1, source_target_pairs={{0,28},{4,24},{8,20},{12,16},{1,29},{5,25},{9,21},{13,17},{2,30},{... | collective-permute-start | bytes 516104 | tf_op jit(solution)/shard_map/ppermute | solution.py:387
  65.3 9.0 %collective-permute-start.21 = (bf16[48,1792]{1,0:T(8,128)(2,1)S(1)}, bf16[48,1792]{1,0:T(8,128)(2,1)S(1)}, u32[]{:S(2)}, u32[]{:S(2)}) collective-permute-start(bf16[48,1792]{1,0:T(8,128)(2,1)S(1)} %get-tuple-element.78), channel_id=1, source_target_pairs={{16,20},{20,16},{24,28},{28,24},{17,21},{21,17},{25,29},{29,25},{1... | collective-permute-start | bytes 516104 | tf_op jit(solution)/shard_map/ppermute | solution.py:376
  79.1 7.9 %collective-permute-start.24 = (bf16[112,1024]{1,0:T(8,128)(2,1)S(1)}, bf16[112,1024]{1,0:T(8,128)(2,1)S(1)}, u32[]{:S(2)}, u32[]{:S(2)}) collective-permute-start(bf16[112,1024]{1,0:T(8,128)(2,1)S(1)} %shard_map.73.refs_0_), channel_id=1, source_target_pairs={{0,2},{1,3},{2,0},{3,1},{4,6},{5,7},{6,4},{7,5},{8,10},{9,11},{10,... | collective-permute-start | bytes 688136 | tf_op jit(solution)/shard_map/ppermute | solution.py:351
  85.6 7.9 %collective-permute-start.31 = (bf16[112,1024]{1,0:T(8,128)(2,1)S(1)}, bf16[112,1024]{1,0:T(8,128)(2,1)S(1)}, u32[]{:S(2)}, u32[]{:S(2)}) collective-permute-start(bf16[112,1024]{1,0:T(8,128)(2,1)S(1)} %shard_map.79.refs_1_), channel_id=1, source_target_pairs={{0,2},{1,3},{2,0},{3,1},{4,6},{5,7},{6,4},{7,5},{8,10},{9,11},{10,... | collective-permute-start | bytes 688136 | tf_op jit(solution)/shard_map/ppermute | solution.py:351
  89.4 14.0 %collective-permute-start.27 = (bf16[48,1792]{1,0:T(8,128)(2,1)S(1)}, bf16[48,1792]{1,0:T(8,128)(2,1)S(1)}, u32[]{:S(2)}, u32[]{:S(2)}) collective-permute-start(bf16[48,1792]{1,0:T(8,128)(2,1)S(1)} %get-tuple-element.85), channel_id=1, source_target_pairs={{0,8},{4,12},{8,0},{12,4},{1,9},{5,13},{9,1},{13,5},{2,10},{6,14},... | collective-permute-start | bytes 516104 | tf_op jit(solution)/shard_map/ppermute | solution.py:363
  93.7 4.4 %collective-permute-start.32 = (bf16[96,512]{1,0:T(8,128)(2,1)S(1)}, bf16[96,512]{1,0:T(8,128)(2,1)S(1)}, u32[]{:S(2)}, u32[]{:S(2)}) collective-permute-start(bf16[96,512]{1,0:T(8,128)(2,1)S(1)} %shard_map.80.refs_2_), channel_id=1, source_target_pairs={{0,1},{1,0},{2,3},{3,2},{4,5},{5,4},{6,7},{7,6},{8,9},{9,8},{10,11... | collective-permute-start | bytes 294920 | tf_op jit(solution)/shard_map/ppermute | solution.py:351
  93.8 9.8 %collective-permute-start.26 = (bf16[24,1792]{1,0:T(8,128)(2,1)S(1)}, bf16[24,1792]{1,0:T(8,128)(2,1)S(1)}, u32[]{:S(2)}, u32[]{:S(2)}) collective-permute-start(bf16[24,1792]{1,0:T(8,128)(2,1)S(1)} %get-tuple-element.84), channel_id=1, source_target_pairs={{0,4},{4,0},{8,12},{12,8},{1,5},{5,1},{9,13},{13,9},{2,6},{6,2},{1... | collective-permute-start | bytes 258056 | tf_op jit(solution)/shard_map/ppermute | solution.py:363
  99.0 5.9 %collective-permute-start.33 = (bf16[24,1792]{1,0:T(8,128)(2,1)S(1)}, bf16[24,1792]{1,0:T(8,128)(2,1)S(1)}, u32[]{:S(2)}, u32[]{:S(2)}) collective-permute-start(bf16[24,1792]{1,0:T(8,128)(2,1)S(1)} %get-tuple-element.90), channel_id=1, source_target_pairs={{0,4},{4,0},{8,12},{12,8},{1,5},{5,1},{9,13},{13,9},{2,6},{6,2},{1... | collective-permute-start | bytes 258056 | tf_op jit(solution)/shard_map/ppermute | solution.py:359
  99.6 9.8 %collective-permute-start.34 = (bf16[24,1792]{1,0:T(8,128)(2,1)S(1)}, bf16[24,1792]{1,0:T(8,128)(2,1)S(1)}, u32[]{:S(2)}, u32[]{:S(2)}) collective-permute-start(bf16[24,1792]{1,0:T(8,128)(2,1)S(1)} %get-tuple-element.91), channel_id=1, source_target_pairs={{0,8},{4,12},{8,0},{12,4},{1,9},{5,13},{9,1},{13,5},{2,10},{6,14},... | collective-permute-start | bytes 258056 | tf_op jit(solution)/shard_map/ppermute | solution.py:359
  101.5 7.9 %collective-permute-start.35 = (bf16[24,1792]{1,0:T(8,128)(2,1)S(1)}, bf16[24,1792]{1,0:T(8,128)(2,1)S(1)}, u32[]{:S(2)}, u32[]{:S(2)}) collective-permute-start(bf16[24,1792]{1,0:T(8,128)(2,1)S(1)} %get-tuple-element.92), channel_id=1, source_target_pairs={{0,12},{4,8},{8,4},{12,0},{1,13},{5,9},{9,5},{13,1},{2,14},{6,10},... | collective-permute-start | bytes 258056 | tf_op jit(solution)/shard_map/ppermute | solution.py:359
  103.5 6.5 %collective-permute-start.28 = (bf16[24,1792]{1,0:T(8,128)(2,1)S(1)}, bf16[24,1792]{1,0:T(8,128)(2,1)S(1)}, u32[]{:S(2)}, u32[]{:S(2)}) collective-permute-start(bf16[24,1792]{1,0:T(8,128)(2,1)S(1)} %shard_map.77), channel_id=1, source_target_pairs={{0,4},{4,0},{8,12},{12,8},{1,5},{5,1},{9,13},{13,9},{2,6},{6,2},{1... | collective-permute-start | bytes 258056 | tf_op jit(solution)/shard_map/ppermute | solution.py:363
  (14 other events, 35.4 us)

commit v9 on v6

--- a/solution.py
+++ b/solution.py
@@ -247,7 +247,7 @@
 def pair_kernel(z, own, *refs):
     *other, out = refs
     products, sums = joined(z, [own[...], jnp.concatenate([ref[...].astype(F32) for ref in other], axis=0)])
-    sums = split_sums(jnp.broadcast_to(sums, (EXTRA, 2 * z.half)), 2 * z.half)
+    sums = split_sums(jnp.broadcast_to(sums, (EXTRA // 2, 2 * z.half)), 2 * z.half)
     out[...] = jnp.concatenate([products, sums], axis=0).astype(BF16)
 
 
@@ -406,7 +406,7 @@
 
     def pair_sums(own, other):
         pair = call(
-            pair_kernel, (z,), 2, [shape(z.partial, BF16)], [VMEM] * (1 + CUTS), [], own, *other
+            pair_kernel, (z,), 2, [shape((z.group_each + EXTRA // 2, 2 * z.half), BF16)], [VMEM] * (1 + CUTS), [], own, *other
         )[0]
         return [pair] + [swap(pair, step) for step in range(2, z.splits, 2)]
 

time: 112 us -> 113 us (level)
  Pallas kernels: 40 us -> 42.7 us
  waiting for transfers between devices: 28.4 us -> 26.5 us
    pallas_call x29, Pallas kernels: 40 us -> 42.7 us  [call(): pl.pallas_call(functools.partial(after_waits, len(waits), functools.parti...]
    ppermute x16, waiting for transfers between devices: 8.82 us -> 6.96 us  [swap(): return lax.ppermute(value, 'hidden', pairs)]
  transfers between devices with their start and end apart: 36 -> 36, of which waited for: 23 -> 22; matrix products, arithmetic and copies ran while one was open for 0% -> 0% of each run, Pallas kernels for 27% -> 29%
where the time goes in v9:
time: 113 us; the launch traced here: 112 us
  starting transfers between devices  42.8 us (38%)
  Pallas kernels  42.7 us (38%)
  waiting for transfers between devices  26.5 us (23%)
    pallas_call x29, Pallas kernels, call(): pl.pallas_call(functools.partial(after_waits, len(waits), functools.parti...  42.7 us
    ppermute x9, starting transfers between devices, exchanged(): result[step] = lax.ppermute(pieces[step], 'expert', pairs)  13.1 us
    ppermute x6, starting transfers between devices, across(): lax.ppermute(value, 'expert', [(i, i ^ step) for i in range(z.peers)])  10.3 us
    ppermute x9, waiting for transfers between devices, exchanged(): result[step] = lax.ppermute(pieces[step], 'expert', pairs)  8 us
    ppermute x16, waiting for transfers between devices, swap(): return lax.ppermute(value, 'hidden', pairs)  6.96 us
    ppermute x16, starting transfers between devices, swap(): return lax.ppermute(value, 'hidden', pairs)  6.88 us
    ppermute x1, starting transfers between devices, within(): return lax.ppermute(value, ('section', 'expert'), pairs)  6.23 us
    ppermute x1, waiting for transfers between devices, relayed(): rows = lax.ppermute(kept, 'section', hop)  5.7 us
  transfers between devices with their start and end apart: 36, of which 22 were waited for; matrix products, arithmetic and copies ran while one was open for 0% of the time, Pallas kernels for 29%

profile of v9, /device:TPU:2, one launch (start us, length us, event | category | flops | bytes accessed | tf_op | source)
XLA Modules:
  0.0 112.4 jit_solution(14354154205698477587)
XLA Ops:
  0.0 1.5 %shard_map.55 = (bf16[48,1792]{1,0:T(8,128)(2,1)S(1)}, bf16[48,1792]{1,0:T(8,128)(2,1)S(1)}, bf16[48,1792]{1,0:T(8,128)(2,1)S(1)}, bf16[48,1792]{1,0:T(8,128)(2,1)S(1)}, bf16[192,64]{1,0:T(8,128)(2,1)S(1)}) custom-call(s32[4,2,16]{2,1,0:T(2,128)} %bitcast.13, bf16[4,2,16]{2,1,0:T(2,128)(2,1)} %bitcast.16, bf16[64,1792]{1,0:T(8,128)(2,1)} %bitcast.10), custom_call_target="tpu_custom_call" | custom-call | tf_op jit(solution)/shard_map/pallas_call | solution.py:327
  1.5 2.6 %collective-permute-start = (bf16[48,1792]{1,0:T(8,128)(2,1)S(1)}, bf16[48,1792]{1,0:T(8,128)(2,1)S(1)}, u32[]{:S(2)}, u32[]{:S(2)}) collective-permute-start(bf16[48,1792]{1,0:T(8,128)(2,1)S(1)} %get-tuple-element.56), channel_id=1, source_target_pairs={{0,8},{4,12},{8,0},{12,4},{1,9},{5,13},{9,1},{13,5},{2,10},{6,14},... | collective-permute-start | bytes 516104 | tf_op jit(solution)/shard_map/ppermute | solution.py:359
  5.8 9.6 %shard_map.56 = (bf16[3584,1024]{1,0:T(8,128)(2,1)S(1)}, bf16[3584,1024]{1,0:T(8,128)(2,1)S(1)}, bf16[3584,1024]{1,0:T(8,128)(2,1)S(1)}, bf16[3584,1024]{1,0:T(8,128)(2,1)S(1)}) custom-call(bf16[192,64]{1,0:T(8,128)(2,1)S(1)} %get-tuple-element.50.refs_0_, bf16[1,1792,2,4096]{3,2,1,0:T(2,128)(2,1)} %refs_1_.3), custom_call_target="tpu_custom_call" | custom-call | tf_op jit(solution)/shard_map/pallas_call | solution.py:327
  15.4 5.8 %shard_map.57 = (bf16[1024,1792]{1,0:T(8,128)(2,1)S(1)}, bf16[1024,1792]{1,0:T(8,128)(2,1)S(1)}) custom-call(bf16[3584,1024]{1,0:T(8,128)(2,1)S(1)} %get-tuple-element.51.refs_0_.refs_2_, bf16[1,4096,1792]{2,1,0:T(8,128)(2,1)} %refs_1_.5), custom_call_target="tpu_custom_call" | custom-call | tf_op jit(solution)/shard_map/pallas_call | solution.py:327
  21.3 3.2 %shard_map.58 = (f32[112,1024]{1,0:T(8,128)S(1)}, bf16[56,1024]{1,0:T(8,128)(2,1)S(1)}, bf16[56,1024]{1,0:T(8,128)(2,1)S(1)}) custom-call(bf16[1024,1792]{1,0:T(8,128)(2,1)S(1)} %get-tuple-element.52.refs_0_, bf16[3584,1024]{1,0:T(8,128)(2,1)S(1)} %get-tuple-element.54.refs_1_, bf16[3584,1024]{1,0:T(8,128)(2,1)S(1)} %get-tuple-element.55.refs_2_, ...), custom_call_target="tpu_custom_call" | custom-call | tf_op jit(solution)/shard_map/pallas_call | solution.py:327
  26.1 1.6 %collective-permute-start.5 = (bf16[104,1024]{1,0:T(8,128)(2,1)S(1)}, bf16[104,1024]{1,0:T(8,128)(2,1)S(1)}, u32[]{:S(2)}, u32[]{:S(2)}) collective-permute-start(bf16[104,1024]{1,0:T(8,128)(2,1)S(1)} %shard_map.59.refs_0_), channel_id=1, source_target_pairs={{0,2},{1,3},{2,0},{3,1},{4,6},{5,7},{6,4},{7,5},{8,10},{9,11},{10,... | collective-permute-start | bytes 638984 | tf_op jit(solution)/shard_map/ppermute | solution.py:351
  27.7 3.2 %shard_map.65 = (f32[112,1024]{1,0:T(8,128)S(1)}, bf16[56,1024]{1,0:T(8,128)(2,1)S(1)}, bf16[56,1024]{1,0:T(8,128)(2,1)S(1)}) custom-call(bf16[104,1024]{1,0:T(8,128)(2,1)S(1)} %shard_map.59.refs_0_, bf16[3584,1024]{1,0:T(8,128)(2,1)S(1)} %get-tuple-element.68.refs_1_, bf16[3584,1024]{1,0:T(8,128)(2,1)S(1)} %get-tuple-element.51.refs_0_.refs_2_, ...), custom_call_target="tpu_custom_call" | custom-call | tf_op jit(solution)/shard_map/pallas_call | solution.py:327
  36.1 2.9 %collective-permute-start.8 = (bf16[48,1792]{1,0:T(8,128)(2,1)S(1)}, bf16[48,1792]{1,0:T(8,128)(2,1)S(1)}, u32[]{:S(2)}, u32[]{:S(2)}) collective-permute-start(bf16[48,1792]{1,0:T(8,128)(2,1)S(1)} %get-tuple-element.65), channel_id=1, source_target_pairs={{0,8},{4,12},{8,0},{12,4},{1,9},{5,13},{9,1},{13,5},{2,10},{6,14},... | collective-permute-start | bytes 516104 | tf_op jit(solution)/shard_map/ppermute | solution.py:363
  39.0 3.2 %shard_map.64 = (bf16[1024,1792]{1,0:T(8,128)(2,1)S(1)}, bf16[1024,1792]{1,0:T(8,128)(2,1)S(1)}) custom-call(bf16[24,1792]{1,0:T(8,128)(2,1)S(1)} %get-tuple-element.63.refs_0_.refs_3_, bf16[1,4096,1792]{2,1,0:T(8,128)(2,1)} %refs_1_.5), custom_call_target="tpu_custom_call" | custom-call | tf_op jit(solution)/shard_map/pallas_call | solution.py:327
  47.0 2.4 %collective-permute-start.16 = (bf16[24,1792]{1,0:T(8,128)(2,1)S(1)}, bf16[24,1792]{1,0:T(8,128)(2,1)S(1)}, u32[]{:S(2)}, u32[]{:S(2)}) collective-permute-start(bf16[24,1792]{1,0:T(8,128)(2,1)S(1)} %get-tuple-element.75), channel_id=1, source_target_pairs={{0,12},{4,8},{8,4},{12,0},{1,13},{5,9},{9,5},{13,1},{2,14},{6,10},... | collective-permute-start | bytes 258056 | tf_op jit(solution)/shard_map/ppermute | solution.py:359
  49.9 2.4 %collective-permute-start.17 = (s32[4,2,16]{2,1,0:T(2,128)S(1)}, s32[4,2,16]{2,1,0:T(2,128)S(1)}, u32[]{:S(2)}, u32[]{:S(2)}) collective-permute-start(s32[4,2,16]{2,1,0:T(2,128)S(1)} %get-tuple-element.76), channel_id=1, source_target_pairs={{16,0},{17,1},{18,2},{19,3},{20,4},{21,5},{22,6},{23,7},{24,8},{25... | collective-permute-start | bytes 1544 | tf_op jit(solution)/shard_map/ppermute | solution.py:485
  53.7 2.2 %collective-permute-done.15.refs_9_ = bf16[24,1792]{1,0:T(8,128)(2,1)S(1)} collective-permute-done((bf16[24,1792]{1,0:T(8,128)(2,1)S(1)}, bf16[24,1792]{1,0:T(8,128)(2,1)S(1)}, u32[]{:S(2)}, u32[]{:S(2)}) %collective-permute-start.15) | collective-permute-done | bytes 86048 | tf_op jit(solution)/shard_map/ppermute | solution.py:359
  61.2 5.7 %collective-permute-done.18.refs_1_ = bf16[64,1792]{1,0:T(8,128)(2,1)S(1)} collective-permute-done((bf16[64,1792]{1,0:T(8,128)(2,1)S(1)}, bf16[64,1792]{1,0:T(8,128)(2,1)S(1)}, u32[]{:S(2)}, u32[]{:S(2)}) %collective-permute-start.18) | collective-permute-done | bytes 229408 | tf_op jit(solution)/shard_map/ppermute | solution.py:380
  67.4 6.2 %collective-permute-start.21 = (bf16[48,1792]{1,0:T(8,128)(2,1)S(1)}, bf16[48,1792]{1,0:T(8,128)(2,1)S(1)}, u32[]{:S(2)}, u32[]{:S(2)}) collective-permute-start(bf16[48,1792]{1,0:T(8,128)(2,1)S(1)} %get-tuple-element.80), channel_id=1, source_target_pairs={{16,20},{20,16},{24,28},{28,24},{17,21},{21,17},{25,29},{29,25},{1... | collective-permute-start | bytes 516104 | tf_op jit(solution)/shard_map/ppermute | solution.py:376
  73.7 2.6 %collective-permute-done.19.refs_3_ = bf16[48,1792]{1,0:T(8,128)(2,1)S(1)} collective-permute-done((bf16[48,1792]{1,0:T(8,128)(2,1)S(1)}, bf16[48,1792]{1,0:T(8,128)(2,1)S(1)}, u32[]{:S(2)}, u32[]{:S(2)}) %collective-permute-start.19) | collective-permute-done | bytes 172064 | tf_op jit(solution)/shard_map/ppermute | solution.py:387
  76.9 3.2 %shard_map.72 = (f32[112,1024]{1,0:T(8,128)S(1)}, bf16[56,1024]{1,0:T(8,128)(2,1)S(1)}, bf16[56,1024]{1,0:T(8,128)(2,1)S(1)}) custom-call(bf16[1024,1792]{1,0:T(8,128)(2,1)S(1)} %get-tuple-element.52.refs_0_, bf16[3584,1024]{1,0:T(8,128)(2,1)S(1)} %get-tuple-element.54.refs_1_, bf16[3584,1024]{1,0:T(8,128)(2,1)S(1)} %bitcast.9, ...), custom_call_target="tpu_custom_call" | custom-call | tf_op jit(solution)/shard_map/pallas_call | solution.py:327
  81.7 1.6 %collective-permute-start.24 = (bf16[104,1024]{1,0:T(8,128)(2,1)S(1)}, bf16[104,1024]{1,0:T(8,128)(2,1)S(1)}, u32[]{:S(2)}, u32[]{:S(2)}) collective-permute-start(bf16[104,1024]{1,0:T(8,128)(2,1)S(1)} %shard_map.73.refs_0_), channel_id=1, source_target_pairs={{0,2},{1,3},{2,0},{3,1},{4,6},{5,7},{6,4},{7,5},{8,10},{9,11},{10,... | collective-permute-start | bytes 638984 | tf_op jit(solution)/shard_map/ppermute | solution.py:351
  83.3 3.2 %shard_map.78 = (f32[112,1024]{1,0:T(8,128)S(1)}, bf16[56,1024]{1,0:T(8,128)(2,1)S(1)}, bf16[56,1024]{1,0:T(8,128)(2,1)S(1)}) custom-call(bf16[104,1024]{1,0:T(8,128)(2,1)S(1)} %shard_map.73.refs_0_, bf16[3584,1024]{1,0:T(8,128)(2,1)S(1)} %get-tuple-element.68.refs_1_, bf16[3584,1024]{1,0:T(8,128)(2,1)S(1)} %get-tuple-element.51.refs_0_.refs_2_, ...), custom_call_target="tpu_custom_call" | custom-call | tf_op jit(solution)/shard_map/pallas_call | solution.py:327
  91.7 3.2 %collective-permute-start.27 = (bf16[48,1792]{1,0:T(8,128)(2,1)S(1)}, bf16[48,1792]{1,0:T(8,128)(2,1)S(1)}, u32[]{:S(2)}, u32[]{:S(2)}) collective-permute-start(bf16[48,1792]{1,0:T(8,128)(2,1)S(1)} %get-tuple-element.87), channel_id=1, source_target_pairs={{0,8},{4,12},{8,0},{12,4},{1,9},{5,13},{9,1},{13,5},{2,10},{6,14},... | collective-permute-start | bytes 516104 | tf_op jit(solution)/shard_map/ppermute | solution.py:363
  95.9 2.9 %collective-permute-start.26 = (bf16[24,1792]{1,0:T(8,128)(2,1)S(1)}, bf16[24,1792]{1,0:T(8,128)(2,1)S(1)}, u32[]{:S(2)}, u32[]{:S(2)}) collective-permute-start(bf16[24,1792]{1,0:T(8,128)(2,1)S(1)} %get-tuple-element.86), channel_id=1, source_target_pairs={{0,4},{4,0},{8,12},{12,8},{1,5},{5,1},{9,13},{13,9},{2,6},{6,2},{1... | collective-permute-start | bytes 258056 | tf_op jit(solution)/shard_map/ppermute | solution.py:363
  101.0 1.9 %collective-permute-start.34 = (bf16[24,1792]{1,0:T(8,128)(2,1)S(1)}, bf16[24,1792]{1,0:T(8,128)(2,1)S(1)}, u32[]{:S(2)}, u32[]{:S(2)}) collective-permute-start(bf16[24,1792]{1,0:T(8,128)(2,1)S(1)} %get-tuple-element.93), channel_id=1, source_target_pairs={{0,8},{4,12},{8,0},{12,4},{1,9},{5,13},{9,1},{13,5},{2,10},{6,14},... | collective-permute-start | bytes 258056 | tf_op jit(solution)/shard_map/ppermute | solution.py:359
  102.9 2.0 %collective-permute-start.35 = (bf16[24,1792]{1,0:T(8,128)(2,1)S(1)}, bf16[24,1792]{1,0:T(8,128)(2,1)S(1)}, u32[]{:S(2)}, u32[]{:S(2)}) collective-permute-start(bf16[24,1792]{1,0:T(8,128)(2,1)S(1)} %get-tuple-element.94), channel_id=1, source_target_pairs={{0,12},{4,8},{8,4},{12,0},{1,13},{5,9},{9,5},{13,1},{2,14},{6,10},... | collective-permute-start | bytes 258056 | tf_op jit(solution)/shard_map/ppermute | solution.py:359
  105.0 1.5 %collective-permute-done.33.refs_8_ = bf16[24,1792]{1,0:T(8,128)(2,1)S(1)} collective-permute-done((bf16[24,1792]{1,0:T(8,128)(2,1)S(1)}, bf16[24,1792]{1,0:T(8,128)(2,1)S(1)}, u32[]{:S(2)}, u32[]{:S(2)}) %collective-permute-start.33) | collective-permute-done | bytes 86048 | tf_op jit(solution)/shard_map/ppermute | solution.py:359
  106.5 4.3 %collective-permute-done.34.refs_9_ = bf16[24,1792]{1,0:T(8,128)(2,1)S(1)} collective-permute-done((bf16[24,1792]{1,0:T(8,128)(2,1)S(1)}, bf16[24,1792]{1,0:T(8,128)(2,1)S(1)}, u32[]{:S(2)}, u32[]{:S(2)}) %collective-permute-start.34) | collective-permute-done | bytes 86048 | tf_op jit(solution)/shard_map/ppermute | solution.py:359
  (88 shorter events, 33.2 us)
Async XLA Ops:
  1.5 19.7 %collective-permute-start = (bf16[48,1792]{1,0:T(8,128)(2,1)S(1)}, bf16[48,1792]{1,0:T(8,128)(2,1)S(1)}, u32[]{:S(2)}, u32[]{:S(2)}) collective-permute-start(bf16[48,1792]{1,0:T(8,128)(2,1)S(1)} %get-tuple-element.56), channel_id=1, source_target_pairs={{0,8},{4,12},{8,0},{12,4},{1,9},{5,13},{9,1},{13,5},{2,10},{6,14},... | collective-permute-start | bytes 516104 | tf_op jit(solution)/shard_map/ppermute | solution.py:359
  4.2 17.1 %collective-permute-start.1 = (bf16[48,1792]{1,0:T(8,128)(2,1)S(1)}, bf16[48,1792]{1,0:T(8,128)(2,1)S(1)}, u32[]{:S(2)}, u32[]{:S(2)}) collective-permute-start(bf16[48,1792]{1,0:T(8,128)(2,1)S(1)} %get-tuple-element.57), channel_id=1, source_target_pairs={{0,12},{4,8},{8,4},{12,0},{1,13},{5,9},{9,5},{13,1},{2,14},{6,10},... | collective-permute-start | bytes 516104 | tf_op jit(solution)/shard_map/ppermute | solution.py:359
  5.5 15.7 %collective-permute-start.2 = (bf16[48,1792]{1,0:T(8,128)(2,1)S(1)}, bf16[48,1792]{1,0:T(8,128)(2,1)S(1)}, u32[]{:S(2)}, u32[]{:S(2)}) collective-permute-start(bf16[48,1792]{1,0:T(8,128)(2,1)S(1)} %get-tuple-element.58), channel_id=1, source_target_pairs={{0,4},{4,0},{8,12},{12,8},{1,5},{5,1},{9,13},{13,9},{2,6},{6,2},{1... | collective-permute-start | bytes 516104 | tf_op jit(solution)/shard_map/ppermute | solution.py:359
  26.1 7.6 %collective-permute-start.5 = (bf16[104,1024]{1,0:T(8,128)(2,1)S(1)}, bf16[104,1024]{1,0:T(8,128)(2,1)S(1)}, u32[]{:S(2)}, u32[]{:S(2)}) collective-permute-start(bf16[104,1024]{1,0:T(8,128)(2,1)S(1)} %shard_map.59.refs_0_), channel_id=1, source_target_pairs={{0,2},{1,3},{2,0},{3,1},{4,6},{5,7},{6,4},{7,5},{8,10},{9,11},{10,... | collective-permute-start | bytes 638984 | tf_op jit(solution)/shard_map/ppermute | solution.py:351
  32.5 9.7 %collective-permute-start.12 = (bf16[104,1024]{1,0:T(8,128)(2,1)S(1)}, bf16[104,1024]{1,0:T(8,128)(2,1)S(1)}, u32[]{:S(2)}, u32[]{:S(2)}) collective-permute-start(bf16[104,1024]{1,0:T(8,128)(2,1)S(1)} %shard_map.66.refs_1_), channel_id=1, source_target_pairs={{0,2},{1,3},{2,0},{3,1},{4,6},{5,7},{6,4},{7,5},{8,10},{9,11},{10,... | collective-permute-start | bytes 638984 | tf_op jit(solution)/shard_map/ppermute | solution.py:351
  36.1 13.3 %collective-permute-start.8 = (bf16[48,1792]{1,0:T(8,128)(2,1)S(1)}, bf16[48,1792]{1,0:T(8,128)(2,1)S(1)}, u32[]{:S(2)}, u32[]{:S(2)}) collective-permute-start(bf16[48,1792]{1,0:T(8,128)(2,1)S(1)} %get-tuple-element.65), channel_id=1, source_target_pairs={{0,8},{4,12},{8,0},{12,4},{1,9},{5,13},{9,1},{13,5},{2,10},{6,14},... | collective-permute-start | bytes 516104 | tf_op jit(solution)/shard_map/ppermute | solution.py:363
  42.5 7.5 %collective-permute-start.7 = (bf16[24,1792]{1,0:T(8,128)(2,1)S(1)}, bf16[24,1792]{1,0:T(8,128)(2,1)S(1)}, u32[]{:S(2)}, u32[]{:S(2)}) collective-permute-start(bf16[24,1792]{1,0:T(8,128)(2,1)S(1)} %get-tuple-element.64), channel_id=1, source_target_pairs={{0,4},{4,0},{8,12},{12,8},{1,5},{5,1},{9,13},{13,9},{2,6},{6,2},{1... | collective-permute-start | bytes 258056 | tf_op jit(solution)/shard_map/ppermute | solution.py:363
  45.0 8.7 %collective-permute-start.14 = (bf16[24,1792]{1,0:T(8,128)(2,1)S(1)}, bf16[24,1792]{1,0:T(8,128)(2,1)S(1)}, u32[]{:S(2)}, u32[]{:S(2)}) collective-permute-start(bf16[24,1792]{1,0:T(8,128)(2,1)S(1)} %get-tuple-element.73), channel_id=1, source_target_pairs={{0,4},{4,0},{8,12},{12,8},{1,5},{5,1},{9,13},{13,9},{2,6},{6,2},{1... | collective-permute-start | bytes 258056 | tf_op jit(solution)/shard_map/ppermute | solution.py:359
  46.4 9.5 %collective-permute-start.15 = (bf16[24,1792]{1,0:T(8,128)(2,1)S(1)}, bf16[24,1792]{1,0:T(8,128)(2,1)S(1)}, u32[]{:S(2)}, u32[]{:S(2)}) collective-permute-start(bf16[24,1792]{1,0:T(8,128)(2,1)S(1)} %get-tuple-element.74), channel_id=1, source_target_pairs={{0,8},{4,12},{8,0},{12,4},{1,9},{5,13},{9,1},{13,5},{2,10},{6,14},... | collective-permute-start | bytes 258056 | tf_op jit(solution)/shard_map/ppermute | solution.py:359
  47.0 8.9 %collective-permute-start.16 = (bf16[24,1792]{1,0:T(8,128)(2,1)S(1)}, bf16[24,1792]{1,0:T(8,128)(2,1)S(1)}, u32[]{:S(2)}, u32[]{:S(2)}) collective-permute-start(bf16[24,1792]{1,0:T(8,128)(2,1)S(1)} %get-tuple-element.75), channel_id=1, source_target_pairs={{0,12},{4,8},{8,4},{12,0},{1,13},{5,9},{9,5},{13,1},{2,14},{6,10},... | collective-permute-start | bytes 258056 | tf_op jit(solution)/shard_map/ppermute | solution.py:359
  49.4 7.2 %collective-permute-start.9 = (bf16[24,1792]{1,0:T(8,128)(2,1)S(1)}, bf16[24,1792]{1,0:T(8,128)(2,1)S(1)}, u32[]{:S(2)}, u32[]{:S(2)}) collective-permute-start(bf16[24,1792]{1,0:T(8,128)(2,1)S(1)} %shard_map.63), channel_id=1, source_target_pairs={{0,4},{4,0},{8,12},{12,8},{1,5},{5,1},{9,13},{13,9},{2,6},{6,2},{1... | collective-permute-start | bytes 258056 | tf_op jit(solution)/shard_map/ppermute | solution.py:363
  49.9 3.8 %collective-permute-start.17 = (s32[4,2,16]{2,1,0:T(2,128)S(1)}, s32[4,2,16]{2,1,0:T(2,128)S(1)}, u32[]{:S(2)}, u32[]{:S(2)}) collective-permute-start(s32[4,2,16]{2,1,0:T(2,128)S(1)} %get-tuple-element.76), channel_id=1, source_target_pairs={{16,0},{17,1},{18,2},{19,3},{20,4},{21,5},{22,6},{23,7},{24,8},{25... | collective-permute-start | bytes 1544 | tf_op jit(solution)/shard_map/ppermute | solution.py:485
  57.3 9.6 %collective-permute-start.18 = (bf16[64,1792]{1,0:T(8,128)(2,1)S(1)}, bf16[64,1792]{1,0:T(8,128)(2,1)S(1)}, u32[]{:S(2)}, u32[]{:S(2)}) collective-permute-start(bf16[64,1792]{1,0:T(8,128)(2,1)S(1)} %get-tuple-element.77.refs_2_), channel_id=1, source_target_pairs={{0,16},{1,17},{2,18},{3,19},{4,20},{5,21},{6,22},{7,23},{8,24},{9,... | collective-permute-start | bytes 688136 | tf_op jit(solution)/shard_map/ppermute | solution.py:380
  58.6 17.6 %collective-permute-start.19 = (bf16[48,1792]{1,0:T(8,128)(2,1)S(1)}, bf16[48,1792]{1,0:T(8,128)(2,1)S(1)}, u32[]{:S(2)}, u32[]{:S(2)}) collective-permute-start(bf16[48,1792]{1,0:T(8,128)(2,1)S(1)} %get-tuple-element.78), channel_id=1, source_target_pairs={{0,24},{4,28},{8,16},{12,20},{1,25},{5,29},{9,17},{13,21},{2,26},{... | collective-permute-start | bytes 516104 | tf_op jit(solution)/shard_map/ppermute | solution.py:387
  59.9 16.3 %collective-permute-start.20 = (bf16[48,1792]{1,0:T(8,128)(2,1)S(1)}, bf16[48,1792]{1,0:T(8,128)(2,1)S(1)}, u32[]{:S(2)}, u32[]{:S(2)}) collective-permute-start(bf16[48,1792]{1,0:T(8,128)(2,1)S(1)} %get-tuple-element.79), channel_id=1, source_target_pairs={{0,28},{4,24},{8,20},{12,16},{1,29},{5,25},{9,21},{13,17},{2,30},{... | collective-permute-start | bytes 516104 | tf_op jit(solution)/shard_map/ppermute | solution.py:387
  67.4 9.4 %collective-permute-start.21 = (bf16[48,1792]{1,0:T(8,128)(2,1)S(1)}, bf16[48,1792]{1,0:T(8,128)(2,1)S(1)}, u32[]{:S(2)}, u32[]{:S(2)}) collective-permute-start(bf16[48,1792]{1,0:T(8,128)(2,1)S(1)} %get-tuple-element.80), channel_id=1, source_target_pairs={{16,20},{20,16},{24,28},{28,24},{17,21},{21,17},{25,29},{29,25},{1... | collective-permute-start | bytes 516104 | tf_op jit(solution)/shard_map/ppermute | solution.py:376
  81.7 7.6 %collective-permute-start.24 = (bf16[104,1024]{1,0:T(8,128)(2,1)S(1)}, bf16[104,1024]{1,0:T(8,128)(2,1)S(1)}, u32[]{:S(2)}, u32[]{:S(2)}) collective-permute-start(bf16[104,1024]{1,0:T(8,128)(2,1)S(1)} %shard_map.73.refs_0_), channel_id=1, source_target_pairs={{0,2},{1,3},{2,0},{3,1},{4,6},{5,7},{6,4},{7,5},{8,10},{9,11},{10,... | collective-permute-start | bytes 638984 | tf_op jit(solution)/shard_map/ppermute | solution.py:351
  88.1 7.6 %collective-permute-start.31 = (bf16[104,1024]{1,0:T(8,128)(2,1)S(1)}, bf16[104,1024]{1,0:T(8,128)(2,1)S(1)}, u32[]{:S(2)}, u32[]{:S(2)}) collective-permute-start(bf16[104,1024]{1,0:T(8,128)(2,1)S(1)} %shard_map.79.refs_1_), channel_id=1, source_target_pairs={{0,2},{1,3},{2,0},{3,1},{4,6},{5,7},{6,4},{7,5},{8,10},{9,11},{10,... | collective-permute-start | bytes 638984 | tf_op jit(solution)/shard_map/ppermute | solution.py:351
  91.7 13.2 %collective-permute-start.27 = (bf16[48,1792]{1,0:T(8,128)(2,1)S(1)}, bf16[48,1792]{1,0:T(8,128)(2,1)S(1)}, u32[]{:S(2)}, u32[]{:S(2)}) collective-permute-start(bf16[48,1792]{1,0:T(8,128)(2,1)S(1)} %get-tuple-element.87), channel_id=1, source_target_pairs={{0,8},{4,12},{8,0},{12,4},{1,9},{5,13},{9,1},{13,5},{2,10},{6,14},... | collective-permute-start | bytes 516104 | tf_op jit(solution)/shard_map/ppermute | solution.py:363
  95.9 9.1 %collective-permute-start.26 = (bf16[24,1792]{1,0:T(8,128)(2,1)S(1)}, bf16[24,1792]{1,0:T(8,128)(2,1)S(1)}, u32[]{:S(2)}, u32[]{:S(2)}) collective-permute-start(bf16[24,1792]{1,0:T(8,128)(2,1)S(1)} %get-tuple-element.86), channel_id=1, source_target_pairs={{0,4},{4,0},{8,12},{12,8},{1,5},{5,1},{9,13},{13,9},{2,6},{6,2},{1... | collective-permute-start | bytes 258056 | tf_op jit(solution)/shard_map/ppermute | solution.py:363
  100.5 6.1 %collective-permute-start.33 = (bf16[24,1792]{1,0:T(8,128)(2,1)S(1)}, bf16[24,1792]{1,0:T(8,128)(2,1)S(1)}, u32[]{:S(2)}, u32[]{:S(2)}) collective-permute-start(bf16[24,1792]{1,0:T(8,128)(2,1)S(1)} %get-tuple-element.92), channel_id=1, source_target_pairs={{0,4},{4,0},{8,12},{12,8},{1,5},{5,1},{9,13},{13,9},{2,6},{6,2},{1... | collective-permute-start | bytes 258056 | tf_op jit(solution)/shard_map/ppermute | solution.py:359
  101.0 9.8 %collective-permute-start.34 = (bf16[24,1792]{1,0:T(8,128)(2,1)S(1)}, bf16[24,1792]{1,0:T(8,128)(2,1)S(1)}, u32[]{:S(2)}, u32[]{:S(2)}) collective-permute-start(bf16[24,1792]{1,0:T(8,128)(2,1)S(1)} %get-tuple-element.93), channel_id=1, source_target_pairs={{0,8},{4,12},{8,0},{12,4},{1,9},{5,13},{9,1},{13,5},{2,10},{6,14},... | collective-permute-start | bytes 258056 | tf_op jit(solution)/shard_map/ppermute | solution.py:359
  102.9 7.9 %collective-permute-start.35 = (bf16[24,1792]{1,0:T(8,128)(2,1)S(1)}, bf16[24,1792]{1,0:T(8,128)(2,1)S(1)}, u32[]{:S(2)}, u32[]{:S(2)}) collective-permute-start(bf16[24,1792]{1,0:T(8,128)(2,1)S(1)} %get-tuple-element.94), channel_id=1, source_target_pairs={{0,12},{4,8},{8,4},{12,0},{1,13},{5,9},{9,5},{13,1},{2,14},{6,10},... | collective-permute-start | bytes 258056 | tf_op jit(solution)/shard_map/ppermute | solution.py:359
  104.9 6.5 %collective-permute-start.28 = (bf16[24,1792]{1,0:T(8,128)(2,1)S(1)}, bf16[24,1792]{1,0:T(8,128)(2,1)S(1)}, u32[]{:S(2)}, u32[]{:S(2)}) collective-permute-start(bf16[24,1792]{1,0:T(8,128)(2,1)S(1)} %shard_map.77), channel_id=1, source_target_pairs={{0,4},{4,0},{8,12},{12,8},{1,5},{5,1},{9,13},{13,9},{2,6},{6,2},{1... | collective-permute-start | bytes 258056 | tf_op jit(solution)/shard_map/ppermute | solution.py:363
  (17 other events, 106.9 us)

commit v10 on v9

--- a/solution.py
+++ b/solution.py
@@ -153,19 +153,19 @@
     send_rows(z, hits, rows_ref[...], outs[:-1], range(z.pieces))
 
 
-def load_kernel(z, parts, gate_up, *refs):
+def load_kernel(z, parts, experts, gate_up, *refs):
     outs, sems = refs[:-1], refs[-1]
     flat = gate_up.reshape(2 * z.width, z.units_dev)
     depth = 2 * z.width // parts
     copies = []
-    for expert in range(z.local):
+    for index, expert in enumerate(experts):
         for part in range(parts):
             rows = pl.ds(part * depth, depth)
             copies.append(
                 pltpu.make_async_copy(
                     flat.at[rows, pl.ds(expert * z.units, z.units)],
-                    outs[expert].at[rows],
-                    sems.at[expert * parts + part],
+                    outs[index].at[rows],
+                    sems.at[index * parts + part],
                 )
             )
     for copy in copies:
@@ -450,11 +450,14 @@
     received = exchanged(sent)
     gate_up = pltpu.with_memory_space_constraint(gate_up, pltpu.HBM)
     down_proj = pltpu.with_memory_space_constraint(down_proj, pltpu.HBM)
-    wide = call(
-        load_kernel, (z, parts), 1,
-        [pltpu.VMEM((2 * z.width, z.units), BF16)] * z.local,
-        [HBM], [pltpu.SemaphoreType.DMA((z.local * parts,))], gate_up, waits=[weight],
-    )
+    def load(experts, after):
+        return call(
+            load_kernel, (z, parts, experts), 1,
+            [pltpu.VMEM((2 * z.width, z.units), BF16)] * len(experts),
+            [HBM], [pltpu.SemaphoreType.DMA((len(experts) * parts,))], gate_up, waits=[after],
+        )
+
+    wide = load(range(z.local), weight)
 
     def load_down(group, after):
         return call(
@@ -493,6 +496,7 @@
         )
         if not last:
             rows, received = relayed(sent, kept, tick)
+            wide[0:1] = load(range(0, 1), kept)
     return kept.reshape(1, z.micro, z.tok, z.width)
 
 

time: 113 us -> 111 us (0.982)
  waiting for transfers between devices: 26.5 us -> 24.6 us
    ppermute x2, waiting for transfers between devices: 2.56 us -> 0.01 us  [relayed(): lax.ppermute(pieces[step - z.near], ('section', 'expert'), pairs)]
    ppermute x16, waiting for transfers between devices: 6.96 us -> 8.16 us  [swap(): return lax.ppermute(value, 'hidden', pairs)]
    pallas_call x29 -> x30, Pallas kernels: 42.7 us -> 43.3 us  [call(): pl.pallas_call(functools.partial(after_waits, len(waits), functools.parti...]
  transfers between devices with their start and end apart: 36 -> 36, of which waited for: 22 -> 21; matrix products, arithmetic and copies ran while one was open for 0% -> 0% of each run, Pallas kernels for 29% -> 30%
where the time goes in v10:
time: 111 us
  Pallas kernels  43.3 us (39%)
  starting transfers between devices  42.4 us (38%)
  waiting for transfers between devices  24.6 us (22%)
    pallas_call x30, Pallas kernels, call(): pl.pallas_call(functools.partial(after_waits, len(waits), functools.parti...  43.3 us
    ppermute x9, starting transfers between devices, exchanged(): result[step] = lax.ppermute(pieces[step], 'expert', pairs)  13.1 us
    ppermute x6, starting transfers between devices, across(): lax.ppermute(value, 'expert', [(i, i ^ step) for i in range(z.peers)])  9.85 us
    ppermute x16, waiting for transfers between devices, swap(): return lax.ppermute(value, 'hidden', pairs)  8.16 us
    ppermute x9, waiting for transfers between devices, exchanged(): result[step] = lax.ppermute(pieces[step], 'expert', pairs)  7.46 us
    ppermute x16, starting transfers between devices, swap(): return lax.ppermute(value, 'hidden', pairs)  6.88 us
    ppermute x1, starting transfers between devices, within(): return lax.ppermute(value, ('section', 'expert'), pairs)  6.23 us
    ppermute x1, waiting for transfers between devices, relayed(): rows = lax.ppermute(kept, 'section', hop)  5.91 us
  transfers between devices with their start and end apart: 36, of which 21 were waited for; matrix products, arithmetic and copies ran while one was open for 0% of the time, Pallas kernels for 30%

profile of v10, /device:TPU:2, one launch (start us, length us, event | category | flops | bytes accessed | tf_op | source)
XLA Modules:
  0.0 110.6 jit_solution(6994627054035313309)
XLA Ops:
  0.0 1.5 %shard_map.55 = (bf16[48,1792]{1,0:T(8,128)(2,1)S(1)}, bf16[48,1792]{1,0:T(8,128)(2,1)S(1)}, bf16[48,1792]{1,0:T(8,128)(2,1)S(1)}, bf16[48,1792]{1,0:T(8,128)(2,1)S(1)}, bf16[192,64]{1,0:T(8,128)(2,1)S(1)}) custom-call(s32[4,2,16]{2,1,0:T(2,128)} %bitcast.11, bf16[4,2,16]{2,1,0:T(2,128)(2,1)} %bitcast.14, bf16[64,1792]{1,0:T(8,128)(2,1)} %bitcast.8), custom_call_target="tpu_custom_call" | custom-call | tf_op jit(solution)/shard_map/pallas_call | solution.py:327
  1.5 2.6 %collective-permute-start = (bf16[48,1792]{1,0:T(8,128)(2,1)S(1)}, bf16[48,1792]{1,0:T(8,128)(2,1)S(1)}, u32[]{:S(2)}, u32[]{:S(2)}) collective-permute-start(bf16[48,1792]{1,0:T(8,128)(2,1)S(1)} %get-tuple-element.56), channel_id=1, source_target_pairs={{0,8},{4,12},{8,0},{12,4},{1,9},{5,13},{9,1},{13,5},{2,10},{6,14},... | collective-permute-start | bytes 516104 | tf_op jit(solution)/shard_map/ppermute | solution.py:359
  5.8 9.6 %shard_map.56 = (bf16[3584,1024]{1,0:T(8,128)(2,1)S(1)}, bf16[3584,1024]{1,0:T(8,128)(2,1)S(1)}, bf16[3584,1024]{1,0:T(8,128)(2,1)S(1)}, bf16[3584,1024]{1,0:T(8,128)(2,1)S(1)}) custom-call(bf16[192,64]{1,0:T(8,128)(2,1)S(1)} %get-tuple-element.50.refs_0_, bf16[1,1792,2,4096]{3,2,1,0:T(2,128)(2,1)} %refs_1_.7), custom_call_target="tpu_custom_call" | custom-call | tf_op jit(solution)/shard_map/pallas_call | solution.py:327
  15.4 3.2 %shard_map.57 = (bf16[1024,1792]{1,0:T(8,128)(2,1)S(1)}, bf16[1024,1792]{1,0:T(8,128)(2,1)S(1)}) custom-call(bf16[3584,1024]{1,0:T(8,128)(2,1)S(1)} %get-tuple-element.51.refs_0_.refs_2_, bf16[1,4096,1792]{2,1,0:T(8,128)(2,1)} %refs_1_.6), custom_call_target="tpu_custom_call" | custom-call | tf_op jit(solution)/shard_map/pallas_call | solution.py:327
  18.6 3.2 %shard_map.58 = (f32[112,1024]{1,0:T(8,128)S(1)}, bf16[56,1024]{1,0:T(8,128)(2,1)S(1)}, bf16[56,1024]{1,0:T(8,128)(2,1)S(1)}) custom-call(bf16[1024,1792]{1,0:T(8,128)(2,1)S(1)} %get-tuple-element.52.refs_0_, bf16[3584,1024]{1,0:T(8,128)(2,1)S(1)} %get-tuple-element.54.refs_1_, bf16[3584,1024]{1,0:T(8,128)(2,1)S(1)} %get-tuple-element.55.refs_2_, ...), custom_call_target="tpu_custom_call" | custom-call | tf_op jit(solution)/shard_map/pallas_call | solution.py:327
  23.5 1.6 %collective-permute-start.5 = (bf16[104,1024]{1,0:T(8,128)(2,1)S(1)}, bf16[104,1024]{1,0:T(8,128)(2,1)S(1)}, u32[]{:S(2)}, u32[]{:S(2)}) collective-permute-start(bf16[104,1024]{1,0:T(8,128)(2,1)S(1)} %shard_map.59.refs_0_), channel_id=1, source_target_pairs={{0,2},{1,3},{2,0},{3,1},{4,6},{5,7},{6,4},{7,5},{8,10},{9,11},{10,... | collective-permute-start | bytes 638984 | tf_op jit(solution)/shard_map/ppermute | solution.py:351
  25.0 3.2 %shard_map.65 = (f32[112,1024]{1,0:T(8,128)S(1)}, bf16[56,1024]{1,0:T(8,128)(2,1)S(1)}, bf16[56,1024]{1,0:T(8,128)(2,1)S(1)}) custom-call(bf16[104,1024]{1,0:T(8,128)(2,1)S(1)} %shard_map.59.refs_0_, bf16[3584,1024]{1,0:T(8,128)(2,1)S(1)} %get-tuple-element.68.refs_1_, bf16[3584,1024]{1,0:T(8,128)(2,1)S(1)} %get-tuple-element.51.refs_0_.refs_2_, ...), custom_call_target="tpu_custom_call" | custom-call | tf_op jit(solution)/shard_map/pallas_call | solution.py:327
  33.5 3.8 %collective-permute-start.8 = (bf16[48,1792]{1,0:T(8,128)(2,1)S(1)}, bf16[48,1792]{1,0:T(8,128)(2,1)S(1)}, u32[]{:S(2)}, u32[]{:S(2)}) collective-permute-start(bf16[48,1792]{1,0:T(8,128)(2,1)S(1)} %get-tuple-element.65), channel_id=1, source_target_pairs={{0,8},{4,12},{8,0},{12,4},{1,9},{5,13},{9,1},{13,5},{2,10},{6,14},... | collective-permute-start | bytes 516104 | tf_op jit(solution)/shard_map/ppermute | solution.py:363
  37.3 3.2 %shard_map.64 = (bf16[1024,1792]{1,0:T(8,128)(2,1)S(1)}, bf16[1024,1792]{1,0:T(8,128)(2,1)S(1)}) custom-call(bf16[24,1792]{1,0:T(8,128)(2,1)S(1)} %get-tuple-element.63.refs_0_.refs_3_, bf16[1,4096,1792]{2,1,0:T(8,128)(2,1)} %refs_1_.6), custom_call_target="tpu_custom_call" | custom-call | tf_op jit(solution)/shard_map/pallas_call | solution.py:327
  42.9 1.6 %collective-permute-start.14 = (bf16[24,1792]{1,0:T(8,128)(2,1)S(1)}, bf16[24,1792]{1,0:T(8,128)(2,1)S(1)}, u32[]{:S(2)}, u32[]{:S(2)}) collective-permute-start(bf16[24,1792]{1,0:T(8,128)(2,1)S(1)} %get-tuple-element.73), channel_id=1, source_target_pairs={{0,4},{4,0},{8,12},{12,8},{1,5},{5,1},{9,13},{13,9},{2,6},{6,2},{1... | collective-permute-start | bytes 258056 | tf_op jit(solution)/shard_map/ppermute | solution.py:359
  45.2 2.2 %collective-permute-start.16 = (bf16[24,1792]{1,0:T(8,128)(2,1)S(1)}, bf16[24,1792]{1,0:T(8,128)(2,1)S(1)}, u32[]{:S(2)}, u32[]{:S(2)}) collective-permute-start(bf16[24,1792]{1,0:T(8,128)(2,1)S(1)} %get-tuple-element.75), channel_id=1, source_target_pairs={{0,12},{4,8},{8,4},{12,0},{1,13},{5,9},{9,5},{13,1},{2,14},{6,10},... | collective-permute-start | bytes 258056 | tf_op jit(solution)/shard_map/ppermute | solution.py:359
  48.2 2.4 %collective-permute-start.17 = (s32[4,2,16]{2,1,0:T(2,128)S(1)}, s32[4,2,16]{2,1,0:T(2,128)S(1)}, u32[]{:S(2)}, u32[]{:S(2)}) collective-permute-start(s32[4,2,16]{2,1,0:T(2,128)S(1)} %get-tuple-element.76), channel_id=1, source_target_pairs={{16,0},{17,1},{18,2},{19,3},{20,4},{21,5},{22,6},{23,7},{24,8},{25... | collective-permute-start | bytes 1544 | tf_op jit(solution)/shard_map/ppermute | solution.py:488
  51.9 1.6 %collective-permute-done.15.refs_9_ = bf16[24,1792]{1,0:T(8,128)(2,1)S(1)} collective-permute-done((bf16[24,1792]{1,0:T(8,128)(2,1)S(1)}, bf16[24,1792]{1,0:T(8,128)(2,1)S(1)}, u32[]{:S(2)}, u32[]{:S(2)}) %collective-permute-start.15) | collective-permute-done | bytes 86048 | tf_op jit(solution)/shard_map/ppermute | solution.py:359
  59.5 5.9 %collective-permute-done.18.refs_1_ = bf16[64,1792]{1,0:T(8,128)(2,1)S(1)} collective-permute-done((bf16[64,1792]{1,0:T(8,128)(2,1)S(1)}, bf16[64,1792]{1,0:T(8,128)(2,1)S(1)}, u32[]{:S(2)}, u32[]{:S(2)}) %collective-permute-start.18) | collective-permute-done | bytes 229408 | tf_op jit(solution)/shard_map/ppermute | solution.py:380
  65.9 6.2 %collective-permute-start.21 = (bf16[48,1792]{1,0:T(8,128)(2,1)S(1)}, bf16[48,1792]{1,0:T(8,128)(2,1)S(1)}, u32[]{:S(2)}, u32[]{:S(2)}) collective-permute-start(bf16[48,1792]{1,0:T(8,128)(2,1)S(1)} %get-tuple-element.80), channel_id=1, source_target_pairs={{16,20},{20,16},{24,28},{28,24},{17,21},{21,17},{25,29},{29,25},{1... | collective-permute-start | bytes 516104 | tf_op jit(solution)/shard_map/ppermute | solution.py:376
  72.1 3.2 %shard_map.71.refs_1_ = bf16[3584,1024]{1,0:T(8,128)(2,1)S(1)} custom-call(bf16[64,1792]{1,0:T(8,128)(2,1)S(1)} %get-tuple-element.77.refs_0_.refs_2_, bf16[1,1792,2,4096]{3,2,1,0:T(2,128)(2,1)} %refs_1_.7), custom_call_target="tpu_custom_call" | custom-call | tf_op jit(solution)/shard_map/pallas_call | solution.py:327
  75.4 3.2 %shard_map.73 = (f32[112,1024]{1,0:T(8,128)S(1)}, bf16[56,1024]{1,0:T(8,128)(2,1)S(1)}, bf16[56,1024]{1,0:T(8,128)(2,1)S(1)}) custom-call(bf16[1024,1792]{1,0:T(8,128)(2,1)S(1)} %get-tuple-element.52.refs_0_, bf16[3584,1024]{1,0:T(8,128)(2,1)S(1)} %shard_map.71.refs_1_, bf16[3584,1024]{1,0:T(8,128)(2,1)S(1)} %get-tuple-element.55.refs_2_, ...), custom_call_target="tpu_custom_call" | custom-call | tf_op jit(solution)/shard_map/pallas_call | solution.py:327
  80.2 1.7 %collective-permute-start.24 = (bf16[104,1024]{1,0:T(8,128)(2,1)S(1)}, bf16[104,1024]{1,0:T(8,128)(2,1)S(1)}, u32[]{:S(2)}, u32[]{:S(2)}) collective-permute-start(bf16[104,1024]{1,0:T(8,128)(2,1)S(1)} %shard_map.74.refs_0_), channel_id=1, source_target_pairs={{0,2},{1,3},{2,0},{3,1},{4,6},{5,7},{6,4},{7,5},{8,10},{9,11},{10,... | collective-permute-start | bytes 638984 | tf_op jit(solution)/shard_map/ppermute | solution.py:351
  81.9 3.2 %shard_map.79 = (f32[112,1024]{1,0:T(8,128)S(1)}, bf16[56,1024]{1,0:T(8,128)(2,1)S(1)}, bf16[56,1024]{1,0:T(8,128)(2,1)S(1)}) custom-call(bf16[104,1024]{1,0:T(8,128)(2,1)S(1)} %shard_map.74.refs_0_, bf16[3584,1024]{1,0:T(8,128)(2,1)S(1)} %get-tuple-element.68.refs_1_, bf16[3584,1024]{1,0:T(8,128)(2,1)S(1)} %get-tuple-element.51.refs_0_.refs_2_, ...), custom_call_target="tpu_custom_call" | custom-call | tf_op jit(solution)/shard_map/pallas_call | solution.py:327
  90.2 2.6 %collective-permute-start.27 = (bf16[48,1792]{1,0:T(8,128)(2,1)S(1)}, bf16[48,1792]{1,0:T(8,128)(2,1)S(1)}, u32[]{:S(2)}, u32[]{:S(2)}) collective-permute-start(bf16[48,1792]{1,0:T(8,128)(2,1)S(1)} %get-tuple-element.87), channel_id=1, source_target_pairs={{0,8},{4,12},{8,0},{12,4},{1,9},{5,13},{9,1},{13,5},{2,10},{6,14},... | collective-permute-start | bytes 516104 | tf_op jit(solution)/shard_map/ppermute | solution.py:363
  92.8 1.5 %collective-permute-done.31.refs_2_ = bf16[104,1024]{1,0:T(8,128)(2,1)S(1)} collective-permute-done((bf16[104,1024]{1,0:T(8,128)(2,1)S(1)}, bf16[104,1024]{1,0:T(8,128)(2,1)S(1)}, u32[]{:S(2)}, u32[]{:S(2)}) %collective-permute-start.31) | collective-permute-done | bytes 213024 | tf_op jit(solution)/shard_map/ppermute | solution.py:351
  94.5 2.7 %collective-permute-start.26 = (bf16[24,1792]{1,0:T(8,128)(2,1)S(1)}, bf16[24,1792]{1,0:T(8,128)(2,1)S(1)}, u32[]{:S(2)}, u32[]{:S(2)}) collective-permute-start(bf16[24,1792]{1,0:T(8,128)(2,1)S(1)} %get-tuple-element.86), channel_id=1, source_target_pairs={{0,4},{4,0},{8,12},{12,8},{1,5},{5,1},{9,13},{13,9},{2,6},{6,2},{1... | collective-permute-start | bytes 258056 | tf_op jit(solution)/shard_map/ppermute | solution.py:363
  100.8 2.5 %collective-permute-start.35 = (bf16[24,1792]{1,0:T(8,128)(2,1)S(1)}, bf16[24,1792]{1,0:T(8,128)(2,1)S(1)}, u32[]{:S(2)}, u32[]{:S(2)}) collective-permute-start(bf16[24,1792]{1,0:T(8,128)(2,1)S(1)} %get-tuple-element.94), channel_id=1, source_target_pairs={{0,12},{4,8},{8,4},{12,0},{1,13},{5,9},{9,5},{13,1},{2,14},{6,10},... | collective-permute-start | bytes 258056 | tf_op jit(solution)/shard_map/ppermute | solution.py:359
  104.5 4.7 %collective-permute-done.34.refs_9_ = bf16[24,1792]{1,0:T(8,128)(2,1)S(1)} collective-permute-done((bf16[24,1792]{1,0:T(8,128)(2,1)S(1)}, bf16[24,1792]{1,0:T(8,128)(2,1)S(1)}, u32[]{:S(2)}, u32[]{:S(2)}) %collective-permute-start.34) | collective-permute-done | bytes 86048 | tf_op jit(solution)/shard_map/ppermute | solution.py:359
  (82 shorter events, 33.1 us)
Async XLA Ops:
  1.5 17.1 %collective-permute-start = (bf16[48,1792]{1,0:T(8,128)(2,1)S(1)}, bf16[48,1792]{1,0:T(8,128)(2,1)S(1)}, u32[]{:S(2)}, u32[]{:S(2)}) collective-permute-start(bf16[48,1792]{1,0:T(8,128)(2,1)S(1)} %get-tuple-element.56), channel_id=1, source_target_pairs={{0,8},{4,12},{8,0},{12,4},{1,9},{5,13},{9,1},{13,5},{2,10},{6,14},... | collective-permute-start | bytes 516104 | tf_op jit(solution)/shard_map/ppermute | solution.py:359
  4.2 14.4 %collective-permute-start.1 = (bf16[48,1792]{1,0:T(8,128)(2,1)S(1)}, bf16[48,1792]{1,0:T(8,128)(2,1)S(1)}, u32[]{:S(2)}, u32[]{:S(2)}) collective-permute-start(bf16[48,1792]{1,0:T(8,128)(2,1)S(1)} %get-tuple-element.57), channel_id=1, source_target_pairs={{0,12},{4,8},{8,4},{12,0},{1,13},{5,9},{9,5},{13,1},{2,14},{6,10},... | collective-permute-start | bytes 516104 | tf_op jit(solution)/shard_map/ppermute | solution.py:359
  5.5 13.1 %collective-permute-start.2 = (bf16[48,1792]{1,0:T(8,128)(2,1)S(1)}, bf16[48,1792]{1,0:T(8,128)(2,1)S(1)}, u32[]{:S(2)}, u32[]{:S(2)}) collective-permute-start(bf16[48,1792]{1,0:T(8,128)(2,1)S(1)} %get-tuple-element.58), channel_id=1, source_target_pairs={{0,4},{4,0},{8,12},{12,8},{1,5},{5,1},{9,13},{13,9},{2,6},{6,2},{1... | collective-permute-start | bytes 516104 | tf_op jit(solution)/shard_map/ppermute | solution.py:359
  23.5 7.6 %collective-permute-start.5 = (bf16[104,1024]{1,0:T(8,128)(2,1)S(1)}, bf16[104,1024]{1,0:T(8,128)(2,1)S(1)}, u32[]{:S(2)}, u32[]{:S(2)}) collective-permute-start(bf16[104,1024]{1,0:T(8,128)(2,1)S(1)} %shard_map.59.refs_0_), channel_id=1, source_target_pairs={{0,2},{1,3},{2,0},{3,1},{4,6},{5,7},{6,4},{7,5},{8,10},{9,11},{10,... | collective-permute-start | bytes 638984 | tf_op jit(solution)/shard_map/ppermute | solution.py:351
  29.8 10.6 %collective-permute-start.12 = (bf16[104,1024]{1,0:T(8,128)(2,1)S(1)}, bf16[104,1024]{1,0:T(8,128)(2,1)S(1)}, u32[]{:S(2)}, u32[]{:S(2)}) collective-permute-start(bf16[104,1024]{1,0:T(8,128)(2,1)S(1)} %shard_map.66.refs_1_), channel_id=1, source_target_pairs={{0,2},{1,3},{2,0},{3,1},{4,6},{5,7},{6,4},{7,5},{8,10},{9,11},{10,... | collective-permute-start | bytes 638984 | tf_op jit(solution)/shard_map/ppermute | solution.py:351
  33.5 13.9 %collective-permute-start.8 = (bf16[48,1792]{1,0:T(8,128)(2,1)S(1)}, bf16[48,1792]{1,0:T(8,128)(2,1)S(1)}, u32[]{:S(2)}, u32[]{:S(2)}) collective-permute-start(bf16[48,1792]{1,0:T(8,128)(2,1)S(1)} %get-tuple-element.65), channel_id=1, source_target_pairs={{0,8},{4,12},{8,0},{12,4},{1,9},{5,13},{9,1},{13,5},{2,10},{6,14},... | collective-permute-start | bytes 516104 | tf_op jit(solution)/shard_map/ppermute | solution.py:363
  40.7 7.4 %collective-permute-start.7 = (bf16[24,1792]{1,0:T(8,128)(2,1)S(1)}, bf16[24,1792]{1,0:T(8,128)(2,1)S(1)}, u32[]{:S(2)}, u32[]{:S(2)}) collective-permute-start(bf16[24,1792]{1,0:T(8,128)(2,1)S(1)} %get-tuple-element.64), channel_id=1, source_target_pairs={{0,4},{4,0},{8,12},{12,8},{1,5},{5,1},{9,13},{13,9},{2,6},{6,2},{1... | collective-permute-start | bytes 258056 | tf_op jit(solution)/shard_map/ppermute | solution.py:363
  42.9 9.0 %collective-permute-start.14 = (bf16[24,1792]{1,0:T(8,128)(2,1)S(1)}, bf16[24,1792]{1,0:T(8,128)(2,1)S(1)}, u32[]{:S(2)}, u32[]{:S(2)}) collective-permute-start(bf16[24,1792]{1,0:T(8,128)(2,1)S(1)} %get-tuple-element.73), channel_id=1, source_target_pairs={{0,4},{4,0},{8,12},{12,8},{1,5},{5,1},{9,13},{13,9},{2,6},{6,2},{1... | collective-permute-start | bytes 258056 | tf_op jit(solution)/shard_map/ppermute | solution.py:359
  44.6 9.0 %collective-permute-start.15 = (bf16[24,1792]{1,0:T(8,128)(2,1)S(1)}, bf16[24,1792]{1,0:T(8,128)(2,1)S(1)}, u32[]{:S(2)}, u32[]{:S(2)}) collective-permute-start(bf16[24,1792]{1,0:T(8,128)(2,1)S(1)} %get-tuple-element.74), channel_id=1, source_target_pairs={{0,8},{4,12},{8,0},{12,4},{1,9},{5,13},{9,1},{13,5},{2,10},{6,14},... | collective-permute-start | bytes 258056 | tf_op jit(solution)/shard_map/ppermute | solution.py:359
  45.2 8.3 %collective-permute-start.16 = (bf16[24,1792]{1,0:T(8,128)(2,1)S(1)}, bf16[24,1792]{1,0:T(8,128)(2,1)S(1)}, u32[]{:S(2)}, u32[]{:S(2)}) collective-permute-start(bf16[24,1792]{1,0:T(8,128)(2,1)S(1)} %get-tuple-element.75), channel_id=1, source_target_pairs={{0,12},{4,8},{8,4},{12,0},{1,13},{5,9},{9,5},{13,1},{2,14},{6,10},... | collective-permute-start | bytes 258056 | tf_op jit(solution)/shard_map/ppermute | solution.py:359
  47.4 7.4 %collective-permute-start.9 = (bf16[24,1792]{1,0:T(8,128)(2,1)S(1)}, bf16[24,1792]{1,0:T(8,128)(2,1)S(1)}, u32[]{:S(2)}, u32[]{:S(2)}) collective-permute-start(bf16[24,1792]{1,0:T(8,128)(2,1)S(1)} %shard_map.63), channel_id=1, source_target_pairs={{0,4},{4,0},{8,12},{12,8},{1,5},{5,1},{9,13},{13,9},{2,6},{6,2},{1... | collective-permute-start | bytes 258056 | tf_op jit(solution)/shard_map/ppermute | solution.py:363
  48.2 3.7 %collective-permute-start.17 = (s32[4,2,16]{2,1,0:T(2,128)S(1)}, s32[4,2,16]{2,1,0:T(2,128)S(1)}, u32[]{:S(2)}, u32[]{:S(2)}) collective-permute-start(s32[4,2,16]{2,1,0:T(2,128)S(1)} %get-tuple-element.76), channel_id=1, source_target_pairs={{16,0},{17,1},{18,2},{19,3},{20,4},{21,5},{22,6},{23,7},{24,8},{25... | collective-permute-start | bytes 1544 | tf_op jit(solution)/shard_map/ppermute | solution.py:488
  55.6 9.8 %collective-permute-start.18 = (bf16[64,1792]{1,0:T(8,128)(2,1)S(1)}, bf16[64,1792]{1,0:T(8,128)(2,1)S(1)}, u32[]{:S(2)}, u32[]{:S(2)}) collective-permute-start(bf16[64,1792]{1,0:T(8,128)(2,1)S(1)} %get-tuple-element.77.refs_0_.refs_2_), channel_id=1, source_target_pairs={{0,16},{1,17},{2,18},{3,19},{4,20},{5,21},{6,22},{7,23},{8,24},{9,... | collective-permute-start | bytes 688136 | tf_op jit(solution)/shard_map/ppermute | solution.py:380
  56.9 18.5 %collective-permute-start.19 = (bf16[48,1792]{1,0:T(8,128)(2,1)S(1)}, bf16[48,1792]{1,0:T(8,128)(2,1)S(1)}, u32[]{:S(2)}, u32[]{:S(2)}) collective-permute-start(bf16[48,1792]{1,0:T(8,128)(2,1)S(1)} %get-tuple-element.78), channel_id=1, source_target_pairs={{0,24},{4,28},{8,16},{12,20},{1,25},{5,29},{9,17},{13,21},{2,26},{... | collective-permute-start | bytes 516104 | tf_op jit(solution)/shard_map/ppermute | solution.py:387
  58.2 17.2 %collective-permute-start.20 = (bf16[48,1792]{1,0:T(8,128)(2,1)S(1)}, bf16[48,1792]{1,0:T(8,128)(2,1)S(1)}, u32[]{:S(2)}, u32[]{:S(2)}) collective-permute-start(bf16[48,1792]{1,0:T(8,128)(2,1)S(1)} %get-tuple-element.79), channel_id=1, source_target_pairs={{0,28},{4,24},{8,20},{12,16},{1,29},{5,25},{9,21},{13,17},{2,30},{... | collective-permute-start | bytes 516104 | tf_op jit(solution)/shard_map/ppermute | solution.py:387
  65.9 9.5 %collective-permute-start.21 = (bf16[48,1792]{1,0:T(8,128)(2,1)S(1)}, bf16[48,1792]{1,0:T(8,128)(2,1)S(1)}, u32[]{:S(2)}, u32[]{:S(2)}) collective-permute-start(bf16[48,1792]{1,0:T(8,128)(2,1)S(1)} %get-tuple-element.80), channel_id=1, source_target_pairs={{16,20},{20,16},{24,28},{28,24},{17,21},{21,17},{25,29},{29,25},{1... | collective-permute-start | bytes 516104 | tf_op jit(solution)/shard_map/ppermute | solution.py:376
  80.2 7.6 %collective-permute-start.24 = (bf16[104,1024]{1,0:T(8,128)(2,1)S(1)}, bf16[104,1024]{1,0:T(8,128)(2,1)S(1)}, u32[]{:S(2)}, u32[]{:S(2)}) collective-permute-start(bf16[104,1024]{1,0:T(8,128)(2,1)S(1)} %shard_map.74.refs_0_), channel_id=1, source_target_pairs={{0,2},{1,3},{2,0},{3,1},{4,6},{5,7},{6,4},{7,5},{8,10},{9,11},{10,... | collective-permute-start | bytes 638984 | tf_op jit(solution)/shard_map/ppermute | solution.py:351
  86.7 7.6 %collective-permute-start.31 = (bf16[104,1024]{1,0:T(8,128)(2,1)S(1)}, bf16[104,1024]{1,0:T(8,128)(2,1)S(1)}, u32[]{:S(2)}, u32[]{:S(2)}) collective-permute-start(bf16[104,1024]{1,0:T(8,128)(2,1)S(1)} %shard_map.80.refs_1_), channel_id=1, source_target_pairs={{0,2},{1,3},{2,0},{3,1},{4,6},{5,7},{6,4},{7,5},{8,10},{9,11},{10,... | collective-permute-start | bytes 638984 | tf_op jit(solution)/shard_map/ppermute | solution.py:351
  90.2 13.1 %collective-permute-start.27 = (bf16[48,1792]{1,0:T(8,128)(2,1)S(1)}, bf16[48,1792]{1,0:T(8,128)(2,1)S(1)}, u32[]{:S(2)}, u32[]{:S(2)}) collective-permute-start(bf16[48,1792]{1,0:T(8,128)(2,1)S(1)} %get-tuple-element.87), channel_id=1, source_target_pairs={{0,8},{4,12},{8,0},{12,4},{1,9},{5,13},{9,1},{13,5},{2,10},{6,14},... | collective-permute-start | bytes 516104 | tf_op jit(solution)/shard_map/ppermute | solution.py:363
  94.5 8.9 %collective-permute-start.26 = (bf16[24,1792]{1,0:T(8,128)(2,1)S(1)}, bf16[24,1792]{1,0:T(8,128)(2,1)S(1)}, u32[]{:S(2)}, u32[]{:S(2)}) collective-permute-start(bf16[24,1792]{1,0:T(8,128)(2,1)S(1)} %get-tuple-element.86), channel_id=1, source_target_pairs={{0,4},{4,0},{8,12},{12,8},{1,5},{5,1},{9,13},{13,9},{2,6},{6,2},{1... | collective-permute-start | bytes 258056 | tf_op jit(solution)/shard_map/ppermute | solution.py:363
  98.9 5.7 %collective-permute-start.33 = (bf16[24,1792]{1,0:T(8,128)(2,1)S(1)}, bf16[24,1792]{1,0:T(8,128)(2,1)S(1)}, u32[]{:S(2)}, u32[]{:S(2)}) collective-permute-start(bf16[24,1792]{1,0:T(8,128)(2,1)S(1)} %get-tuple-element.92), channel_id=1, source_target_pairs={{0,4},{4,0},{8,12},{12,8},{1,5},{5,1},{9,13},{13,9},{2,6},{6,2},{1... | collective-permute-start | bytes 258056 | tf_op jit(solution)/shard_map/ppermute | solution.py:359
  99.4 9.8 %collective-permute-start.34 = (bf16[24,1792]{1,0:T(8,128)(2,1)S(1)}, bf16[24,1792]{1,0:T(8,128)(2,1)S(1)}, u32[]{:S(2)}, u32[]{:S(2)}) collective-permute-start(bf16[24,1792]{1,0:T(8,128)(2,1)S(1)} %get-tuple-element.93), channel_id=1, source_target_pairs={{0,8},{4,12},{8,0},{12,4},{1,9},{5,13},{9,1},{13,5},{2,10},{6,14},... | collective-permute-start | bytes 258056 | tf_op jit(solution)/shard_map/ppermute | solution.py:359
  100.8 8.4 %collective-permute-start.35 = (bf16[24,1792]{1,0:T(8,128)(2,1)S(1)}, bf16[24,1792]{1,0:T(8,128)(2,1)S(1)}, u32[]{:S(2)}, u32[]{:S(2)}) collective-permute-start(bf16[24,1792]{1,0:T(8,128)(2,1)S(1)} %get-tuple-element.94), channel_id=1, source_target_pairs={{0,12},{4,8},{8,4},{12,0},{1,13},{5,9},{9,5},{13,1},{2,14},{6,10},... | collective-permute-start | bytes 258056 | tf_op jit(solution)/shard_map/ppermute | solution.py:359
  103.3 6.3 %collective-permute-start.28 = (bf16[24,1792]{1,0:T(8,128)(2,1)S(1)}, bf16[24,1792]{1,0:T(8,128)(2,1)S(1)}, u32[]{:S(2)}, u32[]{:S(2)}) collective-permute-start(bf16[24,1792]{1,0:T(8,128)(2,1)S(1)} %shard_map.78), channel_id=1, source_target_pairs={{0,4},{4,0},{8,12},{12,8},{1,5},{5,1},{9,13},{13,9},{2,6},{6,2},{1... | collective-permute-start | bytes 258056 | tf_op jit(solution)/shard_map/ppermute | solution.py:363
  (14 other events, 34.6 us)

commit v11 on v10

--- a/solution.py
+++ b/solution.py
@@ -199,7 +199,7 @@
     weights, refs = refs[:z.members], refs[z.members:]
     received, refs = refs[:z.pieces], refs[z.pieces:]
     received = [received[z.listed.index(step)] for step in range(z.pieces)]
-    own, *sent, spread, staged = refs
+    own, *sent, spread = refs
     rows = dot(z.order(), group_rows(z, group, received).astype(BF16))
     squares = rows * rows
     high = squares.astype(BF16)
@@ -220,16 +220,15 @@
             spread[expert, :, 2 * piece * block:2 * (piece + 1) * block] = both
     totals = [dot(spread[expert], weights[expert][...]) for expert in range(z.members)]
     extra = split_sums(sums, 2 * z.half)
+    sides = []
     for side in range(2):
         columns = slice(side * z.half, (side + 1) * z.half)
         gate = jnp.concatenate([total[:z.each, columns] for total in totals], axis=0)
         up = jnp.concatenate([total[z.each:, columns] for total in totals], axis=0)
-        staged[side, :z.group_each, :] = jnp.concatenate([gate, up], axis=1)
-        staged[side, z.group_each:, :] = extra
-    core = lax.axis_index("hidden") & 1
-    own[...] = staged[core]
-    rows = z.partial[0] // CUTS
-    value = staged[1 - core]
+        sides.append(jnp.concatenate([jnp.concatenate([gate, up], axis=1), extra], axis=0))
+    first = (lax.axis_index("hidden") & 1) == 0
+    own[...] = jnp.where(first, sides[0], sides[1])
+    value, rows = jnp.where(first, sides[1], sides[0]), z.partial[0] // CUTS
     for index, out in enumerate(sent):
         out[...] = value[index * rows:(index + 1) * rows].astype(BF16)
 
@@ -397,7 +396,6 @@
             [VMEM] * (z.members + z.pieces),
             [
                 pltpu.VMEM((z.members, 2 * z.each, 2 * z.width), BF16),
-                pltpu.VMEM((2,) + z.partial, F32),
             ],
             *wide[group * z.members:(group + 1) * z.members], *(received[step] for step in z.listed),
             waits=waits,

time: 111 us -> 111 us (level)
  no operation moved by 1% of the time
where the time goes in v11:
time: 111 us; the launch traced here: 110 us
  Pallas kernels  42.8 us (39%)
  starting transfers between devices  42.4 us (38%)
  waiting for transfers between devices  24.6 us (22%)
    pallas_call x30, Pallas kernels, call(): pl.pallas_call(functools.partial(after_waits, len(waits), functools.parti...  42.8 us
    ppermute x9, starting transfers between devices, exchanged(): result[step] = lax.ppermute(pieces[step], 'expert', pairs)  13.1 us
    ppermute x6, starting transfers between devices, across(): lax.ppermute(value, 'expert', [(i, i ^ step) for i in range(z.peers)])  9.89 us
    ppermute x16, waiting for transfers between devices, swap(): return lax.ppermute(value, 'hidden', pairs)  8.24 us
    ppermute x9, waiting for transfers between devices, exchanged(): result[step] = lax.ppermute(pieces[step], 'expert', pairs)  7.46 us
    ppermute x16, starting transfers between devices, swap(): return lax.ppermute(value, 'hidden', pairs)  6.88 us
    ppermute x1, starting transfers between devices, within(): return lax.ppermute(value, ('section', 'expert'), pairs)  6.23 us
    ppermute x1, waiting for transfers between devices, relayed(): rows = lax.ppermute(kept, 'section', hop)  5.91 us
  transfers between devices with their start and end apart: 36, of which 21 were waited for; matrix products, arithmetic and copies ran while one was open for 0% of the time, Pallas kernels for 30%

profile of v11, /device:TPU:2, one launch (start us, length us, event | category | flops | bytes accessed | tf_op | source)
XLA Modules:
  0.0 110.3 jit_solution(15456771194340466161)
XLA Ops:
  0.0 1.5 %shard_map.55 = (bf16[48,1792]{1,0:T(8,128)(2,1)S(1)}, bf16[48,1792]{1,0:T(8,128)(2,1)S(1)}, bf16[48,1792]{1,0:T(8,128)(2,1)S(1)}, bf16[48,1792]{1,0:T(8,128)(2,1)S(1)}, bf16[192,64]{1,0:T(8,128)(2,1)S(1)}) custom-call(s32[4,2,16]{2,1,0:T(2,128)} %bitcast.11, bf16[4,2,16]{2,1,0:T(2,128)(2,1)} %bitcast.14, bf16[64,1792]{1,0:T(8,128)(2,1)} %bitcast.8), custom_call_target="tpu_custom_call" | custom-call | tf_op jit(solution)/shard_map/pallas_call | solution.py:326
  1.5 2.6 %collective-permute-start = (bf16[48,1792]{1,0:T(8,128)(2,1)S(1)}, bf16[48,1792]{1,0:T(8,128)(2,1)S(1)}, u32[]{:S(2)}, u32[]{:S(2)}) collective-permute-start(bf16[48,1792]{1,0:T(8,128)(2,1)S(1)} %get-tuple-element.56), channel_id=1, source_target_pairs={{0,8},{4,12},{8,0},{12,4},{1,9},{5,13},{9,1},{13,5},{2,10},{6,14},... | collective-permute-start | bytes 516104 | tf_op jit(solution)/shard_map/ppermute | solution.py:358
  5.8 9.6 %shard_map.56 = (bf16[3584,1024]{1,0:T(8,128)(2,1)S(1)}, bf16[3584,1024]{1,0:T(8,128)(2,1)S(1)}, bf16[3584,1024]{1,0:T(8,128)(2,1)S(1)}, bf16[3584,1024]{1,0:T(8,128)(2,1)S(1)}) custom-call(bf16[192,64]{1,0:T(8,128)(2,1)S(1)} %get-tuple-element.50.refs_0_, bf16[1,1792,2,4096]{3,2,1,0:T(2,128)(2,1)} %refs_1_.7), custom_call_target="tpu_custom_call" | custom-call | tf_op jit(solution)/shard_map/pallas_call | solution.py:326
  15.4 3.2 %shard_map.57 = (bf16[1024,1792]{1,0:T(8,128)(2,1)S(1)}, bf16[1024,1792]{1,0:T(8,128)(2,1)S(1)}) custom-call(bf16[3584,1024]{1,0:T(8,128)(2,1)S(1)} %get-tuple-element.51.refs_0_.refs_2_, bf16[1,4096,1792]{2,1,0:T(8,128)(2,1)} %refs_1_.6), custom_call_target="tpu_custom_call" | custom-call | tf_op jit(solution)/shard_map/pallas_call | solution.py:326
  18.6 3.1 %shard_map.58 = (f32[112,1024]{1,0:T(8,128)S(1)}, bf16[56,1024]{1,0:T(8,128)(2,1)S(1)}, bf16[56,1024]{1,0:T(8,128)(2,1)S(1)}) custom-call(bf16[1024,1792]{1,0:T(8,128)(2,1)S(1)} %get-tuple-element.52.refs_0_, bf16[3584,1024]{1,0:T(8,128)(2,1)S(1)} %get-tuple-element.54.refs_1_, bf16[3584,1024]{1,0:T(8,128)(2,1)S(1)} %get-tuple-element.55.refs_2_, ...), custom_call_target="tpu_custom_call" | custom-call | tf_op jit(solution)/shard_map/pallas_call | solution.py:326
  23.3 1.6 %collective-permute-start.5 = (bf16[104,1024]{1,0:T(8,128)(2,1)S(1)}, bf16[104,1024]{1,0:T(8,128)(2,1)S(1)}, u32[]{:S(2)}, u32[]{:S(2)}) collective-permute-start(bf16[104,1024]{1,0:T(8,128)(2,1)S(1)} %shard_map.59.refs_0_), channel_id=1, source_target_pairs={{0,2},{1,3},{2,0},{3,1},{4,6},{5,7},{6,4},{7,5},{8,10},{9,11},{10,... | collective-permute-start | bytes 638984 | tf_op jit(solution)/shard_map/ppermute | solution.py:350
  24.9 3.1 %shard_map.65 = (f32[112,1024]{1,0:T(8,128)S(1)}, bf16[56,1024]{1,0:T(8,128)(2,1)S(1)}, bf16[56,1024]{1,0:T(8,128)(2,1)S(1)}) custom-call(bf16[104,1024]{1,0:T(8,128)(2,1)S(1)} %shard_map.59.refs_0_, bf16[3584,1024]{1,0:T(8,128)(2,1)S(1)} %get-tuple-element.68.refs_1_, bf16[3584,1024]{1,0:T(8,128)(2,1)S(1)} %get-tuple-element.51.refs_0_.refs_2_, ...), custom_call_target="tpu_custom_call" | custom-call | tf_op jit(solution)/shard_map/pallas_call | solution.py:326
  33.4 3.7 %collective-permute-start.8 = (bf16[48,1792]{1,0:T(8,128)(2,1)S(1)}, bf16[48,1792]{1,0:T(8,128)(2,1)S(1)}, u32[]{:S(2)}, u32[]{:S(2)}) collective-permute-start(bf16[48,1792]{1,0:T(8,128)(2,1)S(1)} %get-tuple-element.65), channel_id=1, source_target_pairs={{0,8},{4,12},{8,0},{12,4},{1,9},{5,13},{9,1},{13,5},{2,10},{6,14},... | collective-permute-start | bytes 516104 | tf_op jit(solution)/shard_map/ppermute | solution.py:362
  37.1 3.2 %shard_map.64 = (bf16[1024,1792]{1,0:T(8,128)(2,1)S(1)}, bf16[1024,1792]{1,0:T(8,128)(2,1)S(1)}) custom-call(bf16[24,1792]{1,0:T(8,128)(2,1)S(1)} %get-tuple-element.63.refs_0_.refs_3_, bf16[1,4096,1792]{2,1,0:T(8,128)(2,1)} %refs_1_.6), custom_call_target="tpu_custom_call" | custom-call | tf_op jit(solution)/shard_map/pallas_call | solution.py:326
  42.8 1.6 %collective-permute-start.14 = (bf16[24,1792]{1,0:T(8,128)(2,1)S(1)}, bf16[24,1792]{1,0:T(8,128)(2,1)S(1)}, u32[]{:S(2)}, u32[]{:S(2)}) collective-permute-start(bf16[24,1792]{1,0:T(8,128)(2,1)S(1)} %get-tuple-element.73), channel_id=1, source_target_pairs={{0,4},{4,0},{8,12},{12,8},{1,5},{5,1},{9,13},{13,9},{2,6},{6,2},{1... | collective-permute-start | bytes 258056 | tf_op jit(solution)/shard_map/ppermute | solution.py:358
  45.0 2.3 %collective-permute-start.16 = (bf16[24,1792]{1,0:T(8,128)(2,1)S(1)}, bf16[24,1792]{1,0:T(8,128)(2,1)S(1)}, u32[]{:S(2)}, u32[]{:S(2)}) collective-permute-start(bf16[24,1792]{1,0:T(8,128)(2,1)S(1)} %get-tuple-element.75), channel_id=1, source_target_pairs={{0,12},{4,8},{8,4},{12,0},{1,13},{5,9},{9,5},{13,1},{2,14},{6,10},... | collective-permute-start | bytes 258056 | tf_op jit(solution)/shard_map/ppermute | solution.py:358
  48.0 2.4 %collective-permute-start.17 = (s32[4,2,16]{2,1,0:T(2,128)S(1)}, s32[4,2,16]{2,1,0:T(2,128)S(1)}, u32[]{:S(2)}, u32[]{:S(2)}) collective-permute-start(s32[4,2,16]{2,1,0:T(2,128)S(1)} %get-tuple-element.76), channel_id=1, source_target_pairs={{16,0},{17,1},{18,2},{19,3},{20,4},{21,5},{22,6},{23,7},{24,8},{25... | collective-permute-start | bytes 1544 | tf_op jit(solution)/shard_map/ppermute | solution.py:486
  51.8 1.6 %collective-permute-done.15.refs_9_ = bf16[24,1792]{1,0:T(8,128)(2,1)S(1)} collective-permute-done((bf16[24,1792]{1,0:T(8,128)(2,1)S(1)}, bf16[24,1792]{1,0:T(8,128)(2,1)S(1)}, u32[]{:S(2)}, u32[]{:S(2)}) %collective-permute-start.15) | collective-permute-done | bytes 86048 | tf_op jit(solution)/shard_map/ppermute | solution.py:358
  59.3 5.9 %collective-permute-done.18.refs_1_ = bf16[64,1792]{1,0:T(8,128)(2,1)S(1)} collective-permute-done((bf16[64,1792]{1,0:T(8,128)(2,1)S(1)}, bf16[64,1792]{1,0:T(8,128)(2,1)S(1)}, u32[]{:S(2)}, u32[]{:S(2)}) %collective-permute-start.18) | collective-permute-done | bytes 229408 | tf_op jit(solution)/shard_map/ppermute | solution.py:379
  65.7 6.2 %collective-permute-start.21 = (bf16[48,1792]{1,0:T(8,128)(2,1)S(1)}, bf16[48,1792]{1,0:T(8,128)(2,1)S(1)}, u32[]{:S(2)}, u32[]{:S(2)}) collective-permute-start(bf16[48,1792]{1,0:T(8,128)(2,1)S(1)} %get-tuple-element.80), channel_id=1, source_target_pairs={{16,20},{20,16},{24,28},{28,24},{17,21},{21,17},{25,29},{29,25},{1... | collective-permute-start | bytes 516104 | tf_op jit(solution)/shard_map/ppermute | solution.py:375
  72.0 3.2 %shard_map.71.refs_1_ = bf16[3584,1024]{1,0:T(8,128)(2,1)S(1)} custom-call(bf16[64,1792]{1,0:T(8,128)(2,1)S(1)} %get-tuple-element.77.refs_0_.refs_2_, bf16[1,1792,2,4096]{3,2,1,0:T(2,128)(2,1)} %refs_1_.7), custom_call_target="tpu_custom_call" | custom-call | tf_op jit(solution)/shard_map/pallas_call | solution.py:326
  75.2 3.1 %shard_map.73 = (f32[112,1024]{1,0:T(8,128)S(1)}, bf16[56,1024]{1,0:T(8,128)(2,1)S(1)}, bf16[56,1024]{1,0:T(8,128)(2,1)S(1)}) custom-call(bf16[1024,1792]{1,0:T(8,128)(2,1)S(1)} %get-tuple-element.52.refs_0_, bf16[3584,1024]{1,0:T(8,128)(2,1)S(1)} %shard_map.71.refs_1_, bf16[3584,1024]{1,0:T(8,128)(2,1)S(1)} %get-tuple-element.55.refs_2_, ...), custom_call_target="tpu_custom_call" | custom-call | tf_op jit(solution)/shard_map/pallas_call | solution.py:326
  79.9 1.7 %collective-permute-start.24 = (bf16[104,1024]{1,0:T(8,128)(2,1)S(1)}, bf16[104,1024]{1,0:T(8,128)(2,1)S(1)}, u32[]{:S(2)}, u32[]{:S(2)}) collective-permute-start(bf16[104,1024]{1,0:T(8,128)(2,1)S(1)} %shard_map.74.refs_0_), channel_id=1, source_target_pairs={{0,2},{1,3},{2,0},{3,1},{4,6},{5,7},{6,4},{7,5},{8,10},{9,11},{10,... | collective-permute-start | bytes 638984 | tf_op jit(solution)/shard_map/ppermute | solution.py:350
  81.6 3.1 %shard_map.79 = (f32[112,1024]{1,0:T(8,128)S(1)}, bf16[56,1024]{1,0:T(8,128)(2,1)S(1)}, bf16[56,1024]{1,0:T(8,128)(2,1)S(1)}) custom-call(bf16[104,1024]{1,0:T(8,128)(2,1)S(1)} %shard_map.74.refs_0_, bf16[3584,1024]{1,0:T(8,128)(2,1)S(1)} %get-tuple-element.68.refs_1_, bf16[3584,1024]{1,0:T(8,128)(2,1)S(1)} %get-tuple-element.51.refs_0_.refs_2_, ...), custom_call_target="tpu_custom_call" | custom-call | tf_op jit(solution)/shard_map/pallas_call | solution.py:326
  90.0 2.6 %collective-permute-start.27 = (bf16[48,1792]{1,0:T(8,128)(2,1)S(1)}, bf16[48,1792]{1,0:T(8,128)(2,1)S(1)}, u32[]{:S(2)}, u32[]{:S(2)}) collective-permute-start(bf16[48,1792]{1,0:T(8,128)(2,1)S(1)} %get-tuple-element.87), channel_id=1, source_target_pairs={{0,8},{4,12},{8,0},{12,4},{1,9},{5,13},{9,1},{13,5},{2,10},{6,14},... | collective-permute-start | bytes 516104 | tf_op jit(solution)/shard_map/ppermute | solution.py:362
  94.1 2.7 %collective-permute-start.26 = (bf16[24,1792]{1,0:T(8,128)(2,1)S(1)}, bf16[24,1792]{1,0:T(8,128)(2,1)S(1)}, u32[]{:S(2)}, u32[]{:S(2)}) collective-permute-start(bf16[24,1792]{1,0:T(8,128)(2,1)S(1)} %get-tuple-element.86), channel_id=1, source_target_pairs={{0,4},{4,0},{8,12},{12,8},{1,5},{5,1},{9,13},{13,9},{2,6},{6,2},{1... | collective-permute-start | bytes 258056 | tf_op jit(solution)/shard_map/ppermute | solution.py:362
  99.0 1.4 %collective-permute-start.34 = (bf16[24,1792]{1,0:T(8,128)(2,1)S(1)}, bf16[24,1792]{1,0:T(8,128)(2,1)S(1)}, u32[]{:S(2)}, u32[]{:S(2)}) collective-permute-start(bf16[24,1792]{1,0:T(8,128)(2,1)S(1)} %get-tuple-element.93), channel_id=1, source_target_pairs={{0,8},{4,12},{8,0},{12,4},{1,9},{5,13},{9,1},{13,5},{2,10},{6,14},... | collective-permute-start | bytes 258056 | tf_op jit(solution)/shard_map/ppermute | solution.py:358
  100.4 2.5 %collective-permute-start.35 = (bf16[24,1792]{1,0:T(8,128)(2,1)S(1)}, bf16[24,1792]{1,0:T(8,128)(2,1)S(1)}, u32[]{:S(2)}, u32[]{:S(2)}) collective-permute-start(bf16[24,1792]{1,0:T(8,128)(2,1)S(1)} %get-tuple-element.94), channel_id=1, source_target_pairs={{0,12},{4,8},{8,4},{12,0},{1,13},{5,9},{9,5},{13,1},{2,14},{6,10},... | collective-permute-start | bytes 258056 | tf_op jit(solution)/shard_map/ppermute | solution.py:358
  104.2 4.7 %collective-permute-done.34.refs_9_ = bf16[24,1792]{1,0:T(8,128)(2,1)S(1)} collective-permute-done((bf16[24,1792]{1,0:T(8,128)(2,1)S(1)}, bf16[24,1792]{1,0:T(8,128)(2,1)S(1)}, u32[]{:S(2)}, u32[]{:S(2)}) %collective-permute-start.34) | collective-permute-done | bytes 86048 | tf_op jit(solution)/shard_map/ppermute | solution.py:358
  (82 shorter events, 33.2 us)
Async XLA Ops:
  1.5 17.1 %collective-permute-start = (bf16[48,1792]{1,0:T(8,128)(2,1)S(1)}, bf16[48,1792]{1,0:T(8,128)(2,1)S(1)}, u32[]{:S(2)}, u32[]{:S(2)}) collective-permute-start(bf16[48,1792]{1,0:T(8,128)(2,1)S(1)} %get-tuple-element.56), channel_id=1, source_target_pairs={{0,8},{4,12},{8,0},{12,4},{1,9},{5,13},{9,1},{13,5},{2,10},{6,14},... | collective-permute-start | bytes 516104 | tf_op jit(solution)/shard_map/ppermute | solution.py:358
  4.2 14.4 %collective-permute-start.1 = (bf16[48,1792]{1,0:T(8,128)(2,1)S(1)}, bf16[48,1792]{1,0:T(8,128)(2,1)S(1)}, u32[]{:S(2)}, u32[]{:S(2)}) collective-permute-start(bf16[48,1792]{1,0:T(8,128)(2,1)S(1)} %get-tuple-element.57), channel_id=1, source_target_pairs={{0,12},{4,8},{8,4},{12,0},{1,13},{5,9},{9,5},{13,1},{2,14},{6,10},... | collective-permute-start | bytes 516104 | tf_op jit(solution)/shard_map/ppermute | solution.py:358
  5.5 13.1 %collective-permute-start.2 = (bf16[48,1792]{1,0:T(8,128)(2,1)S(1)}, bf16[48,1792]{1,0:T(8,128)(2,1)S(1)}, u32[]{:S(2)}, u32[]{:S(2)}) collective-permute-start(bf16[48,1792]{1,0:T(8,128)(2,1)S(1)} %get-tuple-element.58), channel_id=1, source_target_pairs={{0,4},{4,0},{8,12},{12,8},{1,5},{5,1},{9,13},{13,9},{2,6},{6,2},{1... | collective-permute-start | bytes 516104 | tf_op jit(solution)/shard_map/ppermute | solution.py:358
  23.3 7.6 %collective-permute-start.5 = (bf16[104,1024]{1,0:T(8,128)(2,1)S(1)}, bf16[104,1024]{1,0:T(8,128)(2,1)S(1)}, u32[]{:S(2)}, u32[]{:S(2)}) collective-permute-start(bf16[104,1024]{1,0:T(8,128)(2,1)S(1)} %shard_map.59.refs_0_), channel_id=1, source_target_pairs={{0,2},{1,3},{2,0},{3,1},{4,6},{5,7},{6,4},{7,5},{8,10},{9,11},{10,... | collective-permute-start | bytes 638984 | tf_op jit(solution)/shard_map/ppermute | solution.py:350
  29.6 10.7 %collective-permute-start.12 = (bf16[104,1024]{1,0:T(8,128)(2,1)S(1)}, bf16[104,1024]{1,0:T(8,128)(2,1)S(1)}, u32[]{:S(2)}, u32[]{:S(2)}) collective-permute-start(bf16[104,1024]{1,0:T(8,128)(2,1)S(1)} %shard_map.66.refs_1_), channel_id=1, source_target_pairs={{0,2},{1,3},{2,0},{3,1},{4,6},{5,7},{6,4},{7,5},{8,10},{9,11},{10,... | collective-permute-start | bytes 638984 | tf_op jit(solution)/shard_map/ppermute | solution.py:350
  33.4 13.9 %collective-permute-start.8 = (bf16[48,1792]{1,0:T(8,128)(2,1)S(1)}, bf16[48,1792]{1,0:T(8,128)(2,1)S(1)}, u32[]{:S(2)}, u32[]{:S(2)}) collective-permute-start(bf16[48,1792]{1,0:T(8,128)(2,1)S(1)} %get-tuple-element.65), channel_id=1, source_target_pairs={{0,8},{4,12},{8,0},{12,4},{1,9},{5,13},{9,1},{13,5},{2,10},{6,14},... | collective-permute-start | bytes 516104 | tf_op jit(solution)/shard_map/ppermute | solution.py:362
  40.6 7.4 %collective-permute-start.7 = (bf16[24,1792]{1,0:T(8,128)(2,1)S(1)}, bf16[24,1792]{1,0:T(8,128)(2,1)S(1)}, u32[]{:S(2)}, u32[]{:S(2)}) collective-permute-start(bf16[24,1792]{1,0:T(8,128)(2,1)S(1)} %get-tuple-element.64), channel_id=1, source_target_pairs={{0,4},{4,0},{8,12},{12,8},{1,5},{5,1},{9,13},{13,9},{2,6},{6,2},{1... | collective-permute-start | bytes 258056 | tf_op jit(solution)/shard_map/ppermute | solution.py:362
  42.8 9.0 %collective-permute-start.14 = (bf16[24,1792]{1,0:T(8,128)(2,1)S(1)}, bf16[24,1792]{1,0:T(8,128)(2,1)S(1)}, u32[]{:S(2)}, u32[]{:S(2)}) collective-permute-start(bf16[24,1792]{1,0:T(8,128)(2,1)S(1)} %get-tuple-element.73), channel_id=1, source_target_pairs={{0,4},{4,0},{8,12},{12,8},{1,5},{5,1},{9,13},{13,9},{2,6},{6,2},{1... | collective-permute-start | bytes 258056 | tf_op jit(solution)/shard_map/ppermute | solution.py:358
  44.5 9.0 %collective-permute-start.15 = (bf16[24,1792]{1,0:T(8,128)(2,1)S(1)}, bf16[24,1792]{1,0:T(8,128)(2,1)S(1)}, u32[]{:S(2)}, u32[]{:S(2)}) collective-permute-start(bf16[24,1792]{1,0:T(8,128)(2,1)S(1)} %get-tuple-element.74), channel_id=1, source_target_pairs={{0,8},{4,12},{8,0},{12,4},{1,9},{5,13},{9,1},{13,5},{2,10},{6,14},... | collective-permute-start | bytes 258056 | tf_op jit(solution)/shard_map/ppermute | solution.py:358
  45.0 8.4 %collective-permute-start.16 = (bf16[24,1792]{1,0:T(8,128)(2,1)S(1)}, bf16[24,1792]{1,0:T(8,128)(2,1)S(1)}, u32[]{:S(2)}, u32[]{:S(2)}) collective-permute-start(bf16[24,1792]{1,0:T(8,128)(2,1)S(1)} %get-tuple-element.75), channel_id=1, source_target_pairs={{0,12},{4,8},{8,4},{12,0},{1,13},{5,9},{9,5},{13,1},{2,14},{6,10},... | collective-permute-start | bytes 258056 | tf_op jit(solution)/shard_map/ppermute | solution.py:358
  47.3 7.4 %collective-permute-start.9 = (bf16[24,1792]{1,0:T(8,128)(2,1)S(1)}, bf16[24,1792]{1,0:T(8,128)(2,1)S(1)}, u32[]{:S(2)}, u32[]{:S(2)}) collective-permute-start(bf16[24,1792]{1,0:T(8,128)(2,1)S(1)} %shard_map.63), channel_id=1, source_target_pairs={{0,4},{4,0},{8,12},{12,8},{1,5},{5,1},{9,13},{13,9},{2,6},{6,2},{1... | collective-permute-start | bytes 258056 | tf_op jit(solution)/shard_map/ppermute | solution.py:362
  48.0 3.7 %collective-permute-start.17 = (s32[4,2,16]{2,1,0:T(2,128)S(1)}, s32[4,2,16]{2,1,0:T(2,128)S(1)}, u32[]{:S(2)}, u32[]{:S(2)}) collective-permute-start(s32[4,2,16]{2,1,0:T(2,128)S(1)} %get-tuple-element.76), channel_id=1, source_target_pairs={{16,0},{17,1},{18,2},{19,3},{20,4},{21,5},{22,6},{23,7},{24,8},{25... | collective-permute-start | bytes 1544 | tf_op jit(solution)/shard_map/ppermute | solution.py:486
  55.4 9.8 %collective-permute-start.18 = (bf16[64,1792]{1,0:T(8,128)(2,1)S(1)}, bf16[64,1792]{1,0:T(8,128)(2,1)S(1)}, u32[]{:S(2)}, u32[]{:S(2)}) collective-permute-start(bf16[64,1792]{1,0:T(8,128)(2,1)S(1)} %get-tuple-element.77.refs_0_.refs_2_), channel_id=1, source_target_pairs={{0,16},{1,17},{2,18},{3,19},{4,20},{5,21},{6,22},{7,23},{8,24},{9,... | collective-permute-start | bytes 688136 | tf_op jit(solution)/shard_map/ppermute | solution.py:379
  56.7 18.5 %collective-permute-start.19 = (bf16[48,1792]{1,0:T(8,128)(2,1)S(1)}, bf16[48,1792]{1,0:T(8,128)(2,1)S(1)}, u32[]{:S(2)}, u32[]{:S(2)}) collective-permute-start(bf16[48,1792]{1,0:T(8,128)(2,1)S(1)} %get-tuple-element.78), channel_id=1, source_target_pairs={{0,24},{4,28},{8,16},{12,20},{1,25},{5,29},{9,17},{13,21},{2,26},{... | collective-permute-start | bytes 516104 | tf_op jit(solution)/shard_map/ppermute | solution.py:386
  58.0 17.2 %collective-permute-start.20 = (bf16[48,1792]{1,0:T(8,128)(2,1)S(1)}, bf16[48,1792]{1,0:T(8,128)(2,1)S(1)}, u32[]{:S(2)}, u32[]{:S(2)}) collective-permute-start(bf16[48,1792]{1,0:T(8,128)(2,1)S(1)} %get-tuple-element.79), channel_id=1, source_target_pairs={{0,28},{4,24},{8,20},{12,16},{1,29},{5,25},{9,21},{13,17},{2,30},{... | collective-permute-start | bytes 516104 | tf_op jit(solution)/shard_map/ppermute | solution.py:386
  65.7 9.5 %collective-permute-start.21 = (bf16[48,1792]{1,0:T(8,128)(2,1)S(1)}, bf16[48,1792]{1,0:T(8,128)(2,1)S(1)}, u32[]{:S(2)}, u32[]{:S(2)}) collective-permute-start(bf16[48,1792]{1,0:T(8,128)(2,1)S(1)} %get-tuple-element.80), channel_id=1, source_target_pairs={{16,20},{20,16},{24,28},{28,24},{17,21},{21,17},{25,29},{29,25},{1... | collective-permute-start | bytes 516104 | tf_op jit(solution)/shard_map/ppermute | solution.py:375
  79.9 7.6 %collective-permute-start.24 = (bf16[104,1024]{1,0:T(8,128)(2,1)S(1)}, bf16[104,1024]{1,0:T(8,128)(2,1)S(1)}, u32[]{:S(2)}, u32[]{:S(2)}) collective-permute-start(bf16[104,1024]{1,0:T(8,128)(2,1)S(1)} %shard_map.74.refs_0_), channel_id=1, source_target_pairs={{0,2},{1,3},{2,0},{3,1},{4,6},{5,7},{6,4},{7,5},{8,10},{9,11},{10,... | collective-permute-start | bytes 638984 | tf_op jit(solution)/shard_map/ppermute | solution.py:350
  86.3 7.6 %collective-permute-start.31 = (bf16[104,1024]{1,0:T(8,128)(2,1)S(1)}, bf16[104,1024]{1,0:T(8,128)(2,1)S(1)}, u32[]{:S(2)}, u32[]{:S(2)}) collective-permute-start(bf16[104,1024]{1,0:T(8,128)(2,1)S(1)} %shard_map.80.refs_1_), channel_id=1, source_target_pairs={{0,2},{1,3},{2,0},{3,1},{4,6},{5,7},{6,4},{7,5},{8,10},{9,11},{10,... | collective-permute-start | bytes 638984 | tf_op jit(solution)/shard_map/ppermute | solution.py:350
  90.0 13.0 %collective-permute-start.27 = (bf16[48,1792]{1,0:T(8,128)(2,1)S(1)}, bf16[48,1792]{1,0:T(8,128)(2,1)S(1)}, u32[]{:S(2)}, u32[]{:S(2)}) collective-permute-start(bf16[48,1792]{1,0:T(8,128)(2,1)S(1)} %get-tuple-element.87), channel_id=1, source_target_pairs={{0,8},{4,12},{8,0},{12,4},{1,9},{5,13},{9,1},{13,5},{2,10},{6,14},... | collective-permute-start | bytes 516104 | tf_op jit(solution)/shard_map/ppermute | solution.py:362
  94.1 8.9 %collective-permute-start.26 = (bf16[24,1792]{1,0:T(8,128)(2,1)S(1)}, bf16[24,1792]{1,0:T(8,128)(2,1)S(1)}, u32[]{:S(2)}, u32[]{:S(2)}) collective-permute-start(bf16[24,1792]{1,0:T(8,128)(2,1)S(1)} %get-tuple-element.86), channel_id=1, source_target_pairs={{0,4},{4,0},{8,12},{12,8},{1,5},{5,1},{9,13},{13,9},{2,6},{6,2},{1... | collective-permute-start | bytes 258056 | tf_op jit(solution)/shard_map/ppermute | solution.py:362
  98.5 5.6 %collective-permute-start.33 = (bf16[24,1792]{1,0:T(8,128)(2,1)S(1)}, bf16[24,1792]{1,0:T(8,128)(2,1)S(1)}, u32[]{:S(2)}, u32[]{:S(2)}) collective-permute-start(bf16[24,1792]{1,0:T(8,128)(2,1)S(1)} %get-tuple-element.92), channel_id=1, source_target_pairs={{0,4},{4,0},{8,12},{12,8},{1,5},{5,1},{9,13},{13,9},{2,6},{6,2},{1... | collective-permute-start | bytes 258056 | tf_op jit(solution)/shard_map/ppermute | solution.py:358
  99.0 9.8 %collective-permute-start.34 = (bf16[24,1792]{1,0:T(8,128)(2,1)S(1)}, bf16[24,1792]{1,0:T(8,128)(2,1)S(1)}, u32[]{:S(2)}, u32[]{:S(2)}) collective-permute-start(bf16[24,1792]{1,0:T(8,128)(2,1)S(1)} %get-tuple-element.93), channel_id=1, source_target_pairs={{0,8},{4,12},{8,0},{12,4},{1,9},{5,13},{9,1},{13,5},{2,10},{6,14},... | collective-permute-start | bytes 258056 | tf_op jit(solution)/shard_map/ppermute | solution.py:358
  100.4 8.4 %collective-permute-start.35 = (bf16[24,1792]{1,0:T(8,128)(2,1)S(1)}, bf16[24,1792]{1,0:T(8,128)(2,1)S(1)}, u32[]{:S(2)}, u32[]{:S(2)}) collective-permute-start(bf16[24,1792]{1,0:T(8,128)(2,1)S(1)} %get-tuple-element.94), channel_id=1, source_target_pairs={{0,12},{4,8},{8,4},{12,0},{1,13},{5,9},{9,5},{13,1},{2,14},{6,10},... | collective-permute-start | bytes 258056 | tf_op jit(solution)/shard_map/ppermute | solution.py:358
  103.0 6.3 %collective-permute-start.28 = (bf16[24,1792]{1,0:T(8,128)(2,1)S(1)}, bf16[24,1792]{1,0:T(8,128)(2,1)S(1)}, u32[]{:S(2)}, u32[]{:S(2)}) collective-permute-start(bf16[24,1792]{1,0:T(8,128)(2,1)S(1)} %shard_map.78), channel_id=1, source_target_pairs={{0,4},{4,0},{8,12},{12,8},{1,5},{5,1},{9,13},{13,9},{2,6},{6,2},{1... | collective-permute-start | bytes 258056 | tf_op jit(solution)/shard_map/ppermute | solution.py:362
  (14 other events, 34.6 us)
